TPU v7x, 512 devices: a whole 4x8x8 slice. The times are simulated.
512 devices in a mesh: expert: 8 (over z), blk: 32 (over y, x_lo, core), dp: 2 (over x_hi).
Axes of the slice: x: 4 (x_hi: 2, x_lo: 2; x = x_hi * 2 + x_lo), y: 8, z: 8, core: 2. Of those that a mesh axis runs over, the one named last changes fastest.
Arguments:
- cotangent: bfloat16 [2, 1536, 6144], P('dp', 'expert', 'blk'), may hold values from -6 to 6
- expert_ids: int32 [2, 1536, 2], P('dp', 'expert'), may hold values from 0 to 7, all different within a row; in each aligned block of 192 rows (0 to 191, 192 to 383, ..., all dimensions but the last counted through in order) at most 96 rows name the same one
- combine: float32 [2, 8, 768], P('dp', 'expert'), may hold values from 0.1 to 0.9
- gate_saved: bfloat16 [2, 8, 768, 8192], P('dp', 'expert', None, 'blk'), may hold values from -6 to 6
- up_saved: bfloat16 [2, 8, 768, 8192], P('dp', 'expert', None, 'blk'), may hold values from -6 to 6
- w_down: bfloat16 [8, 6144, 8192], P('expert', 'dp', 'blk'), may hold values from -0.0625 to 0.0625
Outputs:
- grad_gate: bfloat16 [2, 8, 768, 8192], P('dp', 'expert', None, 'blk')
- grad_up: bfloat16 [2, 8, 768, 8192], P('dp', 'expert', None, 'blk')
- grad_weight: bfloat16 [8, 6144, 8192], P('expert', 'dp', 'blk')
- grad_combine: float32 [2, 8, 768], P('dp', 'expert', 'blk')
Inputs may be any that keep to these rules, and one draw needn't show every extreme that they name: `expert_ids`: each token names 2 different experts. In each aligned block of 192 tokens (the tokens of one owner) no expert is named by more than 96 tokens, and in some block some expert is named by exactly 96.
All inputs are finite; a program needn't handle non-finite values.
Results may differ from a plain program's by a relative error of at most 0.01.
Values may be sent and summed in bfloat16 or wider, within the bound.
No kernel may reach another device: no remote copies, remote signals or barrier semaphores. Data moves between devices by JAX's collectives and lax.ppermute only.
A program may use at most 128 MiB of HBM per device.

v0:
```python
import jax
import jax.numpy as jnp
from jax import lax
from jax.sharding import PartitionSpec as P


def dispatch_tables(routing, expert_count, capacity):
    experts = jnp.arange(expert_count, dtype=jnp.int32)
    chosen = (routing[..., None] == experts).astype(jnp.int32)
    per_token = jnp.sum(chosen, axis=-2)
    earlier = jnp.cumsum(per_token, axis=-2) - per_token
    position = jnp.sum(chosen * earlier[..., None, :], axis=-1)
    target = jnp.sum(chosen * experts, axis=-1) * capacity + position
    columns = jnp.arange(expert_count * capacity, dtype=jnp.int32)
    matches = target[..., None, :, :] == columns[:, None, None]
    return jnp.sum(matches.astype(jnp.float32), axis=-1)


def local(cotangent, expert_ids, combine, gate_saved, up_saved, w_down):
    expert_count = lax.axis_size("expert")
    cycle_count = lax.axis_size("blk")
    slot_total = gate_saved.shape[2]
    capacity = slot_total // expert_count
    slice_width = cotangent.shape[2]
    table = dispatch_tables(expert_ids[0], expert_count, capacity).astype(jnp.bfloat16)
    outgoing = jnp.dot(table, cotangent[0], preferred_element_type=jnp.float32).astype(jnp.bfloat16)
    outgoing = outgoing.reshape(expert_count, capacity, slice_width)
    arrived = lax.all_to_all(outgoing, "expert", split_axis=0, concat_axis=0, tiled=True)
    gathered = lax.all_gather(arrived, "blk", axis=2, tiled=True)
    dispatched = gathered.reshape(slot_total, slice_width * cycle_count)
    columns = dispatched
    grad_hidden = jnp.dot(
        columns,
        lax.all_gather(w_down[0], "dp", axis=0, tiled=True),
        preferred_element_type=jnp.float32,
    )
    gate_float = gate_saved[0, 0].astype(jnp.float32)
    upper_float = up_saved[0, 0].astype(jnp.float32)
    combine_rows = combine[0, 0][:, None]
    sigmoid_gate = jax.nn.sigmoid(gate_float)
    activated = gate_float * sigmoid_gate
    hidden = activated * upper_float
    weighted = combine_rows * grad_hidden
    grad_gate = (
        weighted * upper_float * sigmoid_gate * (1.0 + gate_float * (1.0 - sigmoid_gate))
    ).astype(jnp.bfloat16)
    grad_upper = (weighted * activated).astype(jnp.bfloat16)
    scaled = (combine_rows * hidden).astype(jnp.bfloat16)
    columns = dispatched
    grad_weight = lax.psum_scatter(
        lax.dot_general(
            columns, scaled, (((0,), (0,)), ((), ())), preferred_element_type=jnp.float32
        ).astype(jnp.bfloat16),
        "dp",
        scatter_dimension=0,
        tiled=True,
    )
    mixing = jnp.sum(hidden * grad_hidden, axis=1)
    summed = lax.psum(mixing, "blk")
    share_size = slot_total // cycle_count
    mixed_share = lax.dynamic_slice_in_dim(
        summed, lax.axis_index("blk") * share_size, share_size, 0
    )
    return (
        grad_gate[None, None],
        grad_upper[None, None],
        grad_weight[None],
        mixed_share[None, None],
    )


def solution(mesh):
    return jax.shard_map(
        local,
        mesh=mesh,
        in_specs=(
            P("dp", "expert", "blk"),
            P("dp", "expert", None),
            P("dp", "expert", None),
            P("dp", "expert", None, "blk"),
            P("dp", "expert", None, "blk"),
            P("expert", "dp", "blk"),
        ),
        out_specs=(
            P("dp", "expert", None, "blk"),
            P("dp", "expert", None, "blk"),
            P("expert", "dp", "blk"),
            P("dp", "expert", "blk"),
        ),
        check_vma=False,
    )
```

profile of v0, /device:TPU:1, one launch (start us, length us, event | category | flops | bytes accessed | tf_op | source)
XLA Modules:
  0.0 243.5 jit_solution(6147204700956532220)
XLA Ops:
  7.2 0.0 copy-start
  7.2 0.0 copy-start.1
  7.2 0.0 all-gather.4.cloned.1.call-start
  7.2 0.7 convert_reduce_fusion.1
  8.0 0.6 reduce-window.6
  8.6 0.2 slice_reduce_fusion
  8.8 0.1 add_bitcast_fusion
  8.9 0.7 select_reduce_fusion.1
  9.6 0.2 convert_reduce_fusion
  9.8 0.0 copy-done
  9.8 0.0 copy-start.2
  9.8 0.3 convolution_convert_fusion.1
  10.1 0.0 copy-start.3
  10.1 0.4 reshape.46
  10.6 0.1 copy.38
  10.7 24.2 %all_to_all.5 = bf16[8,96,192]{1,2,0:T(8,128)(2,1)S(1)} all-to-all(bf16[8,96,192]{1,2,0:T(8,128)(2,1)S(1)} %copy.38), channel_id=1, replica_groups=mesh['expert'=8,'blk'=32,'dp'=2] {'expert'}, dimensions={0} | all-to-all | bytes 589824 | tf_op jit(solution)/shard_map/all_to_all | solution.py:28
  34.8 1.0 copy.39
  35.8 0.0 all-gather.4.cloned.1.call-update
  35.9 0.0 all-gather.6.cloned.1.call-start
  35.9 0.7 all-gather.6.cloned.1.call-update
  36.6 0.0 reduce-scatter.2.cloned.1.call-start
  36.7 0.0 copy-done.1
  36.7 0.2 copy.41
  36.9 0.0 copy-done.2
  36.9 0.2 copy.42
  37.0 0.0 copy-done.3
  37.1 79.5 %all-gather.4.cloned.1.call-done = bf16[8,96,6144]{1,0,2:T(8,128)(2,1)} async-done(((bf16[8,96,192]{1,0,2:T(8,128)(2,1)}), bf16[8,96,6144]{1,0,2:T(8,128)(2,1)}) %all-gather.4.cloned.1.call-update) | async-done | bytes 9437200 | tf_op jit(solution)/shard_map/all_gather | solution.py:29
  116.6 15.9 %copy.40 = bf16[8,96,6144]{2,1,0:T(8,128)(2,1)} copy(bf16[8,96,6144]{1,0,2:T(8,128)(2,1)} %all-gather.4.cloned.1.call-done) | data formatting | bytes 18874368 | tf_op jit(solution)/shard_map/all_gather | solution.py:29
  132.5 9.1 %convolution_convert_fusion = bf16[6144,256]{1,0:T(8,128)(2,1)} fusion(bf16[768,6144]{1,0:T(8,128)(2,1)} %bitcast.78, bf16[1,1,768,256]{2,3,1,0:T(8,128)(2,1)S(1)} %copy.41, bf16[1,1,768,256]{2,3,1,0:T(8,128)(2,1)S(1)} %copy.42, f32[768]{0:T(1024)S(1)} %reduce), kind=kOutput, calls=%fused_computation | convolution fusion | flops 2419261440 | bytes 13372416 | tf_op jit(solution)/shard_map/dot_general | solution.py:51
  141.5 0.0 reduce-scatter.2.cloned.1.call-update
  141.6 31.4 %all-gather.6.cloned.1.call-done = bf16[1,6144,256]{2,1,0:T(8,128)(2,1)} async-done(((bf16[1,3072,256]{2,1,0:T(8,128)(2,1)}), bf16[1,6144,256]{2,1,0:T(8,128)(2,1)}) %all-gather.6.cloned.1.call-update) | async-done | bytes 3145744 | tf_op jit(solution)/shard_map/all_gather | solution.py:34
  172.9 7.5 %fusion.11 = (f32[768]{0:T(1024)S(1)}, bf16[1,1,768,256]{2,3,1,0:T(8,128)(2,1)S(1)}, bf16[1,1,768,256]{2,3,1,0:T(8,128)(2,1)S(1)}) fusion(bf16[1,1,768,256]{2,3,1,0:T(8,128)(2,1)S(1)} %copy.41, bf16[1,1,768,256]{2,3,1,0:T(8,128)(2,1)S(1)} %copy.42, f32[768]{0:T(1024)S(1)} %reduce, bf16[768,6144]{1,0:T(8,128)(2,1)} %bitcast.79, ...), kind=kOutput, calls=%fused_computation.20 | convolution fusion | flops 2419653888 | bytes 14161920 | tf_op jit(solution)/shard_map/dot_general | solution.py:32
  180.5 0.9 copy.43
  181.4 0.9 copy.44
  182.3 54.0 %psum.7 = f32[768]{0:T(1024)S(1)} all-reduce(f32[768]{0:T(1024)S(1)} %get-tuple-element.26), channel_id=1, replica_groups=mesh['expert'=8,'blk'=32,'dp'=2] {'blk'}, use_global_device_ids=true, to_apply=%region_8.9 | all-reduce | flops 768 | bytes 6144 | tf_op jit(solution)/shard_map/psum | solution.py:59
  236.3 0.6 dynamic-slice_bitcast_fusion
  236.9 0.0 reduce-scatter.2.cloned.1.call-done
  (6 shorter events, 0.1 us)
Async XLA Ops:
  7.2 2.7 %copy-start = (bf16[1,192,192]{2,1,0:T(8,128)(2,1)S(1)}, bf16[1,192,192]{2,1,0:T(8,128)(2,1)}, u32[]{:S(2)}) copy-start(bf16[1,192,192]{2,1,0:T(8,128)(2,1)} %param.6) | copy-start | bytes 221188
  7.2 29.5 %copy-start.1 = (bf16[1,1,768,256]{3,2,1,0:T(8,128)(2,1)S(1)}, bf16[1,1,768,256]{3,2,1,0:T(8,128)(2,1)}, u32[]{:S(2)}) copy-start(bf16[1,1,768,256]{3,2,1,0:T(8,128)(2,1)} %param.10) | copy-start | bytes 1179652
  7.2 109.4 %all-gather.4.cloned.1.call-start = ((), (), s32[]{:S(2)}) async-start(), calls=%async_computation.2 | async-start | bytes 12976128 | tf_op jit(solution)/shard_map/all_gather | solution.py:29
  9.8 27.0 %copy-start.2 = (bf16[1,1,768,256]{3,2,1,0:T(8,128)(2,1)S(1)}, bf16[1,1,768,256]{3,2,1,0:T(8,128)(2,1)}, u32[]{:S(2)}) copy-start(bf16[1,1,768,256]{3,2,1,0:T(8,128)(2,1)} %param.9) | copy-start | bytes 1179652
  10.1 26.9 %copy-start.3 = (f32[1,1,768]{2,1,0:T(1,128)S(1)}, f32[1,1,768]{2,1,0:T(1,128)}, u32[]{:S(2)}) copy-start(f32[1,1,768]{2,1,0:T(1,128)} %param.8) | copy-start | bytes 9220
  35.9 137.1 %all-gather.6.cloned.1.call-start = ((), (), s32[]{:S(2)}) async-start(), calls=%async_computation.4 | async-start | bytes 4718592 | tf_op jit(solution)/shard_map/all_gather | solution.py:34
  36.6 200.3 %reduce-scatter.2.cloned.1.call-start = ((), (), s32[]{:S(2)}) async-start(), calls=%async_computation.3 | async-start | bytes 4718592 | tf_op jit(solution)/shard_map/reduce_scatter | solution.py:50
Sparse Core Ops, SparseCore 0:
  36.0 80.5 all-gather.3
  118.7 54.1 all-gather.5
  176.3 53.2 reduce-scatter.1
where the time goes:
time: 246 us; the launch traced here: 243 us
  waiting for transfers between devices  112 us (46%)
  blocking collectives  78.2 us (32%)
  local copies, waits for them, and re-layouts  20.4 us (8%)
  matrix products  16.9 us (7%)
  between operations  13.9 us (6%)
    all_gather x1, waiting for transfers between devices, local(): gathered = lax.all_gather(arrived, 'blk', axis=2, tiled=True)  79.5 us
    psum x1, blocking collectives, local(): summed = lax.psum(mixing, 'blk')  54 us
    all_gather x1, waiting for transfers between devices, local(): lax.all_gather(w_down[0], 'dp', axis=0, tiled=True)  31.4 us
    all_to_all x1, blocking collectives, local(): lax.all_to_all(outgoing, 'expert', split_axis=0, concat_axis=0, tiled=True)  24.2 us
    all_gather x1, local copies, waits for them, and re-layouts, local(): gathered = lax.all_gather(arrived, 'blk', axis=2, tiled=True)  15.9 us
    dot_general x1, matrix products, local(): lax.dot_general(columns, scaled, (((0,), (0,)), ((), ())), preferred_elem...  9.07 us
    dot_general x1, matrix products, local(): jnp.dot(columns, lax.all_gather(w_down[0], 'dp', axis=0, tiled=True), pre...  7.55 us
  transfers between devices with their start and end apart: 3, of which 2 were waited for; matrix products, arithmetic and copies ran while one was open for 14% of the time, Pallas kernels for 0%

commit v1 on v0

v1 whole, which is shorter than its diff:
```python
import jax
import jax.numpy as jnp
from jax import lax
from jax.sharding import Mesh, PartitionSpec as P

BF = jnp.bfloat16
F32 = jnp.float32


def one_hot_table(ids, expert_count, capacity, core):
    half = capacity // 2
    experts = jnp.arange(expert_count, dtype=jnp.int32)
    chosen = (ids[:, :, None] == experts).astype(F32)
    per_token = jnp.sum(chosen, axis=1)
    count = ids.shape[0]
    before = (jnp.arange(count)[:, None] > jnp.arange(count)[None, :]).astype(BF)
    earlier = jnp.dot(before, per_token.astype(BF), preferred_element_type=F32)
    position = jnp.sum(chosen * earlier[:, None, :], axis=-1).astype(jnp.int32)
    target = ids * capacity + position
    rows = jnp.arange(expert_count * half, dtype=jnp.int32)
    columns = (rows // half) * capacity + core * half + rows % half
    hit = (target[:, 0][None, :] == columns[:, None]) | (target[:, 1][None, :] == columns[:, None])
    return hit.astype(BF)


def make_local(ny):
    half_y = ny // 2

    def token_moves(other_core):
        def flat(y, x, c, d):
            return ((y * 2 + x) * 2 + c) * 2 + d

        pairs = []
        for y in range(ny):
            for x in range(2):
                for c in range(2):
                    for d in range(2):
                        h = y // half_y
                        to_y = (y % half_y) * 2 + x
                        to_x = 0 if d == h else 1
                        to_c = 1 - c if other_core else c
                        pairs.append((flat(y, x, c, d), flat(to_y, to_x, to_c, h)))
        return pairs

    ring = [(y * 2, ((y + 1) % ny) * 2) for y in range(ny)] + [
        (y * 2 + 1, ((y - 1) % ny) * 2 + 1) for y in range(ny)
    ]
    swap = [(0, 1), (1, 0)]

    def on_ring(x):
        return lax.ppermute(x, ("y", "core"), ring)

    def on_core(x):
        return lax.ppermute(x, "core", swap)

    def local(cotangent, expert_ids, combine, gate_saved, up_saved, w_down):
        expert_count = lax.axis_size("expert")
        y = lax.axis_index("y")
        core = lax.axis_index("core")
        xlo = lax.axis_index("xlo")
        dp = lax.axis_index("dp")
        rows = gate_saved.shape[2]
        width = gate_saved.shape[3]
        capacity = rows // expert_count
        half = capacity // 2
        lanes = cotangent.shape[2]
        chip = 2 * lanes

        ids = expert_ids[0].astype(BF)
        moved = lax.ppermute(
            jnp.concatenate([cotangent[0], ids], axis=1), ("y", "xlo", "core", "dp"), token_moves(False)
        )
        across = lax.ppermute(cotangent[0], ("y", "xlo", "core", "dp"), token_moves(True))
        mine = moved[:, :lanes]
        first = jnp.where(core == 0, mine, across)
        second = jnp.where(core == 0, across, mine)
        tokens = jnp.concatenate([first, second], axis=1)
        table = one_hot_table(moved[:, lanes:].astype(jnp.int32), expert_count, capacity, core)
        outgoing = jnp.dot(table, tokens, preferred_element_type=F32).astype(BF)
        outgoing = outgoing.reshape(expert_count, half, chip)
        part = lax.all_to_all(outgoing, "expert", split_axis=0, concat_axis=0, tiled=True)

        gate = gate_saved[0, 0].astype(F32)
        upper = up_saved[0, 0].astype(F32)
        weight_rows = combine[0, 0][:, None]
        sigma = jax.nn.sigmoid(gate)
        active = gate * sigma
        scaled = (weight_rows * (active * upper)).astype(BF)
        scaled_other = lax.ppermute(scaled, "dp", swap)

        def whole(a, b):
            lo = jnp.where(core == 0, a, b)
            hi = jnp.where(core == 0, b, a)
            return jnp.stack([lo, hi], axis=1).reshape(rows, chip)

        part_x = lax.ppermute(part, "xlo", swap)
        mine_rows = whole(part, on_core(part))
        x_rows = whole(part_x, on_core(part_x))
        own = jnp.where(xlo == 0, mine_rows, x_rows)
        other = jnp.where(xlo == 0, x_rows, mine_rows)

        w = w_down[0]
        state = dict(own=jnp.zeros((rows, width), F32), other=jnp.zeros((rows, width), F32))
        grad_weight = jnp.zeros((w.shape[0], width), BF)

        def use(state, grad_weight, block, own, other):
            w_block = lax.dynamic_slice_in_dim(w, block * chip, chip, 0)
            state = dict(
                own=state["own"] + jnp.dot(own, w_block, preferred_element_type=F32),
                other=state["other"] + jnp.dot(other, w_block, preferred_element_type=F32),
            )
            dims = (((0,), (0,)), ((), ()))
            piece = lax.dot_general(own, scaled, dims, preferred_element_type=F32) + lax.dot_general(
                other, scaled_other, dims, preferred_element_type=F32
            )
            return state, lax.dynamic_update_slice_in_dim(grad_weight, piece.astype(BF), block * chip, 0)

        state, grad_weight = use(state, grad_weight, y, own, other)
        turn = jnp.where(core == 0, -1, 1)
        for step in range(1, half_y):
            other = on_ring(other)
            own = on_ring(own)
            other_c = on_core(other)
            own_c = on_core(own)
            state, grad_weight = use(state, grad_weight, (y + turn * step + ny) % ny, own, other)
            state, grad_weight = use(state, grad_weight, (y - turn * step + ny) % ny, own_c, other_c)
        mid = rows // 2
        cut = lambda a: on_ring(lax.dynamic_slice_in_dim(a, core * mid, mid, 0))
        other = cut(other)
        own = cut(own)

        def join(a):
            b = on_core(a)
            return jnp.concatenate([jnp.where(core == 0, a, b), jnp.where(core == 0, b, a)], axis=0)

        state, grad_weight = use(state, grad_weight, (y + half_y) % ny, join(own), join(other))

        arrived = lax.ppermute(state["other"].astype(BF), "dp", swap)
        mix_own = jnp.sum(scaled.astype(F32) * state["own"], axis=1)
        mix_other = jnp.sum(scaled_other.astype(F32) * state["other"], axis=1)
        mix = jnp.stack([jnp.where(dp == 0, mix_own, mix_other), jnp.where(dp == 0, mix_other, mix_own)])
        group = ("dp", "y", "xlo", "core")
        members = 2 * ny * 4
        share = rows // (ny * 4)
        mix = lax.all_to_all(mix.reshape(members, share), group, 0, 0, tiled=True)
        mix = jnp.sum(mix, axis=0)
        blk = (y * 2 + xlo) * 2 + core
        mix = mix / lax.dynamic_slice_in_dim(combine[0, 0], blk * share, share, 0)

        grad_hidden = state["own"] + arrived.astype(F32)
        weighted = weight_rows * grad_hidden
        grad_gate = (weighted * upper * sigma * (1.0 + gate * (1.0 - sigma))).astype(BF)
        grad_upper = (weighted * active).astype(BF)
        return grad_gate[None, None], grad_upper[None, None], grad_weight[None], mix[None, None]

    return local


def solution(mesh):
    ne, nb, nd = mesh.devices.shape
    fine = Mesh(mesh.devices.reshape(ne, nb // 4, 2, 2, nd), ("expert", "y", "xlo", "core", "dp"))
    blk = ("y", "xlo", "core")
    return jax.shard_map(
        make_local(nb // 4),
        mesh=fine,
        in_specs=(
            P("dp", "expert", blk),
            P("dp", "expert", None),
            P("dp", "expert", None),
            P("dp", "expert", None, blk),
            P("dp", "expert", None, blk),
            P("expert", "dp", blk),
        ),
        out_specs=(
            P("dp", "expert", None, blk),
            P("dp", "expert", None, blk),
            P("expert", "dp", blk),
            P("dp", "expert", blk),
        ),
        check_vma=False,
    )
```

time: 246 us -> 180 us (0.73)
  starting transfers between devices: 0.12 us -> 96.5 us
  waiting for transfers between devices: 112 us -> 20.5 us
  blocking collectives: 78.2 us -> 17.1 us
  between operations: 13.9 us -> 1.65 us
  matrix products: 16.9 us -> 26.3 us
  local copies, waits for them, and re-layouts: 20.4 us -> 12.4 us
    all_gather x2 -> x0, waiting for transfers between devices: 111 us -> none  [the longest x1 79.5 us: local(): gathered = lax.all_gather(arrived, 'blk', axis=2, tiled=True)]
    ppermute x0 -> x23, starting transfers between devices: none -> 88.6 us  [the longest x8 39.8 us: on_ring(): return lax.ppermute(x, ('y', 'core'), ring)]
    psum x1 -> x0, blocking collectives: 54 us -> none  [local(): summed = lax.psum(mixing, 'blk')]
    ppermute x0 -> x23, waiting for transfers between devices: none -> 20.5 us  [the longest x1 10.2 us: local(): arrived = lax.ppermute(state['other'].astype(BF), 'dp', swap)]
    all_gather x1 -> x0, local copies, waits for them, and re-layouts: 15.9 us -> none  [local(): gathered = lax.all_gather(arrived, 'blk', axis=2, tiled=True)]
    dot_general x3 -> x34, matrix products: 16.9 us -> 26.3 us  [the longest x8 9.86 us: use(): lax.dot_general(own, scaled, dims, preferred_element_type=F32)]
    unnamed x12 -> x69, local copies, waits for them, and re-layouts: 2.2 us -> 10.4 us
    all_to_all x0 -> x1, starting transfers between devices: none -> 7.9 us  [local(): mix = lax.all_to_all(mix.reshape(members, share), group, 0, 0, tiled=True)]
  transfers between devices with their start and end apart: 3 -> 24, of which waited for: 2 -> 5; matrix products, arithmetic and copies ran while one was open for 14% -> 19% of each run, Pallas kernels for 0% -> 0%
where the time goes in v1:
time: 180 us; the launch traced here: 178 us
  starting transfers between devices  96.5 us (54%)
  matrix products  26.3 us (15%)
  waiting for transfers between devices  20.5 us (11%)
  blocking collectives  17.1 us (10%)
  local copies, waits for them, and re-layouts  12.4 us (7%)
  other arithmetic  3.93 us (2%)
    ppermute x8, starting transfers between devices, on_ring(): return lax.ppermute(x, ('y', 'core'), ring)  39.8 us
    ppermute x10, starting transfers between devices, on_core(): return lax.ppermute(x, 'core', swap)  27.3 us
    all_to_all x1, blocking collectives, local(): lax.all_to_all(outgoing, 'expert', split_axis=0, concat_axis=0, tiled=True)  17.1 us
    unnamed x69, local copies, waits for them, and re-layouts  10.4 us
    ppermute x1, waiting for transfers between devices, local(): arrived = lax.ppermute(state['other'].astype(BF), 'dp', swap)  10.2 us
    dot_general x8, matrix products, use(): lax.dot_general(own, scaled, dims, preferred_element_type=F32)  9.86 us
    ppermute x1, starting transfers between devices, local(): lax.ppermute(cotangent[0], ('y', 'xlo', 'core', 'dp'), token_moves(True))  8.79 us
    ppermute x1, starting transfers between devices, local(): part_x = lax.ppermute(part, 'xlo', swap)  8.15 us
  transfers between devices with their start and end apart: 24, of which 5 were waited for; matrix products, arithmetic and copies ran while one was open for 19% of the time, Pallas kernels for 0%

profile of v1, /device:TPU:1, one launch (start us, length us, event | category | flops | bytes accessed | tf_op | source)
XLA Modules:
  0.0 178.4 jit_solution(14884463564852860139)
XLA Ops:
  0.6 1.1 copy.35
  1.8 8.8 %collective-permute-start.1 = (bf16[192,192]{0,1:T(8,128)(2,1)S(1)}, bf16[192,192]{0,1:T(8,128)(2,1)S(1)}, u32[]{:S(2)}, u32[]{:S(2)}) collective-permute-start(bf16[192,192]{0,1:T(8,128)(2,1)S(1)} %bitcast.206), channel_id=1, source_target_pairs={{0,2},{1,6},{2,0},{3,4},{4,10},{5,14},{6,8},{7,12},{8,18},{9,22},{... | collective-permute-start | bytes 221192 | tf_op jit(solution)/shard_map/ppermute | solution.py:73
  12.6 17.1 %all_to_all.14 = bf16[8,48,384]{2,1,0:T(8,128)(2,1)S(1)} all-to-all(bf16[8,48,384]{2,1,0:T(8,128)(2,1)S(1)} %bitcast.208), channel_id=1, replica_groups=mesh['expert'=8,'y'=8,'xlo'=2,'core'=2,'dp'=2] {'expert'}, dimensions={0} | all-to-all | bytes 589824 | tf_op jit(solution)/shard_map/all_to_all | solution.py:81
  29.7 8.1 %collective-permute-start.3 = (bf16[8,48,384]{2,1,0:T(8,128)(2,1)S(1)}, bf16[8,48,384]{2,1,0:T(8,128)(2,1)S(1)}, u32[]{:S(2)}, u32[]{:S(2)}) collective-permute-start(bf16[8,48,384]{2,1,0:T(8,128)(2,1)S(1)} %all_to_all.14), channel_id=1, source_target_pairs={{0,4},{4,0},{1,5},{5,1},{2,6},{6,2},{3,7},{7,3},{8,12},{12,8},{9,1... | collective-permute-start | bytes 884744 | tf_op jit(solution)/shard_map/ppermute | solution.py:96
  37.9 4.9 %collective-permute-start.2 = (bf16[8,48,384]{2,1,0:T(8,128)(2,1)S(1)}, bf16[8,48,384]{2,1,0:T(8,128)(2,1)S(1)}, u32[]{:S(2)}, u32[]{:S(2)}) collective-permute-start(bf16[8,48,384]{2,1,0:T(8,128)(2,1)S(1)} %all_to_all.14), channel_id=1, source_target_pairs={{0,2},{2,0},{1,3},{3,1},{4,6},{6,4},{5,7},{7,5},{8,10},{10,8},{9,1... | collective-permute-start | bytes 884744 | tf_op jit(solution)/shard_map/ppermute | solution.py:54
  42.8 4.9 %collective-permute-start.4 = (bf16[8,48,384]{2,1,0:T(8,128)(2,1)S(1)}, bf16[8,48,384]{2,1,0:T(8,128)(2,1)S(1)}, u32[]{:S(2)}, u32[]{:S(2)}) collective-permute-start(bf16[8,48,384]{2,1,0:T(8,128)(2,1)S(1)} %collective-permute-done.3), channel_id=1, source_target_pairs={{0,2},{2,0},{1,3},{3,1},{4,6},{6,4},{5,7},{7,5},{8,10},{10,8},{9,1... | collective-permute-start | bytes 884744 | tf_op jit(solution)/shard_map/ppermute | solution.py:54
  47.8 1.1 collective-permute-done.4
  49.2 15.3 %collective-permute-start.5 = (bf16[768,384]{1,0:T(8,128)(2,1)S(1)}, bf16[768,384]{1,0:T(8,128)(2,1)S(1)}, u32[]{:S(2)}, u32[]{:S(2)}) collective-permute-start(bf16[768,384]{1,0:T(8,128)(2,1)S(1)} %bitcast.203), channel_id=1, source_target_pairs={{0,8},{8,16},{16,24},{24,32},{32,40},{40,48},{48,56},{56,0},{2,58}... | collective-permute-start | bytes 1769480 | tf_op jit(solution)/shard_map/ppermute | solution.py:51
  64.5 1.9 %collective-permute-start.13 = (bf16[768,384]{1,0:T(8,128)(2,1)S(1)}, bf16[768,384]{1,0:T(8,128)(2,1)}, u32[]{:S(2)}, u32[]{:S(2)}) collective-permute-start(bf16[768,384]{1,0:T(8,128)(2,1)S(1)} %bitcast.200), channel_id=1, source_target_pairs={{0,8},{8,16},{16,24},{24,32},{32,40},{40,48},{48,56},{56,0},{2,58}... | collective-permute-start | bytes 1769480 | tf_op jit(solution)/shard_map/ppermute | solution.py:51
  66.5 1.9 %copy.39 = bf16[1,1,768,256]{2,3,1,0:T(8,128)(2,1)} copy(bf16[1,1,768,256]{3,2,1,0:T(8,128)(2,1)} %param.10) | data formatting | bytes 786432 | tf_op args[4]
  68.5 1.9 %copy.40 = bf16[1,1,768,256]{2,3,1,0:T(8,128)(2,1)} copy(bf16[1,1,768,256]{3,2,1,0:T(8,128)(2,1)} %param.9) | data formatting | bytes 786432 | tf_op args[3]
  71.3 5.0 %collective-permute-start.7 = (bf16[768,384]{1,0:T(8,128)(2,1)S(1)}, bf16[768,384]{1,0:T(8,128)(2,1)S(1)}, u32[]{:S(2)}, u32[]{:S(2)}) collective-permute-start(bf16[768,384]{1,0:T(8,128)(2,1)S(1)} %collective-permute-done.5), channel_id=1, source_target_pairs={{0,8},{8,16},{16,24},{24,32},{32,40},{40,48},{48,56},{56,0},{2,58}... | collective-permute-start | bytes 1769480 | tf_op jit(solution)/shard_map/ppermute | solution.py:51
  76.8 1.9 %collective-permute-start.6 = (bf16[768,384]{1,0:T(8,128)(2,1)S(1)}, bf16[768,384]{1,0:T(8,128)(2,1)S(1)}, u32[]{:S(2)}, u32[]{:S(2)}) collective-permute-start(bf16[768,384]{1,0:T(8,128)(2,1)S(1)} %collective-permute-done.5), channel_id=1, source_target_pairs={{0,2},{2,0},{1,3},{3,1},{4,6},{6,4},{5,7},{7,5},{8,10},{10,8},{9,1... | collective-permute-start | bytes 1769480 | tf_op jit(solution)/shard_map/ppermute | solution.py:54
  78.7 4.0 %collective-permute-start.15 = (bf16[768,384]{1,0:T(8,128)(2,1)}, bf16[768,384]{1,0:T(8,128)(2,1)S(1)}, u32[]{:S(2)}, u32[]{:S(2)}) collective-permute-start(bf16[768,384]{1,0:T(8,128)(2,1)} %collective-permute-done.13), channel_id=1, source_target_pairs={{0,8},{8,16},{16,24},{24,32},{32,40},{40,48},{48,56},{56,0},{2,58}... | collective-permute-start | bytes 1769480 | tf_op jit(solution)/shard_map/ppermute | solution.py:51
  82.8 1.9 %collective-permute-start.14 = (bf16[768,384]{1,0:T(8,128)(2,1)}, bf16[768,384]{1,0:T(8,128)(2,1)S(1)}, u32[]{:S(2)}, u32[]{:S(2)}) collective-permute-start(bf16[768,384]{1,0:T(8,128)(2,1)} %collective-permute-done.13), channel_id=1, source_target_pairs={{0,2},{2,0},{1,3},{3,1},{4,6},{6,4},{5,7},{7,5},{8,10},{10,8},{9,1... | collective-permute-start | bytes 1769480 | tf_op jit(solution)/shard_map/ppermute | solution.py:54
  85.1 1.5 convolution_add_fusion.3
  86.6 3.4 %collective-permute-start.9 = (bf16[768,384]{1,0:T(8,128)(2,1)S(1)}, bf16[768,384]{1,0:T(8,128)(2,1)S(1)}, u32[]{:S(2)}, u32[]{:S(2)}) collective-permute-start(bf16[768,384]{1,0:T(8,128)(2,1)S(1)} %collective-permute-done.7), channel_id=1, source_target_pairs={{0,8},{8,16},{16,24},{24,32},{32,40},{40,48},{48,56},{56,0},{2,58}... | collective-permute-start | bytes 1769480 | tf_op jit(solution)/shard_map/ppermute | solution.py:51
  90.1 1.9 %collective-permute-start.8 = (bf16[768,384]{1,0:T(8,128)(2,1)S(1)}, bf16[768,384]{1,0:T(8,128)(2,1)S(1)}, u32[]{:S(2)}, u32[]{:S(2)}) collective-permute-start(bf16[768,384]{1,0:T(8,128)(2,1)S(1)} %collective-permute-done.7), channel_id=1, source_target_pairs={{0,2},{2,0},{1,3},{3,1},{4,6},{6,4},{5,7},{7,5},{8,10},{10,8},{9,1... | collective-permute-start | bytes 1769480 | tf_op jit(solution)/shard_map/ppermute | solution.py:54
  92.4 3.8 %collective-permute-start.17 = (bf16[768,384]{1,0:T(8,128)(2,1)S(1)}, bf16[768,384]{1,0:T(8,128)(2,1)S(1)}, u32[]{:S(2)}, u32[]{:S(2)}) collective-permute-start(bf16[768,384]{1,0:T(8,128)(2,1)S(1)} %collective-permute-done.15), channel_id=1, source_target_pairs={{0,8},{8,16},{16,24},{24,32},{32,40},{40,48},{48,56},{56,0},{2,58}... | collective-permute-start | bytes 1769480 | tf_op jit(solution)/shard_map/ppermute | solution.py:51
  96.3 1.9 %collective-permute-start.16 = (bf16[768,384]{1,0:T(8,128)(2,1)S(1)}, bf16[768,384]{1,0:T(8,128)(2,1)S(1)}, u32[]{:S(2)}, u32[]{:S(2)}) collective-permute-start(bf16[768,384]{1,0:T(8,128)(2,1)S(1)} %collective-permute-done.15), channel_id=1, source_target_pairs={{0,2},{2,0},{1,3},{3,1},{4,6},{6,4},{5,7},{7,5},{8,10},{10,8},{9,1... | collective-permute-start | bytes 1769480 | tf_op jit(solution)/shard_map/ppermute | solution.py:54
  100.0 3.9 %collective-permute-done.17 = bf16[768,384]{1,0:T(8,128)(2,1)S(1)} collective-permute-done((bf16[768,384]{1,0:T(8,128)(2,1)S(1)}, bf16[768,384]{1,0:T(8,128)(2,1)S(1)}, u32[]{:S(2)}, u32[]{:S(2)}) %collective-permute-start.17) | collective-permute-done | bytes 589856 | tf_op jit(solution)/shard_map/ppermute | solution.py:51
  103.9 4.3 %collective-permute-start.19 = (bf16[384,384]{1,0:T(8,128)(2,1)S(1)}, bf16[384,384]{1,0:T(8,128)(2,1)S(1)}, u32[]{:S(2)}, u32[]{:S(2)}) collective-permute-start(bf16[384,384]{1,0:T(8,128)(2,1)S(1)} %constant_dynamic-slice_fusion.1), channel_id=1, source_target_pairs={{0,8},{8,16},{16,24},{24,32},{32,40},{40,48},{48,56},{56,0},{2,58}... | collective-permute-start | bytes 884744 | tf_op jit(solution)/shard_map/ppermute | solution.py:51
  108.3 1.9 %collective-permute-start.11 = (bf16[384,384]{1,0:T(8,128)(2,1)S(1)}, bf16[384,384]{1,0:T(8,128)(2,1)S(1)}, u32[]{:S(2)}, u32[]{:S(2)}) collective-permute-start(bf16[384,384]{1,0:T(8,128)(2,1)S(1)} %constant_dynamic-slice_fusion.2), channel_id=1, source_target_pairs={{0,8},{8,16},{16,24},{24,32},{32,40},{40,48},{48,56},{56,0},{2,58}... | collective-permute-start | bytes 884744 | tf_op jit(solution)/shard_map/ppermute | solution.py:51
  110.3 2.1 %collective-permute-start.18 = (bf16[768,384]{1,0:T(8,128)(2,1)S(1)}, bf16[768,384]{1,0:T(8,128)(2,1)S(1)}, u32[]{:S(2)}, u32[]{:S(2)}) collective-permute-start(bf16[768,384]{1,0:T(8,128)(2,1)S(1)} %collective-permute-done.17), channel_id=1, source_target_pairs={{0,2},{2,0},{1,3},{3,1},{4,6},{6,4},{5,7},{7,5},{8,10},{10,8},{9,1... | collective-permute-start | bytes 1769480 | tf_op jit(solution)/shard_map/ppermute | solution.py:54
  112.8 2.3 %collective-permute-start.10 = (bf16[768,384]{1,0:T(8,128)(2,1)S(1)}, bf16[768,384]{1,0:T(8,128)(2,1)S(1)}, u32[]{:S(2)}, u32[]{:S(2)}) collective-permute-start(bf16[768,384]{1,0:T(8,128)(2,1)S(1)} %collective-permute-done.9), channel_id=1, source_target_pairs={{0,2},{2,0},{1,3},{3,1},{4,6},{6,4},{5,7},{7,5},{8,10},{10,8},{9,1... | collective-permute-start | bytes 1769480 | tf_op jit(solution)/shard_map/ppermute | solution.py:54
  115.1 3.2 %collective-permute-start.20 = (bf16[384,384]{1,0:T(8,128)(2,1)S(1)}, bf16[384,384]{1,0:T(8,128)(2,1)S(1)}, u32[]{:S(2)}, u32[]{:S(2)}) collective-permute-start(bf16[384,384]{1,0:T(8,128)(2,1)S(1)} %collective-permute-done.19), channel_id=1, source_target_pairs={{0,2},{2,0},{1,3},{3,1},{4,6},{6,4},{5,7},{7,5},{8,10},{10,8},{9,1... | collective-permute-start | bytes 884744 | tf_op jit(solution)/shard_map/ppermute | solution.py:54
  119.1 2.3 %collective-permute-start.12 = (bf16[384,384]{1,0:T(8,128)(2,1)S(1)}, bf16[384,384]{1,0:T(8,128)(2,1)S(1)}, u32[]{:S(2)}, u32[]{:S(2)}) collective-permute-start(bf16[384,384]{1,0:T(8,128)(2,1)S(1)} %collective-permute-done.11), channel_id=1, source_target_pairs={{0,2},{2,0},{1,3},{3,1},{4,6},{6,4},{5,7},{7,5},{8,10},{10,8},{9,1... | collective-permute-start | bytes 884744 | tf_op jit(solution)/shard_map/ppermute | solution.py:54
  121.9 1.3 fusion.142
  123.2 1.9 %collective-permute-start.21 = (bf16[768,256]{0,1:T(8,128)(2,1)S(1)}, bf16[768,256]{0,1:T(8,128)(2,1)S(1)}, u32[]{:S(2)}, u32[]{:S(2)}) collective-permute-start(bf16[768,256]{0,1:T(8,128)(2,1)S(1)} %get-tuple-element.40), channel_id=1, source_target_pairs={{0,1},{1,0},{2,3},{3,2},{4,5},{5,4},{6,7},{7,6},{8,9},{9,8},{10,11... | collective-permute-start | bytes 1179656 | tf_op jit(solution)/shard_map/ppermute | solution.py:138
  126.9 10.2 %collective-permute-done.21 = bf16[768,256]{0,1:T(8,128)(2,1)S(1)} collective-permute-done((bf16[768,256]{0,1:T(8,128)(2,1)S(1)}, bf16[768,256]{0,1:T(8,128)(2,1)S(1)}, u32[]{:S(2)}, u32[]{:S(2)}) %collective-permute-start.21) | collective-permute-done | bytes 393248 | tf_op jit(solution)/shard_map/ppermute | solution.py:138
  137.2 1.9 %multiply_reduce_fusion.1 = (f32[768]{0:T(1024)S(1)}, bf16[768,256]{0,1:T(8,128)(2,1)S(1)}, bf16[1,1,768,256]{2,3,1,0:T(8,128)(2,1)}, bf16[1,1,768,256]{2,3,1,0:T(8,128)(2,1)}) fusion(bf16[1,1,768,256]{2,3,1,0:T(8,128)(2,1)S(1)} %copy-done.28, bf16[1,1,768,256]{2,3,1,0:T(8,128)(2,1)S(1)} %copy-done.29, f32[768]{0:T(1024)S(1)} %reduce.1, ...), kind=kOutput, calls=%fused_computation.72 | convolution fusion | flops 156105984 | bytes 4725764 | tf_op jit(solution)/shard_map/dot_general | solution.py:109
  139.1 2.0 %collective-permute-start.22 = (bf16[768,256]{0,1:T(8,128)(2,1)S(1)}, bf16[768,256]{0,1:T(8,128)(2,1)S(1)}, u32[]{:S(2)}, u32[]{:S(2)}) collective-permute-start(bf16[768,256]{0,1:T(8,128)(2,1)S(1)} %get-tuple-element.21), channel_id=1, source_target_pairs={{0,1},{1,0},{2,3},{3,2},{4,5},{5,4},{6,7},{7,6},{8,9},{9,8},{10,11... | collective-permute-start | bytes 1179656 | tf_op jit(solution)/shard_map/ppermute | solution.py:89
  141.1 2.5 %fusion.50 = f32[384,256]{1,0:T(8,128)} fusion(bf16[768,384]{1,0:T(8,128)(2,1)} %bitcast.205, bf16[1,1,768,256]{2,3,1,0:T(8,128)(2,1)} %copy.39, bf16[1,1,768,256]{2,3,1,0:T(8,128)(2,1)} %copy.40, f32[768]{0:T(1024)S(1)} %reduce.1), kind=kOutput, calls=%fused_computation.82 | convolution fusion | flops 152764416 | bytes 1772544 | tf_op jit(solution)/shard_map/dot_general | solution.py:113
  143.6 1.9 %copy.42 = bf16[1,1,768,256]{3,2,1,0:T(8,128)(2,1)} copy(bf16[1,1,768,256]{2,3,1,0:T(8,128)(2,1)} %get-tuple-element.22) | data formatting | bytes 786432
  145.5 1.9 %copy.43 = bf16[1,1,768,256]{3,2,1,0:T(8,128)(2,1)} copy(bf16[1,1,768,256]{2,3,1,0:T(8,128)(2,1)} %get-tuple-element.23) | data formatting | bytes 786432
  147.4 4.7 %collective-permute-done.22 = bf16[768,256]{0,1:T(8,128)(2,1)S(1)} collective-permute-done((bf16[768,256]{0,1:T(8,128)(2,1)S(1)}, bf16[768,256]{0,1:T(8,128)(2,1)S(1)}, u32[]{:S(2)}, u32[]{:S(2)}) %collective-permute-start.22) | collective-permute-done | bytes 393248 | tf_op jit(solution)/shard_map/ppermute | solution.py:89
  152.1 1.2 multiply_reduce_fusion
  154.1 7.9 %all-to-all-start.1 = ((f32[64,1,24]{2,1,0:T(1,128)}), f32[64,1,24]{2,1,0:T(1,128)}, u32[]{:S(2)}, u32[]{:S(2)}) async-start(f32[64,1,24]{2,1,0:T(1,128)} %bitcast.209), calls=%async_computation.1 | async-start | bytes 65536 | tf_op jit(solution)/shard_map/all_to_all | solution.py:145
  162.0 1.5 fusion.58
  163.9 1.5 fusion.145
  167.3 1.2 broadcast_in_dim.36
  168.6 1.0 fusion.32
  169.6 1.0 fusion.30
  170.7 1.1 fusion.28
  171.7 1.0 fusion.26
  172.8 1.1 fusion.24
  174.9 1.1 fusion.20
  175.9 1.0 fusion.18
  (130 shorter events, 15.1 us)
Async XLA Ops:
  0.6 69.8 %copy-start = (bf16[1,3072,256]{2,1,0:T(8,128)(2,1)S(1)}, bf16[1,3072,256]{2,1,0:T(8,128)(2,1)}, u32[]{:S(2)}) copy-start(bf16[1,3072,256]{2,1,0:T(8,128)(2,1)} %param.11) | copy-start | bytes 4718596
  1.8 10.5 %collective-permute-start.1 = (bf16[192,192]{0,1:T(8,128)(2,1)S(1)}, bf16[192,192]{0,1:T(8,128)(2,1)S(1)}, u32[]{:S(2)}, u32[]{:S(2)}) collective-permute-start(bf16[192,192]{0,1:T(8,128)(2,1)S(1)} %bitcast.206), channel_id=1, source_target_pairs={{0,2},{1,6},{2,0},{3,4},{4,10},{5,14},{6,8},{7,12},{8,18},{9,22},{... | collective-permute-start | bytes 221192 | tf_op jit(solution)/shard_map/ppermute | solution.py:73
  11.3 0.7 collective-permute-start
  29.7 13.1 %collective-permute-start.3 = (bf16[8,48,384]{2,1,0:T(8,128)(2,1)S(1)}, bf16[8,48,384]{2,1,0:T(8,128)(2,1)S(1)}, u32[]{:S(2)}, u32[]{:S(2)}) collective-permute-start(bf16[8,48,384]{2,1,0:T(8,128)(2,1)S(1)} %all_to_all.14), channel_id=1, source_target_pairs={{0,4},{4,0},{1,5},{5,1},{2,6},{6,2},{3,7},{7,3},{8,12},{12,8},{9,1... | collective-permute-start | bytes 884744 | tf_op jit(solution)/shard_map/ppermute | solution.py:96
  37.9 9.9 %collective-permute-start.2 = (bf16[8,48,384]{2,1,0:T(8,128)(2,1)S(1)}, bf16[8,48,384]{2,1,0:T(8,128)(2,1)S(1)}, u32[]{:S(2)}, u32[]{:S(2)}) collective-permute-start(bf16[8,48,384]{2,1,0:T(8,128)(2,1)S(1)} %all_to_all.14), channel_id=1, source_target_pairs={{0,2},{2,0},{1,3},{3,1},{4,6},{6,4},{5,7},{7,5},{8,10},{10,8},{9,1... | collective-permute-start | bytes 884744 | tf_op jit(solution)/shard_map/ppermute | solution.py:54
  42.8 6.1 %collective-permute-start.4 = (bf16[8,48,384]{2,1,0:T(8,128)(2,1)S(1)}, bf16[8,48,384]{2,1,0:T(8,128)(2,1)S(1)}, u32[]{:S(2)}, u32[]{:S(2)}) collective-permute-start(bf16[8,48,384]{2,1,0:T(8,128)(2,1)S(1)} %collective-permute-done.3), channel_id=1, source_target_pairs={{0,2},{2,0},{1,3},{3,1},{4,6},{6,4},{5,7},{7,5},{8,10},{10,8},{9,1... | collective-permute-start | bytes 884744 | tf_op jit(solution)/shard_map/ppermute | solution.py:54
  49.0 21.4 %copy-start.31 = (f32[1,1,768]{2,1,0:T(1,128)S(1)}, f32[1,1,768]{2,1,0:T(1,128)}, u32[]{:S(2)}) copy-start(f32[1,1,768]{2,1,0:T(1,128)} %param.8) | copy-start | bytes 9220
  49.2 37.4 %copy-start.5 = (bf16[8,2,48,384]{3,2,1,0:T(8,128)(2,1)}, bf16[8,2,48,384]{3,2,1,0:T(8,128)(2,1)S(1)}, u32[]{:S(2)}) copy-start(bf16[8,2,48,384]{3,2,1,0:T(8,128)(2,1)S(1)} %get-tuple-element.25) | copy-start | bytes 1769476
  49.2 22.1 %collective-permute-start.5 = (bf16[768,384]{1,0:T(8,128)(2,1)S(1)}, bf16[768,384]{1,0:T(8,128)(2,1)S(1)}, u32[]{:S(2)}, u32[]{:S(2)}) collective-permute-start(bf16[768,384]{1,0:T(8,128)(2,1)S(1)} %bitcast.203), channel_id=1, source_target_pairs={{0,8},{8,16},{16,24},{24,32},{32,40},{40,48},{48,56},{56,0},{2,58}... | collective-permute-start | bytes 1769480 | tf_op jit(solution)/shard_map/ppermute | solution.py:51
  64.5 14.2 %collective-permute-start.13 = (bf16[768,384]{1,0:T(8,128)(2,1)S(1)}, bf16[768,384]{1,0:T(8,128)(2,1)}, u32[]{:S(2)}, u32[]{:S(2)}) collective-permute-start(bf16[768,384]{1,0:T(8,128)(2,1)S(1)} %bitcast.200), channel_id=1, source_target_pairs={{0,8},{8,16},{16,24},{24,32},{32,40},{40,48},{48,56},{56,0},{2,58}... | collective-permute-start | bytes 1769480 | tf_op jit(solution)/shard_map/ppermute | solution.py:51
  71.3 13.8 %copy-start.3 = (bf16[768,384]{1,0:T(8,128)(2,1)}, bf16[768,384]{1,0:T(8,128)(2,1)S(1)}, u32[]{:S(2)}) copy-start(bf16[768,384]{1,0:T(8,128)(2,1)S(1)} %collective-permute-done.5) | copy-start | bytes 1769476
  71.3 15.3 %collective-permute-start.7 = (bf16[768,384]{1,0:T(8,128)(2,1)S(1)}, bf16[768,384]{1,0:T(8,128)(2,1)S(1)}, u32[]{:S(2)}, u32[]{:S(2)}) collective-permute-start(bf16[768,384]{1,0:T(8,128)(2,1)S(1)} %collective-permute-done.5), channel_id=1, source_target_pairs={{0,8},{8,16},{16,24},{24,32},{32,40},{40,48},{48,56},{56,0},{2,58}... | collective-permute-start | bytes 1769480 | tf_op jit(solution)/shard_map/ppermute | solution.py:51
  76.8 19.5 %collective-permute-start.6 = (bf16[768,384]{1,0:T(8,128)(2,1)S(1)}, bf16[768,384]{1,0:T(8,128)(2,1)S(1)}, u32[]{:S(2)}, u32[]{:S(2)}) collective-permute-start(bf16[768,384]{1,0:T(8,128)(2,1)S(1)} %collective-permute-done.5), channel_id=1, source_target_pairs={{0,2},{2,0},{1,3},{3,1},{4,6},{6,4},{5,7},{7,5},{8,10},{10,8},{9,1... | collective-permute-start | bytes 1769480 | tf_op jit(solution)/shard_map/ppermute | solution.py:54
  78.7 13.7 %collective-permute-start.15 = (bf16[768,384]{1,0:T(8,128)(2,1)}, bf16[768,384]{1,0:T(8,128)(2,1)S(1)}, u32[]{:S(2)}, u32[]{:S(2)}) collective-permute-start(bf16[768,384]{1,0:T(8,128)(2,1)} %collective-permute-done.13), channel_id=1, source_target_pairs={{0,8},{8,16},{16,24},{24,32},{32,40},{40,48},{48,56},{56,0},{2,58}... | collective-permute-start | bytes 1769480 | tf_op jit(solution)/shard_map/ppermute | solution.py:51
  82.8 16.4 %collective-permute-start.14 = (bf16[768,384]{1,0:T(8,128)(2,1)}, bf16[768,384]{1,0:T(8,128)(2,1)S(1)}, u32[]{:S(2)}, u32[]{:S(2)}) collective-permute-start(bf16[768,384]{1,0:T(8,128)(2,1)} %collective-permute-done.13), channel_id=1, source_target_pairs={{0,2},{2,0},{1,3},{3,1},{4,6},{6,4},{5,7},{7,5},{8,10},{10,8},{9,1... | collective-permute-start | bytes 1769480 | tf_op jit(solution)/shard_map/ppermute | solution.py:54
  86.6 12.0 %copy-start.6 = (bf16[768,384]{1,0:T(8,128)(2,1)}, bf16[768,384]{1,0:T(8,128)(2,1)S(1)}, u32[]{:S(2)}) copy-start(bf16[768,384]{1,0:T(8,128)(2,1)S(1)} %collective-permute-done.7) | copy-start | bytes 1769476
  86.6 21.6 %collective-permute-start.9 = (bf16[768,384]{1,0:T(8,128)(2,1)S(1)}, bf16[768,384]{1,0:T(8,128)(2,1)S(1)}, u32[]{:S(2)}, u32[]{:S(2)}) collective-permute-start(bf16[768,384]{1,0:T(8,128)(2,1)S(1)} %collective-permute-done.7), channel_id=1, source_target_pairs={{0,8},{8,16},{16,24},{24,32},{32,40},{40,48},{48,56},{56,0},{2,58}... | collective-permute-start | bytes 1769480 | tf_op jit(solution)/shard_map/ppermute | solution.py:51
  90.1 35.1 %collective-permute-start.8 = (bf16[768,384]{1,0:T(8,128)(2,1)S(1)}, bf16[768,384]{1,0:T(8,128)(2,1)S(1)}, u32[]{:S(2)}, u32[]{:S(2)}) collective-permute-start(bf16[768,384]{1,0:T(8,128)(2,1)S(1)} %collective-permute-done.7), channel_id=1, source_target_pairs={{0,2},{2,0},{1,3},{3,1},{4,6},{6,4},{5,7},{7,5},{8,10},{10,8},{9,1... | collective-permute-start | bytes 1769480 | tf_op jit(solution)/shard_map/ppermute | solution.py:54
  92.4 6.2 %copy-start.12 = (bf16[768,384]{1,0:T(8,128)(2,1)}, bf16[768,384]{1,0:T(8,128)(2,1)S(1)}, u32[]{:S(2)}) copy-start(bf16[768,384]{1,0:T(8,128)(2,1)S(1)} %collective-permute-done.15) | copy-start | bytes 1769476
  92.4 11.4 %collective-permute-start.17 = (bf16[768,384]{1,0:T(8,128)(2,1)S(1)}, bf16[768,384]{1,0:T(8,128)(2,1)S(1)}, u32[]{:S(2)}, u32[]{:S(2)}) collective-permute-start(bf16[768,384]{1,0:T(8,128)(2,1)S(1)} %collective-permute-done.15), channel_id=1, source_target_pairs={{0,8},{8,16},{16,24},{24,32},{32,40},{40,48},{48,56},{56,0},{2,58}... | collective-permute-start | bytes 1769480 | tf_op jit(solution)/shard_map/ppermute | solution.py:51
  96.3 2.4 %copy-start.8 = (bf16[768,384]{1,0:T(8,128)(2,1)}, bf16[768,384]{1,0:T(8,128)(2,1)S(1)}, u32[]{:S(2)}) copy-start(bf16[768,384]{1,0:T(8,128)(2,1)S(1)} %collective-permute-done.6) | copy-start | bytes 1769476
  96.3 16.4 %collective-permute-start.16 = (bf16[768,384]{1,0:T(8,128)(2,1)S(1)}, bf16[768,384]{1,0:T(8,128)(2,1)S(1)}, u32[]{:S(2)}, u32[]{:S(2)}) collective-permute-start(bf16[768,384]{1,0:T(8,128)(2,1)S(1)} %collective-permute-done.15), channel_id=1, source_target_pairs={{0,2},{2,0},{1,3},{3,1},{4,6},{6,4},{5,7},{7,5},{8,10},{10,8},{9,1... | collective-permute-start | bytes 1769480 | tf_op jit(solution)/shard_map/ppermute | solution.py:54
  103.9 14.8 %copy-start.1 = (bf16[768,384]{1,0:T(8,128)(2,1)}, bf16[768,384]{1,0:T(8,128)(2,1)S(1)}, u32[]{:S(2)}) copy-start(bf16[768,384]{1,0:T(8,128)(2,1)S(1)} %collective-permute-done.17) | copy-start | bytes 1769476
  103.9 11.1 %collective-permute-start.19 = (bf16[384,384]{1,0:T(8,128)(2,1)S(1)}, bf16[384,384]{1,0:T(8,128)(2,1)S(1)}, u32[]{:S(2)}, u32[]{:S(2)}) collective-permute-start(bf16[384,384]{1,0:T(8,128)(2,1)S(1)} %constant_dynamic-slice_fusion.1), channel_id=1, source_target_pairs={{0,8},{8,16},{16,24},{24,32},{32,40},{40,48},{48,56},{56,0},{2,58}... | collective-permute-start | bytes 884744 | tf_op jit(solution)/shard_map/ppermute | solution.py:51
  108.3 10.8 %collective-permute-start.11 = (bf16[384,384]{1,0:T(8,128)(2,1)S(1)}, bf16[384,384]{1,0:T(8,128)(2,1)S(1)}, u32[]{:S(2)}, u32[]{:S(2)}) collective-permute-start(bf16[384,384]{1,0:T(8,128)(2,1)S(1)} %constant_dynamic-slice_fusion.2), channel_id=1, source_target_pairs={{0,8},{8,16},{16,24},{24,32},{32,40},{40,48},{48,56},{56,0},{2,58}... | collective-permute-start | bytes 884744 | tf_op jit(solution)/shard_map/ppermute | solution.py:51
  110.3 11.6 %collective-permute-start.18 = (bf16[768,384]{1,0:T(8,128)(2,1)S(1)}, bf16[768,384]{1,0:T(8,128)(2,1)S(1)}, u32[]{:S(2)}, u32[]{:S(2)}) collective-permute-start(bf16[768,384]{1,0:T(8,128)(2,1)S(1)} %collective-permute-done.17), channel_id=1, source_target_pairs={{0,2},{2,0},{1,3},{3,1},{4,6},{6,4},{5,7},{7,5},{8,10},{10,8},{9,1... | collective-permute-start | bytes 1769480 | tf_op jit(solution)/shard_map/ppermute | solution.py:54
  112.8 5.9 %copy-start.16 = (bf16[768,384]{1,0:T(8,128)(2,1)}, bf16[768,384]{1,0:T(8,128)(2,1)S(1)}, u32[]{:S(2)}) copy-start(bf16[768,384]{1,0:T(8,128)(2,1)S(1)} %collective-permute-done.16) | copy-start | bytes 1769476
  112.8 13.7 %collective-permute-start.10 = (bf16[768,384]{1,0:T(8,128)(2,1)S(1)}, bf16[768,384]{1,0:T(8,128)(2,1)S(1)}, u32[]{:S(2)}, u32[]{:S(2)}) collective-permute-start(bf16[768,384]{1,0:T(8,128)(2,1)S(1)} %collective-permute-done.9), channel_id=1, source_target_pairs={{0,2},{2,0},{1,3},{3,1},{4,6},{6,4},{5,7},{7,5},{8,10},{10,8},{9,1... | collective-permute-start | bytes 1769480 | tf_op jit(solution)/shard_map/ppermute | solution.py:54
  115.1 6.3 %collective-permute-start.20 = (bf16[384,384]{1,0:T(8,128)(2,1)S(1)}, bf16[384,384]{1,0:T(8,128)(2,1)S(1)}, u32[]{:S(2)}, u32[]{:S(2)}) collective-permute-start(bf16[384,384]{1,0:T(8,128)(2,1)S(1)} %collective-permute-done.19), channel_id=1, source_target_pairs={{0,2},{2,0},{1,3},{3,1},{4,6},{6,4},{5,7},{7,5},{8,10},{10,8},{9,1... | collective-permute-start | bytes 884744 | tf_op jit(solution)/shard_map/ppermute | solution.py:54
  119.1 6.9 %collective-permute-start.12 = (bf16[384,384]{1,0:T(8,128)(2,1)S(1)}, bf16[384,384]{1,0:T(8,128)(2,1)S(1)}, u32[]{:S(2)}, u32[]{:S(2)}) collective-permute-start(bf16[384,384]{1,0:T(8,128)(2,1)S(1)} %collective-permute-done.11), channel_id=1, source_target_pairs={{0,2},{2,0},{1,3},{3,1},{4,6},{6,4},{5,7},{7,5},{8,10},{10,8},{9,1... | collective-permute-start | bytes 884744 | tf_op jit(solution)/shard_map/ppermute | solution.py:54
  121.5 4.6 %copy-start.24 = (bf16[384,384]{1,0:T(8,128)(2,1)}, bf16[384,384]{1,0:T(8,128)(2,1)S(1)}, u32[]{:S(2)}) copy-start(bf16[384,384]{1,0:T(8,128)(2,1)S(1)} %get-tuple-element.26) | copy-start | bytes 884740
  121.5 4.6 %copy-start.25 = (bf16[384,384]{1,0:T(8,128)(2,1)}, bf16[384,384]{1,0:T(8,128)(2,1)S(1)}, u32[]{:S(2)}) copy-start(bf16[384,384]{1,0:T(8,128)(2,1)S(1)} %get-tuple-element.27) | copy-start | bytes 884740
  123.2 14.0 %collective-permute-start.21 = (bf16[768,256]{0,1:T(8,128)(2,1)S(1)}, bf16[768,256]{0,1:T(8,128)(2,1)S(1)}, u32[]{:S(2)}, u32[]{:S(2)}) collective-permute-start(bf16[768,256]{0,1:T(8,128)(2,1)S(1)} %get-tuple-element.40), channel_id=1, source_target_pairs={{0,1},{1,0},{2,3},{3,2},{4,5},{5,4},{6,7},{7,6},{8,9},{9,8},{10,11... | collective-permute-start | bytes 1179656 | tf_op jit(solution)/shard_map/ppermute | solution.py:138
  126.0 11.2 %copy-start.28 = (bf16[1,1,768,256]{2,3,1,0:T(8,128)(2,1)S(1)}, bf16[1,1,768,256]{2,3,1,0:T(8,128)(2,1)}, u32[]{:S(2)}) copy-start(bf16[1,1,768,256]{2,3,1,0:T(8,128)(2,1)} %copy.39) | copy-start | bytes 1179652
  126.0 11.2 %copy-start.29 = (bf16[1,1,768,256]{2,3,1,0:T(8,128)(2,1)S(1)}, bf16[1,1,768,256]{2,3,1,0:T(8,128)(2,1)}, u32[]{:S(2)}) copy-start(bf16[1,1,768,256]{2,3,1,0:T(8,128)(2,1)} %copy.40) | copy-start | bytes 1179652
  126.9 12.2 %copy-start.26 = (bf16[768,384]{1,0:T(8,128)(2,1)}, bf16[768,384]{1,0:T(8,128)(2,1)S(1)}, u32[]{:S(2)}) copy-start(bf16[768,384]{1,0:T(8,128)(2,1)S(1)} %collective-permute-done.10) | copy-start | bytes 1769476
  139.1 13.0 %collective-permute-start.22 = (bf16[768,256]{0,1:T(8,128)(2,1)S(1)}, bf16[768,256]{0,1:T(8,128)(2,1)S(1)}, u32[]{:S(2)}, u32[]{:S(2)}) collective-permute-start(bf16[768,256]{0,1:T(8,128)(2,1)S(1)} %get-tuple-element.21), channel_id=1, source_target_pairs={{0,1},{1,0},{2,3},{3,2},{4,5},{5,4},{6,7},{7,6},{8,9},{9,8},{10,11... | collective-permute-start | bytes 1179656 | tf_op jit(solution)/shard_map/ppermute | solution.py:89
  154.1 22.9 %all-to-all-start.1 = ((f32[64,1,24]{2,1,0:T(1,128)}), f32[64,1,24]{2,1,0:T(1,128)}, u32[]{:S(2)}, u32[]{:S(2)}) async-start(f32[64,1,24]{2,1,0:T(1,128)} %bitcast.209), calls=%async_computation.1 | async-start | bytes 65536 | tf_op jit(solution)/shard_map/all_to_all | solution.py:145
  163.5 1.9 %copy-start.13 = (bf16[768,384]{1,0:T(8,128)(2,1)S(1)}, bf16[768,384]{1,0:T(8,128)(2,1)}, u32[]{:S(2)}) copy-start(bf16[768,384]{1,0:T(8,128)(2,1)} %copy-done.12) | copy-start | bytes 1769476
  163.9 1.9 %copy-start.17 = (bf16[768,384]{1,0:T(8,128)(2,1)S(1)}, bf16[768,384]{1,0:T(8,128)(2,1)}, u32[]{:S(2)}) copy-start(bf16[768,384]{1,0:T(8,128)(2,1)} %copy-done.16) | copy-start | bytes 1769476
  166.9 1.6 copy-start.30
  167.3 2.3 %copy-start.4 = (bf16[768,384]{1,0:T(8,128)(2,1)S(1)}, bf16[768,384]{1,0:T(8,128)(2,1)}, u32[]{:S(2)}) copy-start(bf16[768,384]{1,0:T(8,128)(2,1)} %copy-done.3) | copy-start | bytes 1769476
  168.6 2.1 %copy-start.9 = (bf16[768,384]{1,0:T(8,128)(2,1)S(1)}, bf16[768,384]{1,0:T(8,128)(2,1)}, u32[]{:S(2)}) copy-start(bf16[768,384]{1,0:T(8,128)(2,1)} %copy-done.8) | copy-start | bytes 1769476
  169.6 2.1 %copy-start.7 = (bf16[768,384]{1,0:T(8,128)(2,1)S(1)}, bf16[768,384]{1,0:T(8,128)(2,1)}, u32[]{:S(2)}) copy-start(bf16[768,384]{1,0:T(8,128)(2,1)} %copy-done.6) | copy-start | bytes 1769476
  170.7 2.1 %copy-start.11 = (bf16[768,384]{1,0:T(8,128)(2,1)S(1)}, bf16[768,384]{1,0:T(8,128)(2,1)}, u32[]{:S(2)}) copy-start(bf16[768,384]{1,0:T(8,128)(2,1)} %copy-done.10) | copy-start | bytes 1769476
  172.8 2.1 %copy-start.27 = (bf16[768,384]{1,0:T(8,128)(2,1)S(1)}, bf16[768,384]{1,0:T(8,128)(2,1)}, u32[]{:S(2)}) copy-start(bf16[768,384]{1,0:T(8,128)(2,1)} %copy-done.26) | copy-start | bytes 1769476
  173.8 2.1 %copy-start.21 = (bf16[384,384]{1,0:T(8,128)(2,1)S(1)}, bf16[384,384]{1,0:T(8,128)(2,1)}, u32[]{:S(2)}) copy-start(bf16[384,384]{1,0:T(8,128)(2,1)} %copy-done.20) | copy-start | bytes 884740
  173.8 2.1 %copy-start.23 = (bf16[384,384]{1,0:T(8,128)(2,1)S(1)}, bf16[384,384]{1,0:T(8,128)(2,1)}, u32[]{:S(2)}) copy-start(bf16[384,384]{1,0:T(8,128)(2,1)} %copy-done.22) | copy-start | bytes 884740
  (8 other events, 8.2 us)

commit v2 on v1

v2 whole, which is shorter than its diff:
```python
import functools

import jax
import jax.numpy as jnp
from jax import lax
from jax.experimental import pallas as pl
from jax.experimental.pallas import tpu as pltpu
from jax.sharding import Mesh, PartitionSpec as P

BF = jnp.bfloat16
F32 = jnp.float32
VMEM_LIMIT = 32 * 1024 * 1024


def one_hot_table(ids, expert_count, capacity, part):
    half = capacity // 2
    experts = jnp.arange(expert_count, dtype=jnp.int32)
    chosen = (ids[:, :, None] == experts).astype(F32)
    per_token = jnp.sum(chosen, axis=1)
    count = ids.shape[0]
    before = (jnp.arange(count)[:, None] > jnp.arange(count)[None, :]).astype(BF)
    earlier = jnp.dot(before, per_token.astype(BF), preferred_element_type=F32)
    position = jnp.sum(chosen * earlier[:, None, :], axis=-1).astype(jnp.int32)
    target = ids * capacity + position
    rows = jnp.arange(expert_count * half, dtype=jnp.int32)
    columns = (rows // half) * capacity + part * half + rows % half
    hit = (target[:, 0][None, :] == columns[:, None]) | (target[:, 1][None, :] == columns[:, None])
    return hit.astype(BF)


def use_kernel(layout, first, *refs):
    pieces = sum(len(b) for b in layout)
    blocks = len(layout)
    it = iter(refs[1:])
    x_refs = [next(it) for _ in range(pieces)]
    w_mine = [next(it) for _ in range(blocks)]
    w_theirs = [next(it) for _ in range(blocks)]
    s_mine, s_theirs = next(it), next(it)
    acc_in = None if first else next(it)
    acc, g_mine, g_theirs = next(it), next(it), next(it)
    width = s_mine.shape[1]
    touched = set()
    n = 0
    for b in range(blocks):
        w = jnp.concatenate([w_mine[b][0], w_theirs[b][0]], axis=1)
        total = None
        for _, start, rows in layout[b]:
            x = x_refs[n][...]
            n += 1
            span = pl.ds(start, rows)
            product = jnp.dot(x, w, preferred_element_type=F32)
            if start not in touched:
                touched.add(start)
                if not first:
                    product = product + acc_in[span, :]
            else:
                product = product + acc[span, :]
            acc[span, :] = product
            s = jnp.concatenate([s_mine[span, :], s_theirs[span, :]], axis=1)
            outer = lax.dot_general(x, s, (((0,), (0,)), ((), ())), preferred_element_type=F32)
            total = outer if total is None else total + outer
        g_mine[b] = total[:, :width].astype(BF)
        g_theirs[b] = total[:, width:].astype(BF)


def use(layout, pieces, index, w_mine, w_theirs, s_mine, s_theirs, acc):
    first = acc is None
    blocks = len(layout)
    rows, width = s_mine.shape
    chip = pieces[0].shape[1]

    def whole(a):
        return pl.BlockSpec(a.shape, lambda i, idx: (0,) * a.ndim)

    def pick(j):
        return pl.BlockSpec((1, chip, width), lambda i, idx: (idx[j], 0, 0))

    ins = list(pieces) + [w_mine] * blocks + [w_theirs] * blocks + [s_mine, s_theirs]
    specs = [whole(a) for a in pieces] + [pick(j) for j in range(blocks)] * 2 + [whole(s_mine), whole(s_theirs)]
    aliases = {}
    if not first:
        aliases = {1 + len(ins): 0}
        ins.append(acc)
        specs.append(whole(acc))
    outs = [
        jax.ShapeDtypeStruct((rows, 2 * width), F32),
        jax.ShapeDtypeStruct((blocks, chip, width), BF),
        jax.ShapeDtypeStruct((blocks, chip, width), BF),
    ]
    return pl.pallas_call(
        functools.partial(use_kernel, layout, first),
        grid_spec=pltpu.PrefetchScalarGridSpec(
            num_scalar_prefetch=1,
            grid=(1,),
            in_specs=specs,
            out_specs=[pl.BlockSpec(o.shape, lambda i, idx, n=len(o.shape): (0,) * n) for o in outs],
        ),
        out_shape=outs,
        input_output_aliases=aliases,
        compiler_params=pltpu.CompilerParams(vmem_limit_bytes=VMEM_LIMIT),
        cost_estimate=pl.CostEstimate(
            flops=8 * blocks * rows * chip * width, bytes_accessed=blocks * 5000000, transcendentals=0
        ),
    )(index, *ins)


def place_kernel(counts, index, *refs):
    n = sum(counts)
    k = len(counts)
    mine, theirs, out = refs[:k], refs[k:-1], refs[-1]
    where = [(a, j) for a in range(k) for j in range(counts[a])]
    spots = []
    for ref in theirs:
        spots += [(ref, j) for j in range(ref.shape[0])]
    for i in range(n):
        a, j = where[i]
        ref, r = spots[i]
        out[index[i]] = (mine[a][j].astype(F32) + ref[r].astype(F32)).astype(BF)


def place(index, mine, theirs):
    counts = tuple(a.shape[0] for a in mine)
    n = sum(counts)
    shape = (n,) + mine[0].shape[1:]
    return pl.pallas_call(
        functools.partial(place_kernel, counts),
        grid_spec=pltpu.PrefetchScalarGridSpec(
            num_scalar_prefetch=1,
            grid=(1,),
            in_specs=[pl.BlockSpec(a.shape, lambda i, idx: (0, 0, 0)) for a in (*mine, *theirs)],
            out_specs=pl.BlockSpec(shape, lambda i, idx: (0, 0, 0)),
        ),
        out_shape=jax.ShapeDtypeStruct(shape, BF),
        compiler_params=pltpu.CompilerParams(vmem_limit_bytes=VMEM_LIMIT),
        cost_estimate=pl.CostEstimate(flops=1000000, bytes_accessed=5000000, transcendentals=0),
    )(index, *mine, *theirs)


def make_local(ny):
    half_y = ny // 2
    swap = [(0, 1), (1, 0)]

    def flat4(y, x, c, d):
        return ((y * 2 + x) * 2 + c) * 2 + d

    def token_moves(cross):
        pairs = []
        for y in range(ny):
            for x in range(2):
                for c in range(2):
                    for d in range(2):
                        to_y = (y % half_y) * 2 + x
                        to_x = 1 - c if cross else c
                        pairs.append((flat4(y, x, c, d), flat4(to_y, to_x, d, y // half_y)))
        return pairs

    def flat2(c, d):
        return c * 2 + d

    scaled_a = [(flat2(c, k), flat2(k, c)) for c in range(2) for k in range(2)]
    scaled_b = [(flat2(c, k), flat2(k, 1 - c)) for c in range(2) for k in range(2)]
    sums_a = [(flat2(1 - g, g), flat2(1 - g, 1 - g)) for g in range(2)] + [
        (flat2(g, g), flat2(1 - g, g)) for g in range(2)
    ]
    sums_b = [(flat2(1 - g, g), flat2(g, 1 - g)) for g in range(2)]
    up_ring = [(y, (y + 1) % ny) for y in range(ny)]
    down_ring = [(y, (y - 1) % ny) for y in range(ny)]

    def local(cotangent, expert_ids, combine, gate_saved, up_saved, w_down):
        expert_count = lax.axis_size("expert")
        y = lax.axis_index("y")
        core = lax.axis_index("core")
        xlo = lax.axis_index("xlo")
        dp = lax.axis_index("dp")
        rows = gate_saved.shape[2]
        width = gate_saved.shape[3]
        capacity = rows // expert_count
        half = capacity // 2
        lanes = cotangent.shape[2]
        chip = 2 * lanes
        every = ("y", "xlo", "core", "dp")

        ids = expert_ids[0].astype(BF)
        moved = lax.ppermute(jnp.concatenate([cotangent[0], ids], axis=1), every, token_moves(False))
        across = lax.ppermute(cotangent[0], every, token_moves(True))
        mine = moved[:, :lanes]
        tokens = jnp.concatenate([jnp.where(xlo == 0, mine, across), jnp.where(xlo == 0, across, mine)], axis=1)
        table = one_hot_table(moved[:, lanes:].astype(jnp.int32), expert_count, capacity, xlo)
        outgoing = jnp.dot(table, tokens, preferred_element_type=F32).astype(BF)
        outgoing = outgoing.reshape(expert_count, half, chip)
        part = lax.all_to_all(outgoing, "expert", split_axis=0, concat_axis=0, tiled=True)

        gate = gate_saved[0, 0].astype(F32)
        upper = up_saved[0, 0].astype(F32)
        weight_rows = combine[0, 0][:, None]
        sigma = jax.nn.sigmoid(gate)
        active = gate * sigma
        scaled = (weight_rows * (active * upper)).astype(BF)
        s_a = lax.ppermute(scaled, ("core", "dp"), scaled_a)
        s_b = lax.ppermute(scaled, ("core", "dp"), scaled_b)
        w_moved = lax.ppermute(w_down[0], "core", swap)

        from_x = lax.ppermute(part, "xlo", swap)
        from_x, s_a, s_b, w_moved = lax.optimization_barrier((from_x, s_a, s_b, w_moved))
        s_mine = jnp.where(dp == core, s_a, s_b)
        s_theirs = jnp.where(dp == core, s_b, s_a)
        w_mine = w_down[0].reshape(ny, chip, width)
        w_theirs = w_moved.reshape(ny, chip, width)
        block = jnp.stack([jnp.where(xlo == 0, part, from_x), jnp.where(xlo == 0, from_x, part)], axis=1)
        block = block.reshape(rows, chip)

        spot = lambda *offsets: jnp.stack([(y + o + ny) % ny for o in offsets]).astype(jnp.int32)
        full = (0, 0, rows)
        mid = rows // 2
        share_args = (w_mine, w_theirs, s_mine, s_theirs)
        g_mine, g_theirs, order = [], [], [0]
        up = down = block
        pending = (((full,),), [block], spot(0))
        acc = None

        def run(pending, acc):
            acc, gm, gt = use(*pending, *share_args, acc)
            g_mine.append(gm)
            g_theirs.append(gt)
            return acc

        for step in range(1, half_y + 1):
            if acc is not None:
                if step < half_y:
                    up, acc = lax.optimization_barrier((up, acc))
                    down, acc = lax.optimization_barrier((down, acc))
                else:
                    up, acc = lax.optimization_barrier((up, acc))
                    down, acc, sent = lax.optimization_barrier((down, acc, tuple(g_theirs)))
            if step < half_y:
                up_next = lax.ppermute(up, "y", up_ring)
                down_next = lax.ppermute(down, "y", down_ring)
                coming = (((full,), (full,)), [up_next, down_next], spot(-step, step))
                order += [-step, step]
            else:
                up_next = lax.ppermute(up[:mid], "y", up_ring)
                down_next = lax.ppermute(down[mid:], "y", down_ring)
                coming = ((((0, 0, mid), (0, mid, mid)),), [up_next, down_next], spot(half_y))
                order.append(half_y)
                early = lax.ppermute(jnp.concatenate(sent, axis=0), "core", swap)
            acc = run(pending, acc)
            up, down, pending = up_next, down_next, coming
        acc, early = lax.optimization_barrier((acc, early))
        acc = run(pending, acc)

        sum_mine, sum_theirs = acc[:, :width].astype(BF), acc[:, width:].astype(BF)
        held_own = dp == core
        got_a = lax.ppermute(jnp.where(held_own, sum_theirs, sum_mine), ("core", "dp"), sums_a)
        got_b = lax.ppermute(sum_theirs, ("core", "dp"), sums_b)

        late = lax.ppermute(jnp.concatenate(g_theirs[3:], axis=0), "core", swap)
        grad_weight = place(spot(*order), g_mine, [early, late]).reshape(ny * chip, width)

        mix = jnp.sum(
            s_mine.astype(F32) * acc[:, :width] + s_theirs.astype(F32) * acc[:, width:], axis=1
        )
        got_a, got_b, _ = lax.optimization_barrier((got_a, got_b, mix))
        members = 2 * ny * 4
        share = rows // (ny * 4)
        mix = jnp.stack([jnp.where(core == 0, mix, 0.0), jnp.where(core == 1, mix, 0.0)])
        mix = lax.all_to_all(mix.reshape(members, share), ("dp", "y", "xlo", "core"), 0, 0, tiled=True)
        mix = jnp.sum(mix, axis=0)
        blk = (y * 2 + xlo) * 2 + core
        mix = mix / lax.dynamic_slice_in_dim(combine[0, 0], blk * share, share, 0)

        grad_hidden = jnp.where(held_own, acc[:, :width], got_b.astype(F32)) + got_a.astype(F32)
        weighted = weight_rows * grad_hidden
        grad_gate = (weighted * upper * sigma * (1.0 + gate * (1.0 - sigma))).astype(BF)
        grad_upper = (weighted * active).astype(BF)
        return grad_gate[None, None], grad_upper[None, None], grad_weight[None], mix[None, None]

    return local


def solution(mesh):
    ne, nb, nd = mesh.devices.shape
    fine = Mesh(mesh.devices.reshape(ne, nb // 4, 2, 2, nd), ("expert", "y", "xlo", "core", "dp"))
    blk = ("y", "xlo", "core")
    return jax.shard_map(
        make_local(nb // 4),
        mesh=fine,
        in_specs=(
            P("dp", "expert", blk),
            P("dp", "expert", None),
            P("dp", "expert", None),
            P("dp", "expert", None, blk),
            P("dp", "expert", None, blk),
            P("expert", "dp", blk),
        ),
        out_specs=(
            P("dp", "expert", None, blk),
            P("dp", "expert", None, blk),
            P("expert", "dp", blk),
            P("dp", "expert", blk),
        ),
        check_vma=False,
    )
```

time: 180 us -> 173 us (0.961)
  matrix products: 26.3 us -> 1.18 us
  Pallas kernels: 0 us -> 17.9 us
  blocking collectives: 17.1 us -> 0 us
  waiting for transfers between devices: 20.5 us -> 36 us
  starting transfers between devices: 96.5 us -> 86.8 us
  local copies, waits for them, and re-layouts: 12.4 us -> 19.3 us
  other arithmetic: 3.93 us -> 9.65 us
    dot_general x32 -> x0, matrix products: 25.8 us -> none  [the longest x8 9.86 us: use(): lax.dot_general(own, scaled, dims, preferred_element_type=F32)]
    pallas_call x0 -> x6, Pallas kernels: none -> 17.9 us  [the longest x5 14.6 us: use(): pl.pallas_call(functools.partial(use_kernel, layout, first), grid_spec=pl...]
    all_to_all x1 -> x0, blocking collectives: 17.1 us -> none  [local(): lax.all_to_all(outgoing, 'expert', split_axis=0, concat_axis=0, tiled=True)]
    ppermute x23 -> x18, starting transfers between devices: 88.6 us -> 77.2 us  [the longest x3 16.4 us: local(): down_next = lax.ppermute(down, 'y', down_ring)]
    all_to_all x1 -> x2, waiting for transfers between devices: 0.01 us -> 9.22 us  [the longest x1 9.22 us: local(): lax.all_to_all(mix.reshape(members, share), ('dp', 'y', 'xlo', 'core'), 0...]
    ppermute x23 -> x18, waiting for transfers between devices: 20.5 us -> 26.7 us  [the longest x3 8.87 us: local(): up_next = lax.ppermute(up, 'y', up_ring)]
    unnamed x69, local copies, waits for them, and re-layouts: 10.4 us -> 15.1 us
    slice x0 -> x2, local copies, waits for them, and re-layouts: none -> 3.4 us  [the longest x1 1.71 us: local(): up_next = lax.ppermute(up[:mid], 'y', up_ring)]
  transfers between devices with their start and end apart: 24 -> 20, of which waited for: 5 -> 10; matrix products, arithmetic and copies ran while one was open for 19% -> 7% of each run, Pallas kernels for 0% -> 7%
where the time goes in v2:
time: 173 us; the launch traced here: 172 us
  starting transfers between devices  86.8 us (50%)
  waiting for transfers between devices  36 us (21%)
  local copies, waits for them, and re-layouts  19.3 us (11%)
  Pallas kernels  17.9 us (10%)
  other arithmetic  9.65 us (6%)
    ppermute x3, starting transfers between devices, local(): down_next = lax.ppermute(down, 'y', down_ring)  16.4 us
    unnamed x69, local copies, waits for them, and re-layouts  15.1 us
    pallas_call x5, Pallas kernels, use(): pl.pallas_call(functools.partial(use_kernel, layout, first), grid_spec=pl...  14.6 us
    ppermute x1, starting transfers between devices, local(): s_a = lax.ppermute(scaled, ('core', 'dp'), scaled_a)  11.8 us
    all_to_all x1, waiting for transfers between devices, local(): lax.all_to_all(mix.reshape(members, share), ('dp', 'y', 'xlo', 'core'), 0...  9.22 us
    ppermute x3, waiting for transfers between devices, local(): up_next = lax.ppermute(up, 'y', up_ring)  8.87 us
    ppermute x1, starting transfers between devices, local(): across = lax.ppermute(cotangent[0], every, token_moves(True))  8.79 us
    ppermute x3, starting transfers between devices, local(): up_next = lax.ppermute(up, 'y', up_ring)  8.52 us
  transfers between devices with their start and end apart: 20, of which 10 were waited for; matrix products, arithmetic and copies ran while one was open for 7% of the time, Pallas kernels for 7%

profile of v2, /device:TPU:1, one launch (start us, length us, event | category | flops | bytes accessed | tf_op | source)
XLA Modules:
  0.0 172.1 jit_solution(2837798260637786987)
XLA Ops:
  0.7 1.1 copy.24
  1.7 8.8 %collective-permute-start.1 = (bf16[192,192]{0,1:T(8,128)(2,1)S(1)}, bf16[192,192]{0,1:T(8,128)(2,1)S(1)}, u32[]{:S(2)}, u32[]{:S(2)}) collective-permute-start(bf16[192,192]{0,1:T(8,128)(2,1)S(1)} %bitcast.67), channel_id=1, source_target_pairs={{0,4},{1,6},{2,0},{3,2},{4,12},{5,14},{6,8},{7,10},{8,20},{9,22},{... | collective-permute-start | bytes 221192 | tf_op jit(solution)/shard_map/ppermute | solution.py:185
  11.2 1.9 %collective-permute-start = (bf16[192,194]{0,1:T(8,128)(2,1)S(1)}, bf16[192,194]{0,1:T(8,128)(2,1)S(1)}, u32[]{:S(2)}, u32[]{:S(2)}) collective-permute-start(bf16[192,194]{0,1:T(8,128)(2,1)S(1)} %pad_maximum_fusion.3), channel_id=1, source_target_pairs={{0,0},{1,2},{2,4},{3,6},{4,8},{5,10},{6,12},{7,14},{8,16},{9,18},{... | collective-permute-start | bytes 223496 | tf_op jit(solution)/shard_map/ppermute | solution.py:184
  13.2 1.9 %collective-permute-start.5 = (bf16[3072,256]{1,0:T(8,128)(2,1)}, bf16[3072,256]{1,0:T(8,128)(2,1)S(1)}, u32[]{:S(2)}, u32[]{:S(2)}) collective-permute-start(bf16[3072,256]{1,0:T(8,128)(2,1)} %bitcast.49), channel_id=1, source_target_pairs={{0,2},{2,0},{1,3},{3,1},{4,6},{6,4},{5,7},{7,5},{8,10},{10,8},{9,1... | collective-permute-start | bytes 4718600 | tf_op jit(solution)/shard_map/ppermute | solution.py:201
  15.1 4.4 %collective-permute-done = bf16[192,194]{0,1:T(8,128)(2,1)S(1)} collective-permute-done((bf16[192,194]{0,1:T(8,128)(2,1)S(1)}, bf16[192,194]{0,1:T(8,128)(2,1)S(1)}, u32[]{:S(2)}, u32[]{:S(2)}) %collective-permute-start) | collective-permute-done | bytes 74528 | tf_op jit(solution)/shard_map/ppermute | solution.py:184
  19.8 1.0 convolution_convert_fusion
  20.8 3.9 %all-to-all-start = ((bf16[8,48,384]{2,1,0:T(8,128)(2,1)}), bf16[8,48,384]{2,1,0:T(8,128)(2,1)S(1)}, u32[]{:S(2)}, u32[]{:S(2)}) async-start(bf16[8,48,384]{2,1,0:T(8,128)(2,1)} %bitcast.5), calls=%async_computation | async-start | bytes 589824 | tf_op jit(solution)/shard_map/all_to_all | solution.py:191
  25.0 11.8 %collective-permute-start.3 = (bf16[768,256]{1,0:T(8,128)(2,1)S(1)}, bf16[768,256]{1,0:T(8,128)(2,1)S(1)}, u32[]{:S(2)}, u32[]{:S(2)}) collective-permute-start(bf16[768,256]{1,0:T(8,128)(2,1)S(1)} %fusion.1), channel_id=1, source_target_pairs={{0,0},{1,2},{2,1},{3,3},{4,4},{5,6},{6,5},{7,7},{8,8},{9,10},{10,9... | collective-permute-start | bytes 1179656 | tf_op jit(solution)/shard_map/ppermute | solution.py:199
  36.8 1.9 %collective-permute-start.4 = (bf16[768,256]{1,0:T(8,128)(2,1)S(1)}, bf16[768,256]{1,0:T(8,128)(2,1)S(1)}, u32[]{:S(2)}, u32[]{:S(2)}) collective-permute-start(bf16[768,256]{1,0:T(8,128)(2,1)S(1)} %fusion.1), channel_id=1, source_target_pairs={{0,1},{1,3},{2,0},{3,2},{4,5},{5,7},{6,4},{7,6},{8,9},{9,11},{10,8... | collective-permute-start | bytes 1179656 | tf_op jit(solution)/shard_map/ppermute | solution.py:200
  38.8 2.7 %collective-permute-start.2 = (bf16[8,48,384]{2,1,0:T(8,128)(2,1)S(1)}, bf16[8,48,384]{2,1,0:T(8,128)(2,1)S(1)}, u32[]{:S(2)}, u32[]{:S(2)}) collective-permute-start(bf16[8,48,384]{2,1,0:T(8,128)(2,1)S(1)} %all-to-all-done), channel_id=1, source_target_pairs={{0,4},{4,0},{1,5},{5,1},{2,6},{6,2},{3,7},{7,3},{8,12},{12,8},{9,1... | collective-permute-start | bytes 884744 | tf_op jit(solution)/shard_map/ppermute | solution.py:203
  41.5 1.7 collective-permute-done.3
  43.2 3.7 %collective-permute-done.4 = bf16[768,256]{1,0:T(8,128)(2,1)S(1)} collective-permute-done((bf16[768,256]{1,0:T(8,128)(2,1)S(1)}, bf16[768,256]{1,0:T(8,128)(2,1)S(1)}, u32[]{:S(2)}, u32[]{:S(2)}) %collective-permute-start.4) | collective-permute-done | bytes 393248 | tf_op jit(solution)/shard_map/ppermute | solution.py:200
  46.9 4.1 %collective-permute-done.2 = bf16[8,48,384]{2,1,0:T(8,128)(2,1)S(1)} collective-permute-done((bf16[8,48,384]{2,1,0:T(8,128)(2,1)S(1)}, bf16[8,48,384]{2,1,0:T(8,128)(2,1)S(1)}, u32[]{:S(2)}, u32[]{:S(2)}) %collective-permute-start.2) | collective-permute-done | bytes 294944 | tf_op jit(solution)/shard_map/ppermute | solution.py:203
  52.0 4.7 %collective-permute-start.6 = (bf16[768,384]{1,0:T(8,128)(2,1)}, bf16[768,384]{1,0:T(8,128)(2,1)}, u32[]{:S(2)}, u32[]{:S(2)}) collective-permute-start(bf16[768,384]{1,0:T(8,128)(2,1)} %bitcast.13.refs_1_), channel_id=1, source_target_pairs={{0,8},{8,16},{16,24},{24,32},{32,40},{40,48},{48,56},{56,0},{1,9},... | collective-permute-start | bytes 1769480 | tf_op jit(solution)/shard_map/ppermute | solution.py:236
  56.7 7.3 %collective-permute-start.8 = (bf16[768,384]{1,0:T(8,128)(2,1)}, bf16[768,384]{1,0:T(8,128)(2,1)}, u32[]{:S(2)}, u32[]{:S(2)}) collective-permute-start(bf16[768,384]{1,0:T(8,128)(2,1)} %bitcast.13.refs_1_), channel_id=1, source_target_pairs={{0,56},{8,0},{16,8},{24,16},{32,24},{40,32},{48,40},{56,48},{1,57}... | collective-permute-start | bytes 1769480 | tf_op jit(solution)/shard_map/ppermute | solution.py:237
  64.0 1.2 broadcast_select_fusion
  65.2 2.1 %shard_map.93 = (f32[768,512]{1,0:T(8,128)S(1)}, bf16[1,384,256]{2,1,0:T(8,128)(2,1)S(1)}, bf16[1,384,256]{2,1,0:T(8,128)(2,1)S(1)}) custom-call(s32[1]{0:T(128)} %bitcast.14.refs_0_, bf16[768,384]{1,0:T(8,128)(2,1)} %bitcast.13.refs_1_, bf16[8,384,256]{2,1,0:T(8,128)(2,1)S(1)} %bitcast.50, bf16[8,384,256]{2,1,0:T(8,128)(2,1)S(1)} %bitcast.58, ...), custom_call_target="tpu_custom_call" | custom-call | flops 603979776 | bytes 5000000 | tf_op jit(solution)/shard_map/pallas_call | solution.py:90
  67.3 1.1 copy-done.1
  69.8 4.9 %collective-permute-done.6.refs_1_ = bf16[768,384]{1,0:T(8,128)(2,1)} collective-permute-done((bf16[768,384]{1,0:T(8,128)(2,1)}, bf16[768,384]{1,0:T(8,128)(2,1)}, u32[]{:S(2)}, u32[]{:S(2)}) %collective-permute-start.6) | collective-permute-done | bytes 589856 | tf_op jit(solution)/shard_map/ppermute | solution.py:236
  74.7 1.9 %collective-permute-start.7 = (bf16[768,384]{1,0:T(8,128)(2,1)}, bf16[768,384]{1,0:T(8,128)(2,1)}, u32[]{:S(2)}, u32[]{:S(2)}) collective-permute-start(bf16[768,384]{1,0:T(8,128)(2,1)} %collective-permute-done.6.refs_1_), channel_id=1, source_target_pairs={{0,8},{8,16},{16,24},{24,32},{32,40},{40,48},{48,56},{56,0},{1,9},... | collective-permute-start | bytes 1769480 | tf_op jit(solution)/shard_map/ppermute | solution.py:236
  76.6 4.6 %collective-permute-start.10 = (bf16[768,384]{1,0:T(8,128)(2,1)}, bf16[768,384]{1,0:T(8,128)(2,1)}, u32[]{:S(2)}, u32[]{:S(2)}) collective-permute-start(bf16[768,384]{1,0:T(8,128)(2,1)} %collective-permute-done.8.refs_2_), channel_id=1, source_target_pairs={{0,56},{8,0},{16,8},{24,16},{32,24},{40,32},{48,40},{56,48},{1,57}... | collective-permute-start | bytes 1769480 | tf_op jit(solution)/shard_map/ppermute | solution.py:237
  81.3 1.4 copy-done.2
  83.7 3.5 %shard_map.94 = (f32[768,512]{1,0:T(8,128)S(1)}, bf16[2,384,256]{2,1,0:T(8,128)(2,1)S(1)}, bf16[2,384,256]{2,1,0:T(8,128)(2,1)S(1)}) custom-call(s32[2]{0:T(128)S(1)} %pad_add_fusion.refs_0_, bf16[768,384]{1,0:T(8,128)(2,1)} %collective-permute-done.6.refs_1_, bf16[768,384]{1,0:T(8,128)(2,1)} %collective-permute-done.8.refs_2_, ...), custom_call_target="tpu_custom_call", output_to_operand_aliasing={{0}: (9, {})} | custom-call | flops 1207959552 | bytes 10000000 | tf_op jit(solution)/shard_map/pallas_call | solution.py:90
  87.2 1.1 copy-done.3
  89.8 1.2 collective-permute-done.7.refs_1_
  91.0 1.9 %collective-permute-start.9 = (bf16[768,384]{1,0:T(8,128)(2,1)}, bf16[768,384]{1,0:T(8,128)(2,1)}, u32[]{:S(2)}, u32[]{:S(2)}) collective-permute-start(bf16[768,384]{1,0:T(8,128)(2,1)} %collective-permute-done.7.refs_1_), channel_id=1, source_target_pairs={{0,8},{8,16},{16,24},{24,32},{32,40},{40,48},{48,56},{56,0},{1,9},... | collective-permute-start | bytes 1769480 | tf_op jit(solution)/shard_map/ppermute | solution.py:236
  92.9 4.6 %collective-permute-start.12 = (bf16[768,384]{1,0:T(8,128)(2,1)}, bf16[768,384]{1,0:T(8,128)(2,1)}, u32[]{:S(2)}, u32[]{:S(2)}) collective-permute-start(bf16[768,384]{1,0:T(8,128)(2,1)} %collective-permute-done.10.refs_2_), channel_id=1, source_target_pairs={{0,56},{8,0},{16,8},{24,16},{32,24},{40,32},{48,40},{56,48},{1,57}... | collective-permute-start | bytes 1769480 | tf_op jit(solution)/shard_map/ppermute | solution.py:237
  97.6 1.4 copy-done.4
  100.0 3.5 %shard_map.95 = (f32[768,512]{1,0:T(8,128)S(1)}, bf16[2,384,256]{2,1,0:T(8,128)(2,1)S(1)}, bf16[2,384,256]{2,1,0:T(8,128)(2,1)S(1)}) custom-call(s32[2]{0:T(128)S(1)} %pad_add_fusion.1.refs_0_, bf16[768,384]{1,0:T(8,128)(2,1)} %collective-permute-done.7.refs_1_, bf16[768,384]{1,0:T(8,128)(2,1)} %collective-permute-done.10.refs_2_, ...), custom_call_target="tpu_custom_call", output_to_operand_aliasing={{0}: (9, {})} | custom-call | flops 1207959552 | bytes 10000000 | tf_op jit(solution)/shard_map/pallas_call | solution.py:90
  103.5 2.8 %collective-permute-done.9.refs_1_ = bf16[768,384]{1,0:T(8,128)(2,1)} collective-permute-done((bf16[768,384]{1,0:T(8,128)(2,1)}, bf16[768,384]{1,0:T(8,128)(2,1)}, u32[]{:S(2)}, u32[]{:S(2)}) %collective-permute-start.9) | collective-permute-done | bytes 589856 | tf_op jit(solution)/shard_map/ppermute | solution.py:236
  107.3 1.1 pad_maximum_fusion
  108.3 6.0 %collective-permute-start.14 = (bf16[5,384,256]{2,1,0:T(8,128)(2,1)}, bf16[5,384,256]{2,1,0:T(8,128)(2,1)}, u32[]{:S(2)}, u32[]{:S(2)}) collective-permute-start(bf16[5,384,256]{2,1,0:T(8,128)(2,1)} %pad_maximum_fusion), channel_id=1, source_target_pairs={{0,2},{2,0},{1,3},{3,1},{4,6},{6,4},{5,7},{7,5},{8,10},{10,8},{9,1... | collective-permute-start | bytes 2949128 | tf_op jit(solution)/shard_map/ppermute | solution.py:245
  114.3 1.7 slice.32
  116.0 5.3 %collective-permute-start.13 = (bf16[384,384]{1,0:T(8,128)(2,1)}, bf16[384,384]{1,0:T(8,128)(2,1)}, u32[]{:S(2)}, u32[]{:S(2)}) collective-permute-start(bf16[384,384]{1,0:T(8,128)(2,1)} %slice.32), channel_id=1, source_target_pairs={{0,56},{8,0},{16,8},{24,16},{32,24},{40,32},{48,40},{56,48},{1,57}... | collective-permute-start | bytes 884744 | tf_op jit(solution)/shard_map/ppermute | solution.py:242
  121.3 1.7 slice.31
  123.0 1.9 %collective-permute-start.11 = (bf16[384,384]{1,0:T(8,128)(2,1)}, bf16[384,384]{1,0:T(8,128)(2,1)}, u32[]{:S(2)}, u32[]{:S(2)}) collective-permute-start(bf16[384,384]{1,0:T(8,128)(2,1)} %slice.31), channel_id=1, source_target_pairs={{0,8},{8,16},{16,24},{24,32},{32,40},{40,48},{48,56},{56,0},{1,9},... | collective-permute-start | bytes 884744 | tf_op jit(solution)/shard_map/ppermute | solution.py:241
  125.1 1.4 copy-done.6
  127.5 3.5 %shard_map.96 = (f32[768,512]{1,0:T(8,128)S(1)}, bf16[2,384,256]{2,1,0:T(8,128)(2,1)S(1)}, bf16[2,384,256]{2,1,0:T(8,128)(2,1)S(1)}) custom-call(s32[2]{0:T(128)S(1)} %pad_add_fusion.2.refs_0_, bf16[768,384]{1,0:T(8,128)(2,1)} %collective-permute-done.9.refs_1_, bf16[768,384]{1,0:T(8,128)(2,1)} %collective-permute-done.12.refs_2_, ...), custom_call_target="tpu_custom_call", output_to_operand_aliasing={{0}: (9, {})} | custom-call | flops 1207959552 | bytes 10000000 | tf_op jit(solution)/shard_map/pallas_call | solution.py:90
  131.7 3.0 %collective-permute-done.11.refs_1_ = bf16[384,384]{1,0:T(8,128)(2,1)} collective-permute-done((bf16[384,384]{1,0:T(8,128)(2,1)}, bf16[384,384]{1,0:T(8,128)(2,1)}, u32[]{:S(2)}, u32[]{:S(2)}) %collective-permute-start.11) | collective-permute-done | bytes 294944 | tf_op jit(solution)/shard_map/ppermute | solution.py:241
  134.7 2.1 %shard_map.97 = (f32[768,512]{1,0:T(8,128)S(1)}, bf16[1,384,256]{2,1,0:T(8,128)(2,1)S(1)}, bf16[1,384,256]{2,1,0:T(8,128)(2,1)S(1)}) custom-call(s32[1]{0:T(128)} %bitcast.refs_0_, bf16[384,384]{1,0:T(8,128)(2,1)} %collective-permute-done.11.refs_1_, bf16[384,384]{1,0:T(8,128)(2,1)} %collective-permute-done.13.refs_2_, ...), custom_call_target="tpu_custom_call", output_to_operand_aliasing={{0}: (7, {})} | custom-call | flops 603979776 | bytes 5000000 | tf_op jit(solution)/shard_map/pallas_call | solution.py:90
  138.1 1.9 %collective-permute-start.15 = (bf16[768,256]{1,0:T(8,128)(2,1)S(1)}, bf16[768,256]{1,0:T(8,128)(2,1)S(1)}, u32[]{:S(2)}, u32[]{:S(2)}) collective-permute-start(bf16[768,256]{1,0:T(8,128)(2,1)S(1)} %get-tuple-element.80), channel_id=1, source_target_pairs={{2,3},{1,0},{0,2},{3,1},{6,7},{5,4},{4,6},{7,5},{10,11},{9,8},{8,1... | collective-permute-start | bytes 1179656 | tf_op jit(solution)/shard_map/ppermute | solution.py:253
  140.0 6.2 %collective-permute-start.16 = (bf16[768,256]{1,0:T(8,128)(2,1)S(1)}, bf16[768,256]{1,0:T(8,128)(2,1)S(1)}, u32[]{:S(2)}, u32[]{:S(2)}) collective-permute-start(bf16[768,256]{1,0:T(8,128)(2,1)S(1)} %get-tuple-element.81), channel_id=1, source_target_pairs={{2,1},{1,2},{6,5},{5,6},{10,9},{9,10},{14,13},{13,14},{18,17},{17,... | collective-permute-start | bytes 1179656 | tf_op jit(solution)/shard_map/ppermute | solution.py:254
  146.2 1.9 %collective-permute-start.17 = (bf16[3,384,256]{2,1,0:T(8,128)(2,1)S(1)}, bf16[3,384,256]{2,1,0:T(8,128)(2,1)S(1)}, u32[]{:S(2)}, u32[]{:S(2)}) collective-permute-start(bf16[3,384,256]{2,1,0:T(8,128)(2,1)S(1)} %pad_maximum_fusion.2), channel_id=1, source_target_pairs={{0,2},{2,0},{1,3},{3,1},{4,6},{6,4},{5,7},{7,5},{8,10},{10,8},{9,1... | collective-permute-start | bytes 1769480 | tf_op jit(solution)/shard_map/ppermute | solution.py:256
  148.9 5.8 %all-to-all-start.1 = ((f32[64,1,24]{2,1,0:T(1,128)}), f32[64,1,24]{2,1,0:T(1,128)}, u32[]{:S(2)}, u32[]{:S(2)}) async-start(f32[64,1,24]{2,1,0:T(1,128)} %bitcast.69), calls=%async_computation.1 | async-start | bytes 65536 | tf_op jit(solution)/shard_map/all_to_all | solution.py:266
  154.8 9.2 %all-to-all-done.1 = f32[64,1,24]{2,1,0:T(1,128)} async-done(((f32[64,1,24]{2,1,0:T(1,128)}), f32[64,1,24]{2,1,0:T(1,128)}, u32[]{:S(2)}, u32[]{:S(2)}) %all-to-all-start.1) | async-done | bytes 6176 | tf_op jit(solution)/shard_map/all_to_all | solution.py:266
  164.8 1.3 bitcast_divide_fusion
  166.2 2.6 %fusion.10 = (bf16[1,1,768,256]{3,2,1,0:T(8,128)(2,1)}, bf16[1,1,768,256]{3,2,1,0:T(8,128)(2,1)}) fusion(bf16[1,1,768,256]{3,2,1,0:T(8,128)(2,1)S(1)} %copy-done.28, bf16[768,256]{1,0:T(8,128)(2,1)S(1)} %collective-permute-done.15, bf16[768,256]{1,0:T(8,128)(2,1)S(1)} %collective-permute-done.16, f32[768,512]{1,0:T(8,128)} %copy-done.7, pred[]{:T(512)S(6)} %eq.77, ...), kind=kLoop, calls=%fused_computation.24 | loop fusion | flops 3932160 | bytes 3148801 | tf_op jit(solution)/shard_map/broadcast_in_dim | solution.py:275
  168.9 3.2 %shard_map.98 = bf16[8,384,256]{2,1,0:T(8,128)(2,1)} custom-call(s32[8]{0:T(128)S(1)} %stack.72.index, bf16[1,384,256]{2,1,0:T(8,128)(2,1)S(1)} %copy-done.22, bf16[2,384,256]{2,1,0:T(8,128)(2,1)S(1)} %copy-done.14, bf16[2,384,256]{2,1,0:T(8,128)(2,1)S(1)} %copy-done.16, bf16[2,384,256]{2,1,0:T(8,128)(2,1)S(1)} %copy-done.18, ...), custom_call_target="tpu_custom_call" | custom-call | flops 1000000 | bytes 5000000 | tf_op jit(solution)/shard_map/pallas_call | solution.py:125
  (101 shorter events, 12.9 us)
Async XLA Ops:
  0.6 24.1 %copy-start.33 = (f32[1,1,768]{2,1,0:T(1,128)S(1)}, f32[1,1,768]{2,1,0:T(1,128)}, u32[]{:S(2)}) copy-start(f32[1,1,768]{2,1,0:T(1,128)} %param.8) | copy-start | bytes 9220
  0.6 24.1 %copy-start.29 = (bf16[1,1,768,256]{3,2,1,0:T(8,128)(2,1)S(1)}, bf16[1,1,768,256]{3,2,1,0:T(8,128)(2,1)}, u32[]{:S(2)}) copy-start(bf16[1,1,768,256]{3,2,1,0:T(8,128)(2,1)} %param.10) | copy-start | bytes 1179652
  0.7 24.1 %copy-start.27 = (bf16[1,1,768,256]{3,2,1,0:T(8,128)(2,1)S(1)}, bf16[1,1,768,256]{3,2,1,0:T(8,128)(2,1)}, u32[]{:S(2)}) copy-start(bf16[1,1,768,256]{3,2,1,0:T(8,128)(2,1)} %param.9) | copy-start | bytes 1179652
  1.7 18.0 %collective-permute-start.1 = (bf16[192,192]{0,1:T(8,128)(2,1)S(1)}, bf16[192,192]{0,1:T(8,128)(2,1)S(1)}, u32[]{:S(2)}, u32[]{:S(2)}) collective-permute-start(bf16[192,192]{0,1:T(8,128)(2,1)S(1)} %bitcast.67), channel_id=1, source_target_pairs={{0,4},{1,6},{2,0},{3,2},{4,12},{5,14},{6,8},{7,10},{8,20},{9,22},{... | collective-permute-start | bytes 221192 | tf_op jit(solution)/shard_map/ppermute | solution.py:185
  11.2 8.3 %collective-permute-start = (bf16[192,194]{0,1:T(8,128)(2,1)S(1)}, bf16[192,194]{0,1:T(8,128)(2,1)S(1)}, u32[]{:S(2)}, u32[]{:S(2)}) collective-permute-start(bf16[192,194]{0,1:T(8,128)(2,1)S(1)} %pad_maximum_fusion.3), channel_id=1, source_target_pairs={{0,0},{1,2},{2,4},{3,6},{4,8},{5,10},{6,12},{7,14},{8,16},{9,18},{... | collective-permute-start | bytes 223496 | tf_op jit(solution)/shard_map/ppermute | solution.py:184
  13.2 37.9 %collective-permute-start.5 = (bf16[3072,256]{1,0:T(8,128)(2,1)}, bf16[3072,256]{1,0:T(8,128)(2,1)S(1)}, u32[]{:S(2)}, u32[]{:S(2)}) collective-permute-start(bf16[3072,256]{1,0:T(8,128)(2,1)} %bitcast.49), channel_id=1, source_target_pairs={{0,2},{2,0},{1,3},{3,1},{4,6},{6,4},{5,7},{7,5},{8,10},{10,8},{9,1... | collective-permute-start | bytes 4718600 | tf_op jit(solution)/shard_map/ppermute | solution.py:201
  20.8 18.0 %all-to-all-start = ((bf16[8,48,384]{2,1,0:T(8,128)(2,1)}), bf16[8,48,384]{2,1,0:T(8,128)(2,1)S(1)}, u32[]{:S(2)}, u32[]{:S(2)}) async-start(bf16[8,48,384]{2,1,0:T(8,128)(2,1)} %bitcast.5), calls=%async_computation | async-start | bytes 589824 | tf_op jit(solution)/shard_map/all_to_all | solution.py:191
  25.0 18.2 %collective-permute-start.3 = (bf16[768,256]{1,0:T(8,128)(2,1)S(1)}, bf16[768,256]{1,0:T(8,128)(2,1)S(1)}, u32[]{:S(2)}, u32[]{:S(2)}) collective-permute-start(bf16[768,256]{1,0:T(8,128)(2,1)S(1)} %fusion.1), channel_id=1, source_target_pairs={{0,0},{1,2},{2,1},{3,3},{4,4},{5,6},{6,5},{7,7},{8,8},{9,10},{10,9... | collective-permute-start | bytes 1179656 | tf_op jit(solution)/shard_map/ppermute | solution.py:199
  36.8 10.0 %collective-permute-start.4 = (bf16[768,256]{1,0:T(8,128)(2,1)S(1)}, bf16[768,256]{1,0:T(8,128)(2,1)S(1)}, u32[]{:S(2)}, u32[]{:S(2)}) collective-permute-start(bf16[768,256]{1,0:T(8,128)(2,1)S(1)} %fusion.1), channel_id=1, source_target_pairs={{0,1},{1,3},{2,0},{3,2},{4,5},{5,7},{6,4},{7,6},{8,9},{9,11},{10,8... | collective-permute-start | bytes 1179656 | tf_op jit(solution)/shard_map/ppermute | solution.py:200
  38.8 12.2 %collective-permute-start.2 = (bf16[8,48,384]{2,1,0:T(8,128)(2,1)S(1)}, bf16[8,48,384]{2,1,0:T(8,128)(2,1)S(1)}, u32[]{:S(2)}, u32[]{:S(2)}) collective-permute-start(bf16[8,48,384]{2,1,0:T(8,128)(2,1)S(1)} %all-to-all-done), channel_id=1, source_target_pairs={{0,4},{4,0},{1,5},{5,1},{2,6},{6,2},{3,7},{7,3},{8,12},{12,8},{9,1... | collective-permute-start | bytes 884744 | tf_op jit(solution)/shard_map/ppermute | solution.py:203
  43.2 7.8 %copy-start.31 = (bf16[768,256]{1,0:T(8,128)(2,1)}, bf16[768,256]{1,0:T(8,128)(2,1)S(1)}, u32[]{:S(2)}) copy-start(bf16[768,256]{1,0:T(8,128)(2,1)S(1)} %collective-permute-done.3) | copy-start | bytes 1179652
  46.9 4.2 %copy-start.32 = (bf16[768,256]{1,0:T(8,128)(2,1)}, bf16[768,256]{1,0:T(8,128)(2,1)S(1)}, u32[]{:S(2)}) copy-start(bf16[768,256]{1,0:T(8,128)(2,1)S(1)} %collective-permute-done.4) | copy-start | bytes 1179652
  51.1 14.1 %copy-start = (bf16[1,3072,256]{2,1,0:T(8,128)(2,1)S(1)}, bf16[1,3072,256]{2,1,0:T(8,128)(2,1)}, u32[]{:S(2)}) copy-start(bf16[1,3072,256]{2,1,0:T(8,128)(2,1)} %param.11) | copy-start | bytes 4718596
  52.0 22.7 %collective-permute-start.6 = (bf16[768,384]{1,0:T(8,128)(2,1)}, bf16[768,384]{1,0:T(8,128)(2,1)}, u32[]{:S(2)}, u32[]{:S(2)}) collective-permute-start(bf16[768,384]{1,0:T(8,128)(2,1)} %bitcast.13.refs_1_), channel_id=1, source_target_pairs={{0,8},{8,16},{16,24},{24,32},{32,40},{40,48},{48,56},{56,0},{1,9},... | collective-permute-start | bytes 1769480 | tf_op jit(solution)/shard_map/ppermute | solution.py:236
  56.7 19.9 %collective-permute-start.8 = (bf16[768,384]{1,0:T(8,128)(2,1)}, bf16[768,384]{1,0:T(8,128)(2,1)}, u32[]{:S(2)}, u32[]{:S(2)}) collective-permute-start(bf16[768,384]{1,0:T(8,128)(2,1)} %bitcast.13.refs_1_), channel_id=1, source_target_pairs={{0,56},{8,0},{16,8},{24,16},{32,24},{40,32},{48,40},{56,48},{1,57}... | collective-permute-start | bytes 1769480 | tf_op jit(solution)/shard_map/ppermute | solution.py:237
  65.2 2.1 %copy-start.8 = (bf16[768,256]{1,0:T(8,128)(2,1)}, bf16[768,256]{1,0:T(8,128)(2,1)S(1)}, u32[]{:S(2)}) copy-start(bf16[768,256]{1,0:T(8,128)(2,1)S(1)} %get-tuple-element.85.refs_4_.refs_7_.refs_5_) | copy-start | bytes 1179652
  67.3 1.1 copy-start.1
  74.7 16.3 %collective-permute-start.7 = (bf16[768,384]{1,0:T(8,128)(2,1)}, bf16[768,384]{1,0:T(8,128)(2,1)}, u32[]{:S(2)}, u32[]{:S(2)}) collective-permute-start(bf16[768,384]{1,0:T(8,128)(2,1)} %collective-permute-done.6.refs_1_), channel_id=1, source_target_pairs={{0,8},{8,16},{16,24},{24,32},{32,40},{40,48},{48,56},{56,0},{1,9},... | collective-permute-start | bytes 1769480 | tf_op jit(solution)/shard_map/ppermute | solution.py:236
  76.6 16.3 %collective-permute-start.10 = (bf16[768,384]{1,0:T(8,128)(2,1)}, bf16[768,384]{1,0:T(8,128)(2,1)}, u32[]{:S(2)}, u32[]{:S(2)}) collective-permute-start(bf16[768,384]{1,0:T(8,128)(2,1)} %collective-permute-done.8.refs_2_), channel_id=1, source_target_pairs={{0,56},{8,0},{16,8},{24,16},{32,24},{40,32},{48,40},{56,48},{1,57}... | collective-permute-start | bytes 1769480 | tf_op jit(solution)/shard_map/ppermute | solution.py:237
  81.3 1.4 copy-start.2
  82.7 1.0 copy-start.9
  87.2 1.1 copy-start.3
  91.0 15.4 %collective-permute-start.9 = (bf16[768,384]{1,0:T(8,128)(2,1)}, bf16[768,384]{1,0:T(8,128)(2,1)}, u32[]{:S(2)}, u32[]{:S(2)}) collective-permute-start(bf16[768,384]{1,0:T(8,128)(2,1)} %collective-permute-done.7.refs_1_), channel_id=1, source_target_pairs={{0,8},{8,16},{16,24},{24,32},{32,40},{40,48},{48,56},{56,0},{1,9},... | collective-permute-start | bytes 1769480 | tf_op jit(solution)/shard_map/ppermute | solution.py:236
  92.9 14.3 %collective-permute-start.12 = (bf16[768,384]{1,0:T(8,128)(2,1)}, bf16[768,384]{1,0:T(8,128)(2,1)}, u32[]{:S(2)}, u32[]{:S(2)}) collective-permute-start(bf16[768,384]{1,0:T(8,128)(2,1)} %collective-permute-done.10.refs_2_), channel_id=1, source_target_pairs={{0,56},{8,0},{16,8},{24,16},{32,24},{40,32},{48,40},{56,48},{1,57}... | collective-permute-start | bytes 1769480 | tf_op jit(solution)/shard_map/ppermute | solution.py:237
  97.6 1.4 copy-start.4
  99.0 1.0 copy-start.10
  100.0 7.3 %copy-start.20 = (bf16[2,384,256]{2,1,0:T(8,128)(2,1)S(1)}, bf16[2,384,256]{2,1,0:T(8,128)(2,1)}, u32[]{:S(2)}) copy-start(bf16[2,384,256]{2,1,0:T(8,128)(2,1)} %copy-done.19) | copy-start | bytes 1179652
  100.0 7.3 %copy-start.26 = (bf16[1,384,256]{2,1,0:T(8,128)(2,1)S(1)}, bf16[1,384,256]{2,1,0:T(8,128)(2,1)}, u32[]{:S(2)}) copy-start(bf16[1,384,256]{2,1,0:T(8,128)(2,1)} %copy-done.25) | copy-start | bytes 589828
  103.5 19.5 %copy-start.5 = (f32[768,512]{1,0:T(8,128)}, f32[768,512]{1,0:T(8,128)S(1)}, u32[]{:S(2)}) copy-start(f32[768,512]{1,0:T(8,128)S(1)} %get-tuple-element.63.refs_9_) | copy-start | bytes 4718596
  103.5 19.5 %copy-start.15 = (bf16[2,384,256]{2,1,0:T(8,128)(2,1)}, bf16[2,384,256]{2,1,0:T(8,128)(2,1)S(1)}, u32[]{:S(2)}) copy-start(bf16[2,384,256]{2,1,0:T(8,128)(2,1)S(1)} %get-tuple-element.74.refs_2_) | copy-start | bytes 1179652
  108.3 23.4 %collective-permute-start.14 = (bf16[5,384,256]{2,1,0:T(8,128)(2,1)}, bf16[5,384,256]{2,1,0:T(8,128)(2,1)}, u32[]{:S(2)}, u32[]{:S(2)}) collective-permute-start(bf16[5,384,256]{2,1,0:T(8,128)(2,1)} %pad_maximum_fusion), channel_id=1, source_target_pairs={{0,2},{2,0},{1,3},{3,1},{4,6},{6,4},{5,7},{7,5},{8,10},{10,8},{9,1... | collective-permute-start | bytes 2949128 | tf_op jit(solution)/shard_map/ppermute | solution.py:245
  116.0 15.7 %collective-permute-start.13 = (bf16[384,384]{1,0:T(8,128)(2,1)}, bf16[384,384]{1,0:T(8,128)(2,1)}, u32[]{:S(2)}, u32[]{:S(2)}) collective-permute-start(bf16[384,384]{1,0:T(8,128)(2,1)} %slice.32), channel_id=1, source_target_pairs={{0,56},{8,0},{16,8},{24,16},{32,24},{40,32},{48,40},{56,48},{1,57}... | collective-permute-start | bytes 884744 | tf_op jit(solution)/shard_map/ppermute | solution.py:242
  123.0 11.7 %collective-permute-start.11 = (bf16[384,384]{1,0:T(8,128)(2,1)}, bf16[384,384]{1,0:T(8,128)(2,1)}, u32[]{:S(2)}, u32[]{:S(2)}) collective-permute-start(bf16[384,384]{1,0:T(8,128)(2,1)} %slice.31), channel_id=1, source_target_pairs={{0,8},{8,16},{16,24},{24,32},{32,40},{40,48},{48,56},{56,0},{1,9},... | collective-permute-start | bytes 884744 | tf_op jit(solution)/shard_map/ppermute | solution.py:241
  125.1 1.4 copy-start.6
  127.5 7.3 %copy-start.12 = (bf16[768,256]{1,0:T(8,128)(2,1)S(1)}, bf16[768,256]{1,0:T(8,128)(2,1)}, u32[]{:S(2)}) copy-start(bf16[768,256]{1,0:T(8,128)(2,1)} %copy-done.8) | copy-start | bytes 1179652
  136.9 1.1 copy-start.7
  136.9 1.2 copy-start.23
  137.1 29.0 %copy-start.28 = (bf16[1,1,768,256]{3,2,1,0:T(8,128)(2,1)S(1)}, bf16[1,1,768,256]{3,2,1,0:T(8,128)(2,1)}, u32[]{:S(2)}) copy-start(bf16[1,1,768,256]{3,2,1,0:T(8,128)(2,1)} %param.9) | copy-start | bytes 1179652
  137.1 29.0 %copy-start.30 = (bf16[1,1,768,256]{3,2,1,0:T(8,128)(2,1)S(1)}, bf16[1,1,768,256]{3,2,1,0:T(8,128)(2,1)}, u32[]{:S(2)}) copy-start(bf16[1,1,768,256]{3,2,1,0:T(8,128)(2,1)} %param.10) | copy-start | bytes 1179652
  138.1 28.1 %collective-permute-start.15 = (bf16[768,256]{1,0:T(8,128)(2,1)S(1)}, bf16[768,256]{1,0:T(8,128)(2,1)S(1)}, u32[]{:S(2)}, u32[]{:S(2)}) collective-permute-start(bf16[768,256]{1,0:T(8,128)(2,1)S(1)} %get-tuple-element.80), channel_id=1, source_target_pairs={{2,3},{1,0},{0,2},{3,1},{6,7},{5,4},{4,6},{7,5},{10,11},{9,8},{8,1... | collective-permute-start | bytes 1179656 | tf_op jit(solution)/shard_map/ppermute | solution.py:253
  140.0 26.2 %collective-permute-start.16 = (bf16[768,256]{1,0:T(8,128)(2,1)S(1)}, bf16[768,256]{1,0:T(8,128)(2,1)S(1)}, u32[]{:S(2)}, u32[]{:S(2)}) collective-permute-start(bf16[768,256]{1,0:T(8,128)(2,1)S(1)} %get-tuple-element.81), channel_id=1, source_target_pairs={{2,1},{1,2},{6,5},{5,6},{10,9},{9,10},{14,13},{13,14},{18,17},{17,... | collective-permute-start | bytes 1179656 | tf_op jit(solution)/shard_map/ppermute | solution.py:254
  146.2 22.6 %collective-permute-start.17 = (bf16[3,384,256]{2,1,0:T(8,128)(2,1)S(1)}, bf16[3,384,256]{2,1,0:T(8,128)(2,1)S(1)}, u32[]{:S(2)}, u32[]{:S(2)}) collective-permute-start(bf16[3,384,256]{2,1,0:T(8,128)(2,1)S(1)} %pad_maximum_fusion.2), channel_id=1, source_target_pairs={{0,2},{2,0},{1,3},{3,1},{4,6},{6,4},{5,7},{7,5},{8,10},{10,8},{9,1... | collective-permute-start | bytes 1769480 | tf_op jit(solution)/shard_map/ppermute | solution.py:256
  148.9 15.1 %all-to-all-start.1 = ((f32[64,1,24]{2,1,0:T(1,128)}), f32[64,1,24]{2,1,0:T(1,128)}, u32[]{:S(2)}, u32[]{:S(2)}) async-start(f32[64,1,24]{2,1,0:T(1,128)} %bitcast.69), calls=%async_computation.1 | async-start | bytes 65536 | tf_op jit(solution)/shard_map/all_to_all | solution.py:266
  166.1 2.7 %copy-start.14 = (bf16[2,384,256]{2,1,0:T(8,128)(2,1)S(1)}, bf16[2,384,256]{2,1,0:T(8,128)(2,1)}, u32[]{:S(2)}) copy-start(bf16[2,384,256]{2,1,0:T(8,128)(2,1)} %copy-done.13) | copy-start | bytes 1179652
  166.1 2.7 %copy-start.16 = (bf16[2,384,256]{2,1,0:T(8,128)(2,1)S(1)}, bf16[2,384,256]{2,1,0:T(8,128)(2,1)}, u32[]{:S(2)}) copy-start(bf16[2,384,256]{2,1,0:T(8,128)(2,1)} %copy-done.15) | copy-start | bytes 1179652
  166.1 2.7 %copy-start.18 = (bf16[2,384,256]{2,1,0:T(8,128)(2,1)S(1)}, bf16[2,384,256]{2,1,0:T(8,128)(2,1)}, u32[]{:S(2)}) copy-start(bf16[2,384,256]{2,1,0:T(8,128)(2,1)} %copy-done.17) | copy-start | bytes 1179652
  166.1 2.7 %copy-start.22 = (bf16[1,384,256]{2,1,0:T(8,128)(2,1)S(1)}, bf16[1,384,256]{2,1,0:T(8,128)(2,1)}, u32[]{:S(2)}) copy-start(bf16[1,384,256]{2,1,0:T(8,128)(2,1)} %copy-done.21) | copy-start | bytes 589828
  166.1 2.7 %copy-start.24 = (bf16[1,384,256]{2,1,0:T(8,128)(2,1)S(1)}, bf16[1,384,256]{2,1,0:T(8,128)(2,1)}, u32[]{:S(2)}) copy-start(bf16[1,384,256]{2,1,0:T(8,128)(2,1)} %copy-done.23) | copy-start | bytes 589828
  (6 other events, 4.6 us)

commit v3 on v2

v3 whole, which is shorter than its diff:
```python
import functools

import jax
import jax.numpy as jnp
from jax import lax
from jax.experimental import pallas as pl
from jax.experimental.pallas import tpu as pltpu
from jax.sharding import Mesh, PartitionSpec as P

BF = jnp.bfloat16
F32 = jnp.float32
VMEM_LIMIT = 60 * 1024 * 1024


def one_hot_table(ids, expert_count, capacity):
    experts = jnp.arange(expert_count, dtype=jnp.int32)
    chosen = (ids[:, :, None] == experts).astype(F32)
    per_token = jnp.sum(chosen, axis=1)
    count = ids.shape[0]
    before = (jnp.arange(count)[:, None] > jnp.arange(count)[None, :]).astype(BF)
    earlier = jnp.dot(before, per_token.astype(BF), preferred_element_type=F32)
    position = jnp.sum(chosen * earlier[:, None, :], axis=-1).astype(jnp.int32)
    target = ids * capacity + position
    columns = jnp.arange(expert_count * capacity, dtype=jnp.int32)
    hit = (target[:, 0][None, :] == columns[:, None]) | (target[:, 1][None, :] == columns[:, None])
    return hit.astype(BF)


def use_kernel(parts, first, carried, *refs):
    blocks = len(parts)
    it = iter(refs[1:])
    x_refs = [[next(it) for _ in range(n)] for n in parts]
    w_mine = [next(it) for _ in range(blocks)]
    w_theirs = [next(it) for _ in range(blocks)]
    s_mine, s_theirs = next(it), next(it)
    carry = next(it) if carried else None
    acc_in = None if first else next(it)
    acc, g_mine, g_theirs = next(it), next(it), next(it)
    width = s_mine.shape[1]
    s = jnp.concatenate([s_mine[...], s_theirs[...]], axis=1)
    for b in range(blocks):
        x = x_refs[b][0][...]
        for more in x_refs[b][1:]:
            x = x + more[...]
        w = jnp.concatenate([w_mine[b][0], w_theirs[b][0]], axis=1)
        product = jnp.dot(x, w, preferred_element_type=F32)
        if b == 0:
            acc[...] = product if first else product + acc_in[...]
        else:
            acc[...] += product
        outer = lax.dot_general(x, s, (((0,), (0,)), ((), ())), preferred_element_type=F32)
        g_mine[b] = outer[:, :width].astype(BF)
        g_theirs[carried + b] = outer[:, width:].astype(BF)
    if carried:
        g_theirs[:carried] = carry[...]


def use(pieces, index, w_mine, w_theirs, s_mine, s_theirs, acc, carry=None):
    first = acc is None
    parts = tuple(len(p) for p in pieces)
    blocks = len(parts)
    carried = 0 if carry is None else carry.shape[0]
    rows, width = s_mine.shape
    chip = pieces[0][0].shape[1]

    def whole(a):
        return pl.BlockSpec(a.shape, lambda i, idx: (0,) * len(a.shape))

    def pick(j):
        return pl.BlockSpec((1, chip, width), lambda i, idx: (idx[j], 0, 0))

    flat = [a for p in pieces for a in p]
    ins = flat + [w_mine] * blocks + [w_theirs] * blocks + [s_mine, s_theirs]
    specs = [whole(a) for a in flat] + [pick(j) for j in range(blocks)] * 2 + [whole(s_mine), whole(s_theirs)]
    if carried:
        ins.append(carry)
        specs.append(whole(carry))
    aliases = {}
    if not first:
        aliases = {1 + len(ins): 0}
        ins.append(acc)
        specs.append(whole(acc))
    outs = [
        jax.ShapeDtypeStruct((rows, 2 * width), F32),
        jax.ShapeDtypeStruct((blocks, chip, width), BF),
        jax.ShapeDtypeStruct((carried + blocks, chip, width), BF),
    ]
    return pl.pallas_call(
        functools.partial(use_kernel, parts, first, carried),
        grid_spec=pltpu.PrefetchScalarGridSpec(
            num_scalar_prefetch=1,
            grid=(1,),
            in_specs=specs,
            out_specs=[whole(o) for o in outs],
        ),
        out_shape=outs,
        input_output_aliases=aliases,
        compiler_params=pltpu.CompilerParams(vmem_limit_bytes=VMEM_LIMIT),
        cost_estimate=pl.CostEstimate(
            flops=8 * blocks * rows * chip * width, bytes_accessed=blocks * 4000000, transcendentals=0
        ),
    )(index, *ins)


def place_kernel(counts, index, *refs):
    n = sum(counts)
    k = len(counts)
    mine, theirs, out = refs[:k], refs[k:-1], refs[-1]
    where = [(a, j) for a in range(k) for j in range(counts[a])]
    spots = []
    for ref in theirs:
        spots += [(ref, j) for j in range(ref.shape[0])]
    for i in range(n):
        a, j = where[i]
        ref, r = spots[i]
        out[index[i]] = (mine[a][j].astype(F32) + ref[r].astype(F32)).astype(BF)


def place(index, mine, theirs):
    counts = tuple(a.shape[0] for a in mine)
    n = sum(counts)
    shape = (n,) + mine[0].shape[1:]
    return pl.pallas_call(
        functools.partial(place_kernel, counts),
        grid_spec=pltpu.PrefetchScalarGridSpec(
            num_scalar_prefetch=1,
            grid=(1,),
            in_specs=[pl.BlockSpec(a.shape, lambda i, idx: (0, 0, 0)) for a in (*mine, *theirs)],
            out_specs=pl.BlockSpec(shape, lambda i, idx: (0, 0, 0)),
        ),
        out_shape=jax.ShapeDtypeStruct(shape, BF),
        compiler_params=pltpu.CompilerParams(vmem_limit_bytes=VMEM_LIMIT),
        cost_estimate=pl.CostEstimate(flops=1000000, bytes_accessed=5000000, transcendentals=0),
    )(index, *mine, *theirs)


def make_local(ny):
    half_y = ny // 2
    swap = [(0, 1), (1, 0)]

    def flat4(y, x, c, d):
        return ((y * 2 + x) * 2 + c) * 2 + d

    def token_moves(cross):
        pairs = []
        for y in range(ny):
            for x in range(2):
                for c in range(2):
                    for d in range(2):
                        to_y = (y % half_y) * 2 + x
                        to_x = 1 - c if cross else c
                        pairs.append((flat4(y, x, c, d), flat4(to_y, to_x, d, y // half_y)))
        return pairs

    def flat2(c, d):
        return c * 2 + d

    scaled_a = [(flat2(c, k), flat2(k, c)) for c in range(2) for k in range(2)]
    scaled_b = [(flat2(c, k), flat2(k, 1 - c)) for c in range(2) for k in range(2)]
    sums_a = [(flat2(1 - g, g), flat2(1 - g, 1 - g)) for g in range(2)] + [
        (flat2(g, g), flat2(1 - g, g)) for g in range(2)
    ]
    sums_b = [(flat2(1 - g, g), flat2(g, 1 - g)) for g in range(2)]
    up_ring = [(y, (y + 1) % ny) for y in range(ny)]
    down_ring = [(y, (y - 1) % ny) for y in range(ny)]

    def local(cotangent, expert_ids, combine, gate_saved, up_saved, w_down):
        expert_count = lax.axis_size("expert")
        y = lax.axis_index("y")
        core = lax.axis_index("core")
        xlo = lax.axis_index("xlo")
        dp = lax.axis_index("dp")
        rows = gate_saved.shape[2]
        width = gate_saved.shape[3]
        capacity = rows // expert_count
        lanes = cotangent.shape[2]
        chip = 2 * lanes
        every = ("y", "xlo", "core", "dp")

        ids = expert_ids[0].astype(BF)
        moved = lax.ppermute(jnp.concatenate([cotangent[0], ids], axis=1), every, token_moves(False))
        across = lax.ppermute(cotangent[0], every, token_moves(True))
        mine = moved[:, :lanes]
        tokens = jnp.concatenate([jnp.where(xlo == 0, mine, across), jnp.where(xlo == 0, across, mine)], axis=1)
        table = one_hot_table(moved[:, lanes:].astype(jnp.int32), expert_count, capacity)
        outgoing = jnp.dot(table, tokens, preferred_element_type=F32).astype(BF)
        outgoing = outgoing.reshape(expert_count, capacity, chip)
        part = lax.all_to_all(outgoing, "expert", split_axis=0, concat_axis=0, tiled=True)

        gate = gate_saved[0, 0].astype(F32)
        upper = up_saved[0, 0].astype(F32)
        weight_rows = combine[0, 0][:, None]
        sigma = jax.nn.sigmoid(gate)
        active = gate * sigma
        scaled = (weight_rows * (active * upper)).astype(BF)
        w_sent, scaled = lax.optimization_barrier((w_down[0], scaled))
        s_a = lax.ppermute(scaled, ("core", "dp"), scaled_a)
        s_b = lax.ppermute(scaled, ("core", "dp"), scaled_b)
        w_moved = lax.ppermute(w_sent, "core", swap)

        spot = lambda *offsets: jnp.stack([(y + o + ny) % ny for o in offsets]).astype(jnp.int32)
        block = part.reshape(rows, chip)
        up = lax.ppermute(block, "y", up_ring)
        down = lax.ppermute(block, "y", down_ring)
        waiting, offsets, order = [[block], [up], [down]], (0, -1, 1), [0, -1, 1]
        acc, share_args, theirs = None, None, None
        g_mine, g_moved = [], []
        for step in range(2, half_y + 1):
            if acc is None:
                up, s_a, s_b, w_moved = lax.optimization_barrier((up, s_a, s_b, w_moved))
                share_args = (
                    w_down[0].reshape(ny, chip, width),
                    w_moved.reshape(ny, chip, width),
                    jnp.where(dp == core, s_a, s_b),
                    jnp.where(dp == core, s_b, s_a),
                )
            else:
                up, acc = lax.optimization_barrier((up, acc))
                down, acc, theirs = lax.optimization_barrier((down, acc, theirs))
                g_moved.append(lax.ppermute(theirs, "core", swap))
            if step < half_y:
                up = lax.ppermute(up, "y", up_ring)
                down = lax.ppermute(down, "y", down_ring)
                arriving = [[up], [down]]
            else:
                up = lax.ppermute(up, ("y", "core"), [(2 * a, 2 * b) for a, b in up_ring])
                down = lax.ppermute(down, ("y", "core"), [(2 * a + 1, 2 * b + 1) for a, b in down_ring])
                arriving = [[up, down]]
            acc, gm, theirs = use(waiting, spot(*offsets), *share_args, acc)
            g_mine.append(gm)
            waiting = arriving
            offsets = (-step, step) if step < half_y else (half_y,)
            order += list(offsets)
        acc, *g_moved = lax.optimization_barrier((acc, *g_moved))
        acc, gm, theirs = use(waiting, spot(*offsets), *share_args, acc, theirs)
        g_mine.append(gm)
        share_s = share_args[2:]

        sum_mine, sum_theirs = acc[:, :width].astype(BF), acc[:, width:].astype(BF)
        held_own = dp == core
        got_a = lax.ppermute(jnp.where(held_own, sum_theirs, sum_mine), ("core", "dp"), sums_a)
        got_b = lax.ppermute(sum_theirs, ("core", "dp"), sums_b)

        mix = jnp.sum(
            share_s[0].astype(F32) * acc[:, :width] + share_s[1].astype(F32) * acc[:, width:], axis=1
        )
        late = lax.ppermute(theirs, "core", swap)
        grad_weight = place(spot(*order), g_mine, [*g_moved, late]).reshape(ny * chip, width)
        got_a, got_b, _ = lax.optimization_barrier((got_a, got_b, mix))
        members = 2 * ny * 4
        share = rows // (ny * 4)
        mix = jnp.stack([jnp.where(core == 0, mix, 0.0), jnp.where(core == 1, mix, 0.0)])
        mix = lax.all_to_all(mix.reshape(members, share), ("dp", "y", "xlo", "core"), 0, 0, tiled=True)
        grad_hidden = jnp.where(held_own, acc[:, :width], got_b.astype(F32)) + got_a.astype(F32)
        weighted = weight_rows * grad_hidden
        grad_gate = (weighted * upper * sigma * (1.0 + gate * (1.0 - sigma))).astype(BF)
        grad_upper = (weighted * active).astype(BF)
        mix, grad_gate, grad_upper, grad_weight = lax.optimization_barrier((mix, grad_gate, grad_upper, grad_weight))
        mix = jnp.sum(mix, axis=0)
        blk = (y * 2 + xlo) * 2 + core
        mix = mix / lax.dynamic_slice_in_dim(combine[0, 0], blk * share, share, 0)
        return grad_gate[None, None], grad_upper[None, None], grad_weight[None], mix[None, None]

    return local


def solution(mesh):
    ne, nb, nd = mesh.devices.shape
    fine = Mesh(mesh.devices.reshape(ne, nb // 4, 2, 2, nd), ("expert", "y", "xlo", "core", "dp"))
    blk = ("y", "xlo", "core")
    return jax.shard_map(
        make_local(nb // 4),
        mesh=fine,
        in_specs=(
            P("dp", "expert", blk),
            P("dp", "expert", None),
            P("dp", "expert", None),
            P("dp", "expert", None, blk),
            P("dp", "expert", None, blk),
            P("expert", "dp", blk),
        ),
        out_specs=(
            P("dp", "expert", None, blk),
            P("dp", "expert", None, blk),
            P("expert", "dp", blk),
            P("dp", "expert", blk),
        ),
        check_vma=False,
    )
```

time: 173 us -> 162 us (0.936)
  local copies, waits for them, and re-layouts: 19.3 us -> 4.88 us
  Pallas kernels: 17.9 us -> 25.8 us
  starting transfers between devices: 86.8 us -> 80.7 us
  other arithmetic: 9.65 us -> 12.9 us
    all_to_all x1, waiting for transfers between devices: 0.01 us -> 16.6 us  [local(): lax.all_to_all(outgoing, 'expert', split_axis=0, concat_axis=0, tiled=True)]
    unnamed x69 -> x29, local copies, waits for them, and re-layouts: 15.1 us -> 3.49 us
    ppermute x12, waiting for transfers between devices: 17 us -> 6.54 us  [the longest x2 4.34 us: local(): up = lax.ppermute(up, 'y', up_ring)]
    ppermute x1, starting transfers between devices: 11.8 us -> 1.92 us  [local(): s_a = lax.ppermute(scaled, ('core', 'dp'), scaled_a)]
    all_to_all x1, waiting for transfers between devices: 9.22 us -> 1.6 us  [local(): lax.all_to_all(mix.reshape(members, share), ('dp', 'y', 'xlo', 'core'), 0...]
    pallas_call x5 -> x4, Pallas kernels: 14.6 us -> 21.8 us  [use(): pl.pallas_call(functools.partial(use_kernel, parts, first, carried), grid...]
    all_to_all x1, starting transfers between devices: 3.89 us -> 10 us  [local(): lax.all_to_all(outgoing, 'expert', split_axis=0, concat_axis=0, tiled=True)]
    ppermute x1, waiting for transfers between devices: 1.7 us -> 6.65 us  [local(): s_a = lax.ppermute(scaled, ('core', 'dp'), scaled_a)]
  transfers between devices with their start and end apart: 20 -> 20, of which waited for: 10 -> 9; matrix products, arithmetic and copies ran while one was open for 7% -> 6% of each run, Pallas kernels for 7% -> 13%
where the time goes in v3:
time: 162 us; the launch traced here: 161 us
  starting transfers between devices  80.7 us (50%)
  waiting for transfers between devices  34.3 us (21%)
  Pallas kernels  25.8 us (16%)
  other arithmetic  12.9 us (8%)
  local copies, waits for them, and re-layouts  4.88 us (3%)
    pallas_call x4, Pallas kernels, use(): pl.pallas_call(functools.partial(use_kernel, parts, first, carried), grid...  21.8 us
    all_to_all x1, waiting for transfers between devices, local(): lax.all_to_all(outgoing, 'expert', split_axis=0, concat_axis=0, tiled=True)  16.6 us
    ppermute x1, starting transfers between devices, local(): down = lax.ppermute(block, 'y', down_ring)  10.7 us
    all_to_all x1, starting transfers between devices, local(): lax.all_to_all(outgoing, 'expert', split_axis=0, concat_axis=0, tiled=True)  10 us
    ppermute x2, starting transfers between devices, local(): down = lax.ppermute(down, 'y', down_ring)  9.43 us
    ppermute x1, waiting for transfers between devices, local(): s_a = lax.ppermute(scaled, ('core', 'dp'), scaled_a)  6.65 us
    ppermute x1, starting transfers between devices, local(): got_b = lax.ppermute(sum_theirs, ('core', 'dp'), sums_b)  5.53 us
    ppermute x1, starting transfers between devices, local(): s_b = lax.ppermute(scaled, ('core', 'dp'), scaled_b)  5.13 us
  transfers between devices with their start and end apart: 20, of which 9 were waited for; matrix products, arithmetic and copies ran while one was open for 6% of the time, Pallas kernels for 13%

profile of v3, /device:TPU:1, one launch (start us, length us, event | category | flops | bytes accessed | tf_op | source)
XLA Modules:
  0.0 161.1 jit_solution(15361638219953360196)
XLA Ops:
  0.6 1.0 copy.20
  1.6 0.7 convert_bitcast_fusion
  2.3 4.6 %collective-permute-start = (bf16[192,194]{0,1:T(8,128)(2,1)S(1)}, bf16[192,194]{0,1:T(8,128)(2,1)S(1)}, u32[]{:S(2)}, u32[]{:S(2)}) collective-permute-start(bf16[192,194]{0,1:T(8,128)(2,1)S(1)} %pad_maximum_fusion), channel_id=1, source_target_pairs={{0,0},{1,2},{2,4},{3,6},{4,8},{5,10},{6,12},{7,14},{8,16},{9,18},{... | collective-permute-start | bytes 223496 | tf_op jit(solution)/shard_map/ppermute | solution.py:181
  7.0 4.9 %collective-permute-start.1 = (bf16[192,192]{0,1:T(8,128)(2,1)S(1)}, bf16[192,192]{0,1:T(8,128)(2,1)S(1)}, u32[]{:S(2)}, u32[]{:S(2)}) collective-permute-start(bf16[192,192]{0,1:T(8,128)(2,1)S(1)} %bitcast.58), channel_id=1, source_target_pairs={{0,4},{1,6},{2,0},{3,2},{4,12},{5,14},{6,8},{7,10},{8,20},{9,22},{... | collective-permute-start | bytes 221192 | tf_op jit(solution)/shard_map/ppermute | solution.py:182
  12.0 0.7 reduce
  12.9 0.9 collective-permute-done.1
  13.9 1.2 convolution_convert_fusion
  15.1 10.0 %all-to-all-start = ((bf16[8,96,384]{2,1,0:T(8,128)(2,1)}), bf16[8,96,384]{2,1,0:T(8,128)(2,1)}, u32[]{:S(2)}, u32[]{:S(2)}) async-start(bf16[8,96,384]{2,1,0:T(8,128)(2,1)} %bitcast.4), calls=%async_computation | async-start | bytes 1179648 | tf_op jit(solution)/shard_map/all_to_all | solution.py:188
  25.2 1.0 fusion.1
  26.2 1.9 %collective-permute-start.5 = (bf16[3072,256]{1,0:T(8,128)(2,1)S(1)}, bf16[3072,256]{1,0:T(8,128)(2,1)S(1)}, u32[]{:S(2)}, u32[]{:S(2)}) collective-permute-start(bf16[3072,256]{1,0:T(8,128)(2,1)S(1)} %bitcast.47), channel_id=1, source_target_pairs={{0,2},{2,0},{1,3},{3,1},{4,6},{6,4},{5,7},{7,5},{8,10},{10,8},{9,1... | collective-permute-start | bytes 4718600 | tf_op jit(solution)/shard_map/ppermute | solution.py:199
  28.1 16.6 %all-to-all-done = bf16[8,96,384]{2,1,0:T(8,128)(2,1)} async-done(((bf16[8,96,384]{2,1,0:T(8,128)(2,1)}), bf16[8,96,384]{2,1,0:T(8,128)(2,1)}, u32[]{:S(2)}, u32[]{:S(2)}) %all-to-all-start) | async-done | bytes 589856 | tf_op jit(solution)/shard_map/all_to_all | solution.py:188
  44.7 4.7 %collective-permute-start.2 = (bf16[768,384]{1,0:T(8,128)(2,1)}, bf16[768,384]{1,0:T(8,128)(2,1)}, u32[]{:S(2)}, u32[]{:S(2)}) collective-permute-start(bf16[768,384]{1,0:T(8,128)(2,1)} %bitcast.5.refs_1_), channel_id=1, source_target_pairs={{0,8},{8,16},{16,24},{24,32},{32,40},{40,48},{48,56},{56,0},{1,9},... | collective-permute-start | bytes 1769480 | tf_op jit(solution)/shard_map/ppermute | solution.py:203
  49.4 10.7 %collective-permute-start.7 = (bf16[768,384]{1,0:T(8,128)(2,1)}, bf16[768,384]{1,0:T(8,128)(2,1)}, u32[]{:S(2)}, u32[]{:S(2)}) collective-permute-start(bf16[768,384]{1,0:T(8,128)(2,1)} %bitcast.5.refs_1_), channel_id=1, source_target_pairs={{0,56},{8,0},{16,8},{24,16},{32,24},{40,32},{48,40},{56,48},{1,57}... | collective-permute-start | bytes 1769480 | tf_op jit(solution)/shard_map/ppermute | solution.py:204
  60.1 1.9 %collective-permute-start.3 = (bf16[768,256]{1,0:T(8,128)(2,1)}, bf16[768,256]{1,0:T(8,128)(2,1)}, u32[]{:S(2)}, u32[]{:S(2)}) collective-permute-start(bf16[768,256]{1,0:T(8,128)(2,1)} %fusion.1), channel_id=1, source_target_pairs={{0,0},{1,2},{2,1},{3,3},{4,4},{5,6},{6,5},{7,7},{8,8},{9,10},{10,9... | collective-permute-start | bytes 1179656 | tf_op jit(solution)/shard_map/ppermute | solution.py:197
  62.0 5.1 %collective-permute-start.4 = (bf16[768,256]{1,0:T(8,128)(2,1)}, bf16[768,256]{1,0:T(8,128)(2,1)}, u32[]{:S(2)}, u32[]{:S(2)}) collective-permute-start(bf16[768,256]{1,0:T(8,128)(2,1)} %fusion.1), channel_id=1, source_target_pairs={{0,1},{1,3},{2,0},{3,2},{4,5},{5,7},{6,4},{7,6},{8,9},{9,11},{10,8... | collective-permute-start | bytes 1179656 | tf_op jit(solution)/shard_map/ppermute | solution.py:198
  67.2 6.7 %collective-permute-done.3 = bf16[768,256]{1,0:T(8,128)(2,1)} collective-permute-done((bf16[768,256]{1,0:T(8,128)(2,1)}, bf16[768,256]{1,0:T(8,128)(2,1)}, u32[]{:S(2)}, u32[]{:S(2)}) %collective-permute-start.3) | collective-permute-done | bytes 393248 | tf_op jit(solution)/shard_map/ppermute | solution.py:197
  73.8 1.4 collective-permute-done.4
  75.3 1.9 %collective-permute-start.6 = (bf16[768,384]{1,0:T(8,128)(2,1)}, bf16[768,384]{1,0:T(8,128)(2,1)}, u32[]{:S(2)}, u32[]{:S(2)}) collective-permute-start(bf16[768,384]{1,0:T(8,128)(2,1)} %collective-permute-done.2.refs_2_), channel_id=1, source_target_pairs={{0,8},{8,16},{16,24},{24,32},{32,40},{40,48},{48,56},{56,0},{1,9},... | collective-permute-start | bytes 1769480 | tf_op jit(solution)/shard_map/ppermute | solution.py:222
  77.2 4.6 %collective-permute-start.9 = (bf16[768,384]{1,0:T(8,128)(2,1)}, bf16[768,384]{1,0:T(8,128)(2,1)}, u32[]{:S(2)}, u32[]{:S(2)}) collective-permute-start(bf16[768,384]{1,0:T(8,128)(2,1)} %collective-permute-done.7.refs_3_), channel_id=1, source_target_pairs={{0,56},{8,0},{16,8},{24,16},{32,24},{40,32},{48,40},{56,48},{1,57}... | collective-permute-start | bytes 1769480 | tf_op jit(solution)/shard_map/ppermute | solution.py:223
  82.4 2.0 %broadcast_select_fusion.1 = (bf16[768,256]{1,0:T(8,128)(2,1)}, bf16[768,256]{1,0:T(8,128)(2,1)}) fusion(bf16[768,256]{1,0:T(8,128)(2,1)} %collective-permute-done.3, bf16[768,256]{1,0:T(8,128)(2,1)} %collective-permute-done.4, pred[]{:T(512)S(6)} %eq.76), kind=kLoop, calls=%fused_computation.27 | loop fusion | flops 393216 | bytes 1572865 | tf_op jit(solution)/shard_map/jit(_where)/select_n | solution.py:214
  84.5 6.2 %shard_map.93 = (f32[768,512]{1,0:T(8,128)}, bf16[3,384,256]{2,1,0:T(8,128)(2,1)}, bf16[3,384,256]{2,1,0:T(8,128)(2,1)}) custom-call(s32[3]{0:T(128)} %pad_add_fusion.refs_0_, bf16[768,384]{1,0:T(8,128)(2,1)} %bitcast.5.refs_1_, bf16[768,384]{1,0:T(8,128)(2,1)} %collective-permute-done.2.refs_2_, bf16[768,384]{1,0:T(8,128)(2,1)} %collective-permute-done.7.refs_3_, ...), custom_call_target="tpu_custom_call" | custom-call | flops 1811939328 | bytes 12000000 | tf_op jit(solution)/shard_map/pallas_call | solution.py:88
  90.6 1.5 collective-permute-done.6.refs_1_
  92.1 1.9 %collective-permute-start.8 = (bf16[768,384]{1,0:T(8,128)(2,1)}, bf16[768,384]{1,0:T(8,128)(2,1)S(1)}, u32[]{:S(2)}, u32[]{:S(2)}) collective-permute-start(bf16[768,384]{1,0:T(8,128)(2,1)} %collective-permute-done.6.refs_1_), channel_id=1, source_target_pairs={{0,8},{8,16},{16,24},{24,32},{32,40},{40,48},{48,56},{56,0},{1,9},... | collective-permute-start | bytes 1769480 | tf_op jit(solution)/shard_map/ppermute | solution.py:222
  94.0 4.9 %collective-permute-start.11 = (bf16[768,384]{1,0:T(8,128)(2,1)}, bf16[768,384]{1,0:T(8,128)(2,1)S(1)}, u32[]{:S(2)}, u32[]{:S(2)}) collective-permute-start(bf16[768,384]{1,0:T(8,128)(2,1)} %collective-permute-done.9.refs_2_), channel_id=1, source_target_pairs={{0,56},{8,0},{16,8},{24,16},{32,24},{40,32},{48,40},{56,48},{1,57}... | collective-permute-start | bytes 1769480 | tf_op jit(solution)/shard_map/ppermute | solution.py:223
  99.5 1.9 %collective-permute-start.13 = (bf16[3,384,256]{2,1,0:T(8,128)(2,1)}, bf16[3,384,256]{2,1,0:T(8,128)(2,1)S(1)}, u32[]{:S(2)}, u32[]{:S(2)}) collective-permute-start(bf16[3,384,256]{2,1,0:T(8,128)(2,1)} %get-tuple-element.61), channel_id=1, source_target_pairs={{0,2},{2,0},{1,3},{3,1},{4,6},{6,4},{5,7},{7,5},{8,10},{10,8},{9,1... | collective-permute-start | bytes 1769480 | tf_op jit(solution)/shard_map/ppermute | solution.py:220
  101.4 5.7 %shard_map.94 = (f32[768,512]{1,0:T(8,128)}, bf16[2,384,256]{2,1,0:T(8,128)(2,1)}, bf16[2,384,256]{2,1,0:T(8,128)(2,1)}) custom-call(s32[2]{0:T(128)} %pad_add_fusion.1.refs_0_, bf16[768,384]{1,0:T(8,128)(2,1)} %collective-permute-done.6.refs_1_, bf16[768,384]{1,0:T(8,128)(2,1)} %collective-permute-done.9.refs_2_, ...), custom_call_target="tpu_custom_call", output_to_operand_aliasing={{0}: (9, {})} | custom-call | flops 1207959552 | bytes 8000000 | tf_op jit(solution)/shard_map/pallas_call | solution.py:88
  107.1 2.9 %collective-permute-done.8.refs_1_ = bf16[768,384]{1,0:T(8,128)(2,1)S(1)} collective-permute-done((bf16[768,384]{1,0:T(8,128)(2,1)}, bf16[768,384]{1,0:T(8,128)(2,1)S(1)}, u32[]{:S(2)}, u32[]{:S(2)}) %collective-permute-start.8) | collective-permute-done | bytes 589856 | tf_op jit(solution)/shard_map/ppermute | solution.py:222
  110.0 2.2 %collective-permute-done.11.refs_2_ = bf16[768,384]{1,0:T(8,128)(2,1)S(1)} collective-permute-done((bf16[768,384]{1,0:T(8,128)(2,1)}, bf16[768,384]{1,0:T(8,128)(2,1)S(1)}, u32[]{:S(2)}, u32[]{:S(2)}) %collective-permute-start.11) | collective-permute-done | bytes 589856 | tf_op jit(solution)/shard_map/ppermute | solution.py:223
  112.1 5.0 %collective-permute-start.12 = (bf16[768,384]{1,0:T(8,128)(2,1)S(1)}, bf16[768,384]{1,0:T(8,128)(2,1)S(1)}, u32[]{:S(2)}, u32[]{:S(2)}) collective-permute-start(bf16[768,384]{1,0:T(8,128)(2,1)S(1)} %collective-permute-done.11.refs_2_), channel_id=1, source_target_pairs={{2,58},{10,2},{18,10},{26,18},{34,26},{42,34},{50,42},{58,50},{3,5... | collective-permute-start | bytes 1769480 | tf_op jit(solution)/shard_map/ppermute | solution.py:227
  117.1 0.7 collective-permute-start.10
  117.8 1.9 %collective-permute-start.14 = (bf16[2,384,256]{2,1,0:T(8,128)(2,1)}, bf16[2,384,256]{2,1,0:T(8,128)(2,1)}, u32[]{:S(2)}, u32[]{:S(2)}) collective-permute-start(bf16[2,384,256]{2,1,0:T(8,128)(2,1)} %get-tuple-element.62), channel_id=1, source_target_pairs={{0,2},{2,0},{1,3},{3,1},{4,6},{6,4},{5,7},{7,5},{8,10},{10,8},{9,1... | collective-permute-start | bytes 1179656 | tf_op jit(solution)/shard_map/ppermute | solution.py:220
  119.8 0.7 stack.61.index
  120.5 0.7 pad_add_fusion.2.refs_0_
  121.1 5.6 %shard_map.95 = (f32[768,512]{1,0:T(8,128)}, bf16[2,384,256]{2,1,0:T(8,128)(2,1)}, bf16[2,384,256]{2,1,0:T(8,128)(2,1)}) custom-call(s32[2]{0:T(128)} %pad_add_fusion.2.refs_0_, bf16[768,384]{1,0:T(8,128)(2,1)} %copy-done.9, bf16[768,384]{1,0:T(8,128)(2,1)} %copy-done.10, bf16[8,384,256]{2,1,0:T(8,128)(2,1)} %bitcast.44, ...), custom_call_target="tpu_custom_call", output_to_operand_aliasing={{0}: (9, {})} | custom-call | flops 1207959552 | bytes 8000000 | tf_op jit(solution)/shard_map/pallas_call | solution.py:88
  126.8 0.8 copy-done.11
  127.6 0.8 copy-done.12
  128.4 4.3 %shard_map.96 = (f32[768,512]{1,0:T(8,128)}, bf16[1,384,256]{2,1,0:T(8,128)(2,1)}, bf16[3,384,256]{2,1,0:T(8,128)(2,1)}) custom-call(s32[1]{0:T(128)} %bitcast.10.refs_0_, bf16[768,384]{1,0:T(8,128)(2,1)} %copy-done.12, bf16[768,384]{1,0:T(8,128)(2,1)} %copy-done.11, bf16[8,384,256]{2,1,0:T(8,128)(2,1)} %bitcast.46, ...), custom_call_target="tpu_custom_call", output_to_operand_aliasing={{0}: (8, {})} | custom-call | flops 603979776 | bytes 4000000 | tf_op jit(solution)/shard_map/pallas_call | solution.py:88
  132.8 2.4 %fusion.11 = (bf16[768,256]{1,0:T(8,128)(2,1)}, bf16[768,256]{1,0:T(8,128)(2,1)}) fusion(f32[768,512]{1,0:T(8,128)} %get-tuple-element.64, pred[]{:T(512)S(6)} %eq.76), kind=kLoop, calls=%fused_computation.23 | loop fusion | flops 196608 | bytes 1572865 | tf_op jit(solution)/shard_map/jit(_where)/select_n | solution.py:241
  135.2 2.0 %collective-permute-start.15 = (bf16[768,256]{1,0:T(8,128)(2,1)}, bf16[768,256]{1,0:T(8,128)(2,1)}, u32[]{:S(2)}, u32[]{:S(2)}) collective-permute-start(bf16[768,256]{1,0:T(8,128)(2,1)} %get-tuple-element.78), channel_id=1, source_target_pairs={{2,3},{1,0},{0,2},{3,1},{6,7},{5,4},{4,6},{7,5},{10,11},{9,8},{8,1... | collective-permute-start | bytes 1179656 | tf_op jit(solution)/shard_map/ppermute | solution.py:241
  137.2 5.5 %collective-permute-start.16 = (bf16[768,256]{1,0:T(8,128)(2,1)}, bf16[768,256]{1,0:T(8,128)(2,1)}, u32[]{:S(2)}, u32[]{:S(2)}) collective-permute-start(bf16[768,256]{1,0:T(8,128)(2,1)} %get-tuple-element.79), channel_id=1, source_target_pairs={{2,1},{1,2},{6,5},{5,6},{10,9},{9,10},{14,13},{13,14},{18,17},{17,... | collective-permute-start | bytes 1179656 | tf_op jit(solution)/shard_map/ppermute | solution.py:242
  143.0 1.9 %collective-permute-start.17 = (bf16[3,384,256]{2,1,0:T(8,128)(2,1)}, bf16[3,384,256]{2,1,0:T(8,128)(2,1)S(1)}, u32[]{:S(2)}, u32[]{:S(2)}) collective-permute-start(bf16[3,384,256]{2,1,0:T(8,128)(2,1)} %get-tuple-element.73), channel_id=1, source_target_pairs={{0,2},{2,0},{1,3},{3,1},{4,6},{6,4},{5,7},{7,5},{8,10},{10,8},{9,1... | collective-permute-start | bytes 1769480 | tf_op jit(solution)/shard_map/ppermute | solution.py:247
  145.0 0.7 all_to_all.12
  145.7 4.5 %all-to-all-start.1 = ((f32[64,1,24]{2,1,0:T(1,128)}), f32[64,1,24]{2,1,0:T(1,128)S(1)}, u32[]{:S(2)}, u32[]{:S(2)}) async-start(f32[64,1,24]{2,1,0:T(1,128)} %bitcast.20), calls=%async_computation.1 | async-start | bytes 65536 | tf_op jit(solution)/shard_map/all_to_all | solution.py:253
  150.8 2.5 %multiply_convert_fusion = (bf16[768,256]{1,0:T(8,128)(2,1)}, bf16[768,256]{1,0:T(8,128)(2,1)}) fusion(bf16[1,1,768,256]{3,2,1,0:T(8,128)(2,1)S(1)} %copy-done.5, bf16[768,256]{1,0:T(8,128)(2,1)} %collective-permute-done.15, bf16[768,256]{1,0:T(8,128)(2,1)} %collective-permute-done.16, f32[768,512]{1,0:T(8,128)S(1)} %copy-done.2, pred[]{:T(512)S(6)} %eq.76, ...), kind=kLoop, calls=%fused_computation.15 | loop fusion | flops 3932160 | bytes 3148801 | tf_op jit(solution)/shard_map/convert_element_type | solution.py:257
  153.4 0.8 copy-done.13
  154.2 4.0 %shard_map.97 = bf16[8,384,256]{2,1,0:T(8,128)(2,1)} custom-call(s32[8]{0:T(128)} %stack.61.index, bf16[3,384,256]{2,1,0:T(8,128)(2,1)} %get-tuple-element.67.refs_0_, bf16[2,384,256]{2,1,0:T(8,128)(2,1)} %get-tuple-element.68.refs_1_, bf16[2,384,256]{2,1,0:T(8,128)(2,1)} %get-tuple-element.69.refs_2_, bf16[1,384,256]{2,1,0:T(8,128)(2,1)} %get-tuple-element.70.refs_3_, ...), custom_call_target="tpu_custom_call" | custom-call | flops 1000000 | bytes 5000000 | tf_op jit(solution)/shard_map/pallas_call | solution.py:123
  158.2 1.6 all-to-all-done.1
  159.8 1.3 bitcast_divide_fusion
  (53 shorter events, 2.4 us)
Async XLA Ops:
  2.3 22.8 %copy-start.5 = (bf16[1,1,768,256]{3,2,1,0:T(8,128)(2,1)S(1)}, bf16[1,1,768,256]{3,2,1,0:T(8,128)(2,1)}, u32[]{:S(2)}) copy-start(bf16[1,1,768,256]{3,2,1,0:T(8,128)(2,1)} %param.9) | copy-start | bytes 1179652
  2.3 22.8 %copy-start.6 = (bf16[1,1,768,256]{3,2,1,0:T(8,128)(2,1)S(1)}, bf16[1,1,768,256]{3,2,1,0:T(8,128)(2,1)}, u32[]{:S(2)}) copy-start(bf16[1,1,768,256]{3,2,1,0:T(8,128)(2,1)} %param.10) | copy-start | bytes 1179652
  2.3 10.3 %collective-permute-start = (bf16[192,194]{0,1:T(8,128)(2,1)S(1)}, bf16[192,194]{0,1:T(8,128)(2,1)S(1)}, u32[]{:S(2)}, u32[]{:S(2)}) collective-permute-start(bf16[192,194]{0,1:T(8,128)(2,1)S(1)} %pad_maximum_fusion), channel_id=1, source_target_pairs={{0,0},{1,2},{2,4},{3,6},{4,8},{5,10},{6,12},{7,14},{8,16},{9,18},{... | collective-permute-start | bytes 223496 | tf_op jit(solution)/shard_map/ppermute | solution.py:181
  7.0 6.9 %collective-permute-start.1 = (bf16[192,192]{0,1:T(8,128)(2,1)S(1)}, bf16[192,192]{0,1:T(8,128)(2,1)S(1)}, u32[]{:S(2)}, u32[]{:S(2)}) collective-permute-start(bf16[192,192]{0,1:T(8,128)(2,1)S(1)} %bitcast.58), channel_id=1, source_target_pairs={{0,4},{1,6},{2,0},{3,2},{4,12},{5,14},{6,8},{7,10},{8,20},{9,22},{... | collective-permute-start | bytes 221192 | tf_op jit(solution)/shard_map/ppermute | solution.py:182
  13.9 12.3 %copy-start = (bf16[1,3072,256]{2,1,0:T(8,128)(2,1)S(1)}, bf16[1,3072,256]{2,1,0:T(8,128)(2,1)}, u32[]{:S(2)}) copy-start(bf16[1,3072,256]{2,1,0:T(8,128)(2,1)} %param.11) | copy-start | bytes 4718596
  15.1 29.6 %all-to-all-start = ((bf16[8,96,384]{2,1,0:T(8,128)(2,1)}), bf16[8,96,384]{2,1,0:T(8,128)(2,1)}, u32[]{:S(2)}, u32[]{:S(2)}) async-start(bf16[8,96,384]{2,1,0:T(8,128)(2,1)} %bitcast.4), calls=%async_computation | async-start | bytes 1179648 | tf_op jit(solution)/shard_map/all_to_all | solution.py:188
  26.2 49.1 %collective-permute-start.5 = (bf16[3072,256]{1,0:T(8,128)(2,1)S(1)}, bf16[3072,256]{1,0:T(8,128)(2,1)S(1)}, u32[]{:S(2)}, u32[]{:S(2)}) collective-permute-start(bf16[3072,256]{1,0:T(8,128)(2,1)S(1)} %bitcast.47), channel_id=1, source_target_pairs={{0,2},{2,0},{1,3},{3,1},{4,6},{6,4},{5,7},{7,5},{8,10},{10,8},{9,1... | collective-permute-start | bytes 4718600 | tf_op jit(solution)/shard_map/ppermute | solution.py:199
  44.7 30.6 %collective-permute-start.2 = (bf16[768,384]{1,0:T(8,128)(2,1)}, bf16[768,384]{1,0:T(8,128)(2,1)}, u32[]{:S(2)}, u32[]{:S(2)}) collective-permute-start(bf16[768,384]{1,0:T(8,128)(2,1)} %bitcast.5.refs_1_), channel_id=1, source_target_pairs={{0,8},{8,16},{16,24},{24,32},{32,40},{40,48},{48,56},{56,0},{1,9},... | collective-permute-start | bytes 1769480 | tf_op jit(solution)/shard_map/ppermute | solution.py:203
  49.4 27.8 %collective-permute-start.7 = (bf16[768,384]{1,0:T(8,128)(2,1)}, bf16[768,384]{1,0:T(8,128)(2,1)}, u32[]{:S(2)}, u32[]{:S(2)}) collective-permute-start(bf16[768,384]{1,0:T(8,128)(2,1)} %bitcast.5.refs_1_), channel_id=1, source_target_pairs={{0,56},{8,0},{16,8},{24,16},{32,24},{40,32},{48,40},{56,48},{1,57}... | collective-permute-start | bytes 1769480 | tf_op jit(solution)/shard_map/ppermute | solution.py:204
  60.1 13.7 %collective-permute-start.3 = (bf16[768,256]{1,0:T(8,128)(2,1)}, bf16[768,256]{1,0:T(8,128)(2,1)}, u32[]{:S(2)}, u32[]{:S(2)}) collective-permute-start(bf16[768,256]{1,0:T(8,128)(2,1)} %fusion.1), channel_id=1, source_target_pairs={{0,0},{1,2},{2,1},{3,3},{4,4},{5,6},{6,5},{7,7},{8,8},{9,10},{10,9... | collective-permute-start | bytes 1179656 | tf_op jit(solution)/shard_map/ppermute | solution.py:197
  62.0 13.2 %collective-permute-start.4 = (bf16[768,256]{1,0:T(8,128)(2,1)}, bf16[768,256]{1,0:T(8,128)(2,1)}, u32[]{:S(2)}, u32[]{:S(2)}) collective-permute-start(bf16[768,256]{1,0:T(8,128)(2,1)} %fusion.1), channel_id=1, source_target_pairs={{0,1},{1,3},{2,0},{3,2},{4,5},{5,7},{6,4},{7,6},{8,9},{9,11},{10,8... | collective-permute-start | bytes 1179656 | tf_op jit(solution)/shard_map/ppermute | solution.py:198
  75.2 9.2 %copy-start.1 = (bf16[3072,256]{1,0:T(8,128)(2,1)}, bf16[3072,256]{1,0:T(8,128)(2,1)S(1)}, u32[]{:S(2)}) copy-start(bf16[3072,256]{1,0:T(8,128)(2,1)S(1)} %collective-permute-done.5) | copy-start | bytes 4718596
  75.3 16.9 %collective-permute-start.6 = (bf16[768,384]{1,0:T(8,128)(2,1)}, bf16[768,384]{1,0:T(8,128)(2,1)}, u32[]{:S(2)}, u32[]{:S(2)}) collective-permute-start(bf16[768,384]{1,0:T(8,128)(2,1)} %collective-permute-done.2.refs_2_), channel_id=1, source_target_pairs={{0,8},{8,16},{16,24},{24,32},{32,40},{40,48},{48,56},{56,0},{1,9},... | collective-permute-start | bytes 1769480 | tf_op jit(solution)/shard_map/ppermute | solution.py:222
  77.2 16.8 %collective-permute-start.9 = (bf16[768,384]{1,0:T(8,128)(2,1)}, bf16[768,384]{1,0:T(8,128)(2,1)}, u32[]{:S(2)}, u32[]{:S(2)}) collective-permute-start(bf16[768,384]{1,0:T(8,128)(2,1)} %collective-permute-done.7.refs_3_), channel_id=1, source_target_pairs={{0,56},{8,0},{16,8},{24,16},{32,24},{40,32},{48,40},{56,48},{1,57}... | collective-permute-start | bytes 1769480 | tf_op jit(solution)/shard_map/ppermute | solution.py:223
  92.1 17.8 %collective-permute-start.8 = (bf16[768,384]{1,0:T(8,128)(2,1)}, bf16[768,384]{1,0:T(8,128)(2,1)S(1)}, u32[]{:S(2)}, u32[]{:S(2)}) collective-permute-start(bf16[768,384]{1,0:T(8,128)(2,1)} %collective-permute-done.6.refs_1_), channel_id=1, source_target_pairs={{0,8},{8,16},{16,24},{24,32},{32,40},{40,48},{48,56},{56,0},{1,9},... | collective-permute-start | bytes 1769480 | tf_op jit(solution)/shard_map/ppermute | solution.py:222
  94.0 18.1 %collective-permute-start.11 = (bf16[768,384]{1,0:T(8,128)(2,1)}, bf16[768,384]{1,0:T(8,128)(2,1)S(1)}, u32[]{:S(2)}, u32[]{:S(2)}) collective-permute-start(bf16[768,384]{1,0:T(8,128)(2,1)} %collective-permute-done.9.refs_2_), channel_id=1, source_target_pairs={{0,56},{8,0},{16,8},{24,16},{32,24},{40,32},{48,40},{56,48},{1,57}... | collective-permute-start | bytes 1769480 | tf_op jit(solution)/shard_map/ppermute | solution.py:223
  99.5 27.2 %collective-permute-start.13 = (bf16[3,384,256]{2,1,0:T(8,128)(2,1)}, bf16[3,384,256]{2,1,0:T(8,128)(2,1)S(1)}, u32[]{:S(2)}, u32[]{:S(2)}) collective-permute-start(bf16[3,384,256]{2,1,0:T(8,128)(2,1)} %get-tuple-element.61), channel_id=1, source_target_pairs={{0,2},{2,0},{1,3},{3,1},{4,6},{6,4},{5,7},{7,5},{8,10},{10,8},{9,1... | collective-permute-start | bytes 1769480 | tf_op jit(solution)/shard_map/ppermute | solution.py:220
  110.0 11.2 %copy-start.9 = (bf16[768,384]{1,0:T(8,128)(2,1)}, bf16[768,384]{1,0:T(8,128)(2,1)S(1)}, u32[]{:S(2)}) copy-start(bf16[768,384]{1,0:T(8,128)(2,1)S(1)} %collective-permute-done.8.refs_1_) | copy-start | bytes 1769476
  112.1 9.0 %copy-start.10 = (bf16[768,384]{1,0:T(8,128)(2,1)}, bf16[768,384]{1,0:T(8,128)(2,1)S(1)}, u32[]{:S(2)}) copy-start(bf16[768,384]{1,0:T(8,128)(2,1)S(1)} %collective-permute-done.11.refs_2_) | copy-start | bytes 1769476
  112.1 14.6 %collective-permute-start.12 = (bf16[768,384]{1,0:T(8,128)(2,1)S(1)}, bf16[768,384]{1,0:T(8,128)(2,1)S(1)}, u32[]{:S(2)}, u32[]{:S(2)}) collective-permute-start(bf16[768,384]{1,0:T(8,128)(2,1)S(1)} %collective-permute-done.11.refs_2_), channel_id=1, source_target_pairs={{2,58},{10,2},{18,10},{26,18},{34,26},{42,34},{50,42},{58,50},{3,5... | collective-permute-start | bytes 1769480 | tf_op jit(solution)/shard_map/ppermute | solution.py:227
  117.1 9.7 %collective-permute-start.10 = (bf16[768,384]{1,0:T(8,128)(2,1)S(1)}, bf16[768,384]{1,0:T(8,128)(2,1)S(1)}, u32[]{:S(2)}, u32[]{:S(2)}) collective-permute-start(bf16[768,384]{1,0:T(8,128)(2,1)S(1)} %collective-permute-done.8.refs_1_), channel_id=1, source_target_pairs={{0,8},{8,16},{16,24},{24,32},{32,40},{40,48},{48,56},{56,0},{1,9},... | collective-permute-start | bytes 1769480 | tf_op jit(solution)/shard_map/ppermute | solution.py:226
  117.8 8.9 %collective-permute-start.14 = (bf16[2,384,256]{2,1,0:T(8,128)(2,1)}, bf16[2,384,256]{2,1,0:T(8,128)(2,1)}, u32[]{:S(2)}, u32[]{:S(2)}) collective-permute-start(bf16[2,384,256]{2,1,0:T(8,128)(2,1)} %get-tuple-element.62), channel_id=1, source_target_pairs={{0,2},{2,0},{1,3},{3,1},{4,6},{6,4},{5,7},{7,5},{8,10},{10,8},{9,1... | collective-permute-start | bytes 1179656 | tf_op jit(solution)/shard_map/ppermute | solution.py:220
  126.7 6.0 %copy-start.8 = (bf16[3,384,256]{2,1,0:T(8,128)(2,1)}, bf16[3,384,256]{2,1,0:T(8,128)(2,1)S(1)}, u32[]{:S(2)}) copy-start(bf16[3,384,256]{2,1,0:T(8,128)(2,1)S(1)} %collective-permute-done.13.refs_4_) | copy-start | bytes 1769476
  126.8 0.9 copy-start.11
  127.6 0.8 copy-start.12
  128.4 14.4 %copy-start.3 = (bf16[768,256]{1,0:T(8,128)(2,1)S(1)}, bf16[768,256]{1,0:T(8,128)(2,1)}, u32[]{:S(2)}) copy-start(bf16[768,256]{1,0:T(8,128)(2,1)} %get-tuple-element.82.refs_10_.refs_7_.refs_5_) | copy-start | bytes 1179652
  128.4 14.4 %copy-start.4 = (bf16[768,256]{1,0:T(8,128)(2,1)S(1)}, bf16[768,256]{1,0:T(8,128)(2,1)}, u32[]{:S(2)}) copy-start(bf16[768,256]{1,0:T(8,128)(2,1)} %get-tuple-element.83.refs_11_.refs_8_.refs_6_) | copy-start | bytes 1179652
  132.8 10.1 %copy-start.2 = (f32[768,512]{1,0:T(8,128)S(1)}, f32[768,512]{1,0:T(8,128)}, u32[]{:S(2)}) copy-start(f32[768,512]{1,0:T(8,128)} %get-tuple-element.64) | copy-start | bytes 4718596
  135.2 15.6 %copy-start.7 = (bf16[1,1,768,256]{3,2,1,0:T(8,128)(2,1)S(1)}, bf16[1,1,768,256]{3,2,1,0:T(8,128)(2,1)}, u32[]{:S(2)}) copy-start(bf16[1,1,768,256]{3,2,1,0:T(8,128)(2,1)} %param.10) | copy-start | bytes 1179652
  135.2 15.0 %collective-permute-start.15 = (bf16[768,256]{1,0:T(8,128)(2,1)}, bf16[768,256]{1,0:T(8,128)(2,1)}, u32[]{:S(2)}, u32[]{:S(2)}) collective-permute-start(bf16[768,256]{1,0:T(8,128)(2,1)} %get-tuple-element.78), channel_id=1, source_target_pairs={{2,3},{1,0},{0,2},{3,1},{6,7},{5,4},{4,6},{7,5},{10,11},{9,8},{8,1... | collective-permute-start | bytes 1179656 | tf_op jit(solution)/shard_map/ppermute | solution.py:241
  137.2 13.6 %collective-permute-start.16 = (bf16[768,256]{1,0:T(8,128)(2,1)}, bf16[768,256]{1,0:T(8,128)(2,1)}, u32[]{:S(2)}, u32[]{:S(2)}) collective-permute-start(bf16[768,256]{1,0:T(8,128)(2,1)} %get-tuple-element.79), channel_id=1, source_target_pairs={{2,1},{1,2},{6,5},{5,6},{10,9},{9,10},{14,13},{13,14},{18,17},{17,... | collective-permute-start | bytes 1179656 | tf_op jit(solution)/shard_map/ppermute | solution.py:242
  143.0 10.3 %collective-permute-start.17 = (bf16[3,384,256]{2,1,0:T(8,128)(2,1)}, bf16[3,384,256]{2,1,0:T(8,128)(2,1)S(1)}, u32[]{:S(2)}, u32[]{:S(2)}) collective-permute-start(bf16[3,384,256]{2,1,0:T(8,128)(2,1)} %get-tuple-element.73), channel_id=1, source_target_pairs={{0,2},{2,0},{1,3},{3,1},{4,6},{6,4},{5,7},{7,5},{8,10},{10,8},{9,1... | collective-permute-start | bytes 1769480 | tf_op jit(solution)/shard_map/ppermute | solution.py:247
  145.7 14.1 %all-to-all-start.1 = ((f32[64,1,24]{2,1,0:T(1,128)}), f32[64,1,24]{2,1,0:T(1,128)S(1)}, u32[]{:S(2)}, u32[]{:S(2)}) async-start(f32[64,1,24]{2,1,0:T(1,128)} %bitcast.20), calls=%async_computation.1 | async-start | bytes 65536 | tf_op jit(solution)/shard_map/all_to_all | solution.py:253
  153.4 0.8 copy-start.13

commit v4 on v3

--- a/solution.py
+++ b/solution.py
@@ -26,67 +26,87 @@
     return hit.astype(BF)
 
 
-def use_kernel(parts, first, carried, *refs):
-    blocks = len(parts)
-    it = iter(refs[1:])
-    x_refs = [[next(it) for _ in range(n)] for n in parts]
+def use_kernel(blocks, first, last, carried, index, *refs):
+    it = iter(refs)
+    x_refs = [next(it) for _ in range(blocks)]
     w_mine = [next(it) for _ in range(blocks)]
     w_theirs = [next(it) for _ in range(blocks)]
-    s_mine, s_theirs = next(it), next(it)
+    s_a, s_b = next(it), next(it)
     carry = next(it) if carried else None
     acc_in = None if first else next(it)
     acc, g_mine, g_theirs = next(it), next(it), next(it)
-    width = s_mine.shape[1]
-    s = jnp.concatenate([s_mine[...], s_theirs[...]], axis=1)
+    width = s_a.shape[1]
+    flags = index.shape[0] - 2
+    own = index[flags] == 1
+    s_mine = jnp.where(own, s_a[...], s_b[...])
+    s_theirs = jnp.where(own, s_b[...], s_a[...])
+    s = jnp.concatenate([s_mine, s_theirs], axis=1)
     for b in range(blocks):
-        x = x_refs[b][0][...]
-        for more in x_refs[b][1:]:
-            x = x + more[...]
+        x = x_refs[b][...]
         w = jnp.concatenate([w_mine[b][0], w_theirs[b][0]], axis=1)
         product = jnp.dot(x, w, preferred_element_type=F32)
-        if b == 0:
+        if last:
+            total = product + acc_in[...]
+        elif b == 0:
             acc[...] = product if first else product + acc_in[...]
         else:
             acc[...] += product
         outer = lax.dot_general(x, s, (((0,), (0,)), ((), ())), preferred_element_type=F32)
         g_mine[b] = outer[:, :width].astype(BF)
         g_theirs[carried + b] = outer[:, width:].astype(BF)
+    if last:
+        sum_a, sum_b, mix = next(it), next(it), next(it)
+        mine, theirs = total[:, :width], total[:, width:]
+        acc[...] = mine
+        sum_b[...] = theirs.astype(BF)
+        sum_a[...] = jnp.where(own, theirs, mine).astype(BF)
+        terms = s_mine.astype(F32) * mine + s_theirs.astype(F32) * theirs
+        line = lax.dot_general(
+            jnp.ones((8, width), F32),
+            terms,
+            (((1,), (1,)), ((), ())),
+            precision=lax.Precision.HIGHEST,
+            preferred_element_type=F32,
+        )
+        row = lax.broadcasted_iota(jnp.int32, (2, line.shape[1]), 0)
+        mix[...] = jnp.where(row == index[flags + 1], line[:2], 0.0)
     if carried:
         g_theirs[:carried] = carry[...]
 
 
-def use(pieces, index, w_mine, w_theirs, s_mine, s_theirs, acc, carry=None):
+def use(pieces, index, start, w_mine, w_theirs, s_a, s_b, acc, last=False, carry=None):
     first = acc is None
-    parts = tuple(len(p) for p in pieces)
-    blocks = len(parts)
+    blocks = len(pieces)
     carried = 0 if carry is None else carry.shape[0]
-    rows, width = s_mine.shape
-    chip = pieces[0][0].shape[1]
+    rows, width = s_a.shape
+    chip = pieces[0].shape[1]
 
     def whole(a):
         return pl.BlockSpec(a.shape, lambda i, idx: (0,) * len(a.shape))
 
     def pick(j):
-        return pl.BlockSpec((1, chip, width), lambda i, idx: (idx[j], 0, 0))
-
-    flat = [a for p in pieces for a in p]
-    ins = flat + [w_mine] * blocks + [w_theirs] * blocks + [s_mine, s_theirs]
-    specs = [whole(a) for a in flat] + [pick(j) for j in range(blocks)] * 2 + [whole(s_mine), whole(s_theirs)]
+        return pl.BlockSpec((1, chip, width), lambda i, idx: (idx[start + j], 0, 0))
+
+    ins = list(pieces) + [w_mine] * blocks + [w_theirs] * blocks + [s_a, s_b]
+    specs = [whole(a) for a in pieces] + [pick(j) for j in range(blocks)] * 2 + [whole(s_a), whole(s_b)]
     if carried:
         ins.append(carry)
         specs.append(whole(carry))
     aliases = {}
     if not first:
-        aliases = {1 + len(ins): 0}
+        if not last:
+            aliases = {1 + len(ins): 0}
         ins.append(acc)
         specs.append(whole(acc))
     outs = [
-        jax.ShapeDtypeStruct((rows, 2 * width), F32),
+        jax.ShapeDtypeStruct((rows, width if last else 2 * width), F32),
         jax.ShapeDtypeStruct((blocks, chip, width), BF),
         jax.ShapeDtypeStruct((carried + blocks, chip, width), BF),
     ]
+    if last:
+        outs += [jax.ShapeDtypeStruct((rows, width), BF)] * 2 + [jax.ShapeDtypeStruct((2, rows), F32)]
     return pl.pallas_call(
-        functools.partial(use_kernel, parts, first, carried),
+        functools.partial(use_kernel, blocks, first, last, carried),
         grid_spec=pltpu.PrefetchScalarGridSpec(
             num_scalar_prefetch=1,
             grid=(1,),
@@ -112,7 +132,8 @@
         spots += [(ref, j) for j in range(ref.shape[0])]
     for i in range(n):
         a, j = where[i]
-        ref, r = spots[i]
+        partner = i if i in (0, n - 1) else i + 1 - 2 * ((i - 1) % 2)
+        ref, r = spots[partner]
         out[index[i]] = (mine[a][j].astype(F32) + ref[r].astype(F32)).astype(BF)
 
 
@@ -161,8 +182,8 @@
         (flat2(g, g), flat2(1 - g, g)) for g in range(2)
     ]
     sums_b = [(flat2(1 - g, g), flat2(g, 1 - g)) for g in range(2)]
-    up_ring = [(y, (y + 1) % ny) for y in range(ny)]
-    down_ring = [(y, (y - 1) % ny) for y in range(ny)]
+    ring_a = [(y * 2 + c, ((y + 1 - 2 * c) % ny) * 2 + c) for y in range(ny) for c in range(2)]
+    ring_b = [(y * 2 + c, ((y - 1 + 2 * c) % ny) * 2 + c) for y in range(ny) for c in range(2)]
 
     def local(cotangent, expert_ids, combine, gate_saved, up_saved, w_down):
         expert_count = lax.axis_size("expert")
@@ -198,60 +219,47 @@
         s_b = lax.ppermute(scaled, ("core", "dp"), scaled_b)
         w_moved = lax.ppermute(w_sent, "core", swap)
 
-        spot = lambda *offsets: jnp.stack([(y + o + ny) % ny for o in offsets]).astype(jnp.int32)
+        held_own = dp == core
+        turn = jnp.where(core == 0, -1, 1)
+        order = [0] + [sign * step for step in range(1, half_y) for sign in (1, -1)] + [half_y]
+        index = jnp.stack(
+            [(y + turn * o + ny) % ny for o in order] + [held_own.astype(jnp.int32), core]
+        ).astype(jnp.int32)
+        on_a = lambda v: lax.ppermute(v, ("y", "core"), ring_a)
+        on_b = lambda v: lax.ppermute(v, ("y", "core"), ring_b)
         block = part.reshape(rows, chip)
-        up = lax.ppermute(block, "y", up_ring)
-        down = lax.ppermute(block, "y", down_ring)
-        waiting, offsets, order = [[block], [up], [down]], (0, -1, 1), [0, -1, 1]
-        acc, share_args, theirs = None, None, None
+        a = on_a(block)
+        block_b, s_a, s_b, w_moved = lax.optimization_barrier((block, s_a, s_b, w_moved))
+        b = on_b(block_b)
+        args = (w_down[0].reshape(ny, chip, width), w_moved.reshape(ny, chip, width), s_a, s_b)
+        waiting, start, acc, theirs = [block_b, a, b], 0, None, None
         g_mine, g_moved = [], []
         for step in range(2, half_y + 1):
-            if acc is None:
-                up, s_a, s_b, w_moved = lax.optimization_barrier((up, s_a, s_b, w_moved))
-                share_args = (
-                    w_down[0].reshape(ny, chip, width),
-                    w_moved.reshape(ny, chip, width),
-                    jnp.where(dp == core, s_a, s_b),
-                    jnp.where(dp == core, s_b, s_a),
-                )
-            else:
-                up, acc = lax.optimization_barrier((up, acc))
-                down, acc, theirs = lax.optimization_barrier((down, acc, theirs))
+            if acc is not None:
+                a, acc = lax.optimization_barrier((a, acc))
+                b, acc, theirs = lax.optimization_barrier((b, acc, theirs))
                 g_moved.append(lax.ppermute(theirs, "core", swap))
+            a = on_a(a)
+            arriving = [a]
             if step < half_y:
-                up = lax.ppermute(up, "y", up_ring)
-                down = lax.ppermute(down, "y", down_ring)
-                arriving = [[up], [down]]
-            else:
-                up = lax.ppermute(up, ("y", "core"), [(2 * a, 2 * b) for a, b in up_ring])
-                down = lax.ppermute(down, ("y", "core"), [(2 * a + 1, 2 * b + 1) for a, b in down_ring])
-                arriving = [[up, down]]
-            acc, gm, theirs = use(waiting, spot(*offsets), *share_args, acc)
+                b = on_b(b)
+                arriving.append(b)
+            acc, gm, theirs = use(waiting, index, start, *args, acc)
             g_mine.append(gm)
+            start += len(waiting)
             waiting = arriving
-            offsets = (-step, step) if step < half_y else (half_y,)
-            order += list(offsets)
         acc, *g_moved = lax.optimization_barrier((acc, *g_moved))
-        acc, gm, theirs = use(waiting, spot(*offsets), *share_args, acc, theirs)
+        acc, gm, theirs, sum_a, sum_b, mix = use(waiting, index, start, *args, acc, last=True, carry=theirs)
         g_mine.append(gm)
-        share_s = share_args[2:]
-
-        sum_mine, sum_theirs = acc[:, :width].astype(BF), acc[:, width:].astype(BF)
-        held_own = dp == core
-        got_a = lax.ppermute(jnp.where(held_own, sum_theirs, sum_mine), ("core", "dp"), sums_a)
-        got_b = lax.ppermute(sum_theirs, ("core", "dp"), sums_b)
-
-        mix = jnp.sum(
-            share_s[0].astype(F32) * acc[:, :width] + share_s[1].astype(F32) * acc[:, width:], axis=1
-        )
-        late = lax.ppermute(theirs, "core", swap)
-        grad_weight = place(spot(*order), g_mine, [*g_moved, late]).reshape(ny * chip, width)
-        got_a, got_b, _ = lax.optimization_barrier((got_a, got_b, mix))
+
+        got_a = lax.ppermute(sum_a, ("core", "dp"), sums_a)
+        got_b = lax.ppermute(sum_b, ("core", "dp"), sums_b)
         members = 2 * ny * 4
         share = rows // (ny * 4)
-        mix = jnp.stack([jnp.where(core == 0, mix, 0.0), jnp.where(core == 1, mix, 0.0)])
         mix = lax.all_to_all(mix.reshape(members, share), ("dp", "y", "xlo", "core"), 0, 0, tiled=True)
-        grad_hidden = jnp.where(held_own, acc[:, :width], got_b.astype(F32)) + got_a.astype(F32)
+        late = lax.ppermute(theirs, "core", swap)
+        grad_weight = place(index, g_mine, [*g_moved, late]).reshape(ny * chip, width)
+        grad_hidden = jnp.where(held_own, acc, got_b.astype(F32)) + got_a.astype(F32)
         weighted = weight_rows * grad_hidden
         grad_gate = (weighted * upper * sigma * (1.0 + gate * (1.0 - sigma))).astype(BF)
         grad_upper = (weighted * active).astype(BF)

time: 162 us -> 154 us (0.951)
  waiting for transfers between devices: 34.3 us -> 21.9 us
  starting transfers between devices: 80.7 us -> 90.2 us
  other arithmetic: 12.9 us -> 6.34 us
    all_to_all x1, waiting for transfers between devices: 16.6 us -> 7.62 us  [local(): lax.all_to_all(outgoing, 'expert', split_axis=0, concat_axis=0, tiled=True)]
    ppermute x1, starting transfers between devices: 1.92 us -> 9.91 us  [local(): s_a = lax.ppermute(scaled, ('core', 'dp'), scaled_a)]
    ppermute x1, waiting for transfers between devices: 6.65 us -> 0.01 us  [local(): s_a = lax.ppermute(scaled, ('core', 'dp'), scaled_a)]
    ppermute x2, starting transfers between devices: 3.83 us -> 8.47 us  [local(): g_moved.append(lax.ppermute(theirs, 'core', swap))]
    select_n x3 -> x0, other arithmetic: 4.49 us -> none  [the longest x1 2.45 us: local(): jnp.where(held_own, sum_theirs, sum_mine)]
    all_to_all x1, starting transfers between devices: 10 us -> 5.77 us  [local(): lax.all_to_all(outgoing, 'expert', split_axis=0, concat_axis=0, tiled=True)]
    all_to_all x1, starting transfers between devices: 4.49 us -> 8.5 us  [local(): lax.all_to_all(mix.reshape(members, share), ('dp', 'y', 'xlo', 'core'), 0...]
    ppermute x1, starting transfers between devices: 4.94 us -> 8.79 us  [local(): across = lax.ppermute(cotangent[0], every, token_moves(True))]
  transfers between devices with their start and end apart: 20 -> 19, of which waited for: 9 -> 7; matrix products, arithmetic and copies ran while one was open for 6% -> 5% of each run, Pallas kernels for 13% -> 14%
where the time goes in v4:
time: 154 us; the launch traced here: 153 us
  starting transfers between devices  90.2 us (59%)
  Pallas kernels  26.7 us (17%)
  waiting for transfers between devices  21.9 us (14%)
  other arithmetic  6.34 us (4%)
  local copies, waits for them, and re-layouts  4.95 us (3%)
    ppermute x4, starting transfers between devices, local(): on_a = lambda v: lax.ppermute(v, ('y', 'core'), ring_a)  25.7 us
    pallas_call x4, Pallas kernels, use(): pl.pallas_call(functools.partial(use_kernel, blocks, first, last, carried...  22.7 us
    ppermute x1, starting transfers between devices, local(): s_a = lax.ppermute(scaled, ('core', 'dp'), scaled_a)  9.91 us
    ppermute x4, waiting for transfers between devices, local(): on_a = lambda v: lax.ppermute(v, ('y', 'core'), ring_a)  9.05 us
    ppermute x1, starting transfers between devices, local(): across = lax.ppermute(cotangent[0], every, token_moves(True))  8.79 us
    all_to_all x1, starting transfers between devices, local(): lax.all_to_all(mix.reshape(members, share), ('dp', 'y', 'xlo', 'core'), 0...  8.5 us
    ppermute x2, starting transfers between devices, local(): g_moved.append(lax.ppermute(theirs, 'core', swap))  8.47 us
    all_to_all x1, waiting for transfers between devices, local(): lax.all_to_all(outgoing, 'expert', split_axis=0, concat_axis=0, tiled=True)  7.62 us
  transfers between devices with their start and end apart: 19, of which 7 were waited for; matrix products, arithmetic and copies ran while one was open for 5% of the time, Pallas kernels for 14%

profile of v4, /device:TPU:1, one launch (start us, length us, event | category | flops | bytes accessed | tf_op | source)
XLA Modules:
  0.0 152.6 jit_solution(16614176237280238558)
XLA Ops:
  0.6 0.0 copy-start
  0.6 1.1 copy.19
  1.8 8.8 %collective-permute-start.1 = (bf16[192,192]{0,1:T(8,128)(2,1)S(1)}, bf16[192,192]{0,1:T(8,128)(2,1)S(1)}, u32[]{:S(2)}, u32[]{:S(2)}) collective-permute-start(bf16[192,192]{0,1:T(8,128)(2,1)S(1)} %bitcast.60), channel_id=1, source_target_pairs={{0,4},{1,6},{2,0},{3,2},{4,12},{5,14},{6,8},{7,10},{8,20},{9,22},{... | collective-permute-start | bytes 221192 | tf_op jit(solution)/shard_map/ppermute | solution.py:203
  10.6 0.7 convert_bitcast_fusion
  11.3 1.9 %collective-permute-start = (bf16[192,194]{0,1:T(8,128)(2,1)S(1)}, bf16[192,194]{0,1:T(8,128)(2,1)S(1)}, u32[]{:S(2)}, u32[]{:S(2)}) collective-permute-start(bf16[192,194]{0,1:T(8,128)(2,1)S(1)} %pad_maximum_fusion), channel_id=1, source_target_pairs={{0,0},{1,2},{2,4},{3,6},{4,8},{5,10},{6,12},{7,14},{8,16},{9,18},{... | collective-permute-start | bytes 223496 | tf_op jit(solution)/shard_map/ppermute | solution.py:202
  13.2 0.7 reduce
  13.9 2.1 %fusion.1 = bf16[768,256]{1,0:T(8,128)(2,1)} fusion(bf16[1,1,768,256]{3,2,1,0:T(8,128)(2,1)} %param.10, f32[768]{0:T(1024)S(1)} %reduce, bf16[1,1,768,256]{3,2,1,0:T(8,128)(2,1)} %param.9), kind=kLoop, calls=%fused_computation.7 | loop fusion | flops 1769472 | bytes 1182720 | tf_op jit(solution)/shard_map/convert_element_type | solution.py:216
  16.0 1.9 %collective-permute-start.6 = (bf16[3072,256]{1,0:T(8,128)(2,1)S(1)}, bf16[3072,256]{1,0:T(8,128)(2,1)S(1)}, u32[]{:S(2)}, u32[]{:S(2)}) collective-permute-start(bf16[3072,256]{1,0:T(8,128)(2,1)S(1)} %bitcast.49), channel_id=1, source_target_pairs={{0,2},{2,0},{1,3},{3,1},{4,6},{6,4},{5,7},{7,5},{8,10},{10,8},{9,1... | collective-permute-start | bytes 4718600 | tf_op jit(solution)/shard_map/ppermute | solution.py:220
  18.0 1.6 %collective-permute-done = bf16[192,194]{0,1:T(8,128)(2,1)S(1)} collective-permute-done((bf16[192,194]{0,1:T(8,128)(2,1)S(1)}, bf16[192,194]{0,1:T(8,128)(2,1)S(1)}, u32[]{:S(2)}, u32[]{:S(2)}) %collective-permute-start) | collective-permute-done | bytes 74528 | tf_op jit(solution)/shard_map/ppermute | solution.py:202
  19.5 0.1 fusion.16
  19.8 1.2 convolution_convert_fusion
  21.0 5.8 %all-to-all-start = ((bf16[8,96,384]{2,1,0:T(8,128)(2,1)}), bf16[8,96,384]{2,1,0:T(8,128)(2,1)}, u32[]{:S(2)}, u32[]{:S(2)}) async-start(bf16[8,96,384]{2,1,0:T(8,128)(2,1)} %bitcast.59), calls=%async_computation | async-start | bytes 1179648 | tf_op jit(solution)/shard_map/all_to_all | solution.py:209
  26.8 9.9 %collective-permute-start.4 = (bf16[768,256]{1,0:T(8,128)(2,1)}, bf16[768,256]{1,0:T(8,128)(2,1)S(1)}, u32[]{:S(2)}, u32[]{:S(2)}) collective-permute-start(bf16[768,256]{1,0:T(8,128)(2,1)} %fusion.1), channel_id=1, source_target_pairs={{0,0},{1,2},{2,1},{3,3},{4,4},{5,6},{6,5},{7,7},{8,8},{9,10},{10,9... | collective-permute-start | bytes 1179656 | tf_op jit(solution)/shard_map/ppermute | solution.py:218
  36.7 1.9 %collective-permute-start.5 = (bf16[768,256]{1,0:T(8,128)(2,1)}, bf16[768,256]{1,0:T(8,128)(2,1)}, u32[]{:S(2)}, u32[]{:S(2)}) collective-permute-start(bf16[768,256]{1,0:T(8,128)(2,1)} %fusion.1), channel_id=1, source_target_pairs={{0,1},{1,3},{2,0},{3,2},{4,5},{5,7},{6,4},{7,6},{8,9},{9,11},{10,8... | collective-permute-start | bytes 1179656 | tf_op jit(solution)/shard_map/ppermute | solution.py:219
  38.6 7.6 %all-to-all-done = bf16[8,96,384]{2,1,0:T(8,128)(2,1)} async-done(((bf16[8,96,384]{2,1,0:T(8,128)(2,1)}), bf16[8,96,384]{2,1,0:T(8,128)(2,1)}, u32[]{:S(2)}, u32[]{:S(2)}) %all-to-all-start) | async-done | bytes 589856 | tf_op jit(solution)/shard_map/all_to_all | solution.py:209
  46.3 11.5 %collective-permute-start.2 = (bf16[768,384]{1,0:T(8,128)(2,1)}, bf16[768,384]{1,0:T(8,128)(2,1)}, u32[]{:S(2)}, u32[]{:S(2)}) collective-permute-start(bf16[768,384]{1,0:T(8,128)(2,1)} %bitcast.15.refs_0_), channel_id=1, source_target_pairs={{0,8},{2,58},{8,16},{10,2},{16,24},{18,10},{24,32},{26,18},{32,40}... | collective-permute-start | bytes 1769480 | tf_op jit(solution)/shard_map/ppermute | solution.py:228
  57.8 0.0 copy-start.2
  57.8 0.0 collective-permute-done.5.refs_10_.refs_7_.refs_4_
  57.8 0.0 collective-permute-done.6
  57.8 0.0 copy-start.1
  57.8 1.9 %collective-permute-start.7 = (bf16[768,384]{1,0:T(8,128)(2,1)}, bf16[768,384]{1,0:T(8,128)(2,1)}, u32[]{:S(2)}, u32[]{:S(2)}) collective-permute-start(bf16[768,384]{1,0:T(8,128)(2,1)} %bitcast.15.refs_0_), channel_id=1, source_target_pairs={{0,56},{2,10},{8,0},{10,18},{16,8},{18,26},{24,16},{26,34},{32,24}... | collective-permute-start | bytes 1769480 | tf_op jit(solution)/shard_map/ppermute | solution.py:229
  59.7 8.5 %collective-permute-done.2.refs_1_ = bf16[768,384]{1,0:T(8,128)(2,1)} collective-permute-done((bf16[768,384]{1,0:T(8,128)(2,1)}, bf16[768,384]{1,0:T(8,128)(2,1)}, u32[]{:S(2)}, u32[]{:S(2)}) %collective-permute-start.2) | collective-permute-done | bytes 589856 | tf_op jit(solution)/shard_map/ppermute | solution.py:228
  68.2 5.3 %collective-permute-start.3 = (bf16[768,384]{1,0:T(8,128)(2,1)}, bf16[768,384]{1,0:T(8,128)(2,1)S(1)}, u32[]{:S(2)}, u32[]{:S(2)}) collective-permute-start(bf16[768,384]{1,0:T(8,128)(2,1)} %collective-permute-done.2.refs_1_), channel_id=1, source_target_pairs={{0,8},{2,58},{8,16},{10,2},{16,24},{18,10},{24,32},{26,18},{32,40}... | collective-permute-start | bytes 1769480 | tf_op jit(solution)/shard_map/ppermute | solution.py:228
  73.5 1.9 %collective-permute-start.9 = (bf16[768,384]{1,0:T(8,128)(2,1)}, bf16[768,384]{1,0:T(8,128)(2,1)S(1)}, u32[]{:S(2)}, u32[]{:S(2)}) collective-permute-start(bf16[768,384]{1,0:T(8,128)(2,1)} %collective-permute-done.7.refs_2_), channel_id=1, source_target_pairs={{0,56},{2,10},{8,0},{10,18},{16,8},{18,26},{24,16},{26,34},{32,24}... | collective-permute-start | bytes 1769480 | tf_op jit(solution)/shard_map/ppermute | solution.py:229
  75.6 0.7 stack.47.index
  76.2 6.3 %shard_map.93 = (f32[768,512]{1,0:T(8,128)}, bf16[3,384,256]{2,1,0:T(8,128)(2,1)}, bf16[3,384,256]{2,1,0:T(8,128)(2,1)}) custom-call(s32[10]{0:T(128)} %stack.47.index, bf16[768,384]{1,0:T(8,128)(2,1)} %bitcast.15.refs_0_, bf16[768,384]{1,0:T(8,128)(2,1)} %collective-permute-done.2.refs_1_, bf16[768,384]{1,0:T(8,128)(2,1)} %collective-permute-done.7.refs_2_, ...), custom_call_target="tpu_custom_call" | custom-call | flops 1811939328 | bytes 12000000 | tf_op jit(solution)/shard_map/pallas_call | solution.py:108
  82.5 0.6 collective-permute-done.3.refs_0_
  83.1 5.2 %collective-permute-start.8 = (bf16[768,384]{1,0:T(8,128)(2,1)S(1)}, bf16[768,384]{1,0:T(8,128)(2,1)S(1)}, u32[]{:S(2)}, u32[]{:S(2)}) collective-permute-start(bf16[768,384]{1,0:T(8,128)(2,1)S(1)} %collective-permute-done.3.refs_0_), channel_id=1, source_target_pairs={{0,8},{2,58},{8,16},{10,2},{16,24},{18,10},{24,32},{26,18},{32,40}... | collective-permute-start | bytes 1769480 | tf_op jit(solution)/shard_map/ppermute | solution.py:228
  88.3 0.2 collective-permute-done.9.refs_1_
  88.5 1.9 %collective-permute-start.11 = (bf16[768,384]{1,0:T(8,128)(2,1)S(1)}, bf16[768,384]{1,0:T(8,128)(2,1)S(1)}, u32[]{:S(2)}, u32[]{:S(2)}) collective-permute-start(bf16[768,384]{1,0:T(8,128)(2,1)S(1)} %collective-permute-done.9.refs_1_), channel_id=1, source_target_pairs={{0,56},{2,10},{8,0},{10,18},{16,8},{18,26},{24,16},{26,34},{32,24}... | collective-permute-start | bytes 1769480 | tf_op jit(solution)/shard_map/ppermute | solution.py:229
  90.4 5.3 %collective-permute-start.12 = (bf16[3,384,256]{2,1,0:T(8,128)(2,1)}, bf16[3,384,256]{2,1,0:T(8,128)(2,1)S(1)}, u32[]{:S(2)}, u32[]{:S(2)}) collective-permute-start(bf16[3,384,256]{2,1,0:T(8,128)(2,1)} %get-tuple-element.60), channel_id=1, source_target_pairs={{0,2},{2,0},{1,3},{3,1},{4,6},{6,4},{5,7},{7,5},{8,10},{10,8},{9,1... | collective-permute-start | bytes 1769480 | tf_op jit(solution)/shard_map/ppermute | solution.py:241
  95.8 5.6 %shard_map.94 = (f32[768,512]{1,0:T(8,128)}, bf16[2,384,256]{2,1,0:T(8,128)(2,1)}, bf16[2,384,256]{2,1,0:T(8,128)(2,1)}) custom-call(s32[10]{0:T(128)} %stack.47.index, bf16[768,384]{1,0:T(8,128)(2,1)} %copy-done.6, bf16[768,384]{1,0:T(8,128)(2,1)} %copy-done.5, bf16[8,384,256]{2,1,0:T(8,128)(2,1)} %bitcast.44, ...), custom_call_target="tpu_custom_call", output_to_operand_aliasing={{0}: (9, {})} | custom-call | flops 1207959552 | bytes 8000000 | tf_op jit(solution)/shard_map/pallas_call | solution.py:108
  101.4 3.7 %collective-permute-start.10 = (bf16[768,384]{1,0:T(8,128)(2,1)S(1)}, bf16[768,384]{1,0:T(8,128)(2,1)S(1)}, u32[]{:S(2)}, u32[]{:S(2)}) collective-permute-start(bf16[768,384]{1,0:T(8,128)(2,1)S(1)} %collective-permute-done.8.refs_0_), channel_id=1, source_target_pairs={{0,8},{2,58},{8,16},{10,2},{16,24},{18,10},{24,32},{26,18},{32,40}... | collective-permute-start | bytes 1769480 | tf_op jit(solution)/shard_map/ppermute | solution.py:228
  105.1 0.2 collective-permute-done.11.refs_1_
  105.3 3.2 %collective-permute-start.13 = (bf16[2,384,256]{2,1,0:T(8,128)(2,1)}, bf16[2,384,256]{2,1,0:T(8,128)(2,1)S(1)}, u32[]{:S(2)}, u32[]{:S(2)}) collective-permute-start(bf16[2,384,256]{2,1,0:T(8,128)(2,1)} %get-tuple-element.61), channel_id=1, source_target_pairs={{0,2},{2,0},{1,3},{3,1},{4,6},{6,4},{5,7},{7,5},{8,10},{10,8},{9,1... | collective-permute-start | bytes 1179656 | tf_op jit(solution)/shard_map/ppermute | solution.py:241
  108.5 5.6 %shard_map.95 = (f32[768,512]{1,0:T(8,128)}, bf16[2,384,256]{2,1,0:T(8,128)(2,1)}, bf16[2,384,256]{2,1,0:T(8,128)(2,1)}) custom-call(s32[10]{0:T(128)} %stack.47.index, bf16[768,384]{1,0:T(8,128)(2,1)} %copy-done.9, bf16[768,384]{1,0:T(8,128)(2,1)} %copy-done.11, bf16[8,384,256]{2,1,0:T(8,128)(2,1)} %bitcast.46, ...), custom_call_target="tpu_custom_call", output_to_operand_aliasing={{0}: (9, {})} | custom-call | flops 1207959552 | bytes 8000000 | tf_op jit(solution)/shard_map/pallas_call | solution.py:108
  114.2 0.9 copy-done.10
  115.1 5.2 %shard_map.96 = (f32[768,256]{1,0:T(8,128)}, bf16[1,384,256]{2,1,0:T(8,128)(2,1)}, bf16[3,384,256]{2,1,0:T(8,128)(2,1)}, bf16[768,256]{1,0:T(8,128)(2,1)}, bf16[768,256]{1,0:T(8,128)(2,1)}, /*index=5*/f32[2,768]{1,0:T(2,128)}) custom-call(s32[10]{0:T(128)} %stack.47.index, bf16[768,384]{1,0:T(8,128)(2,1)} %copy-done.10, bf16[8,384,256]{2,1,0:T(8,128)(2,1)} %bitcast.48, ...), custom_call_target="tpu_custom_call" | custom-call | flops 603979776 | bytes 4000000 | tf_op jit(solution)/shard_map/pallas_call | solution.py:108
  120.4 7.2 %collective-permute-start.14 = (bf16[768,256]{1,0:T(8,128)(2,1)}, bf16[768,256]{1,0:T(8,128)(2,1)S(1)}, u32[]{:S(2)}, u32[]{:S(2)}) collective-permute-start(bf16[768,256]{1,0:T(8,128)(2,1)} %get-tuple-element.65), channel_id=1, source_target_pairs={{2,1},{1,2},{6,5},{5,6},{10,9},{9,10},{14,13},{13,14},{18,17},{17,... | collective-permute-start | bytes 1179656 | tf_op jit(solution)/shard_map/ppermute | solution.py:256
  127.6 1.9 %collective-permute-start.15 = (bf16[768,256]{1,0:T(8,128)(2,1)}, bf16[768,256]{1,0:T(8,128)(2,1)S(1)}, u32[]{:S(2)}, u32[]{:S(2)}) collective-permute-start(bf16[768,256]{1,0:T(8,128)(2,1)} %get-tuple-element.66), channel_id=1, source_target_pairs={{2,3},{1,0},{0,2},{3,1},{6,7},{5,4},{4,6},{7,5},{10,11},{9,8},{8,1... | collective-permute-start | bytes 1179656 | tf_op jit(solution)/shard_map/ppermute | solution.py:255
  129.5 2.4 %collective-permute-start.16 = (bf16[3,384,256]{2,1,0:T(8,128)(2,1)}, bf16[3,384,256]{2,1,0:T(8,128)(2,1)S(1)}, u32[]{:S(2)}, u32[]{:S(2)}) collective-permute-start(bf16[3,384,256]{2,1,0:T(8,128)(2,1)} %get-tuple-element.73), channel_id=1, source_target_pairs={{0,2},{2,0},{1,3},{3,1},{4,6},{6,4},{5,7},{7,5},{8,10},{10,8},{9,1... | collective-permute-start | bytes 1769480 | tf_op jit(solution)/shard_map/ppermute | solution.py:260
  131.9 1.4 all_to_all.12
  133.3 8.5 %all-to-all-start.1 = ((f32[64,1,24]{2,1,0:T(1,128)}), f32[64,1,24]{2,1,0:T(1,128)S(1)}, u32[]{:S(2)}, u32[]{:S(2)}) async-start(f32[64,1,24]{2,1,0:T(1,128)} %bitcast.22), calls=%async_computation.1 | async-start | bytes 65536 | tf_op jit(solution)/shard_map/all_to_all | solution.py:259
  141.9 1.4 multiply_convert_fusion
  143.3 0.8 copy-done.8
  144.1 4.0 %shard_map.97 = bf16[8,384,256]{2,1,0:T(8,128)(2,1)} custom-call(s32[10]{0:T(128)} %stack.47.index, bf16[3,384,256]{2,1,0:T(8,128)(2,1)} %get-tuple-element.67.refs_0_, bf16[2,384,256]{2,1,0:T(8,128)(2,1)} %get-tuple-element.68.refs_1_, bf16[2,384,256]{2,1,0:T(8,128)(2,1)} %get-tuple-element.69.refs_2_, bf16[1,384,256]{2,1,0:T(8,128)(2,1)} %get-tuple-element.70.refs_3_, ...), custom_call_target="tpu_custom_call" | custom-call | flops 1000000 | bytes 5000000 | tf_op jit(solution)/shard_map/pallas_call | solution.py:144
  148.2 3.2 %all-to-all-done.1 = f32[64,1,24]{2,1,0:T(1,128)S(1)} async-done(((f32[64,1,24]{2,1,0:T(1,128)}), f32[64,1,24]{2,1,0:T(1,128)S(1)}, u32[]{:S(2)}, u32[]{:S(2)}) %all-to-all-start.1) | async-done | bytes 6176 | tf_op jit(solution)/shard_map/all_to_all | solution.py:259
  151.4 1.3 bitcast_divide_fusion
  (39 shorter events, 0.2 us)
Async XLA Ops:
  0.6 15.4 %copy-start = (bf16[1,3072,256]{2,1,0:T(8,128)(2,1)S(1)}, bf16[1,3072,256]{2,1,0:T(8,128)(2,1)}, u32[]{:S(2)}) copy-start(bf16[1,3072,256]{2,1,0:T(8,128)(2,1)} %param.11) | copy-start | bytes 4718596
  1.8 18.0 %collective-permute-start.1 = (bf16[192,192]{0,1:T(8,128)(2,1)S(1)}, bf16[192,192]{0,1:T(8,128)(2,1)S(1)}, u32[]{:S(2)}, u32[]{:S(2)}) collective-permute-start(bf16[192,192]{0,1:T(8,128)(2,1)S(1)} %bitcast.60), channel_id=1, source_target_pairs={{0,4},{1,6},{2,0},{3,2},{4,12},{5,14},{6,8},{7,10},{8,20},{9,22},{... | collective-permute-start | bytes 221192 | tf_op jit(solution)/shard_map/ppermute | solution.py:203
  11.3 8.3 %collective-permute-start = (bf16[192,194]{0,1:T(8,128)(2,1)S(1)}, bf16[192,194]{0,1:T(8,128)(2,1)S(1)}, u32[]{:S(2)}, u32[]{:S(2)}) collective-permute-start(bf16[192,194]{0,1:T(8,128)(2,1)S(1)} %pad_maximum_fusion), channel_id=1, source_target_pairs={{0,0},{1,2},{2,4},{3,6},{4,8},{5,10},{6,12},{7,14},{8,16},{9,18},{... | collective-permute-start | bytes 223496 | tf_op jit(solution)/shard_map/ppermute | solution.py:202
  16.0 41.8 %collective-permute-start.6 = (bf16[3072,256]{1,0:T(8,128)(2,1)S(1)}, bf16[3072,256]{1,0:T(8,128)(2,1)S(1)}, u32[]{:S(2)}, u32[]{:S(2)}) collective-permute-start(bf16[3072,256]{1,0:T(8,128)(2,1)S(1)} %bitcast.49), channel_id=1, source_target_pairs={{0,2},{2,0},{1,3},{3,1},{4,6},{6,4},{5,7},{7,5},{8,10},{10,8},{9,1... | collective-permute-start | bytes 4718600 | tf_op jit(solution)/shard_map/ppermute | solution.py:220
  21.0 25.2 %all-to-all-start = ((bf16[8,96,384]{2,1,0:T(8,128)(2,1)}), bf16[8,96,384]{2,1,0:T(8,128)(2,1)}, u32[]{:S(2)}, u32[]{:S(2)}) async-start(bf16[8,96,384]{2,1,0:T(8,128)(2,1)} %bitcast.59), calls=%async_computation | async-start | bytes 1179648 | tf_op jit(solution)/shard_map/all_to_all | solution.py:209
  26.8 31.0 %collective-permute-start.4 = (bf16[768,256]{1,0:T(8,128)(2,1)}, bf16[768,256]{1,0:T(8,128)(2,1)S(1)}, u32[]{:S(2)}, u32[]{:S(2)}) collective-permute-start(bf16[768,256]{1,0:T(8,128)(2,1)} %fusion.1), channel_id=1, source_target_pairs={{0,0},{1,2},{2,1},{3,3},{4,4},{5,6},{6,5},{7,7},{8,8},{9,10},{10,9... | collective-permute-start | bytes 1179656 | tf_op jit(solution)/shard_map/ppermute | solution.py:218
  36.7 21.1 %collective-permute-start.5 = (bf16[768,256]{1,0:T(8,128)(2,1)}, bf16[768,256]{1,0:T(8,128)(2,1)}, u32[]{:S(2)}, u32[]{:S(2)}) collective-permute-start(bf16[768,256]{1,0:T(8,128)(2,1)} %fusion.1), channel_id=1, source_target_pairs={{0,1},{1,3},{2,0},{3,2},{4,5},{5,7},{6,4},{7,6},{8,9},{9,11},{10,8... | collective-permute-start | bytes 1179656 | tf_op jit(solution)/shard_map/ppermute | solution.py:219
  46.3 22.0 %collective-permute-start.2 = (bf16[768,384]{1,0:T(8,128)(2,1)}, bf16[768,384]{1,0:T(8,128)(2,1)}, u32[]{:S(2)}, u32[]{:S(2)}) collective-permute-start(bf16[768,384]{1,0:T(8,128)(2,1)} %bitcast.15.refs_0_), channel_id=1, source_target_pairs={{0,8},{2,58},{8,16},{10,2},{16,24},{18,10},{24,32},{26,18},{32,40}... | collective-permute-start | bytes 1769480 | tf_op jit(solution)/shard_map/ppermute | solution.py:228
  57.8 18.5 %copy-start.2 = (bf16[768,256]{1,0:T(8,128)(2,1)}, bf16[768,256]{1,0:T(8,128)(2,1)S(1)}, u32[]{:S(2)}) copy-start(bf16[768,256]{1,0:T(8,128)(2,1)S(1)} %collective-permute-done.4.refs_9_.refs_6_.refs_3_) | copy-start | bytes 1179652
  57.8 18.5 %copy-start.1 = (bf16[3072,256]{1,0:T(8,128)(2,1)}, bf16[3072,256]{1,0:T(8,128)(2,1)S(1)}, u32[]{:S(2)}) copy-start(bf16[3072,256]{1,0:T(8,128)(2,1)S(1)} %collective-permute-done.6) | copy-start | bytes 4718596
  57.8 15.7 %collective-permute-start.7 = (bf16[768,384]{1,0:T(8,128)(2,1)}, bf16[768,384]{1,0:T(8,128)(2,1)}, u32[]{:S(2)}, u32[]{:S(2)}) collective-permute-start(bf16[768,384]{1,0:T(8,128)(2,1)} %bitcast.15.refs_0_), channel_id=1, source_target_pairs={{0,56},{2,10},{8,0},{10,18},{16,8},{18,26},{24,16},{26,34},{32,24}... | collective-permute-start | bytes 1769480 | tf_op jit(solution)/shard_map/ppermute | solution.py:229
  68.2 14.9 %collective-permute-start.3 = (bf16[768,384]{1,0:T(8,128)(2,1)}, bf16[768,384]{1,0:T(8,128)(2,1)S(1)}, u32[]{:S(2)}, u32[]{:S(2)}) collective-permute-start(bf16[768,384]{1,0:T(8,128)(2,1)} %collective-permute-done.2.refs_1_), channel_id=1, source_target_pairs={{0,8},{2,58},{8,16},{10,2},{16,24},{18,10},{24,32},{26,18},{32,40}... | collective-permute-start | bytes 1769480 | tf_op jit(solution)/shard_map/ppermute | solution.py:228
  73.5 15.0 %collective-permute-start.9 = (bf16[768,384]{1,0:T(8,128)(2,1)}, bf16[768,384]{1,0:T(8,128)(2,1)S(1)}, u32[]{:S(2)}, u32[]{:S(2)}) collective-permute-start(bf16[768,384]{1,0:T(8,128)(2,1)} %collective-permute-done.7.refs_2_), channel_id=1, source_target_pairs={{0,56},{2,10},{8,0},{10,18},{16,8},{18,26},{24,16},{26,34},{32,24}... | collective-permute-start | bytes 1769480 | tf_op jit(solution)/shard_map/ppermute | solution.py:229
  83.1 12.7 %copy-start.6 = (bf16[768,384]{1,0:T(8,128)(2,1)}, bf16[768,384]{1,0:T(8,128)(2,1)S(1)}, u32[]{:S(2)}) copy-start(bf16[768,384]{1,0:T(8,128)(2,1)S(1)} %collective-permute-done.3.refs_0_) | copy-start | bytes 1769476
  83.1 18.3 %collective-permute-start.8 = (bf16[768,384]{1,0:T(8,128)(2,1)S(1)}, bf16[768,384]{1,0:T(8,128)(2,1)S(1)}, u32[]{:S(2)}, u32[]{:S(2)}) collective-permute-start(bf16[768,384]{1,0:T(8,128)(2,1)S(1)} %collective-permute-done.3.refs_0_), channel_id=1, source_target_pairs={{0,8},{2,58},{8,16},{10,2},{16,24},{18,10},{24,32},{26,18},{32,40}... | collective-permute-start | bytes 1769480 | tf_op jit(solution)/shard_map/ppermute | solution.py:228
  88.5 7.2 %copy-start.5 = (bf16[768,384]{1,0:T(8,128)(2,1)}, bf16[768,384]{1,0:T(8,128)(2,1)S(1)}, u32[]{:S(2)}) copy-start(bf16[768,384]{1,0:T(8,128)(2,1)S(1)} %collective-permute-done.9.refs_1_) | copy-start | bytes 1769476
  88.5 16.8 %collective-permute-start.11 = (bf16[768,384]{1,0:T(8,128)(2,1)S(1)}, bf16[768,384]{1,0:T(8,128)(2,1)S(1)}, u32[]{:S(2)}, u32[]{:S(2)}) collective-permute-start(bf16[768,384]{1,0:T(8,128)(2,1)S(1)} %collective-permute-done.9.refs_1_), channel_id=1, source_target_pairs={{0,56},{2,10},{8,0},{10,18},{16,8},{18,26},{24,16},{26,34},{32,24}... | collective-permute-start | bytes 1769480 | tf_op jit(solution)/shard_map/ppermute | solution.py:229
  90.4 23.7 %collective-permute-start.12 = (bf16[3,384,256]{2,1,0:T(8,128)(2,1)}, bf16[3,384,256]{2,1,0:T(8,128)(2,1)S(1)}, u32[]{:S(2)}, u32[]{:S(2)}) collective-permute-start(bf16[3,384,256]{2,1,0:T(8,128)(2,1)} %get-tuple-element.60), channel_id=1, source_target_pairs={{0,2},{2,0},{1,3},{3,1},{4,6},{6,4},{5,7},{7,5},{8,10},{10,8},{9,1... | collective-permute-start | bytes 1769480 | tf_op jit(solution)/shard_map/ppermute | solution.py:241
  101.3 7.2 %copy-start.9 = (bf16[768,384]{1,0:T(8,128)(2,1)}, bf16[768,384]{1,0:T(8,128)(2,1)S(1)}, u32[]{:S(2)}) copy-start(bf16[768,384]{1,0:T(8,128)(2,1)S(1)} %collective-permute-done.8.refs_0_) | copy-start | bytes 1769476
  101.4 12.8 %collective-permute-start.10 = (bf16[768,384]{1,0:T(8,128)(2,1)S(1)}, bf16[768,384]{1,0:T(8,128)(2,1)S(1)}, u32[]{:S(2)}, u32[]{:S(2)}) collective-permute-start(bf16[768,384]{1,0:T(8,128)(2,1)S(1)} %collective-permute-done.8.refs_0_), channel_id=1, source_target_pairs={{0,8},{2,58},{8,16},{10,2},{16,24},{18,10},{24,32},{26,18},{32,40}... | collective-permute-start | bytes 1769480 | tf_op jit(solution)/shard_map/ppermute | solution.py:228
  105.3 3.2 %copy-start.11 = (bf16[768,384]{1,0:T(8,128)(2,1)}, bf16[768,384]{1,0:T(8,128)(2,1)S(1)}, u32[]{:S(2)}) copy-start(bf16[768,384]{1,0:T(8,128)(2,1)S(1)} %collective-permute-done.11.refs_1_) | copy-start | bytes 1769476
  105.3 8.8 %collective-permute-start.13 = (bf16[2,384,256]{2,1,0:T(8,128)(2,1)}, bf16[2,384,256]{2,1,0:T(8,128)(2,1)S(1)}, u32[]{:S(2)}, u32[]{:S(2)}) collective-permute-start(bf16[2,384,256]{2,1,0:T(8,128)(2,1)} %get-tuple-element.61), channel_id=1, source_target_pairs={{0,2},{2,0},{1,3},{3,1},{4,6},{6,4},{5,7},{7,5},{8,10},{10,8},{9,1... | collective-permute-start | bytes 1179656 | tf_op jit(solution)/shard_map/ppermute | solution.py:241
  114.2 6.2 %copy-start.7 = (bf16[3,384,256]{2,1,0:T(8,128)(2,1)}, bf16[3,384,256]{2,1,0:T(8,128)(2,1)S(1)}, u32[]{:S(2)}) copy-start(bf16[3,384,256]{2,1,0:T(8,128)(2,1)S(1)} %collective-permute-done.12.refs_4_) | copy-start | bytes 1769476
  114.2 15.3 %copy-start.12 = (bf16[2,384,256]{2,1,0:T(8,128)(2,1)}, bf16[2,384,256]{2,1,0:T(8,128)(2,1)S(1)}, u32[]{:S(2)}) copy-start(bf16[2,384,256]{2,1,0:T(8,128)(2,1)S(1)} %collective-permute-done.13.refs_5_) | copy-start | bytes 1179652
  114.2 0.9 copy-start.10
  115.1 26.8 %copy-start.3 = (bf16[1,1,768,256]{3,2,1,0:T(8,128)(2,1)S(1)}, bf16[1,1,768,256]{3,2,1,0:T(8,128)(2,1)}, u32[]{:S(2)}) copy-start(bf16[1,1,768,256]{3,2,1,0:T(8,128)(2,1)} %param.9) | copy-start | bytes 1179652
  115.1 26.8 %copy-start.4 = (bf16[1,1,768,256]{3,2,1,0:T(8,128)(2,1)S(1)}, bf16[1,1,768,256]{3,2,1,0:T(8,128)(2,1)}, u32[]{:S(2)}) copy-start(bf16[1,1,768,256]{3,2,1,0:T(8,128)(2,1)} %param.10) | copy-start | bytes 1179652
  120.4 21.5 %collective-permute-start.14 = (bf16[768,256]{1,0:T(8,128)(2,1)}, bf16[768,256]{1,0:T(8,128)(2,1)S(1)}, u32[]{:S(2)}, u32[]{:S(2)}) collective-permute-start(bf16[768,256]{1,0:T(8,128)(2,1)} %get-tuple-element.65), channel_id=1, source_target_pairs={{2,1},{1,2},{6,5},{5,6},{10,9},{9,10},{14,13},{13,14},{18,17},{17,... | collective-permute-start | bytes 1179656 | tf_op jit(solution)/shard_map/ppermute | solution.py:256
  127.6 14.3 %collective-permute-start.15 = (bf16[768,256]{1,0:T(8,128)(2,1)}, bf16[768,256]{1,0:T(8,128)(2,1)S(1)}, u32[]{:S(2)}, u32[]{:S(2)}) collective-permute-start(bf16[768,256]{1,0:T(8,128)(2,1)} %get-tuple-element.66), channel_id=1, source_target_pairs={{2,3},{1,0},{0,2},{3,1},{6,7},{5,4},{4,6},{7,5},{10,11},{9,8},{8,1... | collective-permute-start | bytes 1179656 | tf_op jit(solution)/shard_map/ppermute | solution.py:255
  129.5 13.8 %collective-permute-start.16 = (bf16[3,384,256]{2,1,0:T(8,128)(2,1)}, bf16[3,384,256]{2,1,0:T(8,128)(2,1)S(1)}, u32[]{:S(2)}, u32[]{:S(2)}) collective-permute-start(bf16[3,384,256]{2,1,0:T(8,128)(2,1)} %get-tuple-element.73), channel_id=1, source_target_pairs={{0,2},{2,0},{1,3},{3,1},{4,6},{6,4},{5,7},{7,5},{8,10},{10,8},{9,1... | collective-permute-start | bytes 1769480 | tf_op jit(solution)/shard_map/ppermute | solution.py:260
  133.3 18.0 %all-to-all-start.1 = ((f32[64,1,24]{2,1,0:T(1,128)}), f32[64,1,24]{2,1,0:T(1,128)S(1)}, u32[]{:S(2)}, u32[]{:S(2)}) async-start(f32[64,1,24]{2,1,0:T(1,128)} %bitcast.22), calls=%async_computation.1 | async-start | bytes 65536 | tf_op jit(solution)/shard_map/all_to_all | solution.py:259
  143.3 0.8 copy-start.8

commit v5 on v4

--- a/solution.py
+++ b/solution.py
@@ -162,13 +162,16 @@
     def flat4(y, x, c, d):
         return ((y * 2 + x) * 2 + c) * 2 + d
 
+    def shift(h):
+        return (4 * h - 2) % ny
+
     def token_moves(cross):
         pairs = []
         for y in range(ny):
             for x in range(2):
                 for c in range(2):
                     for d in range(2):
-                        to_y = (y % half_y) * 2 + x
+                        to_y = ((y % half_y) * 2 + x + shift(y // half_y)) % ny
                         to_x = 1 - c if cross else c
                         pairs.append((flat4(y, x, c, d), flat4(to_y, to_x, d, y // half_y)))
         return pairs
@@ -214,40 +217,46 @@
         sigma = jax.nn.sigmoid(gate)
         active = gate * sigma
         scaled = (weight_rows * (active * upper)).astype(BF)
-        w_sent, scaled = lax.optimization_barrier((w_down[0], scaled))
         s_a = lax.ppermute(scaled, ("core", "dp"), scaled_a)
         s_b = lax.ppermute(scaled, ("core", "dp"), scaled_b)
-        w_moved = lax.ppermute(w_sent, "core", swap)
+        w_moved = lax.ppermute(w_down[0], "core", swap)
 
         held_own = dp == core
         turn = jnp.where(core == 0, -1, 1)
+        shift_here = jnp.where(dp == 0, shift(0), shift(1))
         order = [0] + [sign * step for step in range(1, half_y) for sign in (1, -1)] + [half_y]
         index = jnp.stack(
-            [(y + turn * o + ny) % ny for o in order] + [held_own.astype(jnp.int32), core]
+            [(y + turn * o + 2 * ny - shift_here) % ny for o in order] + [held_own.astype(jnp.int32), core]
         ).astype(jnp.int32)
         on_a = lambda v: lax.ppermute(v, ("y", "core"), ring_a)
         on_b = lambda v: lax.ppermute(v, ("y", "core"), ring_b)
         block = part.reshape(rows, chip)
         a = on_a(block)
-        block_b, s_a, s_b, w_moved = lax.optimization_barrier((block, s_a, s_b, w_moved))
+        block_b, s_a, s_b = lax.optimization_barrier((block, s_a, s_b))
         b = on_b(block_b)
         args = (w_down[0].reshape(ny, chip, width), w_moved.reshape(ny, chip, width), s_a, s_b)
         waiting, start, acc, theirs = [block_b, a, b], 0, None, None
         g_mine, g_moved = [], []
         for step in range(2, half_y + 1):
-            if acc is not None:
+            ready = theirs
+            if step == half_y:
+                a, acc, ready = lax.optimization_barrier((a, acc, ready))
+                g_moved.append(lax.ppermute(ready, "core", swap))
+            elif acc is not None:
                 a, acc = lax.optimization_barrier((a, acc))
-                b, acc, theirs = lax.optimization_barrier((b, acc, theirs))
-                g_moved.append(lax.ppermute(theirs, "core", swap))
             a = on_a(a)
-            arriving = [a]
-            if step < half_y:
-                b = on_b(b)
-                arriving.append(b)
             acc, gm, theirs = use(waiting, index, start, *args, acc)
             g_mine.append(gm)
             start += len(waiting)
-            waiting = arriving
+            waiting = [a]
+            if step < half_y:
+                if ready is None:
+                    b, acc = lax.optimization_barrier((b, acc))
+                else:
+                    b, acc, ready = lax.optimization_barrier((b, acc, ready))
+                    g_moved.append(lax.ppermute(ready, "core", swap))
+                b = on_b(b)
+                waiting.append(b)
         acc, *g_moved = lax.optimization_barrier((acc, *g_moved))
         acc, gm, theirs, sum_a, sum_b, mix = use(waiting, index, start, *args, acc, last=True, carry=theirs)
         g_mine.append(gm)

time: 154 us -> 158 us (1.026)
  waiting for transfers between devices: 21.9 us -> 30.1 us
  starting transfers between devices: 90.2 us -> 85.4 us
  local copies, waits for them, and re-layouts: 4.95 us -> 7.53 us
    ppermute x4, starting transfers between devices: 25.7 us -> 14.9 us  [local(): on_a = lambda v: lax.ppermute(v, ('y', 'core'), ring_a)]
    ppermute x1, starting transfers between devices: 1.92 us -> 8.33 us  [local(): lax.ppermute(jnp.concatenate([cotangent[0], ids], axis=1), every, token_m...]
    ppermute x3, waiting for transfers between devices: 0.46 us -> 6.36 us  [local(): on_b = lambda v: lax.ppermute(v, ('y', 'core'), ring_b)]
    ppermute x1, starting transfers between devices: 8.79 us -> 4 us  [local(): across = lax.ppermute(cotangent[0], every, token_moves(True))]
    all_to_all x1, starting transfers between devices: 5.77 us -> 10 us  [local(): lax.all_to_all(outgoing, 'expert', split_axis=0, concat_axis=0, tiled=True)]
    ppermute x3, starting transfers between devices: 10.4 us -> 14.6 us  [the longest x2 12.7 us: local(): g_moved.append(lax.ppermute(ready, 'core', swap))]
    ppermute x1, starting transfers between devices: 9.91 us -> 5.98 us  [local(): s_a = lax.ppermute(scaled, ('core', 'dp'), scaled_a)]
    ppermute x1, waiting for transfers between devices: 0.01 us -> 3.49 us  [local(): across = lax.ppermute(cotangent[0], every, token_moves(True))]
  transfers between devices with their start and end apart: 19 -> 19, of which waited for: 7 -> 5; matrix products, arithmetic and copies ran while one was open for 5% -> 3% of each run, Pallas kernels for 14% -> 14%
where the time goes in v5:
time: 158 us; the launch traced here: 157 us
  starting transfers between devices  85.4 us (54%)
  waiting for transfers between devices  30.1 us (19%)
  Pallas kernels  26.7 us (17%)
  local copies, waits for them, and re-layouts  7.53 us (5%)
  other arithmetic  4.97 us (3%)
    pallas_call x4, Pallas kernels, use(): pl.pallas_call(functools.partial(use_kernel, blocks, first, last, carried...  22.7 us
    ppermute x4, starting transfers between devices, local(): on_a = lambda v: lax.ppermute(v, ('y', 'core'), ring_a)  14.9 us
    ppermute x2, starting transfers between devices, local(): g_moved.append(lax.ppermute(ready, 'core', swap))  12.7 us
    all_to_all x1, starting transfers between devices, local(): lax.all_to_all(mix.reshape(members, share), ('dp', 'y', 'xlo', 'core'), 0...  10.9 us
    all_to_all x1, starting transfers between devices, local(): lax.all_to_all(outgoing, 'expert', split_axis=0, concat_axis=0, tiled=True)  10 us
    ppermute x4, waiting for transfers between devices, local(): on_a = lambda v: lax.ppermute(v, ('y', 'core'), ring_a)  9.35 us
    ppermute x1, starting transfers between devices, local(): lax.ppermute(jnp.concatenate([cotangent[0], ids], axis=1), every, token_m...  8.33 us
    all_to_all x1, waiting for transfers between devices, local(): lax.all_to_all(outgoing, 'expert', split_axis=0, concat_axis=0, tiled=True)  7.66 us
  transfers between devices with their start and end apart: 19, of which 5 were waited for; matrix products, arithmetic and copies ran while one was open for 3% of the time, Pallas kernels for 14%

profile of v5, /device:TPU:1, one launch (start us, length us, event | category | flops | bytes accessed | tf_op | source)
XLA Modules:
  0.0 157.2 jit_solution(15697870737899200181)
XLA Ops:
  0.6 1.0 copy.19
  1.6 0.0 copy-start
  1.6 0.0 copy-start.13
  1.7 0.8 convert_bitcast_fusion
  2.5 8.3 %collective-permute-start = (bf16[192,194]{0,1:T(8,128)(2,1)S(1)}, bf16[192,194]{0,1:T(8,128)(2,1)S(1)}, u32[]{:S(2)}, u32[]{:S(2)}) collective-permute-start(bf16[192,194]{0,1:T(8,128)(2,1)S(1)} %pad_maximum_fusion), channel_id=1, source_target_pairs={{0,48},{1,50},{2,52},{3,54},{4,56},{5,58},{6,60},{7,62},{8,0},{9,2... | collective-permute-start | bytes 223496 | tf_op jit(solution)/shard_map/ppermute | solution.py:205
  10.8 4.0 %collective-permute-start.1 = (bf16[192,192]{0,1:T(8,128)(2,1)S(1)}, bf16[192,192]{0,1:T(8,128)(2,1)S(1)}, u32[]{:S(2)}, u32[]{:S(2)}) collective-permute-start(bf16[192,192]{0,1:T(8,128)(2,1)S(1)} %bitcast.60), channel_id=1, source_target_pairs={{0,52},{1,54},{2,48},{3,50},{4,60},{5,62},{6,56},{7,58},{8,4},{9,6... | collective-permute-start | bytes 221192 | tf_op jit(solution)/shard_map/ppermute | solution.py:206
  14.9 0.1 fusion.16
  15.1 3.5 %collective-permute-done.1 = bf16[192,192]{0,1:T(8,128)(2,1)S(1)} collective-permute-done((bf16[192,192]{0,1:T(8,128)(2,1)S(1)}, bf16[192,192]{0,1:T(8,128)(2,1)S(1)}, u32[]{:S(2)}, u32[]{:S(2)}) %collective-permute-start.1) | collective-permute-done | bytes 73760 | tf_op jit(solution)/shard_map/ppermute | solution.py:206
  18.6 1.2 convolution_convert_fusion
  19.8 10.0 %all-to-all-start = ((bf16[8,96,384]{2,1,0:T(8,128)(2,1)}), bf16[8,96,384]{2,1,0:T(8,128)(2,1)}, u32[]{:S(2)}, u32[]{:S(2)}) async-start(bf16[8,96,384]{2,1,0:T(8,128)(2,1)} %bitcast.14), calls=%async_computation | async-start | bytes 1179648 | tf_op jit(solution)/shard_map/all_to_all | solution.py:212
  29.9 1.9 %collective-permute-start.7 = (bf16[3072,256]{1,0:T(8,128)(2,1)S(1)}, bf16[3072,256]{1,0:T(8,128)(2,1)S(1)}, u32[]{:S(2)}, u32[]{:S(2)}) collective-permute-start(bf16[3072,256]{1,0:T(8,128)(2,1)S(1)} %bitcast.49), channel_id=1, source_target_pairs={{0,2},{2,0},{1,3},{3,1},{4,6},{6,4},{5,7},{7,5},{8,10},{10,8},{9,1... | collective-permute-start | bytes 4718600 | tf_op jit(solution)/shard_map/ppermute | solution.py:222
  31.8 2.0 %fusion.1 = bf16[768,256]{1,0:T(8,128)(2,1)} fusion(bf16[1,1,768,256]{3,2,1,0:T(8,128)(2,1)} %param.10, f32[768]{0:T(1024)S(1)} %reduce, bf16[1,1,768,256]{3,2,1,0:T(8,128)(2,1)S(1)} %copy-done.3), kind=kLoop, calls=%fused_computation.7 | loop fusion | flops 1769472 | bytes 1182720 | tf_op jit(solution)/shard_map/convert_element_type | solution.py:219
  33.8 6.0 %collective-permute-start.4 = (bf16[768,256]{1,0:T(8,128)(2,1)}, bf16[768,256]{1,0:T(8,128)(2,1)S(1)}, u32[]{:S(2)}, u32[]{:S(2)}) collective-permute-start(bf16[768,256]{1,0:T(8,128)(2,1)} %fusion.1), channel_id=1, source_target_pairs={{0,0},{1,2},{2,1},{3,3},{4,4},{5,6},{6,5},{7,7},{8,8},{9,10},{10,9... | collective-permute-start | bytes 1179656 | tf_op jit(solution)/shard_map/ppermute | solution.py:220
  39.8 1.9 %collective-permute-start.5 = (bf16[768,256]{1,0:T(8,128)(2,1)}, bf16[768,256]{1,0:T(8,128)(2,1)}, u32[]{:S(2)}, u32[]{:S(2)}) collective-permute-start(bf16[768,256]{1,0:T(8,128)(2,1)} %fusion.1), channel_id=1, source_target_pairs={{0,1},{1,3},{2,0},{3,2},{4,5},{5,7},{6,4},{7,6},{8,9},{9,11},{10,8... | collective-permute-start | bytes 1179656 | tf_op jit(solution)/shard_map/ppermute | solution.py:221
  41.8 7.7 %all-to-all-done = bf16[8,96,384]{2,1,0:T(8,128)(2,1)} async-done(((bf16[8,96,384]{2,1,0:T(8,128)(2,1)}), bf16[8,96,384]{2,1,0:T(8,128)(2,1)}, u32[]{:S(2)}, u32[]{:S(2)}) %all-to-all-start) | async-done | bytes 589856 | tf_op jit(solution)/shard_map/all_to_all | solution.py:212
  49.4 2.6 %collective-permute-start.2 = (bf16[768,384]{1,0:T(8,128)(2,1)}, bf16[768,384]{1,0:T(8,128)(2,1)}, u32[]{:S(2)}, u32[]{:S(2)}) collective-permute-start(bf16[768,384]{1,0:T(8,128)(2,1)} %bitcast.15.refs_0_), channel_id=1, source_target_pairs={{0,8},{2,58},{8,16},{10,2},{16,24},{18,10},{24,32},{26,18},{32,40}... | collective-permute-start | bytes 1769480 | tf_op jit(solution)/shard_map/ppermute | solution.py:231
  52.0 0.0 collective-permute-done.4.refs_9_.refs_6_.refs_3_
  52.0 0.0 copy-start.2
  52.1 2.7 %collective-permute-start.6 = (bf16[768,384]{1,0:T(8,128)(2,1)}, bf16[768,384]{1,0:T(8,128)(2,1)}, u32[]{:S(2)}, u32[]{:S(2)}) collective-permute-start(bf16[768,384]{1,0:T(8,128)(2,1)} %bitcast.15.refs_0_), channel_id=1, source_target_pairs={{0,56},{2,10},{8,0},{10,18},{16,8},{18,26},{24,16},{26,34},{32,24}... | collective-permute-start | bytes 1769480 | tf_op jit(solution)/shard_map/ppermute | solution.py:232
  54.8 9.3 %collective-permute-done.2.refs_1_ = bf16[768,384]{1,0:T(8,128)(2,1)} collective-permute-done((bf16[768,384]{1,0:T(8,128)(2,1)}, bf16[768,384]{1,0:T(8,128)(2,1)}, u32[]{:S(2)}, u32[]{:S(2)}) %collective-permute-start.2) | collective-permute-done | bytes 589856 | tf_op jit(solution)/shard_map/ppermute | solution.py:231
  64.1 4.2 %collective-permute-start.3 = (bf16[768,384]{1,0:T(8,128)(2,1)}, bf16[768,384]{1,0:T(8,128)(2,1)}, u32[]{:S(2)}, u32[]{:S(2)}) collective-permute-start(bf16[768,384]{1,0:T(8,128)(2,1)} %collective-permute-done.2.refs_1_), channel_id=1, source_target_pairs={{0,8},{2,58},{8,16},{10,2},{16,24},{18,10},{24,32},{26,18},{32,40}... | collective-permute-start | bytes 1769480 | tf_op jit(solution)/shard_map/ppermute | solution.py:231
  68.4 0.6 stack.47.index
  69.0 1.1 copy-done.1
  70.2 6.2 %shard_map.93 = (f32[768,512]{1,0:T(8,128)}, bf16[3,384,256]{2,1,0:T(8,128)(2,1)}, bf16[3,384,256]{2,1,0:T(8,128)(2,1)}) custom-call(s32[10]{0:T(128)} %stack.47.index, bf16[768,384]{1,0:T(8,128)(2,1)} %bitcast.15.refs_0_, bf16[768,384]{1,0:T(8,128)(2,1)} %collective-permute-done.2.refs_1_, bf16[768,384]{1,0:T(8,128)(2,1)} %collective-permute-done.6.refs_2_, ...), custom_call_target="tpu_custom_call" | custom-call | flops 1811939328 | bytes 12000000 | tf_op jit(solution)/shard_map/pallas_call | solution.py:108
  76.4 2.0 %collective-permute-start.9 = (bf16[768,384]{1,0:T(8,128)(2,1)}, bf16[768,384]{1,0:T(8,128)(2,1)S(1)}, u32[]{:S(2)}, u32[]{:S(2)}) collective-permute-start(bf16[768,384]{1,0:T(8,128)(2,1)} %collective-permute-done.6.refs_2_), channel_id=1, source_target_pairs={{0,56},{2,10},{8,0},{10,18},{16,8},{18,26},{24,16},{26,34},{32,24}... | collective-permute-start | bytes 1769480 | tf_op jit(solution)/shard_map/ppermute | solution.py:232
  78.4 4.6 %collective-permute-start.8 = (bf16[768,384]{1,0:T(8,128)(2,1)}, bf16[768,384]{1,0:T(8,128)(2,1)S(1)}, u32[]{:S(2)}, u32[]{:S(2)}) collective-permute-start(bf16[768,384]{1,0:T(8,128)(2,1)} %collective-permute-done.3.refs_0_), channel_id=1, source_target_pairs={{0,8},{2,58},{8,16},{10,2},{16,24},{18,10},{24,32},{26,18},{32,40}... | collective-permute-start | bytes 1769480 | tf_op jit(solution)/shard_map/ppermute | solution.py:231
  83.0 6.4 %collective-permute-done.9.refs_1_ = bf16[768,384]{1,0:T(8,128)(2,1)S(1)} collective-permute-done((bf16[768,384]{1,0:T(8,128)(2,1)}, bf16[768,384]{1,0:T(8,128)(2,1)S(1)}, u32[]{:S(2)}, u32[]{:S(2)}) %collective-permute-start.9) | collective-permute-done | bytes 589856 | tf_op jit(solution)/shard_map/ppermute | solution.py:232
  89.3 0.8 copy-done.9
  90.2 5.6 %shard_map.94 = (f32[768,512]{1,0:T(8,128)}, bf16[2,384,256]{2,1,0:T(8,128)(2,1)}, bf16[2,384,256]{2,1,0:T(8,128)(2,1)}) custom-call(s32[10]{0:T(128)} %stack.47.index, bf16[768,384]{1,0:T(8,128)(2,1)} %collective-permute-done.3.refs_0_, bf16[768,384]{1,0:T(8,128)(2,1)} %copy-done.9, bf16[8,384,256]{2,1,0:T(8,128)(2,1)} %bitcast.44, ...), custom_call_target="tpu_custom_call", output_to_operand_aliasing={{0}: (9, {})} | custom-call | flops 1207959552 | bytes 8000000 | tf_op jit(solution)/shard_map/pallas_call | solution.py:108
  95.8 1.9 %collective-permute-start.11 = (bf16[768,384]{1,0:T(8,128)(2,1)}, bf16[768,384]{1,0:T(8,128)(2,1)S(1)}, u32[]{:S(2)}, u32[]{:S(2)}) collective-permute-start(bf16[768,384]{1,0:T(8,128)(2,1)} %copy-done.9), channel_id=1, source_target_pairs={{0,56},{2,10},{8,0},{10,18},{16,8},{18,26},{24,16},{26,34},{32,24}... | collective-permute-start | bytes 1769480 | tf_op jit(solution)/shard_map/ppermute | solution.py:232
  97.7 10.8 %collective-permute-start.12 = (bf16[3,384,256]{2,1,0:T(8,128)(2,1)S(1)}, bf16[3,384,256]{2,1,0:T(8,128)(2,1)S(1)}, u32[]{:S(2)}, u32[]{:S(2)}) collective-permute-start(bf16[3,384,256]{2,1,0:T(8,128)(2,1)S(1)} %copy-done.14), channel_id=1, source_target_pairs={{0,2},{2,0},{1,3},{3,1},{4,6},{6,4},{5,7},{7,5},{8,10},{10,8},{9,1... | collective-permute-start | bytes 1769480 | tf_op jit(solution)/shard_map/ppermute | solution.py:257
  108.5 0.0 collective-permute-done.8.refs_0_
  108.5 3.6 %collective-permute-start.10 = (bf16[768,384]{1,0:T(8,128)(2,1)S(1)}, bf16[768,384]{1,0:T(8,128)(2,1)S(1)}, u32[]{:S(2)}, u32[]{:S(2)}) collective-permute-start(bf16[768,384]{1,0:T(8,128)(2,1)S(1)} %collective-permute-done.8.refs_0_), channel_id=1, source_target_pairs={{0,8},{2,58},{8,16},{10,2},{16,24},{18,10},{24,32},{26,18},{32,40}... | collective-permute-start | bytes 1769480 | tf_op jit(solution)/shard_map/ppermute | solution.py:231
  112.1 1.9 %collective-permute-start.13 = (bf16[2,384,256]{2,1,0:T(8,128)(2,1)}, bf16[2,384,256]{2,1,0:T(8,128)(2,1)S(1)}, u32[]{:S(2)}, u32[]{:S(2)}) collective-permute-start(bf16[2,384,256]{2,1,0:T(8,128)(2,1)} %get-tuple-element.57), channel_id=1, source_target_pairs={{0,2},{2,0},{1,3},{3,1},{4,6},{6,4},{5,7},{7,5},{8,10},{10,8},{9,1... | collective-permute-start | bytes 1179656 | tf_op jit(solution)/shard_map/ppermute | solution.py:244
  114.0 0.8 copy-done.11
  114.8 5.6 %shard_map.95 = (f32[768,512]{1,0:T(8,128)}, bf16[2,384,256]{2,1,0:T(8,128)(2,1)}, bf16[2,384,256]{2,1,0:T(8,128)(2,1)}) custom-call(s32[10]{0:T(128)} %stack.47.index, bf16[768,384]{1,0:T(8,128)(2,1)} %copy-done.8, bf16[768,384]{1,0:T(8,128)(2,1)} %copy-done.11, bf16[8,384,256]{2,1,0:T(8,128)(2,1)} %bitcast.46, ...), custom_call_target="tpu_custom_call", output_to_operand_aliasing={{0}: (9, {})} | custom-call | flops 1207959552 | bytes 8000000 | tf_op jit(solution)/shard_map/pallas_call | solution.py:108
  120.5 0.9 copy-done.10
  121.4 5.3 %shard_map.96 = (f32[768,256]{1,0:T(8,128)}, bf16[1,384,256]{2,1,0:T(8,128)(2,1)}, bf16[3,384,256]{2,1,0:T(8,128)(2,1)}, bf16[768,256]{1,0:T(8,128)(2,1)}, bf16[768,256]{1,0:T(8,128)(2,1)}, /*index=5*/f32[2,768]{1,0:T(2,128)}) custom-call(s32[10]{0:T(128)} %stack.47.index, bf16[768,384]{1,0:T(8,128)(2,1)} %copy-done.10, bf16[8,384,256]{2,1,0:T(8,128)(2,1)} %bitcast.48, ...), custom_call_target="tpu_custom_call" | custom-call | flops 603979776 | bytes 4000000 | tf_op jit(solution)/shard_map/pallas_call | solution.py:108
  126.7 3.8 %collective-permute-start.14 = (bf16[768,256]{1,0:T(8,128)(2,1)}, bf16[768,256]{1,0:T(8,128)(2,1)S(1)}, u32[]{:S(2)}, u32[]{:S(2)}) collective-permute-start(bf16[768,256]{1,0:T(8,128)(2,1)} %get-tuple-element.61), channel_id=1, source_target_pairs={{2,1},{1,2},{6,5},{5,6},{10,9},{9,10},{14,13},{13,14},{18,17},{17,... | collective-permute-start | bytes 1179656 | tf_op jit(solution)/shard_map/ppermute | solution.py:265
  130.5 1.9 %collective-permute-start.15 = (bf16[768,256]{1,0:T(8,128)(2,1)}, bf16[768,256]{1,0:T(8,128)(2,1)S(1)}, u32[]{:S(2)}, u32[]{:S(2)}) collective-permute-start(bf16[768,256]{1,0:T(8,128)(2,1)} %get-tuple-element.62), channel_id=1, source_target_pairs={{2,3},{1,0},{0,2},{3,1},{6,7},{5,4},{4,6},{7,5},{10,11},{9,8},{8,1... | collective-permute-start | bytes 1179656 | tf_op jit(solution)/shard_map/ppermute | solution.py:264
  132.5 2.4 %collective-permute-start.16 = (bf16[3,384,256]{2,1,0:T(8,128)(2,1)}, bf16[3,384,256]{2,1,0:T(8,128)(2,1)S(1)}, u32[]{:S(2)}, u32[]{:S(2)}) collective-permute-start(bf16[3,384,256]{2,1,0:T(8,128)(2,1)} %get-tuple-element.69), channel_id=1, source_target_pairs={{0,2},{2,0},{1,3},{3,1},{4,6},{6,4},{5,7},{7,5},{8,10},{10,8},{9,1... | collective-permute-start | bytes 1769480 | tf_op jit(solution)/shard_map/ppermute | solution.py:269
  134.9 1.4 all_to_all.12
  136.3 10.9 %all-to-all-start.1 = ((f32[64,1,24]{2,1,0:T(1,128)}), f32[64,1,24]{2,1,0:T(1,128)S(1)}, u32[]{:S(2)}, u32[]{:S(2)}) async-start(f32[64,1,24]{2,1,0:T(1,128)} %bitcast.22), calls=%async_computation.1 | async-start | bytes 65536 | tf_op jit(solution)/shard_map/all_to_all | solution.py:268
  147.2 1.4 multiply_convert_fusion
  148.6 0.8 copy-done.7
  149.4 4.0 %shard_map.97 = bf16[8,384,256]{2,1,0:T(8,128)(2,1)} custom-call(s32[10]{0:T(128)} %stack.47.index, bf16[3,384,256]{2,1,0:T(8,128)(2,1)} %get-tuple-element.63.refs_0_, bf16[2,384,256]{2,1,0:T(8,128)(2,1)} %get-tuple-element.64.refs_1_, bf16[2,384,256]{2,1,0:T(8,128)(2,1)} %get-tuple-element.65.refs_2_, bf16[1,384,256]{2,1,0:T(8,128)(2,1)} %get-tuple-element.66.refs_3_, ...), custom_call_target="tpu_custom_call" | custom-call | flops 1000000 | bytes 5000000 | tf_op jit(solution)/shard_map/pallas_call | solution.py:144
  153.4 3.2 %all-to-all-done.1 = f32[64,1,24]{2,1,0:T(1,128)S(1)} async-done(((f32[64,1,24]{2,1,0:T(1,128)}), f32[64,1,24]{2,1,0:T(1,128)S(1)}, u32[]{:S(2)}, u32[]{:S(2)}) %all-to-all-start.1) | async-done | bytes 6176 | tf_op jit(solution)/shard_map/all_to_all | solution.py:268
  156.6 0.6 bitcast_divide_fusion
  (43 shorter events, 0.2 us)
Async XLA Ops:
  1.6 28.2 %copy-start = (bf16[1,3072,256]{2,1,0:T(8,128)(2,1)S(1)}, bf16[1,3072,256]{2,1,0:T(8,128)(2,1)}, u32[]{:S(2)}) copy-start(bf16[1,3072,256]{2,1,0:T(8,128)(2,1)} %param.11) | copy-start | bytes 4718596
  1.6 30.2 %copy-start.13 = (f32[1,1,768]{2,1,0:T(1,128)S(1)}, f32[1,1,768]{2,1,0:T(1,128)}, u32[]{:S(2)}) copy-start(f32[1,1,768]{2,1,0:T(1,128)} %param.8) | copy-start | bytes 9220
  2.5 29.4 %copy-start.3 = (bf16[1,1,768,256]{3,2,1,0:T(8,128)(2,1)S(1)}, bf16[1,1,768,256]{3,2,1,0:T(8,128)(2,1)}, u32[]{:S(2)}) copy-start(bf16[1,1,768,256]{3,2,1,0:T(8,128)(2,1)} %param.9) | copy-start | bytes 1179652
  2.5 12.4 %collective-permute-start = (bf16[192,194]{0,1:T(8,128)(2,1)S(1)}, bf16[192,194]{0,1:T(8,128)(2,1)S(1)}, u32[]{:S(2)}, u32[]{:S(2)}) collective-permute-start(bf16[192,194]{0,1:T(8,128)(2,1)S(1)} %pad_maximum_fusion), channel_id=1, source_target_pairs={{0,48},{1,50},{2,52},{3,54},{4,56},{5,58},{6,60},{7,62},{8,0},{9,2... | collective-permute-start | bytes 223496 | tf_op jit(solution)/shard_map/ppermute | solution.py:205
  10.8 7.8 %collective-permute-start.1 = (bf16[192,192]{0,1:T(8,128)(2,1)S(1)}, bf16[192,192]{0,1:T(8,128)(2,1)S(1)}, u32[]{:S(2)}, u32[]{:S(2)}) collective-permute-start(bf16[192,192]{0,1:T(8,128)(2,1)S(1)} %bitcast.60), channel_id=1, source_target_pairs={{0,52},{1,54},{2,48},{3,50},{4,60},{5,62},{6,56},{7,58},{8,4},{9,6... | collective-permute-start | bytes 221192 | tf_op jit(solution)/shard_map/ppermute | solution.py:206
  19.8 29.6 %all-to-all-start = ((bf16[8,96,384]{2,1,0:T(8,128)(2,1)}), bf16[8,96,384]{2,1,0:T(8,128)(2,1)}, u32[]{:S(2)}, u32[]{:S(2)}) async-start(bf16[8,96,384]{2,1,0:T(8,128)(2,1)} %bitcast.14), calls=%async_computation | async-start | bytes 1179648 | tf_op jit(solution)/shard_map/all_to_all | solution.py:212
  29.9 39.2 %collective-permute-start.7 = (bf16[3072,256]{1,0:T(8,128)(2,1)S(1)}, bf16[3072,256]{1,0:T(8,128)(2,1)S(1)}, u32[]{:S(2)}, u32[]{:S(2)}) collective-permute-start(bf16[3072,256]{1,0:T(8,128)(2,1)S(1)} %bitcast.49), channel_id=1, source_target_pairs={{0,2},{2,0},{1,3},{3,1},{4,6},{6,4},{5,7},{7,5},{8,10},{10,8},{9,1... | collective-permute-start | bytes 4718600 | tf_op jit(solution)/shard_map/ppermute | solution.py:222
  33.8 18.2 %collective-permute-start.4 = (bf16[768,256]{1,0:T(8,128)(2,1)}, bf16[768,256]{1,0:T(8,128)(2,1)S(1)}, u32[]{:S(2)}, u32[]{:S(2)}) collective-permute-start(bf16[768,256]{1,0:T(8,128)(2,1)} %fusion.1), channel_id=1, source_target_pairs={{0,0},{1,2},{2,1},{3,3},{4,4},{5,6},{6,5},{7,7},{8,8},{9,10},{10,9... | collective-permute-start | bytes 1179656 | tf_op jit(solution)/shard_map/ppermute | solution.py:220
  39.8 12.2 %collective-permute-start.5 = (bf16[768,256]{1,0:T(8,128)(2,1)}, bf16[768,256]{1,0:T(8,128)(2,1)}, u32[]{:S(2)}, u32[]{:S(2)}) collective-permute-start(bf16[768,256]{1,0:T(8,128)(2,1)} %fusion.1), channel_id=1, source_target_pairs={{0,1},{1,3},{2,0},{3,2},{4,5},{5,7},{6,4},{7,6},{8,9},{9,11},{10,8... | collective-permute-start | bytes 1179656 | tf_op jit(solution)/shard_map/ppermute | solution.py:221
  49.4 14.7 %collective-permute-start.2 = (bf16[768,384]{1,0:T(8,128)(2,1)}, bf16[768,384]{1,0:T(8,128)(2,1)}, u32[]{:S(2)}, u32[]{:S(2)}) collective-permute-start(bf16[768,384]{1,0:T(8,128)(2,1)} %bitcast.15.refs_0_), channel_id=1, source_target_pairs={{0,8},{2,58},{8,16},{10,2},{16,24},{18,10},{24,32},{26,18},{32,40}... | collective-permute-start | bytes 1769480 | tf_op jit(solution)/shard_map/ppermute | solution.py:231
  52.0 17.0 %copy-start.2 = (bf16[768,256]{1,0:T(8,128)(2,1)}, bf16[768,256]{1,0:T(8,128)(2,1)S(1)}, u32[]{:S(2)}) copy-start(bf16[768,256]{1,0:T(8,128)(2,1)S(1)} %collective-permute-done.4.refs_9_.refs_6_.refs_3_) | copy-start | bytes 1179652
  52.1 17.0 %collective-permute-start.6 = (bf16[768,384]{1,0:T(8,128)(2,1)}, bf16[768,384]{1,0:T(8,128)(2,1)}, u32[]{:S(2)}, u32[]{:S(2)}) collective-permute-start(bf16[768,384]{1,0:T(8,128)(2,1)} %bitcast.15.refs_0_), channel_id=1, source_target_pairs={{0,56},{2,10},{8,0},{10,18},{16,8},{18,26},{24,16},{26,34},{32,24}... | collective-permute-start | bytes 1769480 | tf_op jit(solution)/shard_map/ppermute | solution.py:232
  64.1 14.3 %collective-permute-start.3 = (bf16[768,384]{1,0:T(8,128)(2,1)}, bf16[768,384]{1,0:T(8,128)(2,1)}, u32[]{:S(2)}, u32[]{:S(2)}) collective-permute-start(bf16[768,384]{1,0:T(8,128)(2,1)} %collective-permute-done.2.refs_1_), channel_id=1, source_target_pairs={{0,8},{2,58},{8,16},{10,2},{16,24},{18,10},{24,32},{26,18},{32,40}... | collective-permute-start | bytes 1769480 | tf_op jit(solution)/shard_map/ppermute | solution.py:231
  69.0 1.1 copy-start.1
  76.4 21.3 %copy-start.14 = (bf16[3,384,256]{2,1,0:T(8,128)(2,1)S(1)}, bf16[3,384,256]{2,1,0:T(8,128)(2,1)}, u32[]{:S(2)}) copy-start(bf16[3,384,256]{2,1,0:T(8,128)(2,1)} %get-tuple-element.56) | copy-start | bytes 1769476
  76.4 13.0 %collective-permute-start.9 = (bf16[768,384]{1,0:T(8,128)(2,1)}, bf16[768,384]{1,0:T(8,128)(2,1)S(1)}, u32[]{:S(2)}, u32[]{:S(2)}) collective-permute-start(bf16[768,384]{1,0:T(8,128)(2,1)} %collective-permute-done.6.refs_2_), channel_id=1, source_target_pairs={{0,56},{2,10},{8,0},{10,18},{16,8},{18,26},{24,16},{26,34},{32,24}... | collective-permute-start | bytes 1769480 | tf_op jit(solution)/shard_map/ppermute | solution.py:232
  78.4 30.0 %collective-permute-start.8 = (bf16[768,384]{1,0:T(8,128)(2,1)}, bf16[768,384]{1,0:T(8,128)(2,1)S(1)}, u32[]{:S(2)}, u32[]{:S(2)}) collective-permute-start(bf16[768,384]{1,0:T(8,128)(2,1)} %collective-permute-done.3.refs_0_), channel_id=1, source_target_pairs={{0,8},{2,58},{8,16},{10,2},{16,24},{18,10},{24,32},{26,18},{32,40}... | collective-permute-start | bytes 1769480 | tf_op jit(solution)/shard_map/ppermute | solution.py:231
  89.3 0.8 copy-start.9
  95.8 18.3 %collective-permute-start.11 = (bf16[768,384]{1,0:T(8,128)(2,1)}, bf16[768,384]{1,0:T(8,128)(2,1)S(1)}, u32[]{:S(2)}, u32[]{:S(2)}) collective-permute-start(bf16[768,384]{1,0:T(8,128)(2,1)} %copy-done.9), channel_id=1, source_target_pairs={{0,56},{2,10},{8,0},{10,18},{16,8},{18,26},{24,16},{26,34},{32,24}... | collective-permute-start | bytes 1769480 | tf_op jit(solution)/shard_map/ppermute | solution.py:232
  97.7 22.8 %collective-permute-start.12 = (bf16[3,384,256]{2,1,0:T(8,128)(2,1)S(1)}, bf16[3,384,256]{2,1,0:T(8,128)(2,1)S(1)}, u32[]{:S(2)}, u32[]{:S(2)}) collective-permute-start(bf16[3,384,256]{2,1,0:T(8,128)(2,1)S(1)} %copy-done.14), channel_id=1, source_target_pairs={{0,2},{2,0},{1,3},{3,1},{4,6},{6,4},{5,7},{7,5},{8,10},{10,8},{9,1... | collective-permute-start | bytes 1769480 | tf_op jit(solution)/shard_map/ppermute | solution.py:257
  108.5 5.6 %copy-start.8 = (bf16[768,384]{1,0:T(8,128)(2,1)}, bf16[768,384]{1,0:T(8,128)(2,1)S(1)}, u32[]{:S(2)}) copy-start(bf16[768,384]{1,0:T(8,128)(2,1)S(1)} %collective-permute-done.8.refs_0_) | copy-start | bytes 1769476
  108.5 12.0 %collective-permute-start.10 = (bf16[768,384]{1,0:T(8,128)(2,1)S(1)}, bf16[768,384]{1,0:T(8,128)(2,1)S(1)}, u32[]{:S(2)}, u32[]{:S(2)}) collective-permute-start(bf16[768,384]{1,0:T(8,128)(2,1)S(1)} %collective-permute-done.8.refs_0_), channel_id=1, source_target_pairs={{0,8},{2,58},{8,16},{10,2},{16,24},{18,10},{24,32},{26,18},{32,40}... | collective-permute-start | bytes 1769480 | tf_op jit(solution)/shard_map/ppermute | solution.py:231
  112.1 8.4 %collective-permute-start.13 = (bf16[2,384,256]{2,1,0:T(8,128)(2,1)}, bf16[2,384,256]{2,1,0:T(8,128)(2,1)S(1)}, u32[]{:S(2)}, u32[]{:S(2)}) collective-permute-start(bf16[2,384,256]{2,1,0:T(8,128)(2,1)} %get-tuple-element.57), channel_id=1, source_target_pairs={{0,2},{2,0},{1,3},{3,1},{4,6},{6,4},{5,7},{7,5},{8,10},{10,8},{9,1... | collective-permute-start | bytes 1179656 | tf_op jit(solution)/shard_map/ppermute | solution.py:244
  114.0 0.8 copy-start.11
  120.5 6.2 %copy-start.6 = (bf16[3,384,256]{2,1,0:T(8,128)(2,1)}, bf16[3,384,256]{2,1,0:T(8,128)(2,1)S(1)}, u32[]{:S(2)}) copy-start(bf16[3,384,256]{2,1,0:T(8,128)(2,1)S(1)} %collective-permute-done.12.refs_4_) | copy-start | bytes 1769476
  120.5 28.1 %copy-start.12 = (bf16[2,384,256]{2,1,0:T(8,128)(2,1)}, bf16[2,384,256]{2,1,0:T(8,128)(2,1)S(1)}, u32[]{:S(2)}) copy-start(bf16[2,384,256]{2,1,0:T(8,128)(2,1)S(1)} %collective-permute-done.13.refs_5_) | copy-start | bytes 1179652
  120.5 0.9 copy-start.10
  121.4 25.7 %copy-start.4 = (bf16[1,1,768,256]{3,2,1,0:T(8,128)(2,1)S(1)}, bf16[1,1,768,256]{3,2,1,0:T(8,128)(2,1)}, u32[]{:S(2)}) copy-start(bf16[1,1,768,256]{3,2,1,0:T(8,128)(2,1)} %param.9) | copy-start | bytes 1179652
  121.4 25.7 %copy-start.5 = (bf16[1,1,768,256]{3,2,1,0:T(8,128)(2,1)S(1)}, bf16[1,1,768,256]{3,2,1,0:T(8,128)(2,1)}, u32[]{:S(2)}) copy-start(bf16[1,1,768,256]{3,2,1,0:T(8,128)(2,1)} %param.10) | copy-start | bytes 1179652
  126.7 20.4 %collective-permute-start.14 = (bf16[768,256]{1,0:T(8,128)(2,1)}, bf16[768,256]{1,0:T(8,128)(2,1)S(1)}, u32[]{:S(2)}, u32[]{:S(2)}) collective-permute-start(bf16[768,256]{1,0:T(8,128)(2,1)} %get-tuple-element.61), channel_id=1, source_target_pairs={{2,1},{1,2},{6,5},{5,6},{10,9},{9,10},{14,13},{13,14},{18,17},{17,... | collective-permute-start | bytes 1179656 | tf_op jit(solution)/shard_map/ppermute | solution.py:265
  130.5 16.6 %collective-permute-start.15 = (bf16[768,256]{1,0:T(8,128)(2,1)}, bf16[768,256]{1,0:T(8,128)(2,1)S(1)}, u32[]{:S(2)}, u32[]{:S(2)}) collective-permute-start(bf16[768,256]{1,0:T(8,128)(2,1)} %get-tuple-element.62), channel_id=1, source_target_pairs={{2,3},{1,0},{0,2},{3,1},{6,7},{5,4},{4,6},{7,5},{10,11},{9,8},{8,1... | collective-permute-start | bytes 1179656 | tf_op jit(solution)/shard_map/ppermute | solution.py:264
  132.5 16.1 %collective-permute-start.16 = (bf16[3,384,256]{2,1,0:T(8,128)(2,1)}, bf16[3,384,256]{2,1,0:T(8,128)(2,1)S(1)}, u32[]{:S(2)}, u32[]{:S(2)}) collective-permute-start(bf16[3,384,256]{2,1,0:T(8,128)(2,1)} %get-tuple-element.69), channel_id=1, source_target_pairs={{0,2},{2,0},{1,3},{3,1},{4,6},{6,4},{5,7},{7,5},{8,10},{10,8},{9,1... | collective-permute-start | bytes 1769480 | tf_op jit(solution)/shard_map/ppermute | solution.py:269
  136.3 20.3 %all-to-all-start.1 = ((f32[64,1,24]{2,1,0:T(1,128)}), f32[64,1,24]{2,1,0:T(1,128)S(1)}, u32[]{:S(2)}, u32[]{:S(2)}) async-start(f32[64,1,24]{2,1,0:T(1,128)} %bitcast.22), calls=%async_computation.1 | async-start | bytes 65536 | tf_op jit(solution)/shard_map/all_to_all | solution.py:268
  148.6 0.8 copy-start.7

commit v6 on v5

--- a/solution.py
+++ b/solution.py
@@ -26,14 +26,15 @@
     return hit.astype(BF)
 
 
-def use_kernel(blocks, first, last, carried, index, *refs):
+def use_kernel(blocks, first, last, index, *refs):
     it = iter(refs)
     x_refs = [next(it) for _ in range(blocks)]
     w_mine = [next(it) for _ in range(blocks)]
     w_theirs = [next(it) for _ in range(blocks)]
     s_a, s_b = next(it), next(it)
-    carry = next(it) if carried else None
-    acc_in = None if first else next(it)
+    acc_in = None
+    if not first:
+        acc_in, _, _ = next(it), next(it), next(it)
     acc, g_mine, g_theirs = next(it), next(it), next(it)
     width = s_a.shape[1]
     flags = index.shape[0] - 2
@@ -53,7 +54,7 @@
             acc[...] += product
         outer = lax.dot_general(x, s, (((0,), (0,)), ((), ())), preferred_element_type=F32)
         g_mine[b] = outer[:, :width].astype(BF)
-        g_theirs[carried + b] = outer[:, width:].astype(BF)
+        g_theirs[b] = outer[:, width:].astype(BF)
     if last:
         sum_a, sum_b, mix = next(it), next(it), next(it)
         mine, theirs = total[:, :width], total[:, width:]
@@ -70,16 +71,14 @@
         )
         row = lax.broadcasted_iota(jnp.int32, (2, line.shape[1]), 0)
         mix[...] = jnp.where(row == index[flags + 1], line[:2], 0.0)
-    if carried:
-        g_theirs[:carried] = carry[...]
-
-
-def use(pieces, index, start, w_mine, w_theirs, s_a, s_b, acc, last=False, carry=None):
-    first = acc is None
+
+
+def use(pieces, index, start, w_mine, w_theirs, s_a, s_b, held, last=False):
+    first = held is None
     blocks = len(pieces)
-    carried = 0 if carry is None else carry.shape[0]
     rows, width = s_a.shape
-    chip = pieces[0].shape[1]
+    total, chip, _ = w_mine.shape
+    assert start % blocks == 0
 
     def whole(a):
         return pl.BlockSpec(a.shape, lambda i, idx: (0,) * len(a.shape))
@@ -89,31 +88,27 @@
 
     ins = list(pieces) + [w_mine] * blocks + [w_theirs] * blocks + [s_a, s_b]
     specs = [whole(a) for a in pieces] + [pick(j) for j in range(blocks)] * 2 + [whole(s_a), whole(s_b)]
-    if carried:
-        ins.append(carry)
-        specs.append(whole(carry))
     aliases = {}
     if not first:
-        if not last:
-            aliases = {1 + len(ins): 0}
-        ins.append(acc)
-        specs.append(whole(acc))
-    outs = [
-        jax.ShapeDtypeStruct((rows, width if last else 2 * width), F32),
-        jax.ShapeDtypeStruct((blocks, chip, width), BF),
-        jax.ShapeDtypeStruct((carried + blocks, chip, width), BF),
-    ]
+        n = 1 + len(ins)
+        aliases = {n + 1: 1, n + 2: 2} if last else {n: 0, n + 1: 1, n + 2: 2}
+        ins += list(held)
+        specs += [whole(held[0]), pl.BlockSpec(memory_space=pl.ANY), pl.BlockSpec(memory_space=pl.ANY)]
+    slot = pl.BlockSpec((blocks, chip, width), lambda i, idx: (start // blocks, 0, 0))
+    outs = [jax.ShapeDtypeStruct((rows, width if last else 2 * width), F32)]
+    outs += [jax.ShapeDtypeStruct((total, chip, width), BF)] * 2
+    extra = []
     if last:
-        outs += [jax.ShapeDtypeStruct((rows, width), BF)] * 2 + [jax.ShapeDtypeStruct((2, rows), F32)]
+        extra = [jax.ShapeDtypeStruct((rows, width), BF)] * 2 + [jax.ShapeDtypeStruct((2, rows), F32)]
     return pl.pallas_call(
-        functools.partial(use_kernel, blocks, first, last, carried),
+        functools.partial(use_kernel, blocks, first, last),
         grid_spec=pltpu.PrefetchScalarGridSpec(
             num_scalar_prefetch=1,
             grid=(1,),
             in_specs=specs,
-            out_specs=[whole(o) for o in outs],
-        ),
-        out_shape=outs,
+            out_specs=[whole(outs[0]), slot, slot] + [whole(o) for o in extra],
+        ),
+        out_shape=outs + extra,
         input_output_aliases=aliases,
         compiler_params=pltpu.CompilerParams(vmem_limit_bytes=VMEM_LIMIT),
         cost_estimate=pl.CostEstimate(
@@ -122,37 +117,28 @@
     )(index, *ins)
 
 
-def place_kernel(counts, index, *refs):
-    n = sum(counts)
-    k = len(counts)
-    mine, theirs, out = refs[:k], refs[k:-1], refs[-1]
-    where = [(a, j) for a in range(k) for j in range(counts[a])]
-    spots = []
-    for ref in theirs:
-        spots += [(ref, j) for j in range(ref.shape[0])]
-    for i in range(n):
-        a, j = where[i]
-        partner = i if i in (0, n - 1) else i + 1 - 2 * ((i - 1) % 2)
-        ref, r = spots[partner]
-        out[index[i]] = (mine[a][j].astype(F32) + ref[r].astype(F32)).astype(BF)
+def place_kernel(index, mine, theirs, out):
+    out[...] = (mine[...].astype(F32) + theirs[...].astype(F32)).astype(BF)
 
 
 def place(index, mine, theirs):
-    counts = tuple(a.shape[0] for a in mine)
-    n = sum(counts)
-    shape = (n,) + mine[0].shape[1:]
+    total, chip, width = mine.shape
+
+    def spec(which):
+        return pl.BlockSpec((1, chip, width), lambda i, idx: (which(i, idx), 0, 0))
+
     return pl.pallas_call(
-        functools.partial(place_kernel, counts),
+        place_kernel,
         grid_spec=pltpu.PrefetchScalarGridSpec(
             num_scalar_prefetch=1,
-            grid=(1,),
-            in_specs=[pl.BlockSpec(a.shape, lambda i, idx: (0, 0, 0)) for a in (*mine, *theirs)],
-            out_specs=pl.BlockSpec(shape, lambda i, idx: (0, 0, 0)),
-        ),
-        out_shape=jax.ShapeDtypeStruct(shape, BF),
+            grid=(total,),
+            in_specs=[spec(lambda i, idx: i), spec(lambda i, idx: idx[total + i])],
+            out_specs=spec(lambda i, idx: idx[i]),
+        ),
+        out_shape=jax.ShapeDtypeStruct(mine.shape, BF),
         compiler_params=pltpu.CompilerParams(vmem_limit_bytes=VMEM_LIMIT),
         cost_estimate=pl.CostEstimate(flops=1000000, bytes_accessed=5000000, transcendentals=0),
-    )(index, *mine, *theirs)
+    )(index, mine, theirs)
 
 
 def make_local(ny):
@@ -224,10 +210,14 @@
         held_own = dp == core
         turn = jnp.where(core == 0, -1, 1)
         shift_here = jnp.where(dp == 0, shift(0), shift(1))
-        order = [0] + [sign * step for step in range(1, half_y) for sign in (1, -1)] + [half_y]
-        index = jnp.stack(
-            [(y + turn * o + 2 * ny - shift_here) % ny for o in order] + [held_own.astype(jnp.int32), core]
-        ).astype(jnp.int32)
+        order = [0, 1]
+        for step in range(2, half_y):
+            order += [step, 1 - step]
+        order += [1 - half_y, half_y]
+        partner = [order.index(-o) if abs(o) < half_y else order.index(o) for o in order]
+        spots = [(y + turn * o + 2 * ny - shift_here) % ny for o in order]
+        index = jnp.stack(spots + [held_own.astype(jnp.int32), core]).astype(jnp.int32)
+        place_index = jnp.stack(spots + [jnp.int32(p) for p in partner]).astype(jnp.int32)
         on_a = lambda v: lax.ppermute(v, ("y", "core"), ring_a)
         on_b = lambda v: lax.ppermute(v, ("y", "core"), ring_b)
         block = part.reshape(rows, chip)
@@ -235,31 +225,21 @@
         block_b, s_a, s_b = lax.optimization_barrier((block, s_a, s_b))
         b = on_b(block_b)
         args = (w_down[0].reshape(ny, chip, width), w_moved.reshape(ny, chip, width), s_a, s_b)
-        waiting, start, acc, theirs = [block_b, a, b], 0, None, None
-        g_mine, g_moved = [], []
+        waiting, start, held = [block_b, a], 0, None
         for step in range(2, half_y + 1):
-            ready = theirs
-            if step == half_y:
-                a, acc, ready = lax.optimization_barrier((a, acc, ready))
-                g_moved.append(lax.ppermute(ready, "core", swap))
-            elif acc is not None:
-                a, acc = lax.optimization_barrier((a, acc))
+            if held is not None:
+                a, acc = lax.optimization_barrier((a, held[0]))
+                held = (acc, *held[1:])
             a = on_a(a)
-            acc, gm, theirs = use(waiting, index, start, *args, acc)
-            g_mine.append(gm)
-            start += len(waiting)
-            waiting = [a]
+            held = use(waiting, index, start, *args, held)
+            start += 2
+            waiting = [a, b]
             if step < half_y:
-                if ready is None:
-                    b, acc = lax.optimization_barrier((b, acc))
-                else:
-                    b, acc, ready = lax.optimization_barrier((b, acc, ready))
-                    g_moved.append(lax.ppermute(ready, "core", swap))
+                b, acc = lax.optimization_barrier((b, held[0]))
+                held = (acc, *held[1:])
                 b = on_b(b)
-                waiting.append(b)
-        acc, *g_moved = lax.optimization_barrier((acc, *g_moved))
-        acc, gm, theirs, sum_a, sum_b, mix = use(waiting, index, start, *args, acc, last=True, carry=theirs)
-        g_mine.append(gm)
+        held = use([b], index, start, *args, held)
+        acc, mine, theirs, sum_a, sum_b, mix = use([a], index, start + 1, *args, held, last=True)
 
         got_a = lax.ppermute(sum_a, ("core", "dp"), sums_a)
         got_b = lax.ppermute(sum_b, ("core", "dp"), sums_b)
@@ -267,7 +247,7 @@
         share = rows // (ny * 4)
         mix = lax.all_to_all(mix.reshape(members, share), ("dp", "y", "xlo", "core"), 0, 0, tiled=True)
         late = lax.ppermute(theirs, "core", swap)
-        grad_weight = place(index, g_mine, [*g_moved, late]).reshape(ny * chip, width)
+        grad_weight = place(place_index, mine, late).reshape(ny * chip, width)
         grad_hidden = jnp.where(held_own, acc, got_b.astype(F32)) + got_a.astype(F32)
         weighted = weight_rows * grad_hidden
         grad_gate = (weighted * upper * sigma * (1.0 + gate * (1.0 - sigma))).astype(BF)

time: 158 us -> 162 us (1.025)
  starting transfers between devices: 85.4 us -> 72.8 us
  waiting for transfers between devices: 30.1 us -> 40.9 us
  Pallas kernels: 26.7 us -> 32.6 us
    ppermute x2 -> x0, starting transfers between devices: 12.7 us -> none  [local(): g_moved.append(lax.ppermute(ready, 'core', swap))]
    all_to_all x1, waiting for transfers between devices: 7.66 us -> 17.6 us  [local(): lax.all_to_all(outgoing, 'expert', split_axis=0, concat_axis=0, tiled=True)]
    ppermute x4, waiting for transfers between devices: 9.35 us -> 0.01 us  [local(): on_a = lambda v: lax.ppermute(v, ('y', 'core'), ring_a)]
    ppermute x1, waiting for transfers between devices: 0.01 us -> 8.59 us  [local(): s_a = lax.ppermute(scaled, ('core', 'dp'), scaled_a)]
    pallas_call x5 -> x6, Pallas kernels: 26.7 us -> 32.6 us  [the longest x5 25.9 us: use(): pl.pallas_call(functools.partial(use_kernel, blocks, first, last), grid_s...]
    ppermute x4, starting transfers between devices: 14.9 us -> 19.8 us  [local(): on_a = lambda v: lax.ppermute(v, ('y', 'core'), ring_a)]
    ppermute x1, starting transfers between devices: 5.98 us -> 2.39 us  [local(): s_a = lax.ppermute(scaled, ('core', 'dp'), scaled_a)]
    all_to_all x1, starting transfers between devices: 10.9 us -> 7.67 us  [local(): lax.all_to_all(mix.reshape(members, share), ('dp', 'y', 'xlo', 'core'), 0...]
  transfers between devices with their start and end apart: 19 -> 17, of which waited for: 5 -> 8; matrix products, arithmetic and copies ran while one was open for 3% -> 3% of each run, Pallas kernels for 14% -> 17%
where the time goes in v6:
time: 162 us; the launch traced here: 161 us
  starting transfers between devices  72.8 us (45%)
  waiting for transfers between devices  40.9 us (25%)
  Pallas kernels  32.6 us (20%)
  local copies, waits for them, and re-layouts  7.68 us (5%)
  other arithmetic  4.22 us (3%)
    pallas_call x5, Pallas kernels, use(): pl.pallas_call(functools.partial(use_kernel, blocks, first, last), grid_s...  25.9 us
    ppermute x4, starting transfers between devices, local(): on_a = lambda v: lax.ppermute(v, ('y', 'core'), ring_a)  19.8 us
    all_to_all x1, waiting for transfers between devices, local(): lax.all_to_all(outgoing, 'expert', split_axis=0, concat_axis=0, tiled=True)  17.6 us
    all_to_all x1, starting transfers between devices, local(): lax.all_to_all(outgoing, 'expert', split_axis=0, concat_axis=0, tiled=True)  10 us
    ppermute x3, waiting for transfers between devices, local(): on_b = lambda v: lax.ppermute(v, ('y', 'core'), ring_b)  8.96 us
    ppermute x1, waiting for transfers between devices, local(): s_a = lax.ppermute(scaled, ('core', 'dp'), scaled_a)  8.59 us
    ppermute x1, starting transfers between devices, local(): lax.ppermute(jnp.concatenate([cotangent[0], ids], axis=1), every, token_m...  8.33 us
    all_to_all x1, starting transfers between devices, local(): lax.all_to_all(mix.reshape(members, share), ('dp', 'y', 'xlo', 'core'), 0...  7.67 us
  transfers between devices with their start and end apart: 17, of which 8 were waited for; matrix products, arithmetic and copies ran while one was open for 3% of the time, Pallas kernels for 17%

profile of v6, /device:TPU:1, one launch (start us, length us, event | category | flops | bytes accessed | tf_op | source)
XLA Modules:
  0.0 160.7 jit_solution(8518521297299404855)
XLA Ops:
  0.6 1.0 copy.28
  1.6 0.0 copy-start
  1.6 0.0 copy-start.11
  1.7 0.8 convert_bitcast_fusion
  2.5 8.3 %collective-permute-start = (bf16[192,194]{0,1:T(8,128)(2,1)S(1)}, bf16[192,194]{0,1:T(8,128)(2,1)S(1)}, u32[]{:S(2)}, u32[]{:S(2)}) collective-permute-start(bf16[192,194]{0,1:T(8,128)(2,1)S(1)} %pad_maximum_fusion), channel_id=1, source_target_pairs={{0,48},{1,50},{2,52},{3,54},{4,56},{5,58},{6,60},{7,62},{8,0},{9,2... | collective-permute-start | bytes 223496 | tf_op jit(solution)/shard_map/ppermute | solution.py:191
  10.8 4.0 %collective-permute-start.1 = (bf16[192,192]{0,1:T(8,128)(2,1)S(1)}, bf16[192,192]{0,1:T(8,128)(2,1)S(1)}, u32[]{:S(2)}, u32[]{:S(2)}) collective-permute-start(bf16[192,192]{0,1:T(8,128)(2,1)S(1)} %bitcast.60), channel_id=1, source_target_pairs={{0,52},{1,54},{2,48},{3,50},{4,60},{5,62},{6,56},{7,58},{8,4},{9,6... | collective-permute-start | bytes 221192 | tf_op jit(solution)/shard_map/ppermute | solution.py:192
  14.9 0.1 fusion.16
  15.1 3.5 %collective-permute-done.1 = bf16[192,192]{0,1:T(8,128)(2,1)S(1)} collective-permute-done((bf16[192,192]{0,1:T(8,128)(2,1)S(1)}, bf16[192,192]{0,1:T(8,128)(2,1)S(1)}, u32[]{:S(2)}, u32[]{:S(2)}) %collective-permute-start.1) | collective-permute-done | bytes 73760 | tf_op jit(solution)/shard_map/ppermute | solution.py:192
  18.6 1.2 convolution_convert_fusion
  19.8 10.0 %all-to-all-start = ((bf16[8,96,384]{2,1,0:T(8,128)(2,1)}), bf16[8,96,384]{2,1,0:T(8,128)(2,1)}, u32[]{:S(2)}, u32[]{:S(2)}) async-start(bf16[8,96,384]{2,1,0:T(8,128)(2,1)} %bitcast.14), calls=%async_computation | async-start | bytes 1179648 | tf_op jit(solution)/shard_map/all_to_all | solution.py:198
  29.9 1.9 %collective-permute-start.7 = (bf16[3072,256]{1,0:T(8,128)(2,1)S(1)}, bf16[3072,256]{1,0:T(8,128)(2,1)S(1)}, u32[]{:S(2)}, u32[]{:S(2)}) collective-permute-start(bf16[3072,256]{1,0:T(8,128)(2,1)S(1)} %bitcast.49), channel_id=1, source_target_pairs={{0,2},{2,0},{1,3},{3,1},{4,6},{6,4},{5,7},{7,5},{8,10},{10,8},{9,1... | collective-permute-start | bytes 4718600 | tf_op jit(solution)/shard_map/ppermute | solution.py:208
  31.8 17.6 %all-to-all-done = bf16[8,96,384]{2,1,0:T(8,128)(2,1)} async-done(((bf16[8,96,384]{2,1,0:T(8,128)(2,1)}), bf16[8,96,384]{2,1,0:T(8,128)(2,1)}, u32[]{:S(2)}, u32[]{:S(2)}) %all-to-all-start) | async-done | bytes 589856 | tf_op jit(solution)/shard_map/all_to_all | solution.py:198
  49.4 2.6 %collective-permute-start.2 = (bf16[768,384]{1,0:T(8,128)(2,1)}, bf16[768,384]{1,0:T(8,128)(2,1)}, u32[]{:S(2)}, u32[]{:S(2)}) collective-permute-start(bf16[768,384]{1,0:T(8,128)(2,1)} %bitcast.15.refs_0_), channel_id=1, source_target_pairs={{0,8},{2,58},{8,16},{10,2},{16,24},{18,10},{24,32},{26,18},{32,40}... | collective-permute-start | bytes 1769480 | tf_op jit(solution)/shard_map/ppermute | solution.py:221
  52.0 1.3 fusion.1
  53.3 2.4 %collective-permute-start.4 = (bf16[768,256]{1,0:T(8,128)(2,1)S(1)}, bf16[768,256]{1,0:T(8,128)(2,1)S(1)}, u32[]{:S(2)}, u32[]{:S(2)}) collective-permute-start(bf16[768,256]{1,0:T(8,128)(2,1)S(1)} %fusion.1), channel_id=1, source_target_pairs={{0,0},{1,2},{2,1},{3,3},{4,4},{5,6},{6,5},{7,7},{8,8},{9,10},{10,9... | collective-permute-start | bytes 1179656 | tf_op jit(solution)/shard_map/ppermute | solution.py:206
  55.7 1.9 %collective-permute-start.5 = (bf16[768,256]{1,0:T(8,128)(2,1)S(1)}, bf16[768,256]{1,0:T(8,128)(2,1)}, u32[]{:S(2)}, u32[]{:S(2)}) collective-permute-start(bf16[768,256]{1,0:T(8,128)(2,1)S(1)} %fusion.1), channel_id=1, source_target_pairs={{0,1},{1,3},{2,0},{3,2},{4,5},{5,7},{6,4},{7,6},{8,9},{9,11},{10,8... | collective-permute-start | bytes 1179656 | tf_op jit(solution)/shard_map/ppermute | solution.py:207
  57.6 8.6 %collective-permute-done.4.refs_6_.refs_3_ = bf16[768,256]{1,0:T(8,128)(2,1)S(1)} collective-permute-done((bf16[768,256]{1,0:T(8,128)(2,1)S(1)}, bf16[768,256]{1,0:T(8,128)(2,1)S(1)}, u32[]{:S(2)}, u32[]{:S(2)}) %collective-permute-start.4) | collective-permute-done | bytes 393248 | tf_op jit(solution)/shard_map/ppermute | solution.py:206
  66.2 2.0 %collective-permute-done.5.refs_7_.refs_4_ = bf16[768,256]{1,0:T(8,128)(2,1)} collective-permute-done((bf16[768,256]{1,0:T(8,128)(2,1)S(1)}, bf16[768,256]{1,0:T(8,128)(2,1)}, u32[]{:S(2)}, u32[]{:S(2)}) %collective-permute-start.5) | collective-permute-done | bytes 393248 | tf_op jit(solution)/shard_map/ppermute | solution.py:207
  68.2 2.7 %collective-permute-start.6 = (bf16[768,384]{1,0:T(8,128)(2,1)}, bf16[768,384]{1,0:T(8,128)(2,1)}, u32[]{:S(2)}, u32[]{:S(2)}) collective-permute-start(bf16[768,384]{1,0:T(8,128)(2,1)} %bitcast.15.refs_0_), channel_id=1, source_target_pairs={{0,56},{2,10},{8,0},{10,18},{16,8},{18,26},{24,16},{26,34},{32,24}... | collective-permute-start | bytes 1769480 | tf_op jit(solution)/shard_map/ppermute | solution.py:222
  70.9 4.9 %collective-permute-start.3 = (bf16[768,384]{1,0:T(8,128)(2,1)}, bf16[768,384]{1,0:T(8,128)(2,1)}, u32[]{:S(2)}, u32[]{:S(2)}) collective-permute-start(bf16[768,384]{1,0:T(8,128)(2,1)} %collective-permute-done.2.refs_1_), channel_id=1, source_target_pairs={{0,8},{2,58},{8,16},{10,2},{16,24},{18,10},{24,32},{26,18},{32,40}... | collective-permute-start | bytes 1769480 | tf_op jit(solution)/shard_map/ppermute | solution.py:221
  76.0 0.7 stack.58.index
  76.6 0.0 collective-permute-done.7
  76.6 1.1 copy-done.1
  77.8 5.1 %shard_map.93 = (f32[768,512]{1,0:T(8,128)}, bf16[8,384,256]{2,1,0:T(8,128)(2,1)}, bf16[8,384,256]{2,1,0:T(8,128)(2,1)}) custom-call(s32[10]{0:T(128)} %stack.58.index, bf16[768,384]{1,0:T(8,128)(2,1)} %bitcast.15.refs_0_, bf16[768,384]{1,0:T(8,128)(2,1)} %collective-permute-done.2.refs_1_, bf16[8,384,256]{2,1,0:T(8,128)(2,1)} %bitcast.41, ...), custom_call_target="tpu_custom_call" | custom-call | flops 1207959552 | bytes 8000000 | tf_op jit(solution)/shard_map/pallas_call | solution.py:103
  82.8 2.0 %collective-permute-done.6.refs_1_ = bf16[768,384]{1,0:T(8,128)(2,1)} collective-permute-done((bf16[768,384]{1,0:T(8,128)(2,1)}, bf16[768,384]{1,0:T(8,128)(2,1)}, u32[]{:S(2)}, u32[]{:S(2)}) %collective-permute-start.6) | collective-permute-done | bytes 589856 | tf_op jit(solution)/shard_map/ppermute | solution.py:222
  84.9 1.9 %collective-permute-start.9 = (bf16[768,384]{1,0:T(8,128)(2,1)}, bf16[768,384]{1,0:T(8,128)(2,1)S(1)}, u32[]{:S(2)}, u32[]{:S(2)}) collective-permute-start(bf16[768,384]{1,0:T(8,128)(2,1)} %collective-permute-done.6.refs_1_), channel_id=1, source_target_pairs={{0,56},{2,10},{8,0},{10,18},{16,8},{18,26},{24,16},{26,34},{32,24}... | collective-permute-start | bytes 1769480 | tf_op jit(solution)/shard_map/ppermute | solution.py:222
  86.8 4.9 %collective-permute-start.8 = (bf16[768,384]{1,0:T(8,128)(2,1)}, bf16[768,384]{1,0:T(8,128)(2,1)S(1)}, u32[]{:S(2)}, u32[]{:S(2)}) collective-permute-start(bf16[768,384]{1,0:T(8,128)(2,1)} %collective-permute-done.3.refs_0_), channel_id=1, source_target_pairs={{0,8},{2,58},{8,16},{10,2},{16,24},{18,10},{24,32},{26,18},{32,40}... | collective-permute-start | bytes 1769480 | tf_op jit(solution)/shard_map/ppermute | solution.py:221
  91.7 5.7 %shard_map.94 = (f32[768,512]{1,0:T(8,128)}, bf16[8,384,256]{2,1,0:T(8,128)(2,1)}, bf16[8,384,256]{2,1,0:T(8,128)(2,1)}) custom-call(s32[10]{0:T(128)} %stack.58.index, bf16[768,384]{1,0:T(8,128)(2,1)} %collective-permute-done.3.refs_0_, ...), custom_call_target="tpu_custom_call", output_to_operand_aliasing={{0}: (9, {}), {1}: (10, {}), {2}: (11, {})} | custom-call | flops 1207959552 | bytes 8000000 | tf_op jit(solution)/shard_map/pallas_call | solution.py:103
  97.4 2.7 %collective-permute-done.9.refs_1_ = bf16[768,384]{1,0:T(8,128)(2,1)S(1)} collective-permute-done((bf16[768,384]{1,0:T(8,128)(2,1)}, bf16[768,384]{1,0:T(8,128)(2,1)S(1)}, u32[]{:S(2)}, u32[]{:S(2)}) %collective-permute-start.9) | collective-permute-done | bytes 589856 | tf_op jit(solution)/shard_map/ppermute | solution.py:222
  100.1 1.9 %collective-permute-start.11 = (bf16[768,384]{1,0:T(8,128)(2,1)S(1)}, bf16[768,384]{1,0:T(8,128)(2,1)S(1)}, u32[]{:S(2)}, u32[]{:S(2)}) collective-permute-start(bf16[768,384]{1,0:T(8,128)(2,1)S(1)} %collective-permute-done.9.refs_1_), channel_id=1, source_target_pairs={{0,56},{2,10},{8,0},{10,18},{16,8},{18,26},{24,16},{26,34},{32,24}... | collective-permute-start | bytes 1769480 | tf_op jit(solution)/shard_map/ppermute | solution.py:222
  102.0 7.4 %collective-permute-start.10 = (bf16[768,384]{1,0:T(8,128)(2,1)S(1)}, bf16[768,384]{1,0:T(8,128)(2,1)S(1)}, u32[]{:S(2)}, u32[]{:S(2)}) collective-permute-start(bf16[768,384]{1,0:T(8,128)(2,1)S(1)} %collective-permute-done.8.refs_0_), channel_id=1, source_target_pairs={{0,8},{2,58},{8,16},{10,2},{16,24},{18,10},{24,32},{26,18},{32,40}... | collective-permute-start | bytes 1769480 | tf_op jit(solution)/shard_map/ppermute | solution.py:221
  109.4 5.7 %shard_map.95 = (f32[768,512]{1,0:T(8,128)}, bf16[8,384,256]{2,1,0:T(8,128)(2,1)}, bf16[8,384,256]{2,1,0:T(8,128)(2,1)}) custom-call(s32[10]{0:T(128)} %stack.58.index, bf16[768,384]{1,0:T(8,128)(2,1)} %copy-done.7, bf16[768,384]{1,0:T(8,128)(2,1)} %copy-done.8, ...), custom_call_target="tpu_custom_call", output_to_operand_aliasing={{0}: (9, {}), {1}: (10, {}), {2}: (11, {})} | custom-call | flops 1207959552 | bytes 8000000 | tf_op jit(solution)/shard_map/pallas_call | solution.py:103
  115.1 4.2 %collective-permute-done.11.refs_0_ = bf16[768,384]{1,0:T(8,128)(2,1)S(1)} collective-permute-done((bf16[768,384]{1,0:T(8,128)(2,1)S(1)}, bf16[768,384]{1,0:T(8,128)(2,1)S(1)}, u32[]{:S(2)}, u32[]{:S(2)}) %collective-permute-start.11) | collective-permute-done | bytes 589856 | tf_op jit(solution)/shard_map/ppermute | solution.py:222
  119.4 0.8 copy-done.10
  120.2 4.6 %shard_map.96 = (f32[768,512]{1,0:T(8,128)}, bf16[8,384,256]{2,1,0:T(8,128)(2,1)}, bf16[8,384,256]{2,1,0:T(8,128)(2,1)}) custom-call(s32[10]{0:T(128)} %stack.58.index, bf16[768,384]{1,0:T(8,128)(2,1)} %copy-done.10, bf16[8,384,256]{2,1,0:T(8,128)(2,1)} %bitcast.47, ...), custom_call_target="tpu_custom_call", output_to_operand_aliasing={{0}: (6, {}), {1}: (7, {}), {2}: (8, {})} | custom-call | flops 603979776 | bytes 4000000 | tf_op jit(solution)/shard_map/pallas_call | solution.py:103
  124.8 0.8 copy-done.9
  125.6 5.0 %shard_map.97 = (f32[768,256]{1,0:T(8,128)}, bf16[8,384,256]{2,1,0:T(8,128)(2,1)}, bf16[8,384,256]{2,1,0:T(8,128)(2,1)}, bf16[768,256]{1,0:T(8,128)(2,1)}, bf16[768,256]{1,0:T(8,128)(2,1)}, /*index=5*/f32[2,768]{1,0:T(2,128)}) custom-call(s32[10]{0:T(128)} %stack.58.index, bf16[768,384]{1,0:T(8,128)(2,1)} %copy-done.9, ...), custom_call_target="tpu_custom_call", output_to_operand_aliasing={{1}: (7, {}), {2}: (8, {})} | custom-call | flops 603979776 | bytes 4000000 | tf_op jit(solution)/shard_map/pallas_call | solution.py:103
  130.6 1.9 %collective-permute-start.14 = (bf16[8,384,256]{2,1,0:T(8,128)(2,1)}, bf16[8,384,256]{2,1,0:T(8,128)(2,1)S(1)}, u32[]{:S(2)}, u32[]{:S(2)}) collective-permute-start(bf16[8,384,256]{2,1,0:T(8,128)(2,1)} %get-tuple-element.65), channel_id=1, source_target_pairs={{0,2},{2,0},{1,3},{3,1},{4,6},{6,4},{5,7},{7,5},{8,10},{10,8},{9,1... | collective-permute-start | bytes 4718600 | tf_op jit(solution)/shard_map/ppermute | solution.py:249
  132.5 6.4 %collective-permute-start.12 = (bf16[768,256]{1,0:T(8,128)(2,1)}, bf16[768,256]{1,0:T(8,128)(2,1)S(1)}, u32[]{:S(2)}, u32[]{:S(2)}) collective-permute-start(bf16[768,256]{1,0:T(8,128)(2,1)} %get-tuple-element.62), channel_id=1, source_target_pairs={{2,1},{1,2},{6,5},{5,6},{10,9},{9,10},{14,13},{13,14},{18,17},{17,... | collective-permute-start | bytes 1179656 | tf_op jit(solution)/shard_map/ppermute | solution.py:245
  138.9 1.9 %collective-permute-start.13 = (bf16[768,256]{1,0:T(8,128)(2,1)}, bf16[768,256]{1,0:T(8,128)(2,1)S(1)}, u32[]{:S(2)}, u32[]{:S(2)}) collective-permute-start(bf16[768,256]{1,0:T(8,128)(2,1)} %get-tuple-element.63), channel_id=1, source_target_pairs={{2,3},{1,0},{0,2},{3,1},{6,7},{5,4},{4,6},{7,5},{10,11},{9,8},{8,1... | collective-permute-start | bytes 1179656 | tf_op jit(solution)/shard_map/ppermute | solution.py:244
  140.9 0.6 stack.59.index
  141.5 1.4 all_to_all.12
  142.9 7.7 %all-to-all-start.1 = ((f32[64,1,24]{2,1,0:T(1,128)}), f32[64,1,24]{2,1,0:T(1,128)S(1)}, u32[]{:S(2)}, u32[]{:S(2)}) async-start(f32[64,1,24]{2,1,0:T(1,128)} %bitcast.22), calls=%async_computation.1 | async-start | bytes 65536 | tf_op jit(solution)/shard_map/all_to_all | solution.py:248
  150.6 1.4 multiply_convert_fusion
  152.0 1.2 copy-done.3
  153.2 6.6 %shard_map.98 = bf16[8,384,256]{2,1,0:T(8,128)(2,1)} custom-call(s32[16]{0:T(128)} %stack.59.index, bf16[8,384,256]{2,1,0:T(8,128)(2,1)} %get-tuple-element.64.mine, bf16[8,384,256]{2,1,0:T(8,128)(2,1)} %copy-done.3), custom_call_target="tpu_custom_call" | custom-call | flops 1000000 | bytes 5000000 | tf_op jit(solution)/shard_map/pallas_call | solution.py:130
  159.8 0.2 all-to-all-done.1
  160.1 0.6 bitcast_divide_fusion
  (35 shorter events, 0.2 us)
Async XLA Ops:
  1.6 28.2 %copy-start = (bf16[1,3072,256]{2,1,0:T(8,128)(2,1)S(1)}, bf16[1,3072,256]{2,1,0:T(8,128)(2,1)}, u32[]{:S(2)}) copy-start(bf16[1,3072,256]{2,1,0:T(8,128)(2,1)} %param.11) | copy-start | bytes 4718596
  1.6 30.2 %copy-start.11 = (f32[1,1,768]{2,1,0:T(1,128)S(1)}, f32[1,1,768]{2,1,0:T(1,128)}, u32[]{:S(2)}) copy-start(f32[1,1,768]{2,1,0:T(1,128)} %param.8) | copy-start | bytes 9220
  2.5 49.6 %copy-start.4 = (bf16[1,1,768,256]{3,2,1,0:T(8,128)(2,1)S(1)}, bf16[1,1,768,256]{3,2,1,0:T(8,128)(2,1)}, u32[]{:S(2)}) copy-start(bf16[1,1,768,256]{3,2,1,0:T(8,128)(2,1)} %param.9) | copy-start | bytes 1179652
  2.5 12.4 %collective-permute-start = (bf16[192,194]{0,1:T(8,128)(2,1)S(1)}, bf16[192,194]{0,1:T(8,128)(2,1)S(1)}, u32[]{:S(2)}, u32[]{:S(2)}) collective-permute-start(bf16[192,194]{0,1:T(8,128)(2,1)S(1)} %pad_maximum_fusion), channel_id=1, source_target_pairs={{0,48},{1,50},{2,52},{3,54},{4,56},{5,58},{6,60},{7,62},{8,0},{9,2... | collective-permute-start | bytes 223496 | tf_op jit(solution)/shard_map/ppermute | solution.py:191
  10.8 7.8 %collective-permute-start.1 = (bf16[192,192]{0,1:T(8,128)(2,1)S(1)}, bf16[192,192]{0,1:T(8,128)(2,1)S(1)}, u32[]{:S(2)}, u32[]{:S(2)}) collective-permute-start(bf16[192,192]{0,1:T(8,128)(2,1)S(1)} %bitcast.60), channel_id=1, source_target_pairs={{0,52},{1,54},{2,48},{3,50},{4,60},{5,62},{6,56},{7,58},{8,4},{9,6... | collective-permute-start | bytes 221192 | tf_op jit(solution)/shard_map/ppermute | solution.py:192
  19.8 29.6 %all-to-all-start = ((bf16[8,96,384]{2,1,0:T(8,128)(2,1)}), bf16[8,96,384]{2,1,0:T(8,128)(2,1)}, u32[]{:S(2)}, u32[]{:S(2)}) async-start(bf16[8,96,384]{2,1,0:T(8,128)(2,1)} %bitcast.14), calls=%async_computation | async-start | bytes 1179648 | tf_op jit(solution)/shard_map/all_to_all | solution.py:198
  29.9 46.8 %collective-permute-start.7 = (bf16[3072,256]{1,0:T(8,128)(2,1)S(1)}, bf16[3072,256]{1,0:T(8,128)(2,1)S(1)}, u32[]{:S(2)}, u32[]{:S(2)}) collective-permute-start(bf16[3072,256]{1,0:T(8,128)(2,1)S(1)} %bitcast.49), channel_id=1, source_target_pairs={{0,2},{2,0},{1,3},{3,1},{4,6},{6,4},{5,7},{7,5},{8,10},{10,8},{9,1... | collective-permute-start | bytes 4718600 | tf_op jit(solution)/shard_map/ppermute | solution.py:208
  49.4 21.5 %collective-permute-start.2 = (bf16[768,384]{1,0:T(8,128)(2,1)}, bf16[768,384]{1,0:T(8,128)(2,1)}, u32[]{:S(2)}, u32[]{:S(2)}) collective-permute-start(bf16[768,384]{1,0:T(8,128)(2,1)} %bitcast.15.refs_0_), channel_id=1, source_target_pairs={{0,8},{2,58},{8,16},{10,2},{16,24},{18,10},{24,32},{26,18},{32,40}... | collective-permute-start | bytes 1769480 | tf_op jit(solution)/shard_map/ppermute | solution.py:221
  53.3 12.9 %collective-permute-start.4 = (bf16[768,256]{1,0:T(8,128)(2,1)S(1)}, bf16[768,256]{1,0:T(8,128)(2,1)S(1)}, u32[]{:S(2)}, u32[]{:S(2)}) collective-permute-start(bf16[768,256]{1,0:T(8,128)(2,1)S(1)} %fusion.1), channel_id=1, source_target_pairs={{0,0},{1,2},{2,1},{3,3},{4,4},{5,6},{6,5},{7,7},{8,8},{9,10},{10,9... | collective-permute-start | bytes 1179656 | tf_op jit(solution)/shard_map/ppermute | solution.py:206
  55.7 12.5 %collective-permute-start.5 = (bf16[768,256]{1,0:T(8,128)(2,1)S(1)}, bf16[768,256]{1,0:T(8,128)(2,1)}, u32[]{:S(2)}, u32[]{:S(2)}) collective-permute-start(bf16[768,256]{1,0:T(8,128)(2,1)S(1)} %fusion.1), channel_id=1, source_target_pairs={{0,1},{1,3},{2,0},{3,2},{4,5},{5,7},{6,4},{7,6},{8,9},{9,11},{10,8... | collective-permute-start | bytes 1179656 | tf_op jit(solution)/shard_map/ppermute | solution.py:207
  66.2 10.4 %copy-start.2 = (bf16[768,256]{1,0:T(8,128)(2,1)}, bf16[768,256]{1,0:T(8,128)(2,1)S(1)}, u32[]{:S(2)}) copy-start(bf16[768,256]{1,0:T(8,128)(2,1)S(1)} %collective-permute-done.4.refs_6_.refs_3_) | copy-start | bytes 1179652
  68.2 16.6 %collective-permute-start.6 = (bf16[768,384]{1,0:T(8,128)(2,1)}, bf16[768,384]{1,0:T(8,128)(2,1)}, u32[]{:S(2)}, u32[]{:S(2)}) collective-permute-start(bf16[768,384]{1,0:T(8,128)(2,1)} %bitcast.15.refs_0_), channel_id=1, source_target_pairs={{0,56},{2,10},{8,0},{10,18},{16,8},{18,26},{24,16},{26,34},{32,24}... | collective-permute-start | bytes 1769480 | tf_op jit(solution)/shard_map/ppermute | solution.py:222
  70.9 15.9 %collective-permute-start.3 = (bf16[768,384]{1,0:T(8,128)(2,1)}, bf16[768,384]{1,0:T(8,128)(2,1)}, u32[]{:S(2)}, u32[]{:S(2)}) collective-permute-start(bf16[768,384]{1,0:T(8,128)(2,1)} %collective-permute-done.2.refs_1_), channel_id=1, source_target_pairs={{0,8},{2,58},{8,16},{10,2},{16,24},{18,10},{24,32},{26,18},{32,40}... | collective-permute-start | bytes 1769480 | tf_op jit(solution)/shard_map/ppermute | solution.py:221
  76.6 1.1 copy-start.1
  84.9 15.2 %collective-permute-start.9 = (bf16[768,384]{1,0:T(8,128)(2,1)}, bf16[768,384]{1,0:T(8,128)(2,1)S(1)}, u32[]{:S(2)}, u32[]{:S(2)}) collective-permute-start(bf16[768,384]{1,0:T(8,128)(2,1)} %collective-permute-done.6.refs_1_), channel_id=1, source_target_pairs={{0,56},{2,10},{8,0},{10,18},{16,8},{18,26},{24,16},{26,34},{32,24}... | collective-permute-start | bytes 1769480 | tf_op jit(solution)/shard_map/ppermute | solution.py:222
  86.8 15.2 %collective-permute-start.8 = (bf16[768,384]{1,0:T(8,128)(2,1)}, bf16[768,384]{1,0:T(8,128)(2,1)S(1)}, u32[]{:S(2)}, u32[]{:S(2)}) collective-permute-start(bf16[768,384]{1,0:T(8,128)(2,1)} %collective-permute-done.3.refs_0_), channel_id=1, source_target_pairs={{0,8},{2,58},{8,16},{10,2},{16,24},{18,10},{24,32},{26,18},{32,40}... | collective-permute-start | bytes 1769480 | tf_op jit(solution)/shard_map/ppermute | solution.py:221
  100.1 9.4 %copy-start.8 = (bf16[768,384]{1,0:T(8,128)(2,1)}, bf16[768,384]{1,0:T(8,128)(2,1)S(1)}, u32[]{:S(2)}) copy-start(bf16[768,384]{1,0:T(8,128)(2,1)S(1)} %collective-permute-done.9.refs_1_) | copy-start | bytes 1769476
  100.1 19.3 %collective-permute-start.11 = (bf16[768,384]{1,0:T(8,128)(2,1)S(1)}, bf16[768,384]{1,0:T(8,128)(2,1)S(1)}, u32[]{:S(2)}, u32[]{:S(2)}) collective-permute-start(bf16[768,384]{1,0:T(8,128)(2,1)S(1)} %collective-permute-done.9.refs_1_), channel_id=1, source_target_pairs={{0,56},{2,10},{8,0},{10,18},{16,8},{18,26},{24,16},{26,34},{32,24}... | collective-permute-start | bytes 1769480 | tf_op jit(solution)/shard_map/ppermute | solution.py:222
  102.0 7.4 %copy-start.7 = (bf16[768,384]{1,0:T(8,128)(2,1)}, bf16[768,384]{1,0:T(8,128)(2,1)S(1)}, u32[]{:S(2)}) copy-start(bf16[768,384]{1,0:T(8,128)(2,1)S(1)} %collective-permute-done.8.refs_0_) | copy-start | bytes 1769476
  102.0 22.7 %collective-permute-start.10 = (bf16[768,384]{1,0:T(8,128)(2,1)S(1)}, bf16[768,384]{1,0:T(8,128)(2,1)S(1)}, u32[]{:S(2)}, u32[]{:S(2)}) collective-permute-start(bf16[768,384]{1,0:T(8,128)(2,1)S(1)} %collective-permute-done.8.refs_0_), channel_id=1, source_target_pairs={{0,8},{2,58},{8,16},{10,2},{16,24},{18,10},{24,32},{26,18},{32,40}... | collective-permute-start | bytes 1769480 | tf_op jit(solution)/shard_map/ppermute | solution.py:221
  119.4 0.8 copy-start.10
  124.8 0.8 copy-start.9
  125.6 25.0 %copy-start.5 = (bf16[1,1,768,256]{3,2,1,0:T(8,128)(2,1)S(1)}, bf16[1,1,768,256]{3,2,1,0:T(8,128)(2,1)}, u32[]{:S(2)}) copy-start(bf16[1,1,768,256]{3,2,1,0:T(8,128)(2,1)} %param.9) | copy-start | bytes 1179652
  125.6 25.0 %copy-start.6 = (bf16[1,1,768,256]{3,2,1,0:T(8,128)(2,1)S(1)}, bf16[1,1,768,256]{3,2,1,0:T(8,128)(2,1)}, u32[]{:S(2)}) copy-start(bf16[1,1,768,256]{3,2,1,0:T(8,128)(2,1)} %param.10) | copy-start | bytes 1179652
  130.6 21.4 %collective-permute-start.14 = (bf16[8,384,256]{2,1,0:T(8,128)(2,1)}, bf16[8,384,256]{2,1,0:T(8,128)(2,1)S(1)}, u32[]{:S(2)}, u32[]{:S(2)}) collective-permute-start(bf16[8,384,256]{2,1,0:T(8,128)(2,1)} %get-tuple-element.65), channel_id=1, source_target_pairs={{0,2},{2,0},{1,3},{3,1},{4,6},{6,4},{5,7},{7,5},{8,10},{10,8},{9,1... | collective-permute-start | bytes 4718600 | tf_op jit(solution)/shard_map/ppermute | solution.py:249
  132.5 18.0 %collective-permute-start.12 = (bf16[768,256]{1,0:T(8,128)(2,1)}, bf16[768,256]{1,0:T(8,128)(2,1)S(1)}, u32[]{:S(2)}, u32[]{:S(2)}) collective-permute-start(bf16[768,256]{1,0:T(8,128)(2,1)} %get-tuple-element.62), channel_id=1, source_target_pairs={{2,1},{1,2},{6,5},{5,6},{10,9},{9,10},{14,13},{13,14},{18,17},{17,... | collective-permute-start | bytes 1179656 | tf_op jit(solution)/shard_map/ppermute | solution.py:245
  138.9 11.6 %collective-permute-start.13 = (bf16[768,256]{1,0:T(8,128)(2,1)}, bf16[768,256]{1,0:T(8,128)(2,1)S(1)}, u32[]{:S(2)}, u32[]{:S(2)}) collective-permute-start(bf16[768,256]{1,0:T(8,128)(2,1)} %get-tuple-element.63), channel_id=1, source_target_pairs={{2,3},{1,0},{0,2},{3,1},{6,7},{5,4},{4,6},{7,5},{10,11},{9,8},{8,1... | collective-permute-start | bytes 1179656 | tf_op jit(solution)/shard_map/ppermute | solution.py:244
  142.9 17.2 %all-to-all-start.1 = ((f32[64,1,24]{2,1,0:T(1,128)}), f32[64,1,24]{2,1,0:T(1,128)S(1)}, u32[]{:S(2)}, u32[]{:S(2)}) async-start(f32[64,1,24]{2,1,0:T(1,128)} %bitcast.22), calls=%async_computation.1 | async-start | bytes 65536 | tf_op jit(solution)/shard_map/all_to_all | solution.py:248
  152.0 1.2 copy-start.3

commit v7 on v6

--- a/solution.py
+++ b/solution.py
@@ -117,26 +117,25 @@
     )(index, *ins)
 
 
-def place_kernel(index, mine, theirs, out):
-    out[...] = (mine[...].astype(F32) + theirs[...].astype(F32)).astype(BF)
-
-
-def place(index, mine, theirs):
-    total, chip, width = mine.shape
-
-    def spec(which):
-        return pl.BlockSpec((1, chip, width), lambda i, idx: (which(i, idx), 0, 0))
+def place_kernel(partner, index, mine, theirs, out):
+    for i, p in enumerate(partner):
+        out[index[i]] = (mine[i].astype(F32) + theirs[p].astype(F32)).astype(BF)
+
+
+def place(index, partner, mine, theirs):
+    def whole(a):
+        return pl.BlockSpec(a.shape, lambda i, idx: (0, 0, 0))
 
     return pl.pallas_call(
-        place_kernel,
+        functools.partial(place_kernel, tuple(partner)),
         grid_spec=pltpu.PrefetchScalarGridSpec(
             num_scalar_prefetch=1,
-            grid=(total,),
-            in_specs=[spec(lambda i, idx: i), spec(lambda i, idx: idx[total + i])],
-            out_specs=spec(lambda i, idx: idx[i]),
+            grid=(1,),
+            in_specs=[whole(mine), whole(theirs)],
+            out_specs=whole(mine),
         ),
         out_shape=jax.ShapeDtypeStruct(mine.shape, BF),
-        compiler_params=pltpu.CompilerParams(vmem_limit_bytes=VMEM_LIMIT),
+        compiler_params=pltpu.CompilerParams(vmem_limit_bytes=16 * 1024 * 1024),
         cost_estimate=pl.CostEstimate(flops=1000000, bytes_accessed=5000000, transcendentals=0),
     )(index, mine, theirs)
 
@@ -217,22 +216,23 @@
         partner = [order.index(-o) if abs(o) < half_y else order.index(o) for o in order]
         spots = [(y + turn * o + 2 * ny - shift_here) % ny for o in order]
         index = jnp.stack(spots + [held_own.astype(jnp.int32), core]).astype(jnp.int32)
-        place_index = jnp.stack(spots + [jnp.int32(p) for p in partner]).astype(jnp.int32)
         on_a = lambda v: lax.ppermute(v, ("y", "core"), ring_a)
         on_b = lambda v: lax.ppermute(v, ("y", "core"), ring_b)
         block = part.reshape(rows, chip)
+        block, s_a, s_b = lax.optimization_barrier((block, s_a, s_b))
         a = on_a(block)
-        block_b, s_a, s_b = lax.optimization_barrier((block, s_a, s_b))
+        args = (w_down[0].reshape(ny, chip, width), w_moved.reshape(ny, chip, width), s_a, s_b)
+        held = use([block], index, 0, *args, None)
+        block_b, acc = lax.optimization_barrier((block, held[0]))
+        held = (acc, *held[1:])
         b = on_b(block_b)
-        args = (w_down[0].reshape(ny, chip, width), w_moved.reshape(ny, chip, width), s_a, s_b)
-        waiting, start, held = [block_b, a], 0, None
+        waiting, start = [a], 1
         for step in range(2, half_y + 1):
-            if held is not None:
-                a, acc = lax.optimization_barrier((a, held[0]))
-                held = (acc, *held[1:])
+            a, acc = lax.optimization_barrier((a, held[0]))
+            held = (acc, *held[1:])
             a = on_a(a)
             held = use(waiting, index, start, *args, held)
-            start += 2
+            start += len(waiting)
             waiting = [a, b]
             if step < half_y:
                 b, acc = lax.optimization_barrier((b, held[0]))
@@ -247,7 +247,7 @@
         share = rows // (ny * 4)
         mix = lax.all_to_all(mix.reshape(members, share), ("dp", "y", "xlo", "core"), 0, 0, tiled=True)
         late = lax.ppermute(theirs, "core", swap)
-        grad_weight = place(place_index, mine, late).reshape(ny * chip, width)
+        grad_weight = place(index, partner, mine, late).reshape(ny * chip, width)
         grad_hidden = jnp.where(held_own, acc, got_b.astype(F32)) + got_a.astype(F32)
         weighted = weight_rows * grad_hidden
         grad_gate = (weighted * upper * sigma * (1.0 + gate * (1.0 - sigma))).astype(BF)

time: 162 us -> 153 us (0.944)
  waiting for transfers between devices: 40.9 us -> 28.6 us
  starting transfers between devices: 72.8 us -> 80.6 us
  local copies, waits for them, and re-layouts: 7.68 us -> 5.87 us
    all_to_all x1, waiting for transfers between devices: 17.6 us -> 2.81 us  [local(): lax.all_to_all(outgoing, 'expert', split_axis=0, concat_axis=0, tiled=True)]
    ppermute x4, waiting for transfers between devices: 0.01 us -> 6.77 us  [local(): on_a = lambda v: lax.ppermute(v, ('y', 'core'), ring_a)]
    ppermute x3, waiting for transfers between devices: 8.96 us -> 3.18 us  [local(): on_b = lambda v: lax.ppermute(v, ('y', 'core'), ring_b)]
    all_to_all x1, waiting for transfers between devices: 0.24 us -> 5.89 us  [local(): lax.all_to_all(mix.reshape(members, share), ('dp', 'y', 'xlo', 'core'), 0...]
    ppermute x1, starting transfers between devices: 1.91 us -> 7.44 us  [local(): late = lax.ppermute(theirs, 'core', swap)]
    pallas_call x1, Pallas kernels: 6.61 us -> 2.09 us  [place(): pl.pallas_call(functools.partial(place_kernel, tuple(partner)), grid_spec...]
    ppermute x1, waiting for transfers between devices: 8.59 us -> 4.41 us  [local(): s_a = lax.ppermute(scaled, ('core', 'dp'), scaled_a)]
    ppermute x1, starting transfers between devices: 2.39 us -> 6 us  [local(): s_a = lax.ppermute(scaled, ('core', 'dp'), scaled_a)]
  transfers between devices with their start and end apart: 17 -> 17, of which waited for: 8 -> 9; matrix products, arithmetic and copies ran while one was open for 3% -> 3% of each run, Pallas kernels for 17% -> 17%
where the time goes in v7:
time: 153 us; the launch traced here: 152 us
  starting transfers between devices  80.6 us (53%)
  Pallas kernels  31.5 us (21%)
  waiting for transfers between devices  28.6 us (19%)
  local copies, waits for them, and re-layouts  5.87 us (4%)
  other arithmetic  3.14 us (2%)
    pallas_call x6, Pallas kernels, use(): pl.pallas_call(functools.partial(use_kernel, blocks, first, last), grid_s...  29.4 us
    ppermute x4, starting transfers between devices, local(): on_a = lambda v: lax.ppermute(v, ('y', 'core'), ring_a)  17.4 us
    all_to_all x1, starting transfers between devices, local(): lax.all_to_all(mix.reshape(members, share), ('dp', 'y', 'xlo', 'core'), 0...  10.1 us
    all_to_all x1, starting transfers between devices, local(): lax.all_to_all(outgoing, 'expert', split_axis=0, concat_axis=0, tiled=True)  10 us
    ppermute x1, starting transfers between devices, local(): lax.ppermute(jnp.concatenate([cotangent[0], ids], axis=1), every, token_m...  8.33 us
    ppermute x1, starting transfers between devices, local(): late = lax.ppermute(theirs, 'core', swap)  7.44 us
    ppermute x4, waiting for transfers between devices, local(): on_a = lambda v: lax.ppermute(v, ('y', 'core'), ring_a)  6.77 us
    ppermute x3, starting transfers between devices, local(): on_b = lambda v: lax.ppermute(v, ('y', 'core'), ring_b)  6.5 us
  transfers between devices with their start and end apart: 17, of which 9 were waited for; matrix products, arithmetic and copies ran while one was open for 3% of the time, Pallas kernels for 17%

profile of v7, /device:TPU:1, one launch (start us, length us, event | category | flops | bytes accessed | tf_op | source)
XLA Modules:
  0.0 152.1 jit_solution(17790681333805386874)
XLA Ops:
  0.6 1.0 copy.31
  1.6 0.0 copy-start.15
  1.6 0.7 convert_bitcast_fusion
  2.4 8.3 %collective-permute-start = (bf16[192,194]{0,1:T(8,128)(2,1)S(1)}, bf16[192,194]{0,1:T(8,128)(2,1)S(1)}, u32[]{:S(2)}, u32[]{:S(2)}) collective-permute-start(bf16[192,194]{0,1:T(8,128)(2,1)S(1)} %pad_maximum_fusion), channel_id=1, source_target_pairs={{0,48},{1,50},{2,52},{3,54},{4,56},{5,58},{6,60},{7,62},{8,0},{9,2... | collective-permute-start | bytes 223496 | tf_op jit(solution)/shard_map/ppermute | solution.py:190
  10.7 4.0 %collective-permute-start.1 = (bf16[192,192]{0,1:T(8,128)(2,1)S(1)}, bf16[192,192]{0,1:T(8,128)(2,1)S(1)}, u32[]{:S(2)}, u32[]{:S(2)}) collective-permute-start(bf16[192,192]{0,1:T(8,128)(2,1)S(1)} %bitcast.64), channel_id=1, source_target_pairs={{0,52},{1,54},{2,48},{3,50},{4,60},{5,62},{6,56},{7,58},{8,4},{9,6... | collective-permute-start | bytes 221192 | tf_op jit(solution)/shard_map/ppermute | solution.py:191
  14.7 1.9 %collective-permute-start.5 = (bf16[3072,256]{1,0:T(8,128)(2,1)}, bf16[3072,256]{1,0:T(8,128)(2,1)S(1)}, u32[]{:S(2)}, u32[]{:S(2)}) collective-permute-start(bf16[3072,256]{1,0:T(8,128)(2,1)} %bitcast.41), channel_id=1, source_target_pairs={{0,2},{2,0},{1,3},{3,1},{4,6},{6,4},{5,7},{7,5},{8,10},{10,8},{9,1... | collective-permute-start | bytes 4718600 | tf_op jit(solution)/shard_map/ppermute | solution.py:207
  16.7 0.1 fusion.16
  16.9 1.6 %collective-permute-done.1 = bf16[192,192]{0,1:T(8,128)(2,1)S(1)} collective-permute-done((bf16[192,192]{0,1:T(8,128)(2,1)S(1)}, bf16[192,192]{0,1:T(8,128)(2,1)S(1)}, u32[]{:S(2)}, u32[]{:S(2)}) %collective-permute-start.1) | collective-permute-done | bytes 73760 | tf_op jit(solution)/shard_map/ppermute | solution.py:191
  18.5 1.2 convolution_convert_fusion
  19.7 10.0 %all-to-all-start = ((bf16[8,96,384]{2,1,0:T(8,128)(2,1)}), bf16[8,96,384]{2,1,0:T(8,128)(2,1)S(1)}, u32[]{:S(2)}, u32[]{:S(2)}) async-start(bf16[8,96,384]{2,1,0:T(8,128)(2,1)} %bitcast.62), calls=%async_computation | async-start | bytes 1179648 | tf_op jit(solution)/shard_map/all_to_all | solution.py:197
  29.8 0.3 fusion.1
  30.1 6.0 %collective-permute-start.2 = (bf16[768,256]{1,0:T(8,128)(2,1)S(1)}, bf16[768,256]{1,0:T(8,128)(2,1)S(1)}, u32[]{:S(2)}, u32[]{:S(2)}) collective-permute-start(bf16[768,256]{1,0:T(8,128)(2,1)S(1)} %fusion.1), channel_id=1, source_target_pairs={{0,0},{1,2},{2,1},{3,3},{4,4},{5,6},{6,5},{7,7},{8,8},{9,10},{10,9... | collective-permute-start | bytes 1179656 | tf_op jit(solution)/shard_map/ppermute | solution.py:205
  36.1 1.9 %collective-permute-start.3 = (bf16[768,256]{1,0:T(8,128)(2,1)S(1)}, bf16[768,256]{1,0:T(8,128)(2,1)S(1)}, u32[]{:S(2)}, u32[]{:S(2)}) collective-permute-start(bf16[768,256]{1,0:T(8,128)(2,1)S(1)} %fusion.1), channel_id=1, source_target_pairs={{0,1},{1,3},{2,0},{3,2},{4,5},{5,7},{6,4},{7,6},{8,9},{9,11},{10,8... | collective-permute-start | bytes 1179656 | tf_op jit(solution)/shard_map/ppermute | solution.py:206
  38.0 4.4 %collective-permute-done.2.refs_3_.refs_6_ = bf16[768,256]{1,0:T(8,128)(2,1)S(1)} collective-permute-done((bf16[768,256]{1,0:T(8,128)(2,1)S(1)}, bf16[768,256]{1,0:T(8,128)(2,1)S(1)}, u32[]{:S(2)}, u32[]{:S(2)}) %collective-permute-start.2) | collective-permute-done | bytes 393248 | tf_op jit(solution)/shard_map/ppermute | solution.py:205
  42.4 4.0 %collective-permute-done.3.refs_4_.refs_7_ = bf16[768,256]{1,0:T(8,128)(2,1)S(1)} collective-permute-done((bf16[768,256]{1,0:T(8,128)(2,1)S(1)}, bf16[768,256]{1,0:T(8,128)(2,1)S(1)}, u32[]{:S(2)}, u32[]{:S(2)}) %collective-permute-start.3) | collective-permute-done | bytes 393248 | tf_op jit(solution)/shard_map/ppermute | solution.py:206
  46.4 2.8 %all-to-all-done = bf16[8,96,384]{2,1,0:T(8,128)(2,1)S(1)} async-done(((bf16[8,96,384]{2,1,0:T(8,128)(2,1)}), bf16[8,96,384]{2,1,0:T(8,128)(2,1)S(1)}, u32[]{:S(2)}, u32[]{:S(2)}) %all-to-all-start) | async-done | bytes 589856 | tf_op jit(solution)/shard_map/all_to_all | solution.py:197
  49.2 2.6 %collective-permute-start.4 = (bf16[768,384]{1,0:T(8,128)(2,1)S(1)}, bf16[768,384]{1,0:T(8,128)(2,1)}, u32[]{:S(2)}, u32[]{:S(2)}) collective-permute-start(bf16[768,384]{1,0:T(8,128)(2,1)S(1)} %bitcast.58), channel_id=1, source_target_pairs={{0,8},{2,58},{8,16},{10,2},{16,24},{18,10},{24,32},{26,18},{32,40}... | collective-permute-start | bytes 1769480 | tf_op jit(solution)/shard_map/ppermute | solution.py:219
  51.9 0.7 stack.47.index
  52.6 1.1 copy-done.2
  53.7 3.9 %shard_map.93 = (f32[768,512]{1,0:T(8,128)}, bf16[8,384,256]{2,1,0:T(8,128)(2,1)}, bf16[8,384,256]{2,1,0:T(8,128)(2,1)}) custom-call(s32[10]{0:T(128)} %stack.47.index, bf16[768,384]{1,0:T(8,128)(2,1)} %bitcast.59, bf16[8,384,256]{2,1,0:T(8,128)(2,1)} %bitcast.42, bf16[8,384,256]{2,1,0:T(8,128)(2,1)} %bitcast.50, bf16[768,256]{1,0:T(8,128)(2,1)} %copy-done.3, ...), custom_call_target="tpu_custom_call" | custom-call | flops 603979776 | bytes 4000000 | tf_op jit(solution)/shard_map/pallas_call | solution.py:103
  57.7 2.7 %collective-permute-start.7 = (bf16[768,384]{1,0:T(8,128)(2,1)}, bf16[768,384]{1,0:T(8,128)(2,1)S(1)}, u32[]{:S(2)}, u32[]{:S(2)}) collective-permute-start(bf16[768,384]{1,0:T(8,128)(2,1)} %bitcast.60), channel_id=1, source_target_pairs={{0,56},{2,10},{8,0},{10,18},{16,8},{18,26},{24,16},{26,34},{32,24}... | collective-permute-start | bytes 1769480 | tf_op jit(solution)/shard_map/ppermute | solution.py:220
  60.3 0.0 collective-permute-done.4.refs_0_
  60.4 4.9 %collective-permute-start.6 = (bf16[768,384]{1,0:T(8,128)(2,1)}, bf16[768,384]{1,0:T(8,128)(2,1)S(1)}, u32[]{:S(2)}, u32[]{:S(2)}) collective-permute-start(bf16[768,384]{1,0:T(8,128)(2,1)} %collective-permute-done.4.refs_0_), channel_id=1, source_target_pairs={{0,8},{2,58},{8,16},{10,2},{16,24},{18,10},{24,32},{26,18},{32,40}... | collective-permute-start | bytes 1769480 | tf_op jit(solution)/shard_map/ppermute | solution.py:219
  65.3 4.5 %shard_map.94 = (f32[768,512]{1,0:T(8,128)}, bf16[8,384,256]{2,1,0:T(8,128)(2,1)}, bf16[8,384,256]{2,1,0:T(8,128)(2,1)}) custom-call(s32[10]{0:T(128)} %stack.47.index, bf16[768,384]{1,0:T(8,128)(2,1)} %collective-permute-done.4.refs_0_, bf16[8,384,256]{2,1,0:T(8,128)(2,1)} %bitcast.43, ...), custom_call_target="tpu_custom_call", output_to_operand_aliasing={{0}: (6, {}), {1}: (7, {}), {2}: (8, {})} | custom-call | flops 603979776 | bytes 4000000 | tf_op jit(solution)/shard_map/pallas_call | solution.py:103
  69.8 3.2 %collective-permute-done.7.refs_1_ = bf16[768,384]{1,0:T(8,128)(2,1)S(1)} collective-permute-done((bf16[768,384]{1,0:T(8,128)(2,1)}, bf16[768,384]{1,0:T(8,128)(2,1)S(1)}, u32[]{:S(2)}, u32[]{:S(2)}) %collective-permute-start.7) | collective-permute-done | bytes 589856 | tf_op jit(solution)/shard_map/ppermute | solution.py:220
  73.0 1.9 %collective-permute-start.9 = (bf16[768,384]{1,0:T(8,128)(2,1)S(1)}, bf16[768,384]{1,0:T(8,128)(2,1)S(1)}, u32[]{:S(2)}, u32[]{:S(2)}) collective-permute-start(bf16[768,384]{1,0:T(8,128)(2,1)S(1)} %collective-permute-done.7.refs_1_), channel_id=1, source_target_pairs={{0,56},{2,10},{8,0},{10,18},{16,8},{18,26},{24,16},{26,34},{32,24}... | collective-permute-start | bytes 1769480 | tf_op jit(solution)/shard_map/ppermute | solution.py:220
  74.9 1.2 collective-permute-done.6.refs_0_
  76.1 4.9 %collective-permute-start.8 = (bf16[768,384]{1,0:T(8,128)(2,1)S(1)}, bf16[768,384]{1,0:T(8,128)(2,1)S(1)}, u32[]{:S(2)}, u32[]{:S(2)}) collective-permute-start(bf16[768,384]{1,0:T(8,128)(2,1)S(1)} %collective-permute-done.6.refs_0_), channel_id=1, source_target_pairs={{0,8},{2,58},{8,16},{10,2},{16,24},{18,10},{24,32},{26,18},{32,40}... | collective-permute-start | bytes 1769480 | tf_op jit(solution)/shard_map/ppermute | solution.py:219
  81.1 5.7 %shard_map.95 = (f32[768,512]{1,0:T(8,128)}, bf16[8,384,256]{2,1,0:T(8,128)(2,1)}, bf16[8,384,256]{2,1,0:T(8,128)(2,1)}) custom-call(s32[10]{0:T(128)} %stack.47.index, bf16[768,384]{1,0:T(8,128)(2,1)} %copy-done.10, bf16[768,384]{1,0:T(8,128)(2,1)} %copy-done.12, ...), custom_call_target="tpu_custom_call", output_to_operand_aliasing={{0}: (9, {}), {1}: (10, {}), {2}: (11, {})} | custom-call | flops 1207959552 | bytes 8000000 | tf_op jit(solution)/shard_map/pallas_call | solution.py:103
  86.7 1.9 %collective-permute-start.11 = (bf16[768,384]{1,0:T(8,128)(2,1)S(1)}, bf16[768,384]{1,0:T(8,128)(2,1)S(1)}, u32[]{:S(2)}, u32[]{:S(2)}) collective-permute-start(bf16[768,384]{1,0:T(8,128)(2,1)S(1)} %collective-permute-done.9.refs_1_), channel_id=1, source_target_pairs={{0,56},{2,10},{8,0},{10,18},{16,8},{18,26},{24,16},{26,34},{32,24}... | collective-permute-start | bytes 1769480 | tf_op jit(solution)/shard_map/ppermute | solution.py:220
  88.7 4.0 %collective-permute-done.8.refs_0_ = bf16[768,384]{1,0:T(8,128)(2,1)S(1)} collective-permute-done((bf16[768,384]{1,0:T(8,128)(2,1)S(1)}, bf16[768,384]{1,0:T(8,128)(2,1)S(1)}, u32[]{:S(2)}, u32[]{:S(2)}) %collective-permute-start.8) | collective-permute-done | bytes 589856 | tf_op jit(solution)/shard_map/ppermute | solution.py:219
  92.7 5.0 %collective-permute-start.10 = (bf16[768,384]{1,0:T(8,128)(2,1)S(1)}, bf16[768,384]{1,0:T(8,128)(2,1)S(1)}, u32[]{:S(2)}, u32[]{:S(2)}) collective-permute-start(bf16[768,384]{1,0:T(8,128)(2,1)S(1)} %collective-permute-done.8.refs_0_), channel_id=1, source_target_pairs={{0,8},{2,58},{8,16},{10,2},{16,24},{18,10},{24,32},{26,18},{32,40}... | collective-permute-start | bytes 1769480 | tf_op jit(solution)/shard_map/ppermute | solution.py:219
  97.7 5.7 %shard_map.96 = (f32[768,512]{1,0:T(8,128)}, bf16[8,384,256]{2,1,0:T(8,128)(2,1)}, bf16[8,384,256]{2,1,0:T(8,128)(2,1)}) custom-call(s32[10]{0:T(128)} %stack.47.index, bf16[768,384]{1,0:T(8,128)(2,1)} %copy-done.9, bf16[768,384]{1,0:T(8,128)(2,1)} %copy-done.11, ...), custom_call_target="tpu_custom_call", output_to_operand_aliasing={{0}: (9, {}), {1}: (10, {}), {2}: (11, {})} | custom-call | flops 1207959552 | bytes 8000000 | tf_op jit(solution)/shard_map/pallas_call | solution.py:103
  103.4 0.8 copy-done.14
  104.2 4.6 %shard_map.97 = (f32[768,512]{1,0:T(8,128)}, bf16[8,384,256]{2,1,0:T(8,128)(2,1)}, bf16[8,384,256]{2,1,0:T(8,128)(2,1)}) custom-call(s32[10]{0:T(128)} %stack.47.index, bf16[768,384]{1,0:T(8,128)(2,1)} %copy-done.14, bf16[8,384,256]{2,1,0:T(8,128)(2,1)} %bitcast.48, ...), custom_call_target="tpu_custom_call", output_to_operand_aliasing={{0}: (6, {}), {1}: (7, {}), {2}: (8, {})} | custom-call | flops 603979776 | bytes 4000000 | tf_op jit(solution)/shard_map/pallas_call | solution.py:103
  108.8 1.6 %collective-permute-done.10.refs_0_ = bf16[768,384]{1,0:T(8,128)(2,1)S(1)} collective-permute-done((bf16[768,384]{1,0:T(8,128)(2,1)S(1)}, bf16[768,384]{1,0:T(8,128)(2,1)S(1)}, u32[]{:S(2)}, u32[]{:S(2)}) %collective-permute-start.10) | collective-permute-done | bytes 589856 | tf_op jit(solution)/shard_map/ppermute | solution.py:219
  110.4 0.8 copy-done.13
  111.2 5.0 %shard_map.98 = (f32[768,256]{1,0:T(8,128)}, bf16[8,384,256]{2,1,0:T(8,128)(2,1)}, bf16[8,384,256]{2,1,0:T(8,128)(2,1)}, bf16[768,256]{1,0:T(8,128)(2,1)}, bf16[768,256]{1,0:T(8,128)(2,1)}, /*index=5*/f32[2,768]{1,0:T(2,128)}) custom-call(s32[10]{0:T(128)} %stack.47.index, ...), custom_call_target="tpu_custom_call", output_to_operand_aliasing={{1}: (7, {}), {2}: (8, {})} | custom-call | flops 603979776 | bytes 4000000 | tf_op jit(solution)/shard_map/pallas_call | solution.py:103
  116.2 7.4 %collective-permute-start.14 = (bf16[8,384,256]{2,1,0:T(8,128)(2,1)}, bf16[8,384,256]{2,1,0:T(8,128)(2,1)S(1)}, u32[]{:S(2)}, u32[]{:S(2)}) collective-permute-start(bf16[8,384,256]{2,1,0:T(8,128)(2,1)} %get-tuple-element.79), channel_id=1, source_target_pairs={{0,2},{2,0},{1,3},{3,1},{4,6},{6,4},{5,7},{7,5},{8,10},{10,8},{9,1... | collective-permute-start | bytes 4718600 | tf_op jit(solution)/shard_map/ppermute | solution.py:249
  123.6 4.9 %collective-permute-start.12 = (bf16[768,256]{1,0:T(8,128)(2,1)}, bf16[768,256]{1,0:T(8,128)(2,1)S(1)}, u32[]{:S(2)}, u32[]{:S(2)}) collective-permute-start(bf16[768,256]{1,0:T(8,128)(2,1)} %get-tuple-element.76), channel_id=1, source_target_pairs={{2,1},{1,2},{6,5},{5,6},{10,9},{9,10},{14,13},{13,14},{18,17},{17,... | collective-permute-start | bytes 1179656 | tf_op jit(solution)/shard_map/ppermute | solution.py:245
  128.6 1.9 %collective-permute-start.13 = (bf16[768,256]{1,0:T(8,128)(2,1)}, bf16[768,256]{1,0:T(8,128)(2,1)S(1)}, u32[]{:S(2)}, u32[]{:S(2)}) collective-permute-start(bf16[768,256]{1,0:T(8,128)(2,1)} %get-tuple-element.77), channel_id=1, source_target_pairs={{2,3},{1,0},{0,2},{3,1},{6,7},{5,4},{4,6},{7,5},{10,11},{9,8},{8,1... | collective-permute-start | bytes 1179656 | tf_op jit(solution)/shard_map/ppermute | solution.py:244
  130.5 1.4 all_to_all.12
  131.9 10.1 %all-to-all-start.1 = ((f32[64,1,24]{2,1,0:T(1,128)}), f32[64,1,24]{2,1,0:T(1,128)S(1)}, u32[]{:S(2)}, u32[]{:S(2)}) async-start(f32[64,1,24]{2,1,0:T(1,128)} %bitcast.22), calls=%async_computation.1 | async-start | bytes 65536 | tf_op jit(solution)/shard_map/all_to_all | solution.py:248
  142.1 0.0 collective-permute-done.13
  142.1 1.4 multiply_convert_fusion
  143.5 2.1 %shard_map.99 = bf16[8,384,256]{2,1,0:T(8,128)(2,1)} custom-call(s32[10]{0:T(128)S(1)} %copy-done.1, bf16[8,384,256]{2,1,0:T(8,128)(2,1)S(1)} %copy-done, bf16[8,384,256]{2,1,0:T(8,128)(2,1)S(1)} %collective-permute-done.14.theirs), custom_call_target="tpu_custom_call" | custom-call | flops 1000000 | bytes 5000000 | tf_op jit(solution)/shard_map/pallas_call | solution.py:129
  145.6 5.9 %all-to-all-done.1 = f32[64,1,24]{2,1,0:T(1,128)S(1)} async-done(((f32[64,1,24]{2,1,0:T(1,128)}), f32[64,1,24]{2,1,0:T(1,128)S(1)}, u32[]{:S(2)}, u32[]{:S(2)}) %all-to-all-start.1) | async-done | bytes 6176 | tf_op jit(solution)/shard_map/all_to_all | solution.py:248
  151.5 0.6 bitcast_divide_fusion
  (43 shorter events, 0.2 us)
Async XLA Ops:
  1.6 28.1 %copy-start.15 = (f32[1,1,768]{2,1,0:T(1,128)S(1)}, f32[1,1,768]{2,1,0:T(1,128)}, u32[]{:S(2)}) copy-start(f32[1,1,768]{2,1,0:T(1,128)} %param.8) | copy-start | bytes 9220
  2.3 27.4 %copy-start.6 = (bf16[1,1,768,256]{3,2,1,0:T(8,128)(2,1)S(1)}, bf16[1,1,768,256]{3,2,1,0:T(8,128)(2,1)}, u32[]{:S(2)}) copy-start(bf16[1,1,768,256]{3,2,1,0:T(8,128)(2,1)} %param.9) | copy-start | bytes 1179652
  2.3 27.4 %copy-start.7 = (bf16[1,1,768,256]{3,2,1,0:T(8,128)(2,1)S(1)}, bf16[1,1,768,256]{3,2,1,0:T(8,128)(2,1)}, u32[]{:S(2)}) copy-start(bf16[1,1,768,256]{3,2,1,0:T(8,128)(2,1)} %param.10) | copy-start | bytes 1179652
  2.4 14.3 %collective-permute-start = (bf16[192,194]{0,1:T(8,128)(2,1)S(1)}, bf16[192,194]{0,1:T(8,128)(2,1)S(1)}, u32[]{:S(2)}, u32[]{:S(2)}) collective-permute-start(bf16[192,194]{0,1:T(8,128)(2,1)S(1)} %pad_maximum_fusion), channel_id=1, source_target_pairs={{0,48},{1,50},{2,52},{3,54},{4,56},{5,58},{6,60},{7,62},{8,0},{9,2... | collective-permute-start | bytes 223496 | tf_op jit(solution)/shard_map/ppermute | solution.py:190
  10.7 7.8 %collective-permute-start.1 = (bf16[192,192]{0,1:T(8,128)(2,1)S(1)}, bf16[192,192]{0,1:T(8,128)(2,1)S(1)}, u32[]{:S(2)}, u32[]{:S(2)}) collective-permute-start(bf16[192,192]{0,1:T(8,128)(2,1)S(1)} %bitcast.64), channel_id=1, source_target_pairs={{0,52},{1,54},{2,48},{3,50},{4,60},{5,62},{6,56},{7,58},{8,4},{9,6... | collective-permute-start | bytes 221192 | tf_op jit(solution)/shard_map/ppermute | solution.py:191
  14.7 37.9 %collective-permute-start.5 = (bf16[3072,256]{1,0:T(8,128)(2,1)}, bf16[3072,256]{1,0:T(8,128)(2,1)S(1)}, u32[]{:S(2)}, u32[]{:S(2)}) collective-permute-start(bf16[3072,256]{1,0:T(8,128)(2,1)} %bitcast.41), channel_id=1, source_target_pairs={{0,2},{2,0},{1,3},{3,1},{4,6},{6,4},{5,7},{7,5},{8,10},{10,8},{9,1... | collective-permute-start | bytes 4718600 | tf_op jit(solution)/shard_map/ppermute | solution.py:207
  19.7 29.5 %all-to-all-start = ((bf16[8,96,384]{2,1,0:T(8,128)(2,1)}), bf16[8,96,384]{2,1,0:T(8,128)(2,1)S(1)}, u32[]{:S(2)}, u32[]{:S(2)}) async-start(bf16[8,96,384]{2,1,0:T(8,128)(2,1)} %bitcast.62), calls=%async_computation | async-start | bytes 1179648 | tf_op jit(solution)/shard_map/all_to_all | solution.py:197
  30.1 12.3 %collective-permute-start.2 = (bf16[768,256]{1,0:T(8,128)(2,1)S(1)}, bf16[768,256]{1,0:T(8,128)(2,1)S(1)}, u32[]{:S(2)}, u32[]{:S(2)}) collective-permute-start(bf16[768,256]{1,0:T(8,128)(2,1)S(1)} %fusion.1), channel_id=1, source_target_pairs={{0,0},{1,2},{2,1},{3,3},{4,4},{5,6},{6,5},{7,7},{8,8},{9,10},{10,9... | collective-permute-start | bytes 1179656 | tf_op jit(solution)/shard_map/ppermute | solution.py:205
  36.1 10.3 %collective-permute-start.3 = (bf16[768,256]{1,0:T(8,128)(2,1)S(1)}, bf16[768,256]{1,0:T(8,128)(2,1)S(1)}, u32[]{:S(2)}, u32[]{:S(2)}) collective-permute-start(bf16[768,256]{1,0:T(8,128)(2,1)S(1)} %fusion.1), channel_id=1, source_target_pairs={{0,1},{1,3},{2,0},{3,2},{4,5},{5,7},{6,4},{7,6},{8,9},{9,11},{10,8... | collective-permute-start | bytes 1179656 | tf_op jit(solution)/shard_map/ppermute | solution.py:206
  42.4 10.2 %copy-start.3 = (bf16[768,256]{1,0:T(8,128)(2,1)}, bf16[768,256]{1,0:T(8,128)(2,1)S(1)}, u32[]{:S(2)}) copy-start(bf16[768,256]{1,0:T(8,128)(2,1)S(1)} %collective-permute-done.2.refs_3_.refs_6_) | copy-start | bytes 1179652
  46.4 6.2 %copy-start.4 = (bf16[768,256]{1,0:T(8,128)(2,1)}, bf16[768,256]{1,0:T(8,128)(2,1)S(1)}, u32[]{:S(2)}) copy-start(bf16[768,256]{1,0:T(8,128)(2,1)S(1)} %collective-permute-done.3.refs_4_.refs_7_) | copy-start | bytes 1179652
  49.2 3.4 %copy-start.5 = (bf16[8,96,384]{2,1,0:T(8,128)(2,1)}, bf16[8,96,384]{2,1,0:T(8,128)(2,1)S(1)}, u32[]{:S(2)}) copy-start(bf16[8,96,384]{2,1,0:T(8,128)(2,1)S(1)} %all-to-all-done) | copy-start | bytes 1769476
  49.2 11.1 %collective-permute-start.4 = (bf16[768,384]{1,0:T(8,128)(2,1)S(1)}, bf16[768,384]{1,0:T(8,128)(2,1)}, u32[]{:S(2)}, u32[]{:S(2)}) collective-permute-start(bf16[768,384]{1,0:T(8,128)(2,1)S(1)} %bitcast.58), channel_id=1, source_target_pairs={{0,8},{2,58},{8,16},{10,2},{16,24},{18,10},{24,32},{26,18},{32,40}... | collective-permute-start | bytes 1769480 | tf_op jit(solution)/shard_map/ppermute | solution.py:219
  52.6 1.1 copy-start.2
  57.7 15.3 %collective-permute-start.7 = (bf16[768,384]{1,0:T(8,128)(2,1)}, bf16[768,384]{1,0:T(8,128)(2,1)S(1)}, u32[]{:S(2)}, u32[]{:S(2)}) collective-permute-start(bf16[768,384]{1,0:T(8,128)(2,1)} %bitcast.60), channel_id=1, source_target_pairs={{0,56},{2,10},{8,0},{10,18},{16,8},{18,26},{24,16},{26,34},{32,24}... | collective-permute-start | bytes 1769480 | tf_op jit(solution)/shard_map/ppermute | solution.py:220
  60.4 15.8 %collective-permute-start.6 = (bf16[768,384]{1,0:T(8,128)(2,1)}, bf16[768,384]{1,0:T(8,128)(2,1)S(1)}, u32[]{:S(2)}, u32[]{:S(2)}) collective-permute-start(bf16[768,384]{1,0:T(8,128)(2,1)} %collective-permute-done.4.refs_0_), channel_id=1, source_target_pairs={{0,8},{2,58},{8,16},{10,2},{16,24},{18,10},{24,32},{26,18},{32,40}... | collective-permute-start | bytes 1769480 | tf_op jit(solution)/shard_map/ppermute | solution.py:219
  73.0 8.0 %copy-start.12 = (bf16[768,384]{1,0:T(8,128)(2,1)}, bf16[768,384]{1,0:T(8,128)(2,1)S(1)}, u32[]{:S(2)}) copy-start(bf16[768,384]{1,0:T(8,128)(2,1)S(1)} %collective-permute-done.7.refs_1_) | copy-start | bytes 1769476
  73.0 13.7 %collective-permute-start.9 = (bf16[768,384]{1,0:T(8,128)(2,1)S(1)}, bf16[768,384]{1,0:T(8,128)(2,1)S(1)}, u32[]{:S(2)}, u32[]{:S(2)}) collective-permute-start(bf16[768,384]{1,0:T(8,128)(2,1)S(1)} %collective-permute-done.7.refs_1_), channel_id=1, source_target_pairs={{0,56},{2,10},{8,0},{10,18},{16,8},{18,26},{24,16},{26,34},{32,24}... | collective-permute-start | bytes 1769480 | tf_op jit(solution)/shard_map/ppermute | solution.py:220
  76.1 4.9 %copy-start.10 = (bf16[768,384]{1,0:T(8,128)(2,1)}, bf16[768,384]{1,0:T(8,128)(2,1)S(1)}, u32[]{:S(2)}) copy-start(bf16[768,384]{1,0:T(8,128)(2,1)S(1)} %collective-permute-done.6.refs_0_) | copy-start | bytes 1769476
  76.1 16.5 %collective-permute-start.8 = (bf16[768,384]{1,0:T(8,128)(2,1)S(1)}, bf16[768,384]{1,0:T(8,128)(2,1)S(1)}, u32[]{:S(2)}, u32[]{:S(2)}) collective-permute-start(bf16[768,384]{1,0:T(8,128)(2,1)S(1)} %collective-permute-done.6.refs_0_), channel_id=1, source_target_pairs={{0,8},{2,58},{8,16},{10,2},{16,24},{18,10},{24,32},{26,18},{32,40}... | collective-permute-start | bytes 1769480 | tf_op jit(solution)/shard_map/ppermute | solution.py:219
  86.7 10.9 %copy-start.11 = (bf16[768,384]{1,0:T(8,128)(2,1)}, bf16[768,384]{1,0:T(8,128)(2,1)S(1)}, u32[]{:S(2)}) copy-start(bf16[768,384]{1,0:T(8,128)(2,1)S(1)} %collective-permute-done.9.refs_1_) | copy-start | bytes 1769476
  86.7 16.6 %collective-permute-start.11 = (bf16[768,384]{1,0:T(8,128)(2,1)S(1)}, bf16[768,384]{1,0:T(8,128)(2,1)S(1)}, u32[]{:S(2)}, u32[]{:S(2)}) collective-permute-start(bf16[768,384]{1,0:T(8,128)(2,1)S(1)} %collective-permute-done.9.refs_1_), channel_id=1, source_target_pairs={{0,56},{2,10},{8,0},{10,18},{16,8},{18,26},{24,16},{26,34},{32,24}... | collective-permute-start | bytes 1769480 | tf_op jit(solution)/shard_map/ppermute | solution.py:220
  92.6 5.0 %copy-start.9 = (bf16[768,384]{1,0:T(8,128)(2,1)}, bf16[768,384]{1,0:T(8,128)(2,1)S(1)}, u32[]{:S(2)}) copy-start(bf16[768,384]{1,0:T(8,128)(2,1)S(1)} %collective-permute-done.8.refs_0_) | copy-start | bytes 1769476
  92.7 17.7 %collective-permute-start.10 = (bf16[768,384]{1,0:T(8,128)(2,1)S(1)}, bf16[768,384]{1,0:T(8,128)(2,1)S(1)}, u32[]{:S(2)}, u32[]{:S(2)}) collective-permute-start(bf16[768,384]{1,0:T(8,128)(2,1)S(1)} %collective-permute-done.8.refs_0_), channel_id=1, source_target_pairs={{0,8},{2,58},{8,16},{10,2},{16,24},{18,10},{24,32},{26,18},{32,40}... | collective-permute-start | bytes 1769480 | tf_op jit(solution)/shard_map/ppermute | solution.py:219
  103.4 0.8 copy-start.14
  110.4 0.8 copy-start.13
  111.2 30.9 %copy-start.8 = (bf16[1,1,768,256]{3,2,1,0:T(8,128)(2,1)S(1)}, bf16[1,1,768,256]{3,2,1,0:T(8,128)(2,1)}, u32[]{:S(2)}) copy-start(bf16[1,1,768,256]{3,2,1,0:T(8,128)(2,1)} %param.10) | copy-start | bytes 1179652
  116.2 27.4 %collective-permute-start.14 = (bf16[8,384,256]{2,1,0:T(8,128)(2,1)}, bf16[8,384,256]{2,1,0:T(8,128)(2,1)S(1)}, u32[]{:S(2)}, u32[]{:S(2)}) collective-permute-start(bf16[8,384,256]{2,1,0:T(8,128)(2,1)} %get-tuple-element.79), channel_id=1, source_target_pairs={{0,2},{2,0},{1,3},{3,1},{4,6},{6,4},{5,7},{7,5},{8,10},{10,8},{9,1... | collective-permute-start | bytes 4718600 | tf_op jit(solution)/shard_map/ppermute | solution.py:249
  123.6 18.4 %collective-permute-start.12 = (bf16[768,256]{1,0:T(8,128)(2,1)}, bf16[768,256]{1,0:T(8,128)(2,1)S(1)}, u32[]{:S(2)}, u32[]{:S(2)}) collective-permute-start(bf16[768,256]{1,0:T(8,128)(2,1)} %get-tuple-element.76), channel_id=1, source_target_pairs={{2,1},{1,2},{6,5},{5,6},{10,9},{9,10},{14,13},{13,14},{18,17},{17,... | collective-permute-start | bytes 1179656 | tf_op jit(solution)/shard_map/ppermute | solution.py:245
  128.6 13.5 %collective-permute-start.13 = (bf16[768,256]{1,0:T(8,128)(2,1)}, bf16[768,256]{1,0:T(8,128)(2,1)S(1)}, u32[]{:S(2)}, u32[]{:S(2)}) collective-permute-start(bf16[768,256]{1,0:T(8,128)(2,1)} %get-tuple-element.77), channel_id=1, source_target_pairs={{2,3},{1,0},{0,2},{3,1},{6,7},{5,4},{4,6},{7,5},{10,11},{9,8},{8,1... | collective-permute-start | bytes 1179656 | tf_op jit(solution)/shard_map/ppermute | solution.py:244
  131.9 19.6 %all-to-all-start.1 = ((f32[64,1,24]{2,1,0:T(1,128)}), f32[64,1,24]{2,1,0:T(1,128)S(1)}, u32[]{:S(2)}, u32[]{:S(2)}) async-start(f32[64,1,24]{2,1,0:T(1,128)} %bitcast.22), calls=%async_computation.1 | async-start | bytes 65536 | tf_op jit(solution)/shard_map/all_to_all | solution.py:248
  142.1 1.5 copy-start
  142.1 1.5 copy-start.1

commit v8 on v7

--- a/solution.py
+++ b/solution.py
@@ -9,7 +9,7 @@
 
 BF = jnp.bfloat16
 F32 = jnp.float32
-VMEM_LIMIT = 60 * 1024 * 1024
+VMEM_LIMIT = 24 * 1024 * 1024
 
 
 def one_hot_table(ids, expert_count, capacity):

time: 153 us -> 147 us (0.961)
  Pallas kernels: 31.5 us -> 19.1 us
  waiting for transfers between devices: 28.6 us -> 34.1 us
  other arithmetic: 3.14 us -> 6.89 us
  starting transfers between devices: 80.6 us -> 77.6 us
    pallas_call x6, Pallas kernels: 29.4 us -> 17.1 us  [use(): pl.pallas_call(functools.partial(use_kernel, blocks, first, last), grid_s...]
    ppermute x4, waiting for transfers between devices: 6.77 us -> 17 us  [local(): on_a = lambda v: lax.ppermute(v, ('y', 'core'), ring_a)]
    ppermute x1, starting transfers between devices: 7.44 us -> 3.23 us  [local(): late = lax.ppermute(theirs, 'core', swap)]
    all_to_all x1, waiting for transfers between devices: 5.89 us -> 3.95 us  [local(): lax.all_to_all(mix.reshape(members, share), ('dp', 'y', 'xlo', 'core'), 0...]
    unnamed x33 -> x21, local copies, waits for them, and re-layouts: 3.82 us -> 5.55 us
    all_to_all x1, waiting for transfers between devices: 2.81 us -> 1.09 us  [local(): lax.all_to_all(outgoing, 'expert', split_axis=0, concat_axis=0, tiled=True)]
  transfers between devices with their start and end apart: 17 -> 17, of which waited for: 9 -> 10; matrix products, arithmetic and copies ran while one was open for 3% -> 4% of each run, Pallas kernels for 17% -> 11%
where the time goes in v8:
time: 147 us; the launch traced here: 146 us
  starting transfers between devices  77.6 us (53%)
  waiting for transfers between devices  34.1 us (23%)
  Pallas kernels  19.1 us (13%)
  other arithmetic  6.89 us (5%)
  local copies, waits for them, and re-layouts  6.36 us (4%)
    pallas_call x6, Pallas kernels, use(): pl.pallas_call(functools.partial(use_kernel, blocks, first, last), grid_s...  17.1 us
    ppermute x4, waiting for transfers between devices, local(): on_a = lambda v: lax.ppermute(v, ('y', 'core'), ring_a)  17 us
    ppermute x4, starting transfers between devices, local(): on_a = lambda v: lax.ppermute(v, ('y', 'core'), ring_a)  16.7 us
    all_to_all x1, starting transfers between devices, local(): lax.all_to_all(mix.reshape(members, share), ('dp', 'y', 'xlo', 'core'), 0...  10.5 us
    all_to_all x1, starting transfers between devices, local(): lax.all_to_all(outgoing, 'expert', split_axis=0, concat_axis=0, tiled=True)  10.2 us
    ppermute x1, starting transfers between devices, local(): lax.ppermute(jnp.concatenate([cotangent[0], ids], axis=1), every, token_m...  8.33 us
    ppermute x3, starting transfers between devices, local(): on_b = lambda v: lax.ppermute(v, ('y', 'core'), ring_b)  6.49 us
    ppermute x1, starting transfers between devices, local(): got_b = lax.ppermute(sum_b, ('core', 'dp'), sums_b)  6.4 us
  transfers between devices with their start and end apart: 17, of which 10 were waited for; matrix products, arithmetic and copies ran while one was open for 4% of the time, Pallas kernels for 11%

profile of v8, /device:TPU:1, one launch (start us, length us, event | category | flops | bytes accessed | tf_op | source)
XLA Modules:
  0.0 146.4 jit_solution(15258819719788142382)
XLA Ops:
  0.6 1.0 copy.31
  1.6 0.7 convert_bitcast_fusion
  2.4 8.3 %collective-permute-start = (bf16[192,194]{0,1:T(8,128)(2,1)S(1)}, bf16[192,194]{0,1:T(8,128)(2,1)S(1)}, u32[]{:S(2)}, u32[]{:S(2)}) collective-permute-start(bf16[192,194]{0,1:T(8,128)(2,1)S(1)} %pad_maximum_fusion), channel_id=1, source_target_pairs={{0,48},{1,50},{2,52},{3,54},{4,56},{5,58},{6,60},{7,62},{8,0},{9,2... | collective-permute-start | bytes 223496 | tf_op jit(solution)/shard_map/ppermute | solution.py:190
  10.7 4.0 %collective-permute-start.1 = (bf16[192,192]{0,1:T(8,128)(2,1)S(1)}, bf16[192,192]{0,1:T(8,128)(2,1)S(1)}, u32[]{:S(2)}, u32[]{:S(2)}) collective-permute-start(bf16[192,192]{0,1:T(8,128)(2,1)S(1)} %bitcast.61), channel_id=1, source_target_pairs={{0,52},{1,54},{2,48},{3,50},{4,60},{5,62},{6,56},{7,58},{8,4},{9,6... | collective-permute-start | bytes 221192 | tf_op jit(solution)/shard_map/ppermute | solution.py:191
  14.7 1.9 %collective-permute-start.5 = (bf16[3072,256]{1,0:T(8,128)(2,1)}, bf16[3072,256]{1,0:T(8,128)(2,1)S(1)}, u32[]{:S(2)}, u32[]{:S(2)}) collective-permute-start(bf16[3072,256]{1,0:T(8,128)(2,1)} %bitcast.41), channel_id=1, source_target_pairs={{0,2},{2,0},{1,3},{3,1},{4,6},{6,4},{5,7},{7,5},{8,10},{10,8},{9,1... | collective-permute-start | bytes 4718600 | tf_op jit(solution)/shard_map/ppermute | solution.py:207
  16.7 0.1 fusion.16
  16.9 1.6 %collective-permute-done.1 = bf16[192,192]{0,1:T(8,128)(2,1)S(1)} collective-permute-done((bf16[192,192]{0,1:T(8,128)(2,1)S(1)}, bf16[192,192]{0,1:T(8,128)(2,1)S(1)}, u32[]{:S(2)}, u32[]{:S(2)}) %collective-permute-start.1) | collective-permute-done | bytes 73760 | tf_op jit(solution)/shard_map/ppermute | solution.py:191
  18.5 1.2 convolution_convert_fusion
  19.7 10.2 %all-to-all-start = ((bf16[8,96,384]{2,1,0:T(8,128)(2,1)}), bf16[8,96,384]{2,1,0:T(8,128)(2,1)}, u32[]{:S(2)}, u32[]{:S(2)}) async-start(bf16[8,96,384]{2,1,0:T(8,128)(2,1)} %bitcast.59), calls=%async_computation | async-start | bytes 1179648 | tf_op jit(solution)/shard_map/all_to_all | solution.py:197
  29.9 1.3 fusion.1
  31.2 6.0 %collective-permute-start.2 = (bf16[768,256]{1,0:T(8,128)(2,1)S(1)}, bf16[768,256]{1,0:T(8,128)(2,1)S(1)}, u32[]{:S(2)}, u32[]{:S(2)}) collective-permute-start(bf16[768,256]{1,0:T(8,128)(2,1)S(1)} %fusion.1), channel_id=1, source_target_pairs={{0,0},{1,2},{2,1},{3,3},{4,4},{5,6},{6,5},{7,7},{8,8},{9,10},{10,9... | collective-permute-start | bytes 1179656 | tf_op jit(solution)/shard_map/ppermute | solution.py:205
  37.2 1.9 %collective-permute-start.3 = (bf16[768,256]{1,0:T(8,128)(2,1)S(1)}, bf16[768,256]{1,0:T(8,128)(2,1)S(1)}, u32[]{:S(2)}, u32[]{:S(2)}) collective-permute-start(bf16[768,256]{1,0:T(8,128)(2,1)S(1)} %fusion.1), channel_id=1, source_target_pairs={{0,1},{1,3},{2,0},{3,2},{4,5},{5,7},{6,4},{7,6},{8,9},{9,11},{10,8... | collective-permute-start | bytes 1179656 | tf_op jit(solution)/shard_map/ppermute | solution.py:206
  39.1 4.4 %collective-permute-done.2.refs_3_.refs_6_ = bf16[768,256]{1,0:T(8,128)(2,1)S(1)} collective-permute-done((bf16[768,256]{1,0:T(8,128)(2,1)S(1)}, bf16[768,256]{1,0:T(8,128)(2,1)S(1)}, u32[]{:S(2)}, u32[]{:S(2)}) %collective-permute-start.2) | collective-permute-done | bytes 393248 | tf_op jit(solution)/shard_map/ppermute | solution.py:205
  43.5 4.1 %collective-permute-done.3.refs_4_.refs_7_ = bf16[768,256]{1,0:T(8,128)(2,1)S(1)} collective-permute-done((bf16[768,256]{1,0:T(8,128)(2,1)S(1)}, bf16[768,256]{1,0:T(8,128)(2,1)S(1)}, u32[]{:S(2)}, u32[]{:S(2)}) %collective-permute-start.3) | collective-permute-done | bytes 393248 | tf_op jit(solution)/shard_map/ppermute | solution.py:206
  47.6 0.7 copy-done.3
  48.4 1.1 all-to-all-done
  49.4 2.6 %collective-permute-start.4 = (bf16[768,384]{1,0:T(8,128)(2,1)}, bf16[768,384]{1,0:T(8,128)(2,1)}, u32[]{:S(2)}, u32[]{:S(2)}) collective-permute-start(bf16[768,384]{1,0:T(8,128)(2,1)} %bitcast.15.refs_0_), channel_id=1, source_target_pairs={{0,8},{2,58},{8,16},{10,2},{16,24},{18,10},{24,32},{26,18},{32,40}... | collective-permute-start | bytes 1769480 | tf_op jit(solution)/shard_map/ppermute | solution.py:219
  52.3 1.0 copy-done.4
  53.2 3.2 %shard_map.93 = (f32[768,512]{1,0:T(8,128)S(1)}, bf16[8,384,256]{2,1,0:T(8,128)(2,1)S(1)}, bf16[8,384,256]{2,1,0:T(8,128)(2,1)}) custom-call(s32[10]{0:T(128)S(1)} %stack.47.index, bf16[768,384]{1,0:T(8,128)(2,1)} %bitcast.15.refs_0_, bf16[8,384,256]{2,1,0:T(8,128)(2,1)S(1)} %bitcast.42, bf16[8,384,256]{2,1,0:T(8,128)(2,1)S(1)} %bitcast.50, ...), custom_call_target="tpu_custom_call" | custom-call | flops 603979776 | bytes 4000000 | tf_op jit(solution)/shard_map/pallas_call | solution.py:103
  56.4 2.7 %collective-permute-start.7 = (bf16[768,384]{1,0:T(8,128)(2,1)}, bf16[768,384]{1,0:T(8,128)(2,1)S(1)}, u32[]{:S(2)}, u32[]{:S(2)}) collective-permute-start(bf16[768,384]{1,0:T(8,128)(2,1)} %bitcast.15.refs_0_), channel_id=1, source_target_pairs={{0,56},{2,10},{8,0},{10,18},{16,8},{18,26},{24,16},{26,34},{32,24}... | collective-permute-start | bytes 1769480 | tf_op jit(solution)/shard_map/ppermute | solution.py:220
  59.1 1.6 %collective-permute-done.4.refs_0_ = bf16[768,384]{1,0:T(8,128)(2,1)} collective-permute-done((bf16[768,384]{1,0:T(8,128)(2,1)}, bf16[768,384]{1,0:T(8,128)(2,1)}, u32[]{:S(2)}, u32[]{:S(2)}) %collective-permute-start.4) | collective-permute-done | bytes 589856 | tf_op jit(solution)/shard_map/ppermute | solution.py:219
  60.7 4.2 %collective-permute-start.6 = (bf16[768,384]{1,0:T(8,128)(2,1)}, bf16[768,384]{1,0:T(8,128)(2,1)S(1)}, u32[]{:S(2)}, u32[]{:S(2)}) collective-permute-start(bf16[768,384]{1,0:T(8,128)(2,1)} %collective-permute-done.4.refs_0_), channel_id=1, source_target_pairs={{0,8},{2,58},{8,16},{10,2},{16,24},{18,10},{24,32},{26,18},{32,40}... | collective-permute-start | bytes 1769480 | tf_op jit(solution)/shard_map/ppermute | solution.py:219
  64.9 3.3 %shard_map.94 = (f32[768,512]{1,0:T(8,128)S(1)}, bf16[8,384,256]{2,1,0:T(8,128)(2,1)S(1)}, bf16[8,384,256]{2,1,0:T(8,128)(2,1)}) custom-call(s32[10]{0:T(128)S(1)} %stack.47.index, bf16[768,384]{1,0:T(8,128)(2,1)} %collective-permute-done.4.refs_0_, bf16[8,384,256]{2,1,0:T(8,128)(2,1)S(1)} %bitcast.43, ...), custom_call_target="tpu_custom_call", output_to_operand_aliasing={{0}: (6, {}), {1}: (7, {}), {2}: (8, {})} | custom-call | flops 603979776 | bytes 4000000 | tf_op jit(solution)/shard_map/pallas_call | solution.py:103
  68.1 1.9 %collective-permute-done.7.refs_1_ = bf16[768,384]{1,0:T(8,128)(2,1)S(1)} collective-permute-done((bf16[768,384]{1,0:T(8,128)(2,1)}, bf16[768,384]{1,0:T(8,128)(2,1)S(1)}, u32[]{:S(2)}, u32[]{:S(2)}) %collective-permute-start.7) | collective-permute-done | bytes 589856 | tf_op jit(solution)/shard_map/ppermute | solution.py:220
  70.1 1.9 %collective-permute-start.9 = (bf16[768,384]{1,0:T(8,128)(2,1)S(1)}, bf16[768,384]{1,0:T(8,128)(2,1)S(1)}, u32[]{:S(2)}, u32[]{:S(2)}) collective-permute-start(bf16[768,384]{1,0:T(8,128)(2,1)S(1)} %collective-permute-done.7.refs_1_), channel_id=1, source_target_pairs={{0,56},{2,10},{8,0},{10,18},{16,8},{18,26},{24,16},{26,34},{32,24}... | collective-permute-start | bytes 1769480 | tf_op jit(solution)/shard_map/ppermute | solution.py:220
  72.0 2.9 %collective-permute-done.6.refs_0_ = bf16[768,384]{1,0:T(8,128)(2,1)S(1)} collective-permute-done((bf16[768,384]{1,0:T(8,128)(2,1)}, bf16[768,384]{1,0:T(8,128)(2,1)S(1)}, u32[]{:S(2)}, u32[]{:S(2)}) %collective-permute-start.6) | collective-permute-done | bytes 589856 | tf_op jit(solution)/shard_map/ppermute | solution.py:219
  74.9 4.9 %collective-permute-start.8 = (bf16[768,384]{1,0:T(8,128)(2,1)S(1)}, bf16[768,384]{1,0:T(8,128)(2,1)S(1)}, u32[]{:S(2)}, u32[]{:S(2)}) collective-permute-start(bf16[768,384]{1,0:T(8,128)(2,1)S(1)} %collective-permute-done.6.refs_0_), channel_id=1, source_target_pairs={{0,8},{2,58},{8,16},{10,2},{16,24},{18,10},{24,32},{26,18},{32,40}... | collective-permute-start | bytes 1769480 | tf_op jit(solution)/shard_map/ppermute | solution.py:219
  79.8 3.0 %shard_map.95 = (f32[768,512]{1,0:T(8,128)S(1)}, bf16[8,384,256]{2,1,0:T(8,128)(2,1)S(1)}, bf16[8,384,256]{2,1,0:T(8,128)(2,1)}) custom-call(s32[10]{0:T(128)S(1)} %stack.47.index, bf16[768,384]{1,0:T(8,128)(2,1)S(1)} %collective-permute-done.6.refs_0_, ...), custom_call_target="tpu_custom_call", output_to_operand_aliasing={{0}: (9, {}), {1}: (10, {}), {2}: (11, {})} | custom-call | flops 1207959552 | bytes 8000000 | tf_op jit(solution)/shard_map/pallas_call | solution.py:103
  82.8 1.9 %collective-permute-start.11 = (bf16[768,384]{1,0:T(8,128)(2,1)S(1)}, bf16[768,384]{1,0:T(8,128)(2,1)S(1)}, u32[]{:S(2)}, u32[]{:S(2)}) collective-permute-start(bf16[768,384]{1,0:T(8,128)(2,1)S(1)} %collective-permute-done.9.refs_1_), channel_id=1, source_target_pairs={{0,56},{2,10},{8,0},{10,18},{16,8},{18,26},{24,16},{26,34},{32,24}... | collective-permute-start | bytes 1769480 | tf_op jit(solution)/shard_map/ppermute | solution.py:220
  84.7 5.9 %collective-permute-done.8.refs_0_ = bf16[768,384]{1,0:T(8,128)(2,1)S(1)} collective-permute-done((bf16[768,384]{1,0:T(8,128)(2,1)S(1)}, bf16[768,384]{1,0:T(8,128)(2,1)S(1)}, u32[]{:S(2)}, u32[]{:S(2)}) %collective-permute-start.8) | collective-permute-done | bytes 589856 | tf_op jit(solution)/shard_map/ppermute | solution.py:219
  90.6 5.0 %collective-permute-start.10 = (bf16[768,384]{1,0:T(8,128)(2,1)S(1)}, bf16[768,384]{1,0:T(8,128)(2,1)S(1)}, u32[]{:S(2)}, u32[]{:S(2)}) collective-permute-start(bf16[768,384]{1,0:T(8,128)(2,1)S(1)} %collective-permute-done.8.refs_0_), channel_id=1, source_target_pairs={{0,8},{2,58},{8,16},{10,2},{16,24},{18,10},{24,32},{26,18},{32,40}... | collective-permute-start | bytes 1769480 | tf_op jit(solution)/shard_map/ppermute | solution.py:219
  95.6 3.0 %shard_map.96 = (f32[768,512]{1,0:T(8,128)S(1)}, bf16[8,384,256]{2,1,0:T(8,128)(2,1)S(1)}, bf16[8,384,256]{2,1,0:T(8,128)(2,1)}) custom-call(s32[10]{0:T(128)S(1)} %stack.47.index, bf16[768,384]{1,0:T(8,128)(2,1)S(1)} %collective-permute-done.8.refs_0_, ...), custom_call_target="tpu_custom_call", output_to_operand_aliasing={{0}: (9, {}), {1}: (10, {}), {2}: (11, {})} | custom-call | flops 1207959552 | bytes 8000000 | tf_op jit(solution)/shard_map/pallas_call | solution.py:103
  98.6 2.2 %shard_map.97 = (f32[768,512]{1,0:T(8,128)S(1)}, bf16[8,384,256]{2,1,0:T(8,128)(2,1)S(1)}, bf16[8,384,256]{2,1,0:T(8,128)(2,1)}) custom-call(s32[10]{0:T(128)S(1)} %stack.47.index, bf16[768,384]{1,0:T(8,128)(2,1)S(1)} %collective-permute-done.11.refs_0_, ...), custom_call_target="tpu_custom_call", output_to_operand_aliasing={{0}: (6, {}), {1}: (7, {}), {2}: (8, {})} | custom-call | flops 603979776 | bytes 4000000 | tf_op jit(solution)/shard_map/pallas_call | solution.py:103
  100.8 6.7 %collective-permute-done.10.refs_0_ = bf16[768,384]{1,0:T(8,128)(2,1)S(1)} collective-permute-done((bf16[768,384]{1,0:T(8,128)(2,1)S(1)}, bf16[768,384]{1,0:T(8,128)(2,1)S(1)}, u32[]{:S(2)}, u32[]{:S(2)}) %collective-permute-start.10) | collective-permute-done | bytes 589856 | tf_op jit(solution)/shard_map/ppermute | solution.py:219
  107.5 2.4 %shard_map.98 = (f32[768,256]{1,0:T(8,128)S(1)}, bf16[8,384,256]{2,1,0:T(8,128)(2,1)S(1)}, bf16[8,384,256]{2,1,0:T(8,128)(2,1)}, bf16[768,256]{1,0:T(8,128)(2,1)...) custom-call(s32[10]{0:T(128)S(1)} %stack.47.index, ...), custom_call_target="tpu_custom_call", output_to_operand_aliasing={{1}: (7, {}), {2}: (8, {})} | custom-call | flops 603979776 | bytes 4000000 | tf_op jit(solution)/shard_map/pallas_call | solution.py:103
  109.9 1.2 copy-done.1
  111.1 0.9 copy-done.6
  112.0 3.2 %collective-permute-start.14 = (bf16[8,384,256]{2,1,0:T(8,128)(2,1)}, bf16[8,384,256]{2,1,0:T(8,128)(2,1)S(1)}, u32[]{:S(2)}, u32[]{:S(2)}) collective-permute-start(bf16[8,384,256]{2,1,0:T(8,128)(2,1)} %get-tuple-element.79), channel_id=1, source_target_pairs={{0,2},{2,0},{1,3},{3,1},{4,6},{6,4},{5,7},{7,5},{8,10},{10,8},{9,1... | collective-permute-start | bytes 4718600 | tf_op jit(solution)/shard_map/ppermute | solution.py:249
  115.2 6.4 %collective-permute-start.12 = (bf16[768,256]{1,0:T(8,128)(2,1)}, bf16[768,256]{1,0:T(8,128)(2,1)S(1)}, u32[]{:S(2)}, u32[]{:S(2)}) collective-permute-start(bf16[768,256]{1,0:T(8,128)(2,1)} %get-tuple-element.76), channel_id=1, source_target_pairs={{2,1},{1,2},{6,5},{5,6},{10,9},{9,10},{14,13},{13,14},{18,17},{17,... | collective-permute-start | bytes 1179656 | tf_op jit(solution)/shard_map/ppermute | solution.py:245
  121.6 1.9 %collective-permute-start.13 = (bf16[768,256]{1,0:T(8,128)(2,1)}, bf16[768,256]{1,0:T(8,128)(2,1)S(1)}, u32[]{:S(2)}, u32[]{:S(2)}) collective-permute-start(bf16[768,256]{1,0:T(8,128)(2,1)} %get-tuple-element.77), channel_id=1, source_target_pairs={{2,3},{1,0},{0,2},{3,1},{6,7},{5,4},{4,6},{7,5},{10,11},{9,8},{8,1... | collective-permute-start | bytes 1179656 | tf_op jit(solution)/shard_map/ppermute | solution.py:244
  123.6 0.7 all_to_all.12
  124.3 10.5 %all-to-all-start.1 = ((f32[64,1,24]{2,1,0:T(1,128)}), f32[64,1,24]{2,1,0:T(1,128)}, u32[]{:S(2)}, u32[]{:S(2)}) async-start(f32[64,1,24]{2,1,0:T(1,128)} %bitcast.22), calls=%async_computation.1 | async-start | bytes 65536 | tf_op jit(solution)/shard_map/all_to_all | solution.py:248
  134.8 0.7 copy-done.8
  135.6 2.8 %multiply_convert_fusion = (bf16[768,256]{1,0:T(8,128)(2,1)}, bf16[768,256]{1,0:T(8,128)(2,1)}) fusion(bf16[1,1,768,256]{3,2,1,0:T(8,128)(2,1)} %param.9, bf16[768,256]{1,0:T(8,128)(2,1)} %copy-done.8, f32[768,256]{1,0:T(8,128)} %copy-done.6, bf16[768,256]{1,0:T(8,128)(2,1)S(1)} %collective-permute-done.12, pred[]{:T(512)S(6)} %eq.67, f32[768]{0:T(1024)S(1)} %reduce, ...), kind=kLoop, calls=%fused_computation.15 | loop fusion | flops 3932160 | bytes 3148801 | tf_op jit(solution)/shard_map/convert_element_type | solution.py:254
  138.3 2.0 %shard_map.99 = bf16[8,384,256]{2,1,0:T(8,128)(2,1)} custom-call(s32[10]{0:T(128)S(1)} %stack.47.index, bf16[8,384,256]{2,1,0:T(8,128)(2,1)S(1)} %copy-done.2, bf16[8,384,256]{2,1,0:T(8,128)(2,1)S(1)} %collective-permute-done.14.theirs), custom_call_target="tpu_custom_call" | custom-call | flops 1000000 | bytes 5000000 | tf_op jit(solution)/shard_map/pallas_call | solution.py:129
  140.4 4.0 %all-to-all-done.1 = f32[64,1,24]{2,1,0:T(1,128)} async-done(((f32[64,1,24]{2,1,0:T(1,128)}), f32[64,1,24]{2,1,0:T(1,128)}, u32[]{:S(2)}, u32[]{:S(2)}) %all-to-all-start.1) | async-done | bytes 6176 | tf_op jit(solution)/shard_map/all_to_all | solution.py:248
  144.3 0.8 reduce_sum.31
  145.1 1.3 bitcast_divide_fusion
  (31 shorter events, 0.3 us)
Async XLA Ops:
  1.6 28.2 %copy-start.9 = (f32[1,1,768]{2,1,0:T(1,128)S(1)}, f32[1,1,768]{2,1,0:T(1,128)}, u32[]{:S(2)}) copy-start(f32[1,1,768]{2,1,0:T(1,128)} %param.8) | copy-start | bytes 9220
  2.3 27.6 %copy-start.7 = (bf16[1,1,768,256]{3,2,1,0:T(8,128)(2,1)S(1)}, bf16[1,1,768,256]{3,2,1,0:T(8,128)(2,1)}, u32[]{:S(2)}) copy-start(bf16[1,1,768,256]{3,2,1,0:T(8,128)(2,1)} %param.9) | copy-start | bytes 1179652
  2.4 14.3 %collective-permute-start = (bf16[192,194]{0,1:T(8,128)(2,1)S(1)}, bf16[192,194]{0,1:T(8,128)(2,1)S(1)}, u32[]{:S(2)}, u32[]{:S(2)}) collective-permute-start(bf16[192,194]{0,1:T(8,128)(2,1)S(1)} %pad_maximum_fusion), channel_id=1, source_target_pairs={{0,48},{1,50},{2,52},{3,54},{4,56},{5,58},{6,60},{7,62},{8,0},{9,2... | collective-permute-start | bytes 223496 | tf_op jit(solution)/shard_map/ppermute | solution.py:190
  10.7 7.8 %collective-permute-start.1 = (bf16[192,192]{0,1:T(8,128)(2,1)S(1)}, bf16[192,192]{0,1:T(8,128)(2,1)S(1)}, u32[]{:S(2)}, u32[]{:S(2)}) collective-permute-start(bf16[192,192]{0,1:T(8,128)(2,1)S(1)} %bitcast.61), channel_id=1, source_target_pairs={{0,52},{1,54},{2,48},{3,50},{4,60},{5,62},{6,56},{7,58},{8,4},{9,6... | collective-permute-start | bytes 221192 | tf_op jit(solution)/shard_map/ppermute | solution.py:191
  14.7 37.5 %collective-permute-start.5 = (bf16[3072,256]{1,0:T(8,128)(2,1)}, bf16[3072,256]{1,0:T(8,128)(2,1)S(1)}, u32[]{:S(2)}, u32[]{:S(2)}) collective-permute-start(bf16[3072,256]{1,0:T(8,128)(2,1)} %bitcast.41), channel_id=1, source_target_pairs={{0,2},{2,0},{1,3},{3,1},{4,6},{6,4},{5,7},{7,5},{8,10},{10,8},{9,1... | collective-permute-start | bytes 4718600 | tf_op jit(solution)/shard_map/ppermute | solution.py:207
  19.7 32.5 %copy-start = (bf16[1,3072,256]{2,1,0:T(8,128)(2,1)S(1)}, bf16[1,3072,256]{2,1,0:T(8,128)(2,1)}, u32[]{:S(2)}) copy-start(bf16[1,3072,256]{2,1,0:T(8,128)(2,1)} %param.11) | copy-start | bytes 4718596
  19.7 29.7 %all-to-all-start = ((bf16[8,96,384]{2,1,0:T(8,128)(2,1)}), bf16[8,96,384]{2,1,0:T(8,128)(2,1)}, u32[]{:S(2)}, u32[]{:S(2)}) async-start(bf16[8,96,384]{2,1,0:T(8,128)(2,1)} %bitcast.59), calls=%async_computation | async-start | bytes 1179648 | tf_op jit(solution)/shard_map/all_to_all | solution.py:197
  31.2 12.3 %collective-permute-start.2 = (bf16[768,256]{1,0:T(8,128)(2,1)S(1)}, bf16[768,256]{1,0:T(8,128)(2,1)S(1)}, u32[]{:S(2)}, u32[]{:S(2)}) collective-permute-start(bf16[768,256]{1,0:T(8,128)(2,1)S(1)} %fusion.1), channel_id=1, source_target_pairs={{0,0},{1,2},{2,1},{3,3},{4,4},{5,6},{6,5},{7,7},{8,8},{9,10},{10,9... | collective-permute-start | bytes 1179656 | tf_op jit(solution)/shard_map/ppermute | solution.py:205
  37.2 10.4 %collective-permute-start.3 = (bf16[768,256]{1,0:T(8,128)(2,1)S(1)}, bf16[768,256]{1,0:T(8,128)(2,1)S(1)}, u32[]{:S(2)}, u32[]{:S(2)}) collective-permute-start(bf16[768,256]{1,0:T(8,128)(2,1)S(1)} %fusion.1), channel_id=1, source_target_pairs={{0,1},{1,3},{2,0},{3,2},{4,5},{5,7},{6,4},{7,6},{8,9},{9,11},{10,8... | collective-permute-start | bytes 1179656 | tf_op jit(solution)/shard_map/ppermute | solution.py:206
  47.6 0.7 copy-start.3
  49.4 11.2 %collective-permute-start.4 = (bf16[768,384]{1,0:T(8,128)(2,1)}, bf16[768,384]{1,0:T(8,128)(2,1)}, u32[]{:S(2)}, u32[]{:S(2)}) collective-permute-start(bf16[768,384]{1,0:T(8,128)(2,1)} %bitcast.15.refs_0_), channel_id=1, source_target_pairs={{0,8},{2,58},{8,16},{10,2},{16,24},{18,10},{24,32},{26,18},{32,40}... | collective-permute-start | bytes 1769480 | tf_op jit(solution)/shard_map/ppermute | solution.py:219
  52.2 1.0 copy-start.4
  53.2 11.6 %copy-start.5 = (bf16[768,256]{1,0:T(8,128)(2,1)S(1)}, bf16[768,256]{1,0:T(8,128)(2,1)}, u32[]{:S(2)}) copy-start(bf16[768,256]{1,0:T(8,128)(2,1)} %copy-done.3) | copy-start | bytes 1179652
  56.4 13.6 %collective-permute-start.7 = (bf16[768,384]{1,0:T(8,128)(2,1)}, bf16[768,384]{1,0:T(8,128)(2,1)S(1)}, u32[]{:S(2)}, u32[]{:S(2)}) collective-permute-start(bf16[768,384]{1,0:T(8,128)(2,1)} %bitcast.15.refs_0_), channel_id=1, source_target_pairs={{0,56},{2,10},{8,0},{10,18},{16,8},{18,26},{24,16},{26,34},{32,24}... | collective-permute-start | bytes 1769480 | tf_op jit(solution)/shard_map/ppermute | solution.py:220
  60.7 14.2 %collective-permute-start.6 = (bf16[768,384]{1,0:T(8,128)(2,1)}, bf16[768,384]{1,0:T(8,128)(2,1)S(1)}, u32[]{:S(2)}, u32[]{:S(2)}) collective-permute-start(bf16[768,384]{1,0:T(8,128)(2,1)} %collective-permute-done.4.refs_0_), channel_id=1, source_target_pairs={{0,8},{2,58},{8,16},{10,2},{16,24},{18,10},{24,32},{26,18},{32,40}... | collective-permute-start | bytes 1769480 | tf_op jit(solution)/shard_map/ppermute | solution.py:219
  70.1 12.7 %collective-permute-start.9 = (bf16[768,384]{1,0:T(8,128)(2,1)S(1)}, bf16[768,384]{1,0:T(8,128)(2,1)S(1)}, u32[]{:S(2)}, u32[]{:S(2)}) collective-permute-start(bf16[768,384]{1,0:T(8,128)(2,1)S(1)} %collective-permute-done.7.refs_1_), channel_id=1, source_target_pairs={{0,56},{2,10},{8,0},{10,18},{16,8},{18,26},{24,16},{26,34},{32,24}... | collective-permute-start | bytes 1769480 | tf_op jit(solution)/shard_map/ppermute | solution.py:220
  74.9 15.7 %collective-permute-start.8 = (bf16[768,384]{1,0:T(8,128)(2,1)S(1)}, bf16[768,384]{1,0:T(8,128)(2,1)S(1)}, u32[]{:S(2)}, u32[]{:S(2)}) collective-permute-start(bf16[768,384]{1,0:T(8,128)(2,1)S(1)} %collective-permute-done.6.refs_0_), channel_id=1, source_target_pairs={{0,8},{2,58},{8,16},{10,2},{16,24},{18,10},{24,32},{26,18},{32,40}... | collective-permute-start | bytes 1769480 | tf_op jit(solution)/shard_map/ppermute | solution.py:219
  82.8 15.8 %collective-permute-start.11 = (bf16[768,384]{1,0:T(8,128)(2,1)S(1)}, bf16[768,384]{1,0:T(8,128)(2,1)S(1)}, u32[]{:S(2)}, u32[]{:S(2)}) collective-permute-start(bf16[768,384]{1,0:T(8,128)(2,1)S(1)} %collective-permute-done.9.refs_1_), channel_id=1, source_target_pairs={{0,56},{2,10},{8,0},{10,18},{16,8},{18,26},{24,16},{26,34},{32,24}... | collective-permute-start | bytes 1769480 | tf_op jit(solution)/shard_map/ppermute | solution.py:220
  90.6 16.9 %collective-permute-start.10 = (bf16[768,384]{1,0:T(8,128)(2,1)S(1)}, bf16[768,384]{1,0:T(8,128)(2,1)S(1)}, u32[]{:S(2)}, u32[]{:S(2)}) collective-permute-start(bf16[768,384]{1,0:T(8,128)(2,1)S(1)} %collective-permute-done.8.refs_0_), channel_id=1, source_target_pairs={{0,8},{2,58},{8,16},{10,2},{16,24},{18,10},{24,32},{26,18},{32,40}... | collective-permute-start | bytes 1769480 | tf_op jit(solution)/shard_map/ppermute | solution.py:219
  109.9 1.2 copy-start.1
  111.1 0.9 copy-start.6
  112.0 26.4 %collective-permute-start.14 = (bf16[8,384,256]{2,1,0:T(8,128)(2,1)}, bf16[8,384,256]{2,1,0:T(8,128)(2,1)S(1)}, u32[]{:S(2)}, u32[]{:S(2)}) collective-permute-start(bf16[8,384,256]{2,1,0:T(8,128)(2,1)} %get-tuple-element.79), channel_id=1, source_target_pairs={{0,2},{2,0},{1,3},{3,1},{4,6},{6,4},{5,7},{7,5},{8,10},{10,8},{9,1... | collective-permute-start | bytes 4718600 | tf_op jit(solution)/shard_map/ppermute | solution.py:249
  115.2 19.6 %collective-permute-start.12 = (bf16[768,256]{1,0:T(8,128)(2,1)}, bf16[768,256]{1,0:T(8,128)(2,1)S(1)}, u32[]{:S(2)}, u32[]{:S(2)}) collective-permute-start(bf16[768,256]{1,0:T(8,128)(2,1)} %get-tuple-element.76), channel_id=1, source_target_pairs={{2,1},{1,2},{6,5},{5,6},{10,9},{9,10},{14,13},{13,14},{18,17},{17,... | collective-permute-start | bytes 1179656 | tf_op jit(solution)/shard_map/ppermute | solution.py:245
  121.6 13.2 %collective-permute-start.13 = (bf16[768,256]{1,0:T(8,128)(2,1)}, bf16[768,256]{1,0:T(8,128)(2,1)S(1)}, u32[]{:S(2)}, u32[]{:S(2)}) collective-permute-start(bf16[768,256]{1,0:T(8,128)(2,1)} %get-tuple-element.77), channel_id=1, source_target_pairs={{2,3},{1,0},{0,2},{3,1},{6,7},{5,4},{4,6},{7,5},{10,11},{9,8},{8,1... | collective-permute-start | bytes 1179656 | tf_op jit(solution)/shard_map/ppermute | solution.py:244
  124.3 20.0 %all-to-all-start.1 = ((f32[64,1,24]{2,1,0:T(1,128)}), f32[64,1,24]{2,1,0:T(1,128)}, u32[]{:S(2)}, u32[]{:S(2)}) async-start(f32[64,1,24]{2,1,0:T(1,128)} %bitcast.22), calls=%async_computation.1 | async-start | bytes 65536 | tf_op jit(solution)/shard_map/all_to_all | solution.py:248
  134.8 0.7 copy-start.8
  135.6 2.8 %copy-start.2 = (bf16[8,384,256]{2,1,0:T(8,128)(2,1)S(1)}, bf16[8,384,256]{2,1,0:T(8,128)(2,1)}, u32[]{:S(2)}) copy-start(bf16[8,384,256]{2,1,0:T(8,128)(2,1)} %copy-done.1) | copy-start | bytes 4718596

commit v9 on v8

--- a/solution.py
+++ b/solution.py
@@ -95,8 +95,9 @@
         ins += list(held)
         specs += [whole(held[0]), pl.BlockSpec(memory_space=pl.ANY), pl.BlockSpec(memory_space=pl.ANY)]
     slot = pl.BlockSpec((blocks, chip, width), lambda i, idx: (start // blocks, 0, 0))
-    outs = [jax.ShapeDtypeStruct((rows, width if last else 2 * width), F32)]
-    outs += [jax.ShapeDtypeStruct((total, chip, width), BF)] * 2
+    sums = (rows, width if last else 2 * width)
+    outs = [pltpu.HBM(sums, F32) if last else jax.ShapeDtypeStruct(sums, F32)]
+    outs += [pltpu.HBM((total, chip, width), BF)] * 2
     extra = []
     if last:
         extra = [jax.ShapeDtypeStruct((rows, width), BF)] * 2 + [jax.ShapeDtypeStruct((2, rows), F32)]
@@ -106,7 +107,7 @@
             num_scalar_prefetch=1,
             grid=(1,),
             in_specs=specs,
-            out_specs=[whole(outs[0]), slot, slot] + [whole(o) for o in extra],
+            out_specs=[pl.BlockSpec(sums, lambda i, idx: (0, 0)), slot, slot] + [whole(o) for o in extra],
         ),
         out_shape=outs + extra,
         input_output_aliases=aliases,
@@ -138,6 +139,36 @@
         compiler_params=pltpu.CompilerParams(vmem_limit_bytes=16 * 1024 * 1024),
         cost_estimate=pl.CostEstimate(flops=1000000, bytes_accessed=5000000, transcendentals=0),
     )(index, mine, theirs)
+
+
+def finish_kernel(index, own, got_a, got_b, gate_ref, up_ref, combine_ref, out_gate, out_up):
+    flags = index.shape[0] - 2
+    total = jnp.where(index[flags] == 1, own[...], got_b[...].astype(F32)) + got_a[...].astype(F32)
+    gate = gate_ref[...].astype(F32)
+    sigma = jax.nn.sigmoid(gate)
+    weighted = combine_ref[:, :1] * total
+    out_gate[...] = (weighted * up_ref[...].astype(F32) * sigma * (1.0 + gate * (1.0 - sigma))).astype(BF)
+    out_up[...] = (weighted * (gate * sigma)).astype(BF)
+
+
+def finish(index, own, got_a, got_b, gate, up, combine_wide):
+    ins = (own, got_a, got_b, gate, up, combine_wide)
+
+    def whole(a):
+        return pl.BlockSpec(a.shape, lambda i, idx: (0, 0))
+
+    return pl.pallas_call(
+        finish_kernel,
+        grid_spec=pltpu.PrefetchScalarGridSpec(
+            num_scalar_prefetch=1,
+            grid=(1,),
+            in_specs=[whole(a) for a in ins],
+            out_specs=[whole(gate), whole(up)],
+        ),
+        out_shape=[pltpu.HBM(gate.shape, BF)] * 2,
+        compiler_params=pltpu.CompilerParams(vmem_limit_bytes=16 * 1024 * 1024),
+        cost_estimate=pl.CostEstimate(flops=3000000, bytes_accessed=3500000, transcendentals=200000),
+    )(index, *ins)
 
 
 def make_local(ny):
@@ -201,12 +232,17 @@
         weight_rows = combine[0, 0][:, None]
         sigma = jax.nn.sigmoid(gate)
         active = gate * sigma
+        combine_wide = jnp.broadcast_to(weight_rows, (rows, 128))
         scaled = (weight_rows * (active * upper)).astype(BF)
+        w_moved = lax.ppermute(w_down[0], "core", swap)
+
+        held_own = dp == core
+        share = rows // (ny * 4)
+        blk = (y * 2 + xlo) * 2 + core
+        combine_share = lax.dynamic_slice_in_dim(combine[0, 0], blk * share, share, 0)
+        combine_share, combine_wide, scaled = lax.optimization_barrier((combine_share, combine_wide, scaled))
         s_a = lax.ppermute(scaled, ("core", "dp"), scaled_a)
         s_b = lax.ppermute(scaled, ("core", "dp"), scaled_b)
-        w_moved = lax.ppermute(w_down[0], "core", swap)
-
-        held_own = dp == core
         turn = jnp.where(core == 0, -1, 1)
         shift_here = jnp.where(dp == 0, shift(0), shift(1))
         order = [0, 1]
@@ -244,18 +280,13 @@
         got_a = lax.ppermute(sum_a, ("core", "dp"), sums_a)
         got_b = lax.ppermute(sum_b, ("core", "dp"), sums_b)
         members = 2 * ny * 4
-        share = rows // (ny * 4)
         mix = lax.all_to_all(mix.reshape(members, share), ("dp", "y", "xlo", "core"), 0, 0, tiled=True)
         late = lax.ppermute(theirs, "core", swap)
         grad_weight = place(index, partner, mine, late).reshape(ny * chip, width)
-        grad_hidden = jnp.where(held_own, acc, got_b.astype(F32)) + got_a.astype(F32)
-        weighted = weight_rows * grad_hidden
-        grad_gate = (weighted * upper * sigma * (1.0 + gate * (1.0 - sigma))).astype(BF)
-        grad_upper = (weighted * active).astype(BF)
+        grad_gate, grad_upper = finish(index, acc, got_a, got_b, gate_saved[0, 0], up_saved[0, 0], combine_wide)
         mix, grad_gate, grad_upper, grad_weight = lax.optimization_barrier((mix, grad_gate, grad_upper, grad_weight))
         mix = jnp.sum(mix, axis=0)
-        blk = (y * 2 + xlo) * 2 + core
-        mix = mix / lax.dynamic_slice_in_dim(combine[0, 0], blk * share, share, 0)
+        mix = mix / combine_share
         return grad_gate[None, None], grad_upper[None, None], grad_weight[None], mix[None, None]
 
     return local

time: 147 us -> 146 us (level)
  waiting for transfers between devices: 34.1 us -> 29.3 us
  other arithmetic: 6.89 us -> 3.38 us
  Pallas kernels: 19.1 us -> 22.6 us
  local copies, waits for them, and re-layouts: 6.36 us -> 8.63 us
    ppermute x1, starting transfers between devices: 1.92 us -> 8.65 us  [local(): got_a = lax.ppermute(sum_a, ('core', 'dp'), sums_a)]
    ppermute x1, starting transfers between devices: 6.4 us -> 1.92 us  [local(): got_b = lax.ppermute(sum_b, ('core', 'dp'), sums_b)]
    all_to_all x1, waiting for transfers between devices: 3.95 us -> 0.45 us  [local(): lax.all_to_all(mix.reshape(members, share), ('dp', 'y', 'xlo', 'core'), 0...]
    pallas_call x0 -> x1, Pallas kernels: none -> 2.89 us  [finish(): pl.pallas_call(finish_kernel, grid_spec=pltpu.PrefetchScalarGridSpec(num_...]
    convert_element_type x1 -> x0, other arithmetic: 2.75 us -> none  [local(): grad_upper = (weighted * active).astype(BF)]
    all_to_all x1, starting transfers between devices: 10.5 us -> 8.79 us  [local(): lax.all_to_all(mix.reshape(members, share), ('dp', 'y', 'xlo', 'core'), 0...]
  transfers between devices with their start and end apart: 17 -> 17, of which waited for: 10 -> 10; matrix products, arithmetic and copies ran while one was open for 4% -> 3% of each run, Pallas kernels for 11% -> 14%
where the time goes in v9:
time: 146 us; the launch traced here: 145 us
  starting transfers between devices  78.4 us (54%)
  waiting for transfers between devices  29.3 us (20%)
  Pallas kernels  22.6 us (15%)
  local copies, waits for them, and re-layouts  8.63 us (6%)
  other arithmetic  3.38 us (2%)
    pallas_call x6, Pallas kernels, use(): pl.pallas_call(functools.partial(use_kernel, blocks, first, last), grid_s...  17.6 us
    ppermute x4, waiting for transfers between devices, local(): on_a = lambda v: lax.ppermute(v, ('y', 'core'), ring_a)  16.7 us
    ppermute x4, starting transfers between devices, local(): on_a = lambda v: lax.ppermute(v, ('y', 'core'), ring_a)  16.7 us
    all_to_all x1, starting transfers between devices, local(): lax.all_to_all(outgoing, 'expert', split_axis=0, concat_axis=0, tiled=True)  10.2 us
    all_to_all x1, starting transfers between devices, local(): lax.all_to_all(mix.reshape(members, share), ('dp', 'y', 'xlo', 'core'), 0...  8.79 us
    ppermute x1, starting transfers between devices, local(): got_a = lax.ppermute(sum_a, ('core', 'dp'), sums_a)  8.65 us
    ppermute x1, starting transfers between devices, local(): lax.ppermute(jnp.concatenate([cotangent[0], ids], axis=1), every, token_m...  8.33 us
    unnamed x21, local copies, waits for them, and re-layouts  6.85 us
  transfers between devices with their start and end apart: 17, of which 10 were waited for; matrix products, arithmetic and copies ran while one was open for 3% of the time, Pallas kernels for 14%

profile of v9, /device:TPU:1, one launch (start us, length us, event | category | flops | bytes accessed | tf_op | source)
XLA Modules:
  0.0 144.7 jit_solution(12218049567445880451)
XLA Ops:
  0.6 1.0 copy.31
  1.6 0.7 convert_bitcast_fusion
  2.3 8.3 %collective-permute-start = (bf16[192,194]{0,1:T(8,128)(2,1)S(1)}, bf16[192,194]{0,1:T(8,128)(2,1)S(1)}, u32[]{:S(2)}, u32[]{:S(2)}) collective-permute-start(bf16[192,194]{0,1:T(8,128)(2,1)S(1)} %pad_maximum_fusion), channel_id=1, source_target_pairs={{0,48},{1,50},{2,52},{3,54},{4,56},{5,58},{6,60},{7,62},{8,0},{9,2... | collective-permute-start | bytes 223496 | tf_op jit(solution)/shard_map/ppermute | solution.py:221
  10.7 4.0 %collective-permute-start.1 = (bf16[192,192]{0,1:T(8,128)(2,1)S(1)}, bf16[192,192]{0,1:T(8,128)(2,1)S(1)}, u32[]{:S(2)}, u32[]{:S(2)}) collective-permute-start(bf16[192,192]{0,1:T(8,128)(2,1)S(1)} %bitcast.57), channel_id=1, source_target_pairs={{0,52},{1,54},{2,48},{3,50},{4,60},{5,62},{6,56},{7,58},{8,4},{9,6... | collective-permute-start | bytes 221192 | tf_op jit(solution)/shard_map/ppermute | solution.py:222
  14.7 1.9 %collective-permute-start.5 = (bf16[3072,256]{1,0:T(8,128)(2,1)}, bf16[3072,256]{1,0:T(8,128)(2,1)S(1)}, u32[]{:S(2)}, u32[]{:S(2)}) collective-permute-start(bf16[3072,256]{1,0:T(8,128)(2,1)} %bitcast.35), channel_id=1, source_target_pairs={{0,2},{2,0},{1,3},{3,1},{4,6},{6,4},{5,7},{7,5},{8,10},{10,8},{9,1... | collective-permute-start | bytes 4718600 | tf_op jit(solution)/shard_map/ppermute | solution.py:237
  16.9 1.6 %collective-permute-done.1 = bf16[192,192]{0,1:T(8,128)(2,1)S(1)} collective-permute-done((bf16[192,192]{0,1:T(8,128)(2,1)S(1)}, bf16[192,192]{0,1:T(8,128)(2,1)S(1)}, u32[]{:S(2)}, u32[]{:S(2)}) %collective-permute-start.1) | collective-permute-done | bytes 73760 | tf_op jit(solution)/shard_map/ppermute | solution.py:222
  18.5 1.2 convolution_convert_fusion
  19.7 10.2 %all-to-all-start = ((bf16[8,96,384]{2,1,0:T(8,128)(2,1)}), bf16[8,96,384]{2,1,0:T(8,128)(2,1)}, u32[]{:S(2)}, u32[]{:S(2)}) async-start(bf16[8,96,384]{2,1,0:T(8,128)(2,1)} %bitcast.55), calls=%async_computation | async-start | bytes 1179648 | tf_op jit(solution)/shard_map/all_to_all | solution.py:228
  30.0 1.3 fusion.5
  31.2 0.9 broadcast_in_dim.13.combine_ref
  32.1 6.0 %collective-permute-start.2 = (bf16[768,256]{1,0:T(8,128)(2,1)S(1)}, bf16[768,256]{1,0:T(8,128)(2,1)S(1)}, u32[]{:S(2)}, u32[]{:S(2)}) collective-permute-start(bf16[768,256]{1,0:T(8,128)(2,1)S(1)} %fusion.5), channel_id=1, source_target_pairs={{0,0},{1,2},{2,1},{3,3},{4,4},{5,6},{6,5},{7,7},{8,8},{9,10},{10,9... | collective-permute-start | bytes 1179656 | tf_op jit(solution)/shard_map/ppermute | solution.py:244
  38.1 1.9 %collective-permute-start.3 = (bf16[768,256]{1,0:T(8,128)(2,1)S(1)}, bf16[768,256]{1,0:T(8,128)(2,1)S(1)}, u32[]{:S(2)}, u32[]{:S(2)}) collective-permute-start(bf16[768,256]{1,0:T(8,128)(2,1)S(1)} %fusion.5), channel_id=1, source_target_pairs={{0,1},{1,3},{2,0},{3,2},{4,5},{5,7},{6,4},{7,6},{8,9},{9,11},{10,8... | collective-permute-start | bytes 1179656 | tf_op jit(solution)/shard_map/ppermute | solution.py:245
  40.1 4.4 %collective-permute-done.2.refs_3_.refs_6_ = bf16[768,256]{1,0:T(8,128)(2,1)S(1)} collective-permute-done((bf16[768,256]{1,0:T(8,128)(2,1)S(1)}, bf16[768,256]{1,0:T(8,128)(2,1)S(1)}, u32[]{:S(2)}, u32[]{:S(2)}) %collective-permute-start.2) | collective-permute-done | bytes 393248 | tf_op jit(solution)/shard_map/ppermute | solution.py:244
  44.5 4.1 %collective-permute-done.3.refs_4_.refs_7_ = bf16[768,256]{1,0:T(8,128)(2,1)S(1)} collective-permute-done((bf16[768,256]{1,0:T(8,128)(2,1)S(1)}, bf16[768,256]{1,0:T(8,128)(2,1)S(1)}, u32[]{:S(2)}, u32[]{:S(2)}) %collective-permute-start.3) | collective-permute-done | bytes 393248 | tf_op jit(solution)/shard_map/ppermute | solution.py:245
  48.6 0.7 copy-done.2
  49.4 2.6 %collective-permute-start.4 = (bf16[768,384]{1,0:T(8,128)(2,1)}, bf16[768,384]{1,0:T(8,128)(2,1)}, u32[]{:S(2)}, u32[]{:S(2)}) collective-permute-start(bf16[768,384]{1,0:T(8,128)(2,1)} %bitcast.15.refs_0_), channel_id=1, source_target_pairs={{0,8},{2,58},{8,16},{10,2},{16,24},{18,10},{24,32},{26,18},{32,40}... | collective-permute-start | bytes 1769480 | tf_op jit(solution)/shard_map/ppermute | solution.py:255
  52.2 1.0 copy-done.3
  53.2 3.2 %shard_map.93 = (f32[768,512]{1,0:T(8,128)S(1)}, bf16[8,384,256]{2,1,0:T(8,128)(2,1)}, bf16[8,384,256]{2,1,0:T(8,128)(2,1)}) custom-call(s32[10]{0:T(128)S(1)} %stack.47.index, bf16[768,384]{1,0:T(8,128)(2,1)} %bitcast.15.refs_0_, bf16[8,384,256]{2,1,0:T(8,128)(2,1)S(1)} %bitcast.36, bf16[8,384,256]{2,1,0:T(8,128)(2,1)S(1)} %bitcast.44, ...), custom_call_target="tpu_custom_call" | custom-call | flops 603979776 | bytes 4000000 | tf_op jit(solution)/shard_map/pallas_call | solution.py:104
  56.5 2.7 %collective-permute-start.7 = (bf16[768,384]{1,0:T(8,128)(2,1)}, bf16[768,384]{1,0:T(8,128)(2,1)S(1)}, u32[]{:S(2)}, u32[]{:S(2)}) collective-permute-start(bf16[768,384]{1,0:T(8,128)(2,1)} %bitcast.15.refs_0_), channel_id=1, source_target_pairs={{0,56},{2,10},{8,0},{10,18},{16,8},{18,26},{24,16},{26,34},{32,24}... | collective-permute-start | bytes 1769480 | tf_op jit(solution)/shard_map/ppermute | solution.py:256
  59.1 1.5 %collective-permute-done.4.refs_0_ = bf16[768,384]{1,0:T(8,128)(2,1)} collective-permute-done((bf16[768,384]{1,0:T(8,128)(2,1)}, bf16[768,384]{1,0:T(8,128)(2,1)}, u32[]{:S(2)}, u32[]{:S(2)}) %collective-permute-start.4) | collective-permute-done | bytes 589856 | tf_op jit(solution)/shard_map/ppermute | solution.py:255
  60.7 4.2 %collective-permute-start.6 = (bf16[768,384]{1,0:T(8,128)(2,1)}, bf16[768,384]{1,0:T(8,128)(2,1)S(1)}, u32[]{:S(2)}, u32[]{:S(2)}) collective-permute-start(bf16[768,384]{1,0:T(8,128)(2,1)} %collective-permute-done.4.refs_0_), channel_id=1, source_target_pairs={{0,8},{2,58},{8,16},{10,2},{16,24},{18,10},{24,32},{26,18},{32,40}... | collective-permute-start | bytes 1769480 | tf_op jit(solution)/shard_map/ppermute | solution.py:255
  64.8 3.3 %shard_map.94 = (f32[768,512]{1,0:T(8,128)S(1)}, bf16[8,384,256]{2,1,0:T(8,128)(2,1)}, bf16[8,384,256]{2,1,0:T(8,128)(2,1)}) custom-call(s32[10]{0:T(128)S(1)} %stack.47.index, bf16[768,384]{1,0:T(8,128)(2,1)} %collective-permute-done.4.refs_0_, bf16[8,384,256]{2,1,0:T(8,128)(2,1)S(1)} %bitcast.37, ...), custom_call_target="tpu_custom_call", output_to_operand_aliasing={{0}: (6, {}), {1}: (7, {}), {2}: (8, {})} | custom-call | flops 603979776 | bytes 4000000 | tf_op jit(solution)/shard_map/pallas_call | solution.py:104
  68.2 2.0 %collective-permute-done.7.refs_1_ = bf16[768,384]{1,0:T(8,128)(2,1)S(1)} collective-permute-done((bf16[768,384]{1,0:T(8,128)(2,1)}, bf16[768,384]{1,0:T(8,128)(2,1)S(1)}, u32[]{:S(2)}, u32[]{:S(2)}) %collective-permute-start.7) | collective-permute-done | bytes 589856 | tf_op jit(solution)/shard_map/ppermute | solution.py:256
  70.2 1.9 %collective-permute-start.9 = (bf16[768,384]{1,0:T(8,128)(2,1)S(1)}, bf16[768,384]{1,0:T(8,128)(2,1)S(1)}, u32[]{:S(2)}, u32[]{:S(2)}) collective-permute-start(bf16[768,384]{1,0:T(8,128)(2,1)S(1)} %collective-permute-done.7.refs_1_), channel_id=1, source_target_pairs={{0,56},{2,10},{8,0},{10,18},{16,8},{18,26},{24,16},{26,34},{32,24}... | collective-permute-start | bytes 1769480 | tf_op jit(solution)/shard_map/ppermute | solution.py:256
  72.1 2.8 %collective-permute-done.6.refs_0_ = bf16[768,384]{1,0:T(8,128)(2,1)S(1)} collective-permute-done((bf16[768,384]{1,0:T(8,128)(2,1)}, bf16[768,384]{1,0:T(8,128)(2,1)S(1)}, u32[]{:S(2)}, u32[]{:S(2)}) %collective-permute-start.6) | collective-permute-done | bytes 589856 | tf_op jit(solution)/shard_map/ppermute | solution.py:255
  74.9 4.9 %collective-permute-start.8 = (bf16[768,384]{1,0:T(8,128)(2,1)S(1)}, bf16[768,384]{1,0:T(8,128)(2,1)S(1)}, u32[]{:S(2)}, u32[]{:S(2)}) collective-permute-start(bf16[768,384]{1,0:T(8,128)(2,1)S(1)} %collective-permute-done.6.refs_0_), channel_id=1, source_target_pairs={{0,8},{2,58},{8,16},{10,2},{16,24},{18,10},{24,32},{26,18},{32,40}... | collective-permute-start | bytes 1769480 | tf_op jit(solution)/shard_map/ppermute | solution.py:255
  79.8 3.1 %shard_map.95 = (f32[768,512]{1,0:T(8,128)S(1)}, bf16[8,384,256]{2,1,0:T(8,128)(2,1)}, bf16[8,384,256]{2,1,0:T(8,128)(2,1)}) custom-call(s32[10]{0:T(128)S(1)} %stack.47.index, bf16[768,384]{1,0:T(8,128)(2,1)S(1)} %collective-permute-done.6.refs_0_, ...), custom_call_target="tpu_custom_call", output_to_operand_aliasing={{0}: (9, {}), {1}: (10, {}), {2}: (11, {})} | custom-call | flops 1207959552 | bytes 8000000 | tf_op jit(solution)/shard_map/pallas_call | solution.py:104
  83.0 1.9 %collective-permute-start.11 = (bf16[768,384]{1,0:T(8,128)(2,1)S(1)}, bf16[768,384]{1,0:T(8,128)(2,1)S(1)}, u32[]{:S(2)}, u32[]{:S(2)}) collective-permute-start(bf16[768,384]{1,0:T(8,128)(2,1)S(1)} %collective-permute-done.9.refs_1_), channel_id=1, source_target_pairs={{0,56},{2,10},{8,0},{10,18},{16,8},{18,26},{24,16},{26,34},{32,24}... | collective-permute-start | bytes 1769480 | tf_op jit(solution)/shard_map/ppermute | solution.py:256
  84.9 5.8 %collective-permute-done.8.refs_0_ = bf16[768,384]{1,0:T(8,128)(2,1)S(1)} collective-permute-done((bf16[768,384]{1,0:T(8,128)(2,1)S(1)}, bf16[768,384]{1,0:T(8,128)(2,1)S(1)}, u32[]{:S(2)}, u32[]{:S(2)}) %collective-permute-start.8) | collective-permute-done | bytes 589856 | tf_op jit(solution)/shard_map/ppermute | solution.py:255
  90.7 5.0 %collective-permute-start.10 = (bf16[768,384]{1,0:T(8,128)(2,1)S(1)}, bf16[768,384]{1,0:T(8,128)(2,1)S(1)}, u32[]{:S(2)}, u32[]{:S(2)}) collective-permute-start(bf16[768,384]{1,0:T(8,128)(2,1)S(1)} %collective-permute-done.8.refs_0_), channel_id=1, source_target_pairs={{0,8},{2,58},{8,16},{10,2},{16,24},{18,10},{24,32},{26,18},{32,40}... | collective-permute-start | bytes 1769480 | tf_op jit(solution)/shard_map/ppermute | solution.py:255
  95.7 3.1 %shard_map.96 = (f32[768,512]{1,0:T(8,128)S(1)}, bf16[8,384,256]{2,1,0:T(8,128)(2,1)}, bf16[8,384,256]{2,1,0:T(8,128)(2,1)}) custom-call(s32[10]{0:T(128)S(1)} %stack.47.index, bf16[768,384]{1,0:T(8,128)(2,1)S(1)} %collective-permute-done.8.refs_0_, ...), custom_call_target="tpu_custom_call", output_to_operand_aliasing={{0}: (9, {}), {1}: (10, {}), {2}: (11, {})} | custom-call | flops 1207959552 | bytes 8000000 | tf_op jit(solution)/shard_map/pallas_call | solution.py:104
  98.9 2.3 %shard_map.97 = (f32[768,512]{1,0:T(8,128)S(1)}, bf16[8,384,256]{2,1,0:T(8,128)(2,1)}, bf16[8,384,256]{2,1,0:T(8,128)(2,1)}) custom-call(s32[10]{0:T(128)S(1)} %stack.47.index, bf16[768,384]{1,0:T(8,128)(2,1)S(1)} %collective-permute-done.11.refs_0_, bf16[8,384,256]{2,1,0:T(8,128)(2,1)S(1)} %bitcast.42, ...), custom_call_target="tpu_custom_call", output_to_operand_aliasing={{0}: (6, {}), {1}: (7, {}), {2}: (8, {})} | custom-call | flops 603979776 | bytes 4000000 | tf_op jit(solution)/shard_map/pallas_call | solution.py:104
  101.2 6.5 %collective-permute-done.10.refs_0_ = bf16[768,384]{1,0:T(8,128)(2,1)S(1)} collective-permute-done((bf16[768,384]{1,0:T(8,128)(2,1)S(1)}, bf16[768,384]{1,0:T(8,128)(2,1)S(1)}, u32[]{:S(2)}, u32[]{:S(2)}) %collective-permute-start.10) | collective-permute-done | bytes 589856 | tf_op jit(solution)/shard_map/ppermute | solution.py:255
  107.7 2.5 %shard_map.98 = (f32[768,256]{1,0:T(8,128)}, bf16[8,384,256]{2,1,0:T(8,128)(2,1)}, bf16[8,384,256]{2,1,0:T(8,128)(2,1)}, bf16[768,256]{1,0:T(8,128)(2,1)}, bf16[...) custom-call(s32[10]{0:T(128)S(1)} %stack.47.index, ...), custom_call_target="tpu_custom_call", output_to_operand_aliasing={{1}: (7, {}), {2}: (8, {})} | custom-call | flops 603979776 | bytes 4000000 | tf_op jit(solution)/shard_map/pallas_call | solution.py:104
  110.2 3.5 %collective-permute-start.14 = (bf16[8,384,256]{2,1,0:T(8,128)(2,1)}, bf16[8,384,256]{2,1,0:T(8,128)(2,1)S(1)}, u32[]{:S(2)}, u32[]{:S(2)}) collective-permute-start(bf16[8,384,256]{2,1,0:T(8,128)(2,1)} %get-tuple-element.88), channel_id=1, source_target_pairs={{0,2},{2,0},{1,3},{3,1},{4,6},{6,4},{5,7},{7,5},{8,10},{10,8},{9,1... | collective-permute-start | bytes 4718600 | tf_op jit(solution)/shard_map/ppermute | solution.py:284
  113.7 8.7 %collective-permute-start.12 = (bf16[768,256]{1,0:T(8,128)(2,1)}, bf16[768,256]{1,0:T(8,128)(2,1)S(1)}, u32[]{:S(2)}, u32[]{:S(2)}) collective-permute-start(bf16[768,256]{1,0:T(8,128)(2,1)} %get-tuple-element.82), channel_id=1, source_target_pairs={{2,3},{1,0},{0,2},{3,1},{6,7},{5,4},{4,6},{7,5},{10,11},{9,8},{8,1... | collective-permute-start | bytes 1179656 | tf_op jit(solution)/shard_map/ppermute | solution.py:280
  122.4 1.9 %collective-permute-start.13 = (bf16[768,256]{1,0:T(8,128)(2,1)}, bf16[768,256]{1,0:T(8,128)(2,1)}, u32[]{:S(2)}, u32[]{:S(2)}) collective-permute-start(bf16[768,256]{1,0:T(8,128)(2,1)} %get-tuple-element.83), channel_id=1, source_target_pairs={{2,1},{1,2},{6,5},{5,6},{10,9},{9,10},{14,13},{13,14},{18,17},{17,... | collective-permute-start | bytes 1179656 | tf_op jit(solution)/shard_map/ppermute | solution.py:281
  124.3 0.7 all_to_all.12
  125.0 8.8 %all-to-all-start.1 = ((f32[64,1,24]{2,1,0:T(1,128)}), f32[64,1,24]{2,1,0:T(1,128)}, u32[]{:S(2)}, u32[]{:S(2)}) async-start(f32[64,1,24]{2,1,0:T(1,128)} %bitcast.58), calls=%async_computation.1 | async-start | bytes 65536 | tf_op jit(solution)/shard_map/all_to_all | solution.py:283
  133.8 1.0 copy-done.4
  134.8 1.0 copy-done.6
  135.8 1.0 copy-done.7
  136.8 1.1 copy-done.8
  138.0 2.9 %shard_map.99 = (bf16[768,256]{1,0:T(8,128)(2,1)}, bf16[768,256]{1,0:T(8,128)(2,1)}) custom-call(s32[10]{0:T(128)S(1)} %stack.47.index, f32[768,256]{1,0:T(8,128)S(1)} %copy-done.8, bf16[768,256]{1,0:T(8,128)(2,1)S(1)} %collective-permute-done.12.got_a, bf16[768,256]{1,0:T(8,128)(2,1)} %collective-permute-done.13.got_b, bf16[768,256]{1,0:T(8,128)(2,1)S(1)} %bitcast.53, ...), custom_call_target="tpu_custom_call" | custom-call | flops 3000000 | bytes 3500000 | tf_op jit(solution)/shard_map/pallas_call | solution.py:160
  140.9 2.0 %shard_map.100 = bf16[8,384,256]{2,1,0:T(8,128)(2,1)} custom-call(s32[10]{0:T(128)S(1)} %stack.47.index, bf16[8,384,256]{2,1,0:T(8,128)(2,1)S(1)} %copy-done.1, bf16[8,384,256]{2,1,0:T(8,128)(2,1)S(1)} %collective-permute-done.14.theirs), custom_call_target="tpu_custom_call" | custom-call | flops 1000000 | bytes 5000000 | tf_op jit(solution)/shard_map/pallas_call | solution.py:130
  142.9 0.4 all-to-all-done.1
  143.3 0.8 reduce_sum.29
  144.1 0.5 divide_bitcast_fusion
  (33 shorter events, 0.6 us)
Async XLA Ops:
  2.3 27.5 %copy-start.9 = (f32[1,1,768]{2,1,0:T(1,128)S(1)}, f32[1,1,768]{2,1,0:T(1,128)}, u32[]{:S(2)}) copy-start(f32[1,1,768]{2,1,0:T(1,128)} %param.8) | copy-start | bytes 9220
  2.3 27.6 %copy-start.5 = (bf16[1,1,768,256]{3,2,1,0:T(8,128)(2,1)S(1)}, bf16[1,1,768,256]{3,2,1,0:T(8,128)(2,1)}, u32[]{:S(2)}) copy-start(bf16[1,1,768,256]{3,2,1,0:T(8,128)(2,1)} %param.10) | copy-start | bytes 1179652
  2.3 14.3 %collective-permute-start = (bf16[192,194]{0,1:T(8,128)(2,1)S(1)}, bf16[192,194]{0,1:T(8,128)(2,1)S(1)}, u32[]{:S(2)}, u32[]{:S(2)}) collective-permute-start(bf16[192,194]{0,1:T(8,128)(2,1)S(1)} %pad_maximum_fusion), channel_id=1, source_target_pairs={{0,48},{1,50},{2,52},{3,54},{4,56},{5,58},{6,60},{7,62},{8,0},{9,2... | collective-permute-start | bytes 223496 | tf_op jit(solution)/shard_map/ppermute | solution.py:221
  10.7 7.8 %collective-permute-start.1 = (bf16[192,192]{0,1:T(8,128)(2,1)S(1)}, bf16[192,192]{0,1:T(8,128)(2,1)S(1)}, u32[]{:S(2)}, u32[]{:S(2)}) collective-permute-start(bf16[192,192]{0,1:T(8,128)(2,1)S(1)} %bitcast.57), channel_id=1, source_target_pairs={{0,52},{1,54},{2,48},{3,50},{4,60},{5,62},{6,56},{7,58},{8,4},{9,6... | collective-permute-start | bytes 221192 | tf_op jit(solution)/shard_map/ppermute | solution.py:222
  14.7 37.5 %collective-permute-start.5 = (bf16[3072,256]{1,0:T(8,128)(2,1)}, bf16[3072,256]{1,0:T(8,128)(2,1)S(1)}, u32[]{:S(2)}, u32[]{:S(2)}) collective-permute-start(bf16[3072,256]{1,0:T(8,128)(2,1)} %bitcast.35), channel_id=1, source_target_pairs={{0,2},{2,0},{1,3},{3,1},{4,6},{6,4},{5,7},{7,5},{8,10},{10,8},{9,1... | collective-permute-start | bytes 4718600 | tf_op jit(solution)/shard_map/ppermute | solution.py:237
  19.7 32.5 %copy-start = (bf16[1,3072,256]{2,1,0:T(8,128)(2,1)S(1)}, bf16[1,3072,256]{2,1,0:T(8,128)(2,1)}, u32[]{:S(2)}) copy-start(bf16[1,3072,256]{2,1,0:T(8,128)(2,1)} %param.11) | copy-start | bytes 4718596
  19.7 29.7 %all-to-all-start = ((bf16[8,96,384]{2,1,0:T(8,128)(2,1)}), bf16[8,96,384]{2,1,0:T(8,128)(2,1)}, u32[]{:S(2)}, u32[]{:S(2)}) async-start(bf16[8,96,384]{2,1,0:T(8,128)(2,1)} %bitcast.55), calls=%async_computation | async-start | bytes 1179648 | tf_op jit(solution)/shard_map/all_to_all | solution.py:228
  32.1 12.3 %collective-permute-start.2 = (bf16[768,256]{1,0:T(8,128)(2,1)S(1)}, bf16[768,256]{1,0:T(8,128)(2,1)S(1)}, u32[]{:S(2)}, u32[]{:S(2)}) collective-permute-start(bf16[768,256]{1,0:T(8,128)(2,1)S(1)} %fusion.5), channel_id=1, source_target_pairs={{0,0},{1,2},{2,1},{3,3},{4,4},{5,6},{6,5},{7,7},{8,8},{9,10},{10,9... | collective-permute-start | bytes 1179656 | tf_op jit(solution)/shard_map/ppermute | solution.py:244
  38.1 10.4 %collective-permute-start.3 = (bf16[768,256]{1,0:T(8,128)(2,1)S(1)}, bf16[768,256]{1,0:T(8,128)(2,1)S(1)}, u32[]{:S(2)}, u32[]{:S(2)}) collective-permute-start(bf16[768,256]{1,0:T(8,128)(2,1)S(1)} %fusion.5), channel_id=1, source_target_pairs={{0,1},{1,3},{2,0},{3,2},{4,5},{5,7},{6,4},{7,6},{8,9},{9,11},{10,8... | collective-permute-start | bytes 1179656 | tf_op jit(solution)/shard_map/ppermute | solution.py:245
  48.6 0.7 copy-start.2
  49.4 11.2 %collective-permute-start.4 = (bf16[768,384]{1,0:T(8,128)(2,1)}, bf16[768,384]{1,0:T(8,128)(2,1)}, u32[]{:S(2)}, u32[]{:S(2)}) collective-permute-start(bf16[768,384]{1,0:T(8,128)(2,1)} %bitcast.15.refs_0_), channel_id=1, source_target_pairs={{0,8},{2,58},{8,16},{10,2},{16,24},{18,10},{24,32},{26,18},{32,40}... | collective-permute-start | bytes 1769480 | tf_op jit(solution)/shard_map/ppermute | solution.py:255
  52.2 1.0 copy-start.3
  56.5 13.7 %collective-permute-start.7 = (bf16[768,384]{1,0:T(8,128)(2,1)}, bf16[768,384]{1,0:T(8,128)(2,1)S(1)}, u32[]{:S(2)}, u32[]{:S(2)}) collective-permute-start(bf16[768,384]{1,0:T(8,128)(2,1)} %bitcast.15.refs_0_), channel_id=1, source_target_pairs={{0,56},{2,10},{8,0},{10,18},{16,8},{18,26},{24,16},{26,34},{32,24}... | collective-permute-start | bytes 1769480 | tf_op jit(solution)/shard_map/ppermute | solution.py:256
  60.7 14.3 %collective-permute-start.6 = (bf16[768,384]{1,0:T(8,128)(2,1)}, bf16[768,384]{1,0:T(8,128)(2,1)S(1)}, u32[]{:S(2)}, u32[]{:S(2)}) collective-permute-start(bf16[768,384]{1,0:T(8,128)(2,1)} %collective-permute-done.4.refs_0_), channel_id=1, source_target_pairs={{0,8},{2,58},{8,16},{10,2},{16,24},{18,10},{24,32},{26,18},{32,40}... | collective-permute-start | bytes 1769480 | tf_op jit(solution)/shard_map/ppermute | solution.py:255
  70.2 12.8 %collective-permute-start.9 = (bf16[768,384]{1,0:T(8,128)(2,1)S(1)}, bf16[768,384]{1,0:T(8,128)(2,1)S(1)}, u32[]{:S(2)}, u32[]{:S(2)}) collective-permute-start(bf16[768,384]{1,0:T(8,128)(2,1)S(1)} %collective-permute-done.7.refs_1_), channel_id=1, source_target_pairs={{0,56},{2,10},{8,0},{10,18},{16,8},{18,26},{24,16},{26,34},{32,24}... | collective-permute-start | bytes 1769480 | tf_op jit(solution)/shard_map/ppermute | solution.py:256
  74.9 15.8 %collective-permute-start.8 = (bf16[768,384]{1,0:T(8,128)(2,1)S(1)}, bf16[768,384]{1,0:T(8,128)(2,1)S(1)}, u32[]{:S(2)}, u32[]{:S(2)}) collective-permute-start(bf16[768,384]{1,0:T(8,128)(2,1)S(1)} %collective-permute-done.6.refs_0_), channel_id=1, source_target_pairs={{0,8},{2,58},{8,16},{10,2},{16,24},{18,10},{24,32},{26,18},{32,40}... | collective-permute-start | bytes 1769480 | tf_op jit(solution)/shard_map/ppermute | solution.py:255
  83.0 15.9 %collective-permute-start.11 = (bf16[768,384]{1,0:T(8,128)(2,1)S(1)}, bf16[768,384]{1,0:T(8,128)(2,1)S(1)}, u32[]{:S(2)}, u32[]{:S(2)}) collective-permute-start(bf16[768,384]{1,0:T(8,128)(2,1)S(1)} %collective-permute-done.9.refs_1_), channel_id=1, source_target_pairs={{0,56},{2,10},{8,0},{10,18},{16,8},{18,26},{24,16},{26,34},{32,24}... | collective-permute-start | bytes 1769480 | tf_op jit(solution)/shard_map/ppermute | solution.py:256
  90.7 17.0 %collective-permute-start.10 = (bf16[768,384]{1,0:T(8,128)(2,1)S(1)}, bf16[768,384]{1,0:T(8,128)(2,1)S(1)}, u32[]{:S(2)}, u32[]{:S(2)}) collective-permute-start(bf16[768,384]{1,0:T(8,128)(2,1)S(1)} %collective-permute-done.8.refs_0_), channel_id=1, source_target_pairs={{0,8},{2,58},{8,16},{10,2},{16,24},{18,10},{24,32},{26,18},{32,40}... | collective-permute-start | bytes 1769480 | tf_op jit(solution)/shard_map/ppermute | solution.py:255
  110.2 30.7 %copy-start.1 = (bf16[8,384,256]{2,1,0:T(8,128)(2,1)S(1)}, bf16[8,384,256]{2,1,0:T(8,128)(2,1)}, u32[]{:S(2)}) copy-start(bf16[8,384,256]{2,1,0:T(8,128)(2,1)} %get-tuple-element.87.mine) | copy-start | bytes 4718596
  110.2 30.7 %collective-permute-start.14 = (bf16[8,384,256]{2,1,0:T(8,128)(2,1)}, bf16[8,384,256]{2,1,0:T(8,128)(2,1)S(1)}, u32[]{:S(2)}, u32[]{:S(2)}) collective-permute-start(bf16[8,384,256]{2,1,0:T(8,128)(2,1)} %get-tuple-element.88), channel_id=1, source_target_pairs={{0,2},{2,0},{1,3},{3,1},{4,6},{6,4},{5,7},{7,5},{8,10},{10,8},{9,1... | collective-permute-start | bytes 4718600 | tf_op jit(solution)/shard_map/ppermute | solution.py:284
  113.7 20.1 %collective-permute-start.12 = (bf16[768,256]{1,0:T(8,128)(2,1)}, bf16[768,256]{1,0:T(8,128)(2,1)S(1)}, u32[]{:S(2)}, u32[]{:S(2)}) collective-permute-start(bf16[768,256]{1,0:T(8,128)(2,1)} %get-tuple-element.82), channel_id=1, source_target_pairs={{2,3},{1,0},{0,2},{3,1},{6,7},{5,4},{4,6},{7,5},{10,11},{9,8},{8,1... | collective-permute-start | bytes 1179656 | tf_op jit(solution)/shard_map/ppermute | solution.py:280
  122.4 11.4 %collective-permute-start.13 = (bf16[768,256]{1,0:T(8,128)(2,1)}, bf16[768,256]{1,0:T(8,128)(2,1)}, u32[]{:S(2)}, u32[]{:S(2)}) collective-permute-start(bf16[768,256]{1,0:T(8,128)(2,1)} %get-tuple-element.83), channel_id=1, source_target_pairs={{2,1},{1,2},{6,5},{5,6},{10,9},{9,10},{14,13},{13,14},{18,17},{17,... | collective-permute-start | bytes 1179656 | tf_op jit(solution)/shard_map/ppermute | solution.py:281
  125.0 18.3 %all-to-all-start.1 = ((f32[64,1,24]{2,1,0:T(1,128)}), f32[64,1,24]{2,1,0:T(1,128)}, u32[]{:S(2)}, u32[]{:S(2)}) async-start(f32[64,1,24]{2,1,0:T(1,128)} %bitcast.58), calls=%async_computation.1 | async-start | bytes 65536 | tf_op jit(solution)/shard_map/all_to_all | solution.py:283
  133.8 1.0 copy-start.4
  134.8 1.0 copy-start.6
  135.8 1.0 copy-start.7
  136.8 1.1 copy-start.8

commit v10 on v9

--- a/solution.py
+++ b/solution.py
@@ -127,6 +127,7 @@
     def whole(a):
         return pl.BlockSpec(a.shape, lambda i, idx: (0, 0, 0))
 
+    mine = pltpu.with_memory_space_constraint(mine, pltpu.HBM)
     return pl.pallas_call(
         functools.partial(place_kernel, tuple(partner)),
         grid_spec=pltpu.PrefetchScalarGridSpec(
@@ -152,7 +153,8 @@
 
 
 def finish(index, own, got_a, got_b, gate, up, combine_wide):
-    ins = (own, got_a, got_b, gate, up, combine_wide)
+    in_hbm = lambda a: pltpu.with_memory_space_constraint(a, pltpu.HBM)
+    ins = (in_hbm(own), got_a, got_b, in_hbm(gate), in_hbm(up), in_hbm(combine_wide))
 
     def whole(a):
         return pl.BlockSpec(a.shape, lambda i, idx: (0, 0))
@@ -245,10 +247,10 @@
         s_b = lax.ppermute(scaled, ("core", "dp"), scaled_b)
         turn = jnp.where(core == 0, -1, 1)
         shift_here = jnp.where(dp == 0, shift(0), shift(1))
-        order = [0, 1]
-        for step in range(2, half_y):
-            order += [step, 1 - step]
-        order += [1 - half_y, half_y]
+        order = []
+        for step in range(1, half_y):
+            order += [step, -step]
+        order += [0, half_y]
         partner = [order.index(-o) if abs(o) < half_y else order.index(o) for o in order]
         spots = [(y + turn * o + 2 * ny - shift_here) % ny for o in order]
         index = jnp.stack(spots + [held_own.astype(jnp.int32), core]).astype(jnp.int32)
@@ -258,24 +260,22 @@
         block, s_a, s_b = lax.optimization_barrier((block, s_a, s_b))
         a = on_a(block)
         args = (w_down[0].reshape(ny, chip, width), w_moved.reshape(ny, chip, width), s_a, s_b)
-        held = use([block], index, 0, *args, None)
+        held = use([block], index, ny - 2, *args, None)
         block_b, acc = lax.optimization_barrier((block, held[0]))
         held = (acc, *held[1:])
         b = on_b(block_b)
-        waiting, start = [a], 1
-        for step in range(2, half_y + 1):
-            a, acc = lax.optimization_barrier((a, held[0]))
-            held = (acc, *held[1:])
-            a = on_a(a)
-            held = use(waiting, index, start, *args, held)
-            start += len(waiting)
-            waiting = [a, b]
-            if step < half_y:
-                b, acc = lax.optimization_barrier((b, held[0]))
+        a_next = on_a(a)
+        for step in range(1, half_y):
+            blocks = [a, b]
+            a = a_next
+            if step < half_y - 1:
+                b = on_b(b)
+            held = use(blocks, index, 2 * (step - 1), *args, held)
+            if step < half_y - 1:
+                a, acc = lax.optimization_barrier((a, held[0]))
                 held = (acc, *held[1:])
-                b = on_b(b)
-        held = use([b], index, start, *args, held)
-        acc, mine, theirs, sum_a, sum_b, mix = use([a], index, start + 1, *args, held, last=True)
+                a_next = on_a(a)
+        acc, mine, theirs, sum_a, sum_b, mix = use([a], index, ny - 1, *args, held, last=True)
 
         got_a = lax.ppermute(sum_a, ("core", "dp"), sums_a)
         got_b = lax.ppermute(sum_b, ("core", "dp"), sums_b)

time: 146 us -> 145 us (level)
  local copies, waits for them, and re-layouts: 8.63 us -> 4.53 us
  waiting for transfers between devices: 29.3 us -> 32.1 us
  starting transfers between devices: 78.4 us -> 79.9 us
    ppermute x3, waiting for transfers between devices: 2.01 us -> 11 us  [local(): on_b = lambda v: lax.ppermute(v, ('y', 'core'), ring_b)]
    ppermute x4, waiting for transfers between devices: 16.7 us -> 8.25 us  [local(): on_a = lambda v: lax.ppermute(v, ('y', 'core'), ring_a)]
    ppermute x1, starting transfers between devices: 3.51 us -> 8.35 us  [local(): late = lax.ppermute(theirs, 'core', swap)]
    unnamed x21 -> x11, local copies, waits for them, and re-layouts: 6.85 us -> 2.74 us
    ppermute x1, starting transfers between devices: 8.65 us -> 5.92 us  [local(): got_a = lax.ppermute(sum_a, ('core', 'dp'), sums_a)]
    all_to_all x1, waiting for transfers between devices: 0.45 us -> 2.52 us  [local(): lax.all_to_all(mix.reshape(members, share), ('dp', 'y', 'xlo', 'core'), 0...]
    pallas_call x6 -> x5, Pallas kernels: 17.6 us -> 16.2 us  [use(): pl.pallas_call(functools.partial(use_kernel, blocks, first, last), grid_s...]
  transfers between devices with their start and end apart: 17 -> 17, of which waited for: 10 -> 12; matrix products, arithmetic and copies ran while one was open for 3% -> 3% of each run, Pallas kernels for 14% -> 14%
where the time goes in v10:
time: 145 us; the launch traced here: 144 us
  starting transfers between devices  79.9 us (55%)
  waiting for transfers between devices  32.1 us (22%)
  Pallas kernels  23 us (16%)
  local copies, waits for them, and re-layouts  4.53 us (3%)
  other arithmetic  2.62 us (2%)
    ppermute x4, starting transfers between devices, local(): on_a = lambda v: lax.ppermute(v, ('y', 'core'), ring_a)  16.9 us
    pallas_call x5, Pallas kernels, use(): pl.pallas_call(functools.partial(use_kernel, blocks, first, last), grid_s...  16.2 us
    ppermute x3, waiting for transfers between devices, local(): on_b = lambda v: lax.ppermute(v, ('y', 'core'), ring_b)  11 us
    all_to_all x1, starting transfers between devices, local(): lax.all_to_all(outgoing, 'expert', split_axis=0, concat_axis=0, tiled=True)  10.2 us
    ppermute x1, starting transfers between devices, local(): late = lax.ppermute(theirs, 'core', swap)  8.35 us
    ppermute x1, starting transfers between devices, local(): lax.ppermute(jnp.concatenate([cotangent[0], ids], axis=1), every, token_m...  8.33 us
    ppermute x4, waiting for transfers between devices, local(): on_a = lambda v: lax.ppermute(v, ('y', 'core'), ring_a)  8.25 us
    all_to_all x1, starting transfers between devices, local(): lax.all_to_all(mix.reshape(members, share), ('dp', 'y', 'xlo', 'core'), 0...  8 us
  transfers between devices with their start and end apart: 17, of which 12 were waited for; matrix products, arithmetic and copies ran while one was open for 3% of the time, Pallas kernels for 14%

profile of v10, /device:TPU:1, one launch (start us, length us, event | category | flops | bytes accessed | tf_op | source)
XLA Modules:
  0.0 144.4 jit_solution(16997847991903524668)
XLA Ops:
  0.6 1.0 copy.28
  1.6 0.7 convert_bitcast_fusion
  2.3 8.3 %collective-permute-start = (bf16[192,194]{0,1:T(8,128)(2,1)S(1)}, bf16[192,194]{0,1:T(8,128)(2,1)S(1)}, u32[]{:S(2)}, u32[]{:S(2)}) collective-permute-start(bf16[192,194]{0,1:T(8,128)(2,1)S(1)} %pad_maximum_fusion), channel_id=1, source_target_pairs={{0,48},{1,50},{2,52},{3,54},{4,56},{5,58},{6,60},{7,62},{8,0},{9,2... | collective-permute-start | bytes 223496 | tf_op jit(solution)/shard_map/ppermute | solution.py:223
  10.7 4.0 %collective-permute-start.1 = (bf16[192,192]{0,1:T(8,128)(2,1)S(1)}, bf16[192,192]{0,1:T(8,128)(2,1)S(1)}, u32[]{:S(2)}, u32[]{:S(2)}) collective-permute-start(bf16[192,192]{0,1:T(8,128)(2,1)S(1)} %bitcast.57), channel_id=1, source_target_pairs={{0,52},{1,54},{2,48},{3,50},{4,60},{5,62},{6,56},{7,58},{8,4},{9,6... | collective-permute-start | bytes 221192 | tf_op jit(solution)/shard_map/ppermute | solution.py:224
  14.7 1.9 %collective-permute-start.6 = (bf16[3072,256]{1,0:T(8,128)(2,1)}, bf16[3072,256]{1,0:T(8,128)(2,1)S(1)}, u32[]{:S(2)}, u32[]{:S(2)}) collective-permute-start(bf16[3072,256]{1,0:T(8,128)(2,1)} %bitcast.35), channel_id=1, source_target_pairs={{0,2},{2,0},{1,3},{3,1},{4,6},{6,4},{5,7},{7,5},{8,10},{10,8},{9,1... | collective-permute-start | bytes 4718600 | tf_op jit(solution)/shard_map/ppermute | solution.py:239
  16.7 0.1 fusion.13
  16.9 1.6 %collective-permute-done.1 = bf16[192,192]{0,1:T(8,128)(2,1)S(1)} collective-permute-done((bf16[192,192]{0,1:T(8,128)(2,1)S(1)}, bf16[192,192]{0,1:T(8,128)(2,1)S(1)}, u32[]{:S(2)}, u32[]{:S(2)}) %collective-permute-start.1) | collective-permute-done | bytes 73760 | tf_op jit(solution)/shard_map/ppermute | solution.py:224
  18.5 1.2 convolution_convert_fusion
  19.7 10.2 %all-to-all-start = ((bf16[8,96,384]{2,1,0:T(8,128)(2,1)}), bf16[8,96,384]{2,1,0:T(8,128)(2,1)}, u32[]{:S(2)}, u32[]{:S(2)}) async-start(bf16[8,96,384]{2,1,0:T(8,128)(2,1)} %bitcast.55), calls=%async_computation | async-start | bytes 1179648 | tf_op jit(solution)/shard_map/all_to_all | solution.py:230
  29.9 0.1 dynamic-slice_bitcast_fusion
  30.0 1.3 fusion.5
  31.2 0.9 broadcast_in_dim.13.combine_ref
  32.2 6.0 %collective-permute-start.2 = (bf16[768,256]{1,0:T(8,128)(2,1)S(1)}, bf16[768,256]{1,0:T(8,128)(2,1)S(1)}, u32[]{:S(2)}, u32[]{:S(2)}) collective-permute-start(bf16[768,256]{1,0:T(8,128)(2,1)S(1)} %fusion.5), channel_id=1, source_target_pairs={{0,0},{1,2},{2,1},{3,3},{4,4},{5,6},{6,5},{7,7},{8,8},{9,10},{10,9... | collective-permute-start | bytes 1179656 | tf_op jit(solution)/shard_map/ppermute | solution.py:246
  38.1 1.9 %collective-permute-start.3 = (bf16[768,256]{1,0:T(8,128)(2,1)S(1)}, bf16[768,256]{1,0:T(8,128)(2,1)S(1)}, u32[]{:S(2)}, u32[]{:S(2)}) collective-permute-start(bf16[768,256]{1,0:T(8,128)(2,1)S(1)} %fusion.5), channel_id=1, source_target_pairs={{0,1},{1,3},{2,0},{3,2},{4,5},{5,7},{6,4},{7,6},{8,9},{9,11},{10,8... | collective-permute-start | bytes 1179656 | tf_op jit(solution)/shard_map/ppermute | solution.py:247
  40.1 4.4 %collective-permute-done.2.refs_3_.refs_6_ = bf16[768,256]{1,0:T(8,128)(2,1)S(1)} collective-permute-done((bf16[768,256]{1,0:T(8,128)(2,1)S(1)}, bf16[768,256]{1,0:T(8,128)(2,1)S(1)}, u32[]{:S(2)}, u32[]{:S(2)}) %collective-permute-start.2) | collective-permute-done | bytes 393248 | tf_op jit(solution)/shard_map/ppermute | solution.py:246
  44.5 4.1 %collective-permute-done.3.refs_4_.refs_7_ = bf16[768,256]{1,0:T(8,128)(2,1)S(1)} collective-permute-done((bf16[768,256]{1,0:T(8,128)(2,1)S(1)}, bf16[768,256]{1,0:T(8,128)(2,1)S(1)}, u32[]{:S(2)}, u32[]{:S(2)}) %collective-permute-start.3) | collective-permute-done | bytes 393248 | tf_op jit(solution)/shard_map/ppermute | solution.py:247
  48.6 0.7 copy-done.1
  49.3 0.1 all-to-all-done
  49.4 2.6 %collective-permute-start.4 = (bf16[768,384]{1,0:T(8,128)(2,1)}, bf16[768,384]{1,0:T(8,128)(2,1)}, u32[]{:S(2)}, u32[]{:S(2)}) collective-permute-start(bf16[768,384]{1,0:T(8,128)(2,1)} %bitcast.15.refs_0_), channel_id=1, source_target_pairs={{0,8},{2,58},{8,16},{10,2},{16,24},{18,10},{24,32},{26,18},{32,40}... | collective-permute-start | bytes 1769480 | tf_op jit(solution)/shard_map/ppermute | solution.py:257
  52.1 0.1 stack.47.index
  52.2 1.0 copy-done.2
  53.2 3.2 %shard_map.93 = (f32[768,512]{1,0:T(8,128)S(1)}, bf16[8,384,256]{2,1,0:T(8,128)(2,1)}, bf16[8,384,256]{2,1,0:T(8,128)(2,1)}) custom-call(s32[10]{0:T(128)S(1)} %stack.47.index, bf16[768,384]{1,0:T(8,128)(2,1)} %bitcast.15.refs_0_, bf16[8,384,256]{2,1,0:T(8,128)(2,1)S(1)} %bitcast.36, bf16[8,384,256]{2,1,0:T(8,128)(2,1)S(1)} %bitcast.44, ...), custom_call_target="tpu_custom_call" | custom-call | flops 603979776 | bytes 4000000 | tf_op jit(solution)/shard_map/pallas_call | solution.py:104
  56.5 2.7 %collective-permute-start.7 = (bf16[768,384]{1,0:T(8,128)(2,1)}, bf16[768,384]{1,0:T(8,128)(2,1)S(1)}, u32[]{:S(2)}, u32[]{:S(2)}) collective-permute-start(bf16[768,384]{1,0:T(8,128)(2,1)} %bitcast.15.refs_0_), channel_id=1, source_target_pairs={{0,56},{2,10},{8,0},{10,18},{16,8},{18,26},{24,16},{26,34},{32,24}... | collective-permute-start | bytes 1769480 | tf_op jit(solution)/shard_map/ppermute | solution.py:258
  59.1 1.5 %collective-permute-done.4.refs_0_ = bf16[768,384]{1,0:T(8,128)(2,1)} collective-permute-done((bf16[768,384]{1,0:T(8,128)(2,1)}, bf16[768,384]{1,0:T(8,128)(2,1)}, u32[]{:S(2)}, u32[]{:S(2)}) %collective-permute-start.4) | collective-permute-done | bytes 589856 | tf_op jit(solution)/shard_map/ppermute | solution.py:257
  60.7 4.2 %collective-permute-start.5 = (bf16[768,384]{1,0:T(8,128)(2,1)}, bf16[768,384]{1,0:T(8,128)(2,1)S(1)}, u32[]{:S(2)}, u32[]{:S(2)}) collective-permute-start(bf16[768,384]{1,0:T(8,128)(2,1)} %collective-permute-done.4.refs_0_), channel_id=1, source_target_pairs={{0,8},{2,58},{8,16},{10,2},{16,24},{18,10},{24,32},{26,18},{32,40}... | collective-permute-start | bytes 1769480 | tf_op jit(solution)/shard_map/ppermute | solution.py:257
  64.8 5.3 %collective-permute-done.7.refs_1_ = bf16[768,384]{1,0:T(8,128)(2,1)S(1)} collective-permute-done((bf16[768,384]{1,0:T(8,128)(2,1)}, bf16[768,384]{1,0:T(8,128)(2,1)S(1)}, u32[]{:S(2)}, u32[]{:S(2)}) %collective-permute-start.7) | collective-permute-done | bytes 589856 | tf_op jit(solution)/shard_map/ppermute | solution.py:258
  70.2 1.9 %collective-permute-start.9 = (bf16[768,384]{1,0:T(8,128)(2,1)S(1)}, bf16[768,384]{1,0:T(8,128)(2,1)S(1)}, u32[]{:S(2)}, u32[]{:S(2)}) collective-permute-start(bf16[768,384]{1,0:T(8,128)(2,1)S(1)} %collective-permute-done.7.refs_1_), channel_id=1, source_target_pairs={{0,56},{2,10},{8,0},{10,18},{16,8},{18,26},{24,16},{26,34},{32,24}... | collective-permute-start | bytes 1769480 | tf_op jit(solution)/shard_map/ppermute | solution.py:258
  72.1 4.2 %shard_map.94 = (f32[768,512]{1,0:T(8,128)S(1)}, bf16[8,384,256]{2,1,0:T(8,128)(2,1)}, bf16[8,384,256]{2,1,0:T(8,128)(2,1)}) custom-call(s32[10]{0:T(128)S(1)} %stack.47.index, bf16[768,384]{1,0:T(8,128)(2,1)} %collective-permute-done.4.refs_0_, ...), custom_call_target="tpu_custom_call", output_to_operand_aliasing={{0}: (9, {}), {1}: (10, {}), {2}: (11, {})} | custom-call | flops 1207959552 | bytes 8000000 | tf_op jit(solution)/shard_map/pallas_call | solution.py:104
  76.2 5.1 %collective-permute-start.8 = (bf16[768,384]{1,0:T(8,128)(2,1)S(1)}, bf16[768,384]{1,0:T(8,128)(2,1)S(1)}, u32[]{:S(2)}, u32[]{:S(2)}) collective-permute-start(bf16[768,384]{1,0:T(8,128)(2,1)S(1)} %collective-permute-done.5.refs_0_), channel_id=1, source_target_pairs={{0,8},{2,58},{8,16},{10,2},{16,24},{18,10},{24,32},{26,18},{32,40}... | collective-permute-start | bytes 1769480 | tf_op jit(solution)/shard_map/ppermute | solution.py:257
  81.4 1.2 collective-permute-done.9.refs_1_
  82.6 1.9 %collective-permute-start.11 = (bf16[768,384]{1,0:T(8,128)(2,1)S(1)}, bf16[768,384]{1,0:T(8,128)(2,1)S(1)}, u32[]{:S(2)}, u32[]{:S(2)}) collective-permute-start(bf16[768,384]{1,0:T(8,128)(2,1)S(1)} %collective-permute-done.9.refs_1_), channel_id=1, source_target_pairs={{0,56},{2,10},{8,0},{10,18},{16,8},{18,26},{24,16},{26,34},{32,24}... | collective-permute-start | bytes 1769480 | tf_op jit(solution)/shard_map/ppermute | solution.py:258
  84.5 3.1 %shard_map.95 = (f32[768,512]{1,0:T(8,128)S(1)}, bf16[8,384,256]{2,1,0:T(8,128)(2,1)}, bf16[8,384,256]{2,1,0:T(8,128)(2,1)}) custom-call(s32[10]{0:T(128)S(1)} %stack.47.index, bf16[768,384]{1,0:T(8,128)(2,1)S(1)} %collective-permute-done.5.refs_0_, ...), custom_call_target="tpu_custom_call", output_to_operand_aliasing={{0}: (9, {}), {1}: (10, {}), {2}: (11, {})} | custom-call | flops 1207959552 | bytes 8000000 | tf_op jit(solution)/shard_map/pallas_call | solution.py:104
  87.6 3.1 %collective-permute-done.8.refs_0_ = bf16[768,384]{1,0:T(8,128)(2,1)S(1)} collective-permute-done((bf16[768,384]{1,0:T(8,128)(2,1)S(1)}, bf16[768,384]{1,0:T(8,128)(2,1)S(1)}, u32[]{:S(2)}, u32[]{:S(2)}) %collective-permute-start.8) | collective-permute-done | bytes 589856 | tf_op jit(solution)/shard_map/ppermute | solution.py:257
  90.7 5.0 %collective-permute-start.10 = (bf16[768,384]{1,0:T(8,128)(2,1)S(1)}, bf16[768,384]{1,0:T(8,128)(2,1)S(1)}, u32[]{:S(2)}, u32[]{:S(2)}) collective-permute-start(bf16[768,384]{1,0:T(8,128)(2,1)S(1)} %collective-permute-done.8.refs_0_), channel_id=1, source_target_pairs={{0,8},{2,58},{8,16},{10,2},{16,24},{18,10},{24,32},{26,18},{32,40}... | collective-permute-start | bytes 1769480 | tf_op jit(solution)/shard_map/ppermute | solution.py:257
  95.7 4.4 %collective-permute-done.11.refs_1_ = bf16[768,384]{1,0:T(8,128)(2,1)S(1)} collective-permute-done((bf16[768,384]{1,0:T(8,128)(2,1)S(1)}, bf16[768,384]{1,0:T(8,128)(2,1)S(1)}, u32[]{:S(2)}, u32[]{:S(2)}) %collective-permute-start.11) | collective-permute-done | bytes 589856 | tf_op jit(solution)/shard_map/ppermute | solution.py:258
  100.2 3.1 %shard_map.96 = (f32[768,512]{1,0:T(8,128)S(1)}, bf16[8,384,256]{2,1,0:T(8,128)(2,1)}, bf16[8,384,256]{2,1,0:T(8,128)(2,1)}) custom-call(s32[10]{0:T(128)S(1)} %stack.47.index, bf16[768,384]{1,0:T(8,128)(2,1)S(1)} %collective-permute-done.8.refs_0_, ...), custom_call_target="tpu_custom_call", output_to_operand_aliasing={{0}: (9, {}), {1}: (10, {}), {2}: (11, {})} | custom-call | flops 1207959552 | bytes 8000000 | tf_op jit(solution)/shard_map/pallas_call | solution.py:104
  103.3 3.6 %collective-permute-done.10.refs_0_ = bf16[768,384]{1,0:T(8,128)(2,1)S(1)} collective-permute-done((bf16[768,384]{1,0:T(8,128)(2,1)S(1)}, bf16[768,384]{1,0:T(8,128)(2,1)S(1)}, u32[]{:S(2)}, u32[]{:S(2)}) %collective-permute-start.10) | collective-permute-done | bytes 589856 | tf_op jit(solution)/shard_map/ppermute | solution.py:257
  106.9 2.5 %shard_map.97 = (f32[768,256]{1,0:T(8,128)}, bf16[8,384,256]{2,1,0:T(8,128)(2,1)}, bf16[8,384,256]{2,1,0:T(8,128)(2,1)}, bf16[768,256]{1,0:T(8,128)(2,1)}, bf16[...) custom-call(s32[10]{0:T(128)S(1)} %stack.47.index, ...), custom_call_target="tpu_custom_call", output_to_operand_aliasing={{1}: (7, {}), {2}: (8, {})} | custom-call | flops 603979776 | bytes 4000000 | tf_op jit(solution)/shard_map/pallas_call | solution.py:104
  109.4 8.3 %collective-permute-start.14 = (bf16[8,384,256]{2,1,0:T(8,128)(2,1)}, bf16[8,384,256]{2,1,0:T(8,128)(2,1)S(1)}, u32[]{:S(2)}, u32[]{:S(2)}) collective-permute-start(bf16[8,384,256]{2,1,0:T(8,128)(2,1)} %get-tuple-element.70), channel_id=1, source_target_pairs={{0,2},{2,0},{1,3},{3,1},{4,6},{6,4},{5,7},{7,5},{8,10},{10,8},{9,1... | collective-permute-start | bytes 4718600 | tf_op jit(solution)/shard_map/ppermute | solution.py:284
  117.8 5.9 %collective-permute-start.12 = (bf16[768,256]{1,0:T(8,128)(2,1)}, bf16[768,256]{1,0:T(8,128)(2,1)S(1)}, u32[]{:S(2)}, u32[]{:S(2)}) collective-permute-start(bf16[768,256]{1,0:T(8,128)(2,1)} %get-tuple-element.64), channel_id=1, source_target_pairs={{2,3},{1,0},{0,2},{3,1},{6,7},{5,4},{4,6},{7,5},{10,11},{9,8},{8,1... | collective-permute-start | bytes 1179656 | tf_op jit(solution)/shard_map/ppermute | solution.py:280
  123.7 1.9 %collective-permute-start.13 = (bf16[768,256]{1,0:T(8,128)(2,1)}, bf16[768,256]{1,0:T(8,128)(2,1)S(1)}, u32[]{:S(2)}, u32[]{:S(2)}) collective-permute-start(bf16[768,256]{1,0:T(8,128)(2,1)} %get-tuple-element.65), channel_id=1, source_target_pairs={{2,1},{1,2},{6,5},{5,6},{10,9},{9,10},{14,13},{13,14},{18,17},{17,... | collective-permute-start | bytes 1179656 | tf_op jit(solution)/shard_map/ppermute | solution.py:281
  125.6 0.7 all_to_all.12
  126.4 8.0 %all-to-all-start.1 = ((f32[64,1,24]{2,1,0:T(1,128)}), f32[64,1,24]{2,1,0:T(1,128)S(1)}, u32[]{:S(2)}, u32[]{:S(2)}) async-start(f32[64,1,24]{2,1,0:T(1,128)} %bitcast.22), calls=%async_computation.1 | async-start | bytes 65536 | tf_op jit(solution)/shard_map/all_to_all | solution.py:283
  134.4 0.2 collective-permute-done.13.got_b
  134.5 3.4 %shard_map.98 = (bf16[768,256]{1,0:T(8,128)(2,1)}, bf16[768,256]{1,0:T(8,128)(2,1)}) custom-call(s32[10]{0:T(128)S(1)} %stack.47.index, f32[768,256]{1,0:T(8,128)} %get-tuple-element.63.own, bf16[768,256]{1,0:T(8,128)(2,1)S(1)} %collective-permute-done.12.got_a, bf16[768,256]{1,0:T(8,128)(2,1)S(1)} %collective-permute-done.13.got_b, ...), custom_call_target="tpu_custom_call" | custom-call | flops 3000000 | bytes 3500000 | tf_op jit(solution)/shard_map/pallas_call | solution.py:162
  137.9 3.4 %shard_map.99 = bf16[8,384,256]{2,1,0:T(8,128)(2,1)} custom-call(s32[10]{0:T(128)S(1)} %stack.47.index, bf16[8,384,256]{2,1,0:T(8,128)(2,1)} %get-tuple-element.69.mine, bf16[8,384,256]{2,1,0:T(8,128)(2,1)S(1)} %collective-permute-done.14.theirs), custom_call_target="tpu_custom_call" | custom-call | flops 1000000 | bytes 5000000 | tf_op jit(solution)/shard_map/pallas_call | solution.py:131
  141.4 2.5 %all-to-all-done.1 = f32[64,1,24]{2,1,0:T(1,128)S(1)} async-done(((f32[64,1,24]{2,1,0:T(1,128)}), f32[64,1,24]{2,1,0:T(1,128)S(1)}, u32[]{:S(2)}, u32[]{:S(2)}) %all-to-all-start.1) | async-done | bytes 6176 | tf_op jit(solution)/shard_map/all_to_all | solution.py:283
  143.9 0.5 divide_bitcast_fusion
  (22 shorter events, 0.2 us)
Async XLA Ops:
  2.3 27.5 %copy-start.4 = (f32[1,1,768]{2,1,0:T(1,128)S(1)}, f32[1,1,768]{2,1,0:T(1,128)}, u32[]{:S(2)}) copy-start(f32[1,1,768]{2,1,0:T(1,128)} %param.8) | copy-start | bytes 9220
  2.3 27.6 %copy-start.3 = (bf16[1,1,768,256]{3,2,1,0:T(8,128)(2,1)S(1)}, bf16[1,1,768,256]{3,2,1,0:T(8,128)(2,1)}, u32[]{:S(2)}) copy-start(bf16[1,1,768,256]{3,2,1,0:T(8,128)(2,1)} %param.10) | copy-start | bytes 1179652
  2.3 14.3 %collective-permute-start = (bf16[192,194]{0,1:T(8,128)(2,1)S(1)}, bf16[192,194]{0,1:T(8,128)(2,1)S(1)}, u32[]{:S(2)}, u32[]{:S(2)}) collective-permute-start(bf16[192,194]{0,1:T(8,128)(2,1)S(1)} %pad_maximum_fusion), channel_id=1, source_target_pairs={{0,48},{1,50},{2,52},{3,54},{4,56},{5,58},{6,60},{7,62},{8,0},{9,2... | collective-permute-start | bytes 223496 | tf_op jit(solution)/shard_map/ppermute | solution.py:223
  10.7 7.8 %collective-permute-start.1 = (bf16[192,192]{0,1:T(8,128)(2,1)S(1)}, bf16[192,192]{0,1:T(8,128)(2,1)S(1)}, u32[]{:S(2)}, u32[]{:S(2)}) collective-permute-start(bf16[192,192]{0,1:T(8,128)(2,1)S(1)} %bitcast.57), channel_id=1, source_target_pairs={{0,52},{1,54},{2,48},{3,50},{4,60},{5,62},{6,56},{7,58},{8,4},{9,6... | collective-permute-start | bytes 221192 | tf_op jit(solution)/shard_map/ppermute | solution.py:224
  14.7 37.5 %collective-permute-start.6 = (bf16[3072,256]{1,0:T(8,128)(2,1)}, bf16[3072,256]{1,0:T(8,128)(2,1)S(1)}, u32[]{:S(2)}, u32[]{:S(2)}) collective-permute-start(bf16[3072,256]{1,0:T(8,128)(2,1)} %bitcast.35), channel_id=1, source_target_pairs={{0,2},{2,0},{1,3},{3,1},{4,6},{6,4},{5,7},{7,5},{8,10},{10,8},{9,1... | collective-permute-start | bytes 4718600 | tf_op jit(solution)/shard_map/ppermute | solution.py:239
  19.7 32.5 %copy-start = (bf16[1,3072,256]{2,1,0:T(8,128)(2,1)S(1)}, bf16[1,3072,256]{2,1,0:T(8,128)(2,1)}, u32[]{:S(2)}) copy-start(bf16[1,3072,256]{2,1,0:T(8,128)(2,1)} %param.11) | copy-start | bytes 4718596
  19.7 29.7 %all-to-all-start = ((bf16[8,96,384]{2,1,0:T(8,128)(2,1)}), bf16[8,96,384]{2,1,0:T(8,128)(2,1)}, u32[]{:S(2)}, u32[]{:S(2)}) async-start(bf16[8,96,384]{2,1,0:T(8,128)(2,1)} %bitcast.55), calls=%async_computation | async-start | bytes 1179648 | tf_op jit(solution)/shard_map/all_to_all | solution.py:230
  32.2 12.3 %collective-permute-start.2 = (bf16[768,256]{1,0:T(8,128)(2,1)S(1)}, bf16[768,256]{1,0:T(8,128)(2,1)S(1)}, u32[]{:S(2)}, u32[]{:S(2)}) collective-permute-start(bf16[768,256]{1,0:T(8,128)(2,1)S(1)} %fusion.5), channel_id=1, source_target_pairs={{0,0},{1,2},{2,1},{3,3},{4,4},{5,6},{6,5},{7,7},{8,8},{9,10},{10,9... | collective-permute-start | bytes 1179656 | tf_op jit(solution)/shard_map/ppermute | solution.py:246
  38.1 10.4 %collective-permute-start.3 = (bf16[768,256]{1,0:T(8,128)(2,1)S(1)}, bf16[768,256]{1,0:T(8,128)(2,1)S(1)}, u32[]{:S(2)}, u32[]{:S(2)}) collective-permute-start(bf16[768,256]{1,0:T(8,128)(2,1)S(1)} %fusion.5), channel_id=1, source_target_pairs={{0,1},{1,3},{2,0},{3,2},{4,5},{5,7},{6,4},{7,6},{8,9},{9,11},{10,8... | collective-permute-start | bytes 1179656 | tf_op jit(solution)/shard_map/ppermute | solution.py:247
  48.6 0.7 copy-start.1
  49.4 11.2 %collective-permute-start.4 = (bf16[768,384]{1,0:T(8,128)(2,1)}, bf16[768,384]{1,0:T(8,128)(2,1)}, u32[]{:S(2)}, u32[]{:S(2)}) collective-permute-start(bf16[768,384]{1,0:T(8,128)(2,1)} %bitcast.15.refs_0_), channel_id=1, source_target_pairs={{0,8},{2,58},{8,16},{10,2},{16,24},{18,10},{24,32},{26,18},{32,40}... | collective-permute-start | bytes 1769480 | tf_op jit(solution)/shard_map/ppermute | solution.py:257
  52.2 1.0 copy-start.2
  56.5 13.7 %collective-permute-start.7 = (bf16[768,384]{1,0:T(8,128)(2,1)}, bf16[768,384]{1,0:T(8,128)(2,1)S(1)}, u32[]{:S(2)}, u32[]{:S(2)}) collective-permute-start(bf16[768,384]{1,0:T(8,128)(2,1)} %bitcast.15.refs_0_), channel_id=1, source_target_pairs={{0,56},{2,10},{8,0},{10,18},{16,8},{18,26},{24,16},{26,34},{32,24}... | collective-permute-start | bytes 1769480 | tf_op jit(solution)/shard_map/ppermute | solution.py:258
  60.7 15.6 %collective-permute-start.5 = (bf16[768,384]{1,0:T(8,128)(2,1)}, bf16[768,384]{1,0:T(8,128)(2,1)S(1)}, u32[]{:S(2)}, u32[]{:S(2)}) collective-permute-start(bf16[768,384]{1,0:T(8,128)(2,1)} %collective-permute-done.4.refs_0_), channel_id=1, source_target_pairs={{0,8},{2,58},{8,16},{10,2},{16,24},{18,10},{24,32},{26,18},{32,40}... | collective-permute-start | bytes 1769480 | tf_op jit(solution)/shard_map/ppermute | solution.py:257
  70.2 12.4 %collective-permute-start.9 = (bf16[768,384]{1,0:T(8,128)(2,1)S(1)}, bf16[768,384]{1,0:T(8,128)(2,1)S(1)}, u32[]{:S(2)}, u32[]{:S(2)}) collective-permute-start(bf16[768,384]{1,0:T(8,128)(2,1)S(1)} %collective-permute-done.7.refs_1_), channel_id=1, source_target_pairs={{0,56},{2,10},{8,0},{10,18},{16,8},{18,26},{24,16},{26,34},{32,24}... | collective-permute-start | bytes 1769480 | tf_op jit(solution)/shard_map/ppermute | solution.py:258
  76.2 14.5 %collective-permute-start.8 = (bf16[768,384]{1,0:T(8,128)(2,1)S(1)}, bf16[768,384]{1,0:T(8,128)(2,1)S(1)}, u32[]{:S(2)}, u32[]{:S(2)}) collective-permute-start(bf16[768,384]{1,0:T(8,128)(2,1)S(1)} %collective-permute-done.5.refs_0_), channel_id=1, source_target_pairs={{0,8},{2,58},{8,16},{10,2},{16,24},{18,10},{24,32},{26,18},{32,40}... | collective-permute-start | bytes 1769480 | tf_op jit(solution)/shard_map/ppermute | solution.py:257
  82.6 17.6 %collective-permute-start.11 = (bf16[768,384]{1,0:T(8,128)(2,1)S(1)}, bf16[768,384]{1,0:T(8,128)(2,1)S(1)}, u32[]{:S(2)}, u32[]{:S(2)}) collective-permute-start(bf16[768,384]{1,0:T(8,128)(2,1)S(1)} %collective-permute-done.9.refs_1_), channel_id=1, source_target_pairs={{0,56},{2,10},{8,0},{10,18},{16,8},{18,26},{24,16},{26,34},{32,24}... | collective-permute-start | bytes 1769480 | tf_op jit(solution)/shard_map/ppermute | solution.py:258
  90.7 16.2 %collective-permute-start.10 = (bf16[768,384]{1,0:T(8,128)(2,1)S(1)}, bf16[768,384]{1,0:T(8,128)(2,1)S(1)}, u32[]{:S(2)}, u32[]{:S(2)}) collective-permute-start(bf16[768,384]{1,0:T(8,128)(2,1)S(1)} %collective-permute-done.8.refs_0_), channel_id=1, source_target_pairs={{0,8},{2,58},{8,16},{10,2},{16,24},{18,10},{24,32},{26,18},{32,40}... | collective-permute-start | bytes 1769480 | tf_op jit(solution)/shard_map/ppermute | solution.py:257
  109.4 28.5 %collective-permute-start.14 = (bf16[8,384,256]{2,1,0:T(8,128)(2,1)}, bf16[8,384,256]{2,1,0:T(8,128)(2,1)S(1)}, u32[]{:S(2)}, u32[]{:S(2)}) collective-permute-start(bf16[8,384,256]{2,1,0:T(8,128)(2,1)} %get-tuple-element.70), channel_id=1, source_target_pairs={{0,2},{2,0},{1,3},{3,1},{4,6},{6,4},{5,7},{7,5},{8,10},{10,8},{9,1... | collective-permute-start | bytes 4718600 | tf_op jit(solution)/shard_map/ppermute | solution.py:284
  117.8 16.6 %collective-permute-start.12 = (bf16[768,256]{1,0:T(8,128)(2,1)}, bf16[768,256]{1,0:T(8,128)(2,1)S(1)}, u32[]{:S(2)}, u32[]{:S(2)}) collective-permute-start(bf16[768,256]{1,0:T(8,128)(2,1)} %get-tuple-element.64), channel_id=1, source_target_pairs={{2,3},{1,0},{0,2},{3,1},{6,7},{5,4},{4,6},{7,5},{10,11},{9,8},{8,1... | collective-permute-start | bytes 1179656 | tf_op jit(solution)/shard_map/ppermute | solution.py:280
  123.7 10.8 %collective-permute-start.13 = (bf16[768,256]{1,0:T(8,128)(2,1)}, bf16[768,256]{1,0:T(8,128)(2,1)S(1)}, u32[]{:S(2)}, u32[]{:S(2)}) collective-permute-start(bf16[768,256]{1,0:T(8,128)(2,1)} %get-tuple-element.65), channel_id=1, source_target_pairs={{2,1},{1,2},{6,5},{5,6},{10,9},{9,10},{14,13},{13,14},{18,17},{17,... | collective-permute-start | bytes 1179656 | tf_op jit(solution)/shard_map/ppermute | solution.py:281
  126.4 17.5 %all-to-all-start.1 = ((f32[64,1,24]{2,1,0:T(1,128)}), f32[64,1,24]{2,1,0:T(1,128)S(1)}, u32[]{:S(2)}, u32[]{:S(2)}) async-start(f32[64,1,24]{2,1,0:T(1,128)} %bitcast.22), calls=%async_computation.1 | async-start | bytes 65536 | tf_op jit(solution)/shard_map/all_to_all | solution.py:283

commit v11 on v10

--- a/solution.py
+++ b/solution.py
@@ -127,7 +127,6 @@
     def whole(a):
         return pl.BlockSpec(a.shape, lambda i, idx: (0, 0, 0))
 
-    mine = pltpu.with_memory_space_constraint(mine, pltpu.HBM)
     return pl.pallas_call(
         functools.partial(place_kernel, tuple(partner)),
         grid_spec=pltpu.PrefetchScalarGridSpec(
@@ -147,7 +146,8 @@
     total = jnp.where(index[flags] == 1, own[...], got_b[...].astype(F32)) + got_a[...].astype(F32)
     gate = gate_ref[...].astype(F32)
     sigma = jax.nn.sigmoid(gate)
-    weighted = combine_ref[:, :1] * total
+    scale = combine_ref[...]
+    weighted = jnp.concatenate([scale] * (gate.shape[1] // scale.shape[1]), axis=1) * total
     out_gate[...] = (weighted * up_ref[...].astype(F32) * sigma * (1.0 + gate * (1.0 - sigma))).astype(BF)
     out_up[...] = (weighted * (gate * sigma)).astype(BF)
 
@@ -242,7 +242,7 @@
         share = rows // (ny * 4)
         blk = (y * 2 + xlo) * 2 + core
         combine_share = lax.dynamic_slice_in_dim(combine[0, 0], blk * share, share, 0)
-        combine_share, combine_wide, scaled = lax.optimization_barrier((combine_share, combine_wide, scaled))
+        combine_share, scaled = lax.optimization_barrier((combine_share, scaled))
         s_a = lax.ppermute(scaled, ("core", "dp"), scaled_a)
         s_b = lax.ppermute(scaled, ("core", "dp"), scaled_b)
         turn = jnp.where(core == 0, -1, 1)
@@ -275,6 +275,8 @@
                 a, acc = lax.optimization_barrier((a, held[0]))
                 held = (acc, *held[1:])
                 a_next = on_a(a)
+        acc, combine_wide = lax.optimization_barrier((held[0], combine_wide))
+        held = (acc, *held[1:])
         acc, mine, theirs, sum_a, sum_b, mix = use([a], index, ny - 1, *args, held, last=True)
 
         got_a = lax.ppermute(sum_a, ("core", "dp"), sums_a)

time: 145 us -> 147 us (1.014)
    ppermute x1, starting transfers between devices: 5.92 us -> 4.22 us  [local(): got_a = lax.ppermute(sum_a, ('core', 'dp'), sums_a)]
  transfers between devices with their start and end apart: 17 -> 17, of which waited for: 12 -> 11; matrix products, arithmetic and copies ran while one was open for 3% -> 3% of each run, Pallas kernels for 14% -> 13%
where the time goes in v11:
time: 147 us; the launch traced here: 146 us
  starting transfers between devices  80.5 us (55%)
  waiting for transfers between devices  33.2 us (23%)
  Pallas kernels  21.6 us (15%)
  local copies, waits for them, and re-layouts  4.53 us (3%)
  other arithmetic  3.38 us (2%)
    ppermute x4, starting transfers between devices, local(): on_a = lambda v: lax.ppermute(v, ('y', 'core'), ring_a)  16.9 us
    pallas_call x5, Pallas kernels, use(): pl.pallas_call(functools.partial(use_kernel, blocks, first, last), grid_s...  16.2 us
    ppermute x3, waiting for transfers between devices, local(): on_b = lambda v: lax.ppermute(v, ('y', 'core'), ring_b)  10.9 us
    all_to_all x1, starting transfers between devices, local(): lax.all_to_all(outgoing, 'expert', split_axis=0, concat_axis=0, tiled=True)  10.2 us
    all_to_all x1, starting transfers between devices, local(): lax.all_to_all(mix.reshape(members, share), ('dp', 'y', 'xlo', 'core'), 0...  9.33 us
    ppermute x1, starting transfers between devices, local(): late = lax.ppermute(theirs, 'core', swap)  8.52 us
    ppermute x1, starting transfers between devices, local(): lax.ppermute(jnp.concatenate([cotangent[0], ids], axis=1), every, token_m...  8.33 us
    ppermute x4, waiting for transfers between devices, local(): on_a = lambda v: lax.ppermute(v, ('y', 'core'), ring_a)  7.3 us
  transfers between devices with their start and end apart: 17, of which 11 were waited for; matrix products, arithmetic and copies ran while one was open for 3% of the time, Pallas kernels for 13%

profile of v11, /device:TPU:1, one launch (start us, length us, event | category | flops | bytes accessed | tf_op | source)
XLA Modules:
  0.0 145.6 jit_solution(2066366614622433839)
XLA Ops:
  0.6 1.0 copy.28
  1.6 0.7 convert_bitcast_fusion
  2.3 8.3 %collective-permute-start = (bf16[192,194]{0,1:T(8,128)(2,1)S(1)}, bf16[192,194]{0,1:T(8,128)(2,1)S(1)}, u32[]{:S(2)}, u32[]{:S(2)}) collective-permute-start(bf16[192,194]{0,1:T(8,128)(2,1)S(1)} %pad_maximum_fusion), channel_id=1, source_target_pairs={{0,48},{1,50},{2,52},{3,54},{4,56},{5,58},{6,60},{7,62},{8,0},{9,2... | collective-permute-start | bytes 223496 | tf_op jit(solution)/shard_map/ppermute | solution.py:223
  10.7 4.0 %collective-permute-start.1 = (bf16[192,192]{0,1:T(8,128)(2,1)S(1)}, bf16[192,192]{0,1:T(8,128)(2,1)S(1)}, u32[]{:S(2)}, u32[]{:S(2)}) collective-permute-start(bf16[192,192]{0,1:T(8,128)(2,1)S(1)} %bitcast.57), channel_id=1, source_target_pairs={{0,52},{1,54},{2,48},{3,50},{4,60},{5,62},{6,56},{7,58},{8,4},{9,6... | collective-permute-start | bytes 221192 | tf_op jit(solution)/shard_map/ppermute | solution.py:224
  14.7 1.9 %collective-permute-start.6 = (bf16[3072,256]{1,0:T(8,128)(2,1)}, bf16[3072,256]{1,0:T(8,128)(2,1)S(1)}, u32[]{:S(2)}, u32[]{:S(2)}) collective-permute-start(bf16[3072,256]{1,0:T(8,128)(2,1)} %bitcast.35), channel_id=1, source_target_pairs={{0,2},{2,0},{1,3},{3,1},{4,6},{6,4},{5,7},{7,5},{8,10},{10,8},{9,1... | collective-permute-start | bytes 4718600 | tf_op jit(solution)/shard_map/ppermute | solution.py:239
  16.7 0.1 fusion.13
  16.9 1.6 %collective-permute-done.1 = bf16[192,192]{0,1:T(8,128)(2,1)S(1)} collective-permute-done((bf16[192,192]{0,1:T(8,128)(2,1)S(1)}, bf16[192,192]{0,1:T(8,128)(2,1)S(1)}, u32[]{:S(2)}, u32[]{:S(2)}) %collective-permute-start.1) | collective-permute-done | bytes 73760 | tf_op jit(solution)/shard_map/ppermute | solution.py:224
  18.5 1.2 convolution_convert_fusion
  19.7 10.2 %all-to-all-start = ((bf16[8,96,384]{2,1,0:T(8,128)(2,1)}), bf16[8,96,384]{2,1,0:T(8,128)(2,1)}, u32[]{:S(2)}, u32[]{:S(2)}) async-start(bf16[8,96,384]{2,1,0:T(8,128)(2,1)} %bitcast.55), calls=%async_computation | async-start | bytes 1179648 | tf_op jit(solution)/shard_map/all_to_all | solution.py:230
  29.9 0.1 dynamic-slice_bitcast_fusion
  30.0 1.3 fusion.5
  31.2 6.0 %collective-permute-start.2 = (bf16[768,256]{1,0:T(8,128)(2,1)S(1)}, bf16[768,256]{1,0:T(8,128)(2,1)S(1)}, u32[]{:S(2)}, u32[]{:S(2)}) collective-permute-start(bf16[768,256]{1,0:T(8,128)(2,1)S(1)} %fusion.5), channel_id=1, source_target_pairs={{0,0},{1,2},{2,1},{3,3},{4,4},{5,6},{6,5},{7,7},{8,8},{9,10},{10,9... | collective-permute-start | bytes 1179656 | tf_op jit(solution)/shard_map/ppermute | solution.py:246
  37.2 1.9 %collective-permute-start.3 = (bf16[768,256]{1,0:T(8,128)(2,1)S(1)}, bf16[768,256]{1,0:T(8,128)(2,1)S(1)}, u32[]{:S(2)}, u32[]{:S(2)}) collective-permute-start(bf16[768,256]{1,0:T(8,128)(2,1)S(1)} %fusion.5), channel_id=1, source_target_pairs={{0,1},{1,3},{2,0},{3,2},{4,5},{5,7},{6,4},{7,6},{8,9},{9,11},{10,8... | collective-permute-start | bytes 1179656 | tf_op jit(solution)/shard_map/ppermute | solution.py:247
  39.2 4.4 %collective-permute-done.2.refs_3_.refs_6_ = bf16[768,256]{1,0:T(8,128)(2,1)S(1)} collective-permute-done((bf16[768,256]{1,0:T(8,128)(2,1)S(1)}, bf16[768,256]{1,0:T(8,128)(2,1)S(1)}, u32[]{:S(2)}, u32[]{:S(2)}) %collective-permute-start.2) | collective-permute-done | bytes 393248 | tf_op jit(solution)/shard_map/ppermute | solution.py:246
  43.6 4.1 %collective-permute-done.3.refs_4_.refs_7_ = bf16[768,256]{1,0:T(8,128)(2,1)S(1)} collective-permute-done((bf16[768,256]{1,0:T(8,128)(2,1)S(1)}, bf16[768,256]{1,0:T(8,128)(2,1)S(1)}, u32[]{:S(2)}, u32[]{:S(2)}) %collective-permute-start.3) | collective-permute-done | bytes 393248 | tf_op jit(solution)/shard_map/ppermute | solution.py:247
  47.7 0.7 copy-done.2
  48.4 1.0 all-to-all-done
  49.4 2.6 %collective-permute-start.4 = (bf16[768,384]{1,0:T(8,128)(2,1)}, bf16[768,384]{1,0:T(8,128)(2,1)}, u32[]{:S(2)}, u32[]{:S(2)}) collective-permute-start(bf16[768,384]{1,0:T(8,128)(2,1)} %bitcast.15.refs_0_), channel_id=1, source_target_pairs={{0,8},{2,58},{8,16},{10,2},{16,24},{18,10},{24,32},{26,18},{32,40}... | collective-permute-start | bytes 1769480 | tf_op jit(solution)/shard_map/ppermute | solution.py:257
  52.1 0.1 stack.47.index
  52.2 1.0 copy-done.3
  53.2 3.2 %shard_map.93 = (f32[768,512]{1,0:T(8,128)S(1)}, bf16[8,384,256]{2,1,0:T(8,128)(2,1)}, bf16[8,384,256]{2,1,0:T(8,128)(2,1)}) custom-call(s32[10]{0:T(128)S(1)} %stack.47.index, bf16[768,384]{1,0:T(8,128)(2,1)} %bitcast.15.refs_0_, bf16[8,384,256]{2,1,0:T(8,128)(2,1)S(1)} %bitcast.36, bf16[8,384,256]{2,1,0:T(8,128)(2,1)S(1)} %bitcast.44, ...), custom_call_target="tpu_custom_call" | custom-call | flops 603979776 | bytes 4000000 | tf_op jit(solution)/shard_map/pallas_call | solution.py:104
  56.5 2.7 %collective-permute-start.7 = (bf16[768,384]{1,0:T(8,128)(2,1)}, bf16[768,384]{1,0:T(8,128)(2,1)S(1)}, u32[]{:S(2)}, u32[]{:S(2)}) collective-permute-start(bf16[768,384]{1,0:T(8,128)(2,1)} %bitcast.15.refs_0_), channel_id=1, source_target_pairs={{0,56},{2,10},{8,0},{10,18},{16,8},{18,26},{24,16},{26,34},{32,24}... | collective-permute-start | bytes 1769480 | tf_op jit(solution)/shard_map/ppermute | solution.py:258
  59.1 1.5 %collective-permute-done.4.refs_0_ = bf16[768,384]{1,0:T(8,128)(2,1)} collective-permute-done((bf16[768,384]{1,0:T(8,128)(2,1)}, bf16[768,384]{1,0:T(8,128)(2,1)}, u32[]{:S(2)}, u32[]{:S(2)}) %collective-permute-start.4) | collective-permute-done | bytes 589856 | tf_op jit(solution)/shard_map/ppermute | solution.py:257
  60.7 4.2 %collective-permute-start.5 = (bf16[768,384]{1,0:T(8,128)(2,1)}, bf16[768,384]{1,0:T(8,128)(2,1)S(1)}, u32[]{:S(2)}, u32[]{:S(2)}) collective-permute-start(bf16[768,384]{1,0:T(8,128)(2,1)} %collective-permute-done.4.refs_0_), channel_id=1, source_target_pairs={{0,8},{2,58},{8,16},{10,2},{16,24},{18,10},{24,32},{26,18},{32,40}... | collective-permute-start | bytes 1769480 | tf_op jit(solution)/shard_map/ppermute | solution.py:257
  64.8 5.3 %collective-permute-done.7.refs_1_ = bf16[768,384]{1,0:T(8,128)(2,1)S(1)} collective-permute-done((bf16[768,384]{1,0:T(8,128)(2,1)}, bf16[768,384]{1,0:T(8,128)(2,1)S(1)}, u32[]{:S(2)}, u32[]{:S(2)}) %collective-permute-start.7) | collective-permute-done | bytes 589856 | tf_op jit(solution)/shard_map/ppermute | solution.py:258
  70.2 1.9 %collective-permute-start.9 = (bf16[768,384]{1,0:T(8,128)(2,1)S(1)}, bf16[768,384]{1,0:T(8,128)(2,1)S(1)}, u32[]{:S(2)}, u32[]{:S(2)}) collective-permute-start(bf16[768,384]{1,0:T(8,128)(2,1)S(1)} %collective-permute-done.7.refs_1_), channel_id=1, source_target_pairs={{0,56},{2,10},{8,0},{10,18},{16,8},{18,26},{24,16},{26,34},{32,24}... | collective-permute-start | bytes 1769480 | tf_op jit(solution)/shard_map/ppermute | solution.py:258
  72.1 4.2 %shard_map.94 = (f32[768,512]{1,0:T(8,128)S(1)}, bf16[8,384,256]{2,1,0:T(8,128)(2,1)}, bf16[8,384,256]{2,1,0:T(8,128)(2,1)}) custom-call(s32[10]{0:T(128)S(1)} %stack.47.index, bf16[768,384]{1,0:T(8,128)(2,1)} %collective-permute-done.4.refs_0_, ...), custom_call_target="tpu_custom_call", output_to_operand_aliasing={{0}: (9, {}), {1}: (10, {}), {2}: (11, {})} | custom-call | flops 1207959552 | bytes 8000000 | tf_op jit(solution)/shard_map/pallas_call | solution.py:104
  76.2 5.1 %collective-permute-start.8 = (bf16[768,384]{1,0:T(8,128)(2,1)S(1)}, bf16[768,384]{1,0:T(8,128)(2,1)S(1)}, u32[]{:S(2)}, u32[]{:S(2)}) collective-permute-start(bf16[768,384]{1,0:T(8,128)(2,1)S(1)} %collective-permute-done.5.refs_0_), channel_id=1, source_target_pairs={{0,8},{2,58},{8,16},{10,2},{16,24},{18,10},{24,32},{26,18},{32,40}... | collective-permute-start | bytes 1769480 | tf_op jit(solution)/shard_map/ppermute | solution.py:257
  81.4 1.2 collective-permute-done.9.refs_1_
  82.5 1.9 %collective-permute-start.11 = (bf16[768,384]{1,0:T(8,128)(2,1)S(1)}, bf16[768,384]{1,0:T(8,128)(2,1)S(1)}, u32[]{:S(2)}, u32[]{:S(2)}) collective-permute-start(bf16[768,384]{1,0:T(8,128)(2,1)S(1)} %collective-permute-done.9.refs_1_), channel_id=1, source_target_pairs={{0,56},{2,10},{8,0},{10,18},{16,8},{18,26},{24,16},{26,34},{32,24}... | collective-permute-start | bytes 1769480 | tf_op jit(solution)/shard_map/ppermute | solution.py:258
  84.5 3.1 %shard_map.95 = (f32[768,512]{1,0:T(8,128)S(1)}, bf16[8,384,256]{2,1,0:T(8,128)(2,1)}, bf16[8,384,256]{2,1,0:T(8,128)(2,1)}) custom-call(s32[10]{0:T(128)S(1)} %stack.47.index, bf16[768,384]{1,0:T(8,128)(2,1)S(1)} %collective-permute-done.5.refs_0_, ...), custom_call_target="tpu_custom_call", output_to_operand_aliasing={{0}: (9, {}), {1}: (10, {}), {2}: (11, {})} | custom-call | flops 1207959552 | bytes 8000000 | tf_op jit(solution)/shard_map/pallas_call | solution.py:104
  87.6 3.1 %collective-permute-done.8.refs_0_ = bf16[768,384]{1,0:T(8,128)(2,1)S(1)} collective-permute-done((bf16[768,384]{1,0:T(8,128)(2,1)S(1)}, bf16[768,384]{1,0:T(8,128)(2,1)S(1)}, u32[]{:S(2)}, u32[]{:S(2)}) %collective-permute-start.8) | collective-permute-done | bytes 589856 | tf_op jit(solution)/shard_map/ppermute | solution.py:257
  90.7 5.0 %collective-permute-start.10 = (bf16[768,384]{1,0:T(8,128)(2,1)S(1)}, bf16[768,384]{1,0:T(8,128)(2,1)S(1)}, u32[]{:S(2)}, u32[]{:S(2)}) collective-permute-start(bf16[768,384]{1,0:T(8,128)(2,1)S(1)} %collective-permute-done.8.refs_0_), channel_id=1, source_target_pairs={{0,8},{2,58},{8,16},{10,2},{16,24},{18,10},{24,32},{26,18},{32,40}... | collective-permute-start | bytes 1769480 | tf_op jit(solution)/shard_map/ppermute | solution.py:257
  95.7 4.5 %collective-permute-done.11.refs_1_ = bf16[768,384]{1,0:T(8,128)(2,1)S(1)} collective-permute-done((bf16[768,384]{1,0:T(8,128)(2,1)S(1)}, bf16[768,384]{1,0:T(8,128)(2,1)S(1)}, u32[]{:S(2)}, u32[]{:S(2)}) %collective-permute-start.11) | collective-permute-done | bytes 589856 | tf_op jit(solution)/shard_map/ppermute | solution.py:258
  100.2 3.1 %shard_map.96 = (f32[768,512]{1,0:T(8,128)S(1)}, bf16[8,384,256]{2,1,0:T(8,128)(2,1)}, bf16[8,384,256]{2,1,0:T(8,128)(2,1)}) custom-call(s32[10]{0:T(128)S(1)} %stack.47.index, bf16[768,384]{1,0:T(8,128)(2,1)S(1)} %collective-permute-done.8.refs_0_, ...), custom_call_target="tpu_custom_call", output_to_operand_aliasing={{0}: (9, {}), {1}: (10, {}), {2}: (11, {})} | custom-call | flops 1207959552 | bytes 8000000 | tf_op jit(solution)/shard_map/pallas_call | solution.py:104
  103.3 0.9 broadcast_in_dim.10.combine_ref
  104.2 2.7 %collective-permute-done.10.refs_0_ = bf16[768,384]{1,0:T(8,128)(2,1)S(1)} collective-permute-done((bf16[768,384]{1,0:T(8,128)(2,1)S(1)}, bf16[768,384]{1,0:T(8,128)(2,1)S(1)}, u32[]{:S(2)}, u32[]{:S(2)}) %collective-permute-start.10) | collective-permute-done | bytes 589856 | tf_op jit(solution)/shard_map/ppermute | solution.py:257
  106.9 2.5 %shard_map.97 = (f32[768,256]{1,0:T(8,128)}, bf16[8,384,256]{2,1,0:T(8,128)(2,1)}, bf16[8,384,256]{2,1,0:T(8,128)(2,1)}, bf16[768,256]{1,0:T(8,128)(2,1)}, bf16[...) custom-call(s32[10]{0:T(128)S(1)} %stack.47.index, ...), custom_call_target="tpu_custom_call", output_to_operand_aliasing={{1}: (7, {}), {2}: (8, {})} | custom-call | flops 603979776 | bytes 4000000 | tf_op jit(solution)/shard_map/pallas_call | solution.py:104
  109.4 8.5 %collective-permute-start.14 = (bf16[8,384,256]{2,1,0:T(8,128)(2,1)}, bf16[8,384,256]{2,1,0:T(8,128)(2,1)S(1)}, u32[]{:S(2)}, u32[]{:S(2)}) collective-permute-start(bf16[8,384,256]{2,1,0:T(8,128)(2,1)} %get-tuple-element.72), channel_id=1, source_target_pairs={{0,2},{2,0},{1,3},{3,1},{4,6},{6,4},{5,7},{7,5},{8,10},{10,8},{9,1... | collective-permute-start | bytes 4718600 | tf_op jit(solution)/shard_map/ppermute | solution.py:286
  118.0 4.2 %collective-permute-start.12 = (bf16[768,256]{1,0:T(8,128)(2,1)}, bf16[768,256]{1,0:T(8,128)(2,1)S(1)}, u32[]{:S(2)}, u32[]{:S(2)}) collective-permute-start(bf16[768,256]{1,0:T(8,128)(2,1)} %get-tuple-element.66), channel_id=1, source_target_pairs={{2,3},{1,0},{0,2},{3,1},{6,7},{5,4},{4,6},{7,5},{10,11},{9,8},{8,1... | collective-permute-start | bytes 1179656 | tf_op jit(solution)/shard_map/ppermute | solution.py:282
  122.2 2.7 %collective-permute-start.13 = (bf16[768,256]{1,0:T(8,128)(2,1)}, bf16[768,256]{1,0:T(8,128)(2,1)}, u32[]{:S(2)}, u32[]{:S(2)}) collective-permute-start(bf16[768,256]{1,0:T(8,128)(2,1)} %get-tuple-element.67), channel_id=1, source_target_pairs={{2,1},{1,2},{6,5},{5,6},{10,9},{9,10},{14,13},{13,14},{18,17},{17,... | collective-permute-start | bytes 1179656 | tf_op jit(solution)/shard_map/ppermute | solution.py:283
  124.9 0.7 all_to_all.12
  125.6 9.3 %all-to-all-start.1 = ((f32[64,1,24]{2,1,0:T(1,128)}), f32[64,1,24]{2,1,0:T(1,128)}, u32[]{:S(2)}, u32[]{:S(2)}) async-start(f32[64,1,24]{2,1,0:T(1,128)} %bitcast.58), calls=%async_computation.1 | async-start | bytes 65536 | tf_op jit(solution)/shard_map/all_to_all | solution.py:285
  135.0 3.4 %shard_map.98 = (bf16[768,256]{1,0:T(8,128)(2,1)}, bf16[768,256]{1,0:T(8,128)(2,1)}) custom-call(s32[10]{0:T(128)S(1)} %stack.47.index, f32[768,256]{1,0:T(8,128)} %get-tuple-element.65.own, bf16[768,256]{1,0:T(8,128)(2,1)S(1)} %collective-permute-done.12.got_a, bf16[768,256]{1,0:T(8,128)(2,1)} %collective-permute-done.13.got_b, bf16[768,256]{1,0:T(8,128)(2,1)} %bitcast.54, ...), custom_call_target="tpu_custom_call" | custom-call | flops 3000000 | bytes 3500000 | tf_op jit(solution)/shard_map/pallas_call | solution.py:162
  138.4 2.0 %shard_map.99 = bf16[8,384,256]{2,1,0:T(8,128)(2,1)} custom-call(s32[10]{0:T(128)S(1)} %stack.47.index, bf16[8,384,256]{2,1,0:T(8,128)(2,1)S(1)} %copy-done.1, bf16[8,384,256]{2,1,0:T(8,128)(2,1)S(1)} %collective-permute-done.14.theirs), custom_call_target="tpu_custom_call" | custom-call | flops 1000000 | bytes 5000000 | tf_op jit(solution)/shard_map/pallas_call | solution.py:130
  140.4 3.9 %all-to-all-done.1 = f32[64,1,24]{2,1,0:T(1,128)} async-done(((f32[64,1,24]{2,1,0:T(1,128)}), f32[64,1,24]{2,1,0:T(1,128)}, u32[]{:S(2)}, u32[]{:S(2)}) %all-to-all-start.1) | async-done | bytes 6176 | tf_op jit(solution)/shard_map/all_to_all | solution.py:285
  144.3 0.8 reduce_sum.29
  145.1 0.5 divide_bitcast_fusion
  (24 shorter events, 0.2 us)
Async XLA Ops:
  2.3 27.5 %copy-start.5 = (f32[1,1,768]{2,1,0:T(1,128)S(1)}, f32[1,1,768]{2,1,0:T(1,128)}, u32[]{:S(2)}) copy-start(f32[1,1,768]{2,1,0:T(1,128)} %param.8) | copy-start | bytes 9220
  2.3 27.6 %copy-start.4 = (bf16[1,1,768,256]{3,2,1,0:T(8,128)(2,1)S(1)}, bf16[1,1,768,256]{3,2,1,0:T(8,128)(2,1)}, u32[]{:S(2)}) copy-start(bf16[1,1,768,256]{3,2,1,0:T(8,128)(2,1)} %param.10) | copy-start | bytes 1179652
  2.3 14.3 %collective-permute-start = (bf16[192,194]{0,1:T(8,128)(2,1)S(1)}, bf16[192,194]{0,1:T(8,128)(2,1)S(1)}, u32[]{:S(2)}, u32[]{:S(2)}) collective-permute-start(bf16[192,194]{0,1:T(8,128)(2,1)S(1)} %pad_maximum_fusion), channel_id=1, source_target_pairs={{0,48},{1,50},{2,52},{3,54},{4,56},{5,58},{6,60},{7,62},{8,0},{9,2... | collective-permute-start | bytes 223496 | tf_op jit(solution)/shard_map/ppermute | solution.py:223
  10.7 7.8 %collective-permute-start.1 = (bf16[192,192]{0,1:T(8,128)(2,1)S(1)}, bf16[192,192]{0,1:T(8,128)(2,1)S(1)}, u32[]{:S(2)}, u32[]{:S(2)}) collective-permute-start(bf16[192,192]{0,1:T(8,128)(2,1)S(1)} %bitcast.57), channel_id=1, source_target_pairs={{0,52},{1,54},{2,48},{3,50},{4,60},{5,62},{6,56},{7,58},{8,4},{9,6... | collective-permute-start | bytes 221192 | tf_op jit(solution)/shard_map/ppermute | solution.py:224
  14.7 37.5 %collective-permute-start.6 = (bf16[3072,256]{1,0:T(8,128)(2,1)}, bf16[3072,256]{1,0:T(8,128)(2,1)S(1)}, u32[]{:S(2)}, u32[]{:S(2)}) collective-permute-start(bf16[3072,256]{1,0:T(8,128)(2,1)} %bitcast.35), channel_id=1, source_target_pairs={{0,2},{2,0},{1,3},{3,1},{4,6},{6,4},{5,7},{7,5},{8,10},{10,8},{9,1... | collective-permute-start | bytes 4718600 | tf_op jit(solution)/shard_map/ppermute | solution.py:239
  19.7 32.5 %copy-start = (bf16[1,3072,256]{2,1,0:T(8,128)(2,1)S(1)}, bf16[1,3072,256]{2,1,0:T(8,128)(2,1)}, u32[]{:S(2)}) copy-start(bf16[1,3072,256]{2,1,0:T(8,128)(2,1)} %param.11) | copy-start | bytes 4718596
  19.7 29.7 %all-to-all-start = ((bf16[8,96,384]{2,1,0:T(8,128)(2,1)}), bf16[8,96,384]{2,1,0:T(8,128)(2,1)}, u32[]{:S(2)}, u32[]{:S(2)}) async-start(bf16[8,96,384]{2,1,0:T(8,128)(2,1)} %bitcast.55), calls=%async_computation | async-start | bytes 1179648 | tf_op jit(solution)/shard_map/all_to_all | solution.py:230
  31.2 12.3 %collective-permute-start.2 = (bf16[768,256]{1,0:T(8,128)(2,1)S(1)}, bf16[768,256]{1,0:T(8,128)(2,1)S(1)}, u32[]{:S(2)}, u32[]{:S(2)}) collective-permute-start(bf16[768,256]{1,0:T(8,128)(2,1)S(1)} %fusion.5), channel_id=1, source_target_pairs={{0,0},{1,2},{2,1},{3,3},{4,4},{5,6},{6,5},{7,7},{8,8},{9,10},{10,9... | collective-permute-start | bytes 1179656 | tf_op jit(solution)/shard_map/ppermute | solution.py:246
  37.2 10.4 %collective-permute-start.3 = (bf16[768,256]{1,0:T(8,128)(2,1)S(1)}, bf16[768,256]{1,0:T(8,128)(2,1)S(1)}, u32[]{:S(2)}, u32[]{:S(2)}) collective-permute-start(bf16[768,256]{1,0:T(8,128)(2,1)S(1)} %fusion.5), channel_id=1, source_target_pairs={{0,1},{1,3},{2,0},{3,2},{4,5},{5,7},{6,4},{7,6},{8,9},{9,11},{10,8... | collective-permute-start | bytes 1179656 | tf_op jit(solution)/shard_map/ppermute | solution.py:247
  47.7 0.7 copy-start.2
  49.4 11.2 %collective-permute-start.4 = (bf16[768,384]{1,0:T(8,128)(2,1)}, bf16[768,384]{1,0:T(8,128)(2,1)}, u32[]{:S(2)}, u32[]{:S(2)}) collective-permute-start(bf16[768,384]{1,0:T(8,128)(2,1)} %bitcast.15.refs_0_), channel_id=1, source_target_pairs={{0,8},{2,58},{8,16},{10,2},{16,24},{18,10},{24,32},{26,18},{32,40}... | collective-permute-start | bytes 1769480 | tf_op jit(solution)/shard_map/ppermute | solution.py:257
  52.2 1.0 copy-start.3
  56.5 13.7 %collective-permute-start.7 = (bf16[768,384]{1,0:T(8,128)(2,1)}, bf16[768,384]{1,0:T(8,128)(2,1)S(1)}, u32[]{:S(2)}, u32[]{:S(2)}) collective-permute-start(bf16[768,384]{1,0:T(8,128)(2,1)} %bitcast.15.refs_0_), channel_id=1, source_target_pairs={{0,56},{2,10},{8,0},{10,18},{16,8},{18,26},{24,16},{26,34},{32,24}... | collective-permute-start | bytes 1769480 | tf_op jit(solution)/shard_map/ppermute | solution.py:258
  60.7 15.6 %collective-permute-start.5 = (bf16[768,384]{1,0:T(8,128)(2,1)}, bf16[768,384]{1,0:T(8,128)(2,1)S(1)}, u32[]{:S(2)}, u32[]{:S(2)}) collective-permute-start(bf16[768,384]{1,0:T(8,128)(2,1)} %collective-permute-done.4.refs_0_), channel_id=1, source_target_pairs={{0,8},{2,58},{8,16},{10,2},{16,24},{18,10},{24,32},{26,18},{32,40}... | collective-permute-start | bytes 1769480 | tf_op jit(solution)/shard_map/ppermute | solution.py:257
  70.2 12.4 %collective-permute-start.9 = (bf16[768,384]{1,0:T(8,128)(2,1)S(1)}, bf16[768,384]{1,0:T(8,128)(2,1)S(1)}, u32[]{:S(2)}, u32[]{:S(2)}) collective-permute-start(bf16[768,384]{1,0:T(8,128)(2,1)S(1)} %collective-permute-done.7.refs_1_), channel_id=1, source_target_pairs={{0,56},{2,10},{8,0},{10,18},{16,8},{18,26},{24,16},{26,34},{32,24}... | collective-permute-start | bytes 1769480 | tf_op jit(solution)/shard_map/ppermute | solution.py:258
  76.2 14.5 %collective-permute-start.8 = (bf16[768,384]{1,0:T(8,128)(2,1)S(1)}, bf16[768,384]{1,0:T(8,128)(2,1)S(1)}, u32[]{:S(2)}, u32[]{:S(2)}) collective-permute-start(bf16[768,384]{1,0:T(8,128)(2,1)S(1)} %collective-permute-done.5.refs_0_), channel_id=1, source_target_pairs={{0,8},{2,58},{8,16},{10,2},{16,24},{18,10},{24,32},{26,18},{32,40}... | collective-permute-start | bytes 1769480 | tf_op jit(solution)/shard_map/ppermute | solution.py:257
  82.5 17.6 %collective-permute-start.11 = (bf16[768,384]{1,0:T(8,128)(2,1)S(1)}, bf16[768,384]{1,0:T(8,128)(2,1)S(1)}, u32[]{:S(2)}, u32[]{:S(2)}) collective-permute-start(bf16[768,384]{1,0:T(8,128)(2,1)S(1)} %collective-permute-done.9.refs_1_), channel_id=1, source_target_pairs={{0,56},{2,10},{8,0},{10,18},{16,8},{18,26},{24,16},{26,34},{32,24}... | collective-permute-start | bytes 1769480 | tf_op jit(solution)/shard_map/ppermute | solution.py:258
  90.7 16.2 %collective-permute-start.10 = (bf16[768,384]{1,0:T(8,128)(2,1)S(1)}, bf16[768,384]{1,0:T(8,128)(2,1)S(1)}, u32[]{:S(2)}, u32[]{:S(2)}) collective-permute-start(bf16[768,384]{1,0:T(8,128)(2,1)S(1)} %collective-permute-done.8.refs_0_), channel_id=1, source_target_pairs={{0,8},{2,58},{8,16},{10,2},{16,24},{18,10},{24,32},{26,18},{32,40}... | collective-permute-start | bytes 1769480 | tf_op jit(solution)/shard_map/ppermute | solution.py:257
  109.4 29.0 %copy-start.1 = (bf16[8,384,256]{2,1,0:T(8,128)(2,1)S(1)}, bf16[8,384,256]{2,1,0:T(8,128)(2,1)}, u32[]{:S(2)}) copy-start(bf16[8,384,256]{2,1,0:T(8,128)(2,1)} %get-tuple-element.71.mine) | copy-start | bytes 4718596
  109.4 29.0 %collective-permute-start.14 = (bf16[8,384,256]{2,1,0:T(8,128)(2,1)}, bf16[8,384,256]{2,1,0:T(8,128)(2,1)S(1)}, u32[]{:S(2)}, u32[]{:S(2)}) collective-permute-start(bf16[8,384,256]{2,1,0:T(8,128)(2,1)} %get-tuple-element.72), channel_id=1, source_target_pairs={{0,2},{2,0},{1,3},{3,1},{4,6},{6,4},{5,7},{7,5},{8,10},{10,8},{9,1... | collective-permute-start | bytes 4718600 | tf_op jit(solution)/shard_map/ppermute | solution.py:286
  118.0 17.0 %collective-permute-start.12 = (bf16[768,256]{1,0:T(8,128)(2,1)}, bf16[768,256]{1,0:T(8,128)(2,1)S(1)}, u32[]{:S(2)}, u32[]{:S(2)}) collective-permute-start(bf16[768,256]{1,0:T(8,128)(2,1)} %get-tuple-element.66), channel_id=1, source_target_pairs={{2,3},{1,0},{0,2},{3,1},{6,7},{5,4},{4,6},{7,5},{10,11},{9,8},{8,1... | collective-permute-start | bytes 1179656 | tf_op jit(solution)/shard_map/ppermute | solution.py:282
  122.2 12.8 %collective-permute-start.13 = (bf16[768,256]{1,0:T(8,128)(2,1)}, bf16[768,256]{1,0:T(8,128)(2,1)}, u32[]{:S(2)}, u32[]{:S(2)}) collective-permute-start(bf16[768,256]{1,0:T(8,128)(2,1)} %get-tuple-element.67), channel_id=1, source_target_pairs={{2,1},{1,2},{6,5},{5,6},{10,9},{9,10},{14,13},{13,14},{18,17},{17,... | collective-permute-start | bytes 1179656 | tf_op jit(solution)/shard_map/ppermute | solution.py:283
  125.6 18.7 %all-to-all-start.1 = ((f32[64,1,24]{2,1,0:T(1,128)}), f32[64,1,24]{2,1,0:T(1,128)}, u32[]{:S(2)}, u32[]{:S(2)}) async-start(f32[64,1,24]{2,1,0:T(1,128)} %bitcast.58), calls=%async_computation.1 | async-start | bytes 65536 | tf_op jit(solution)/shard_map/all_to_all | solution.py:285

commit v12 on v11

--- a/solution.py
+++ b/solution.py
@@ -26,7 +26,7 @@
     return hit.astype(BF)
 
 
-def use_kernel(blocks, first, last, index, *refs):
+def use_kernel(blocks, first, last, carries, index, *refs):
     it = iter(refs)
     x_refs = [next(it) for _ in range(blocks)]
     w_mine = [next(it) for _ in range(blocks)]
@@ -34,7 +34,9 @@
     s_a, s_b = next(it), next(it)
     acc_in = None
     if not first:
-        acc_in, _, _ = next(it), next(it), next(it)
+        acc_in, _ = next(it), next(it)
+    carry_refs = [next(it) for _ in carries]
+    carried = sum(carries)
     acc, g_mine, g_theirs = next(it), next(it), next(it)
     width = s_a.shape[1]
     flags = index.shape[0] - 2
@@ -54,7 +56,11 @@
             acc[...] += product
         outer = lax.dot_general(x, s, (((0,), (0,)), ((), ())), preferred_element_type=F32)
         g_mine[b] = outer[:, :width].astype(BF)
-        g_theirs[b] = outer[:, width:].astype(BF)
+        g_theirs[carried + b] = outer[:, width:].astype(BF)
+    at = 0
+    for ref, n in zip(carry_refs, carries):
+        g_theirs[at : at + n] = ref[...]
+        at += n
     if last:
         sum_a, sum_b, mix = next(it), next(it), next(it)
         mine, theirs = total[:, :width], total[:, width:]
@@ -73,7 +79,7 @@
         mix[...] = jnp.where(row == index[flags + 1], line[:2], 0.0)
 
 
-def use(pieces, index, start, w_mine, w_theirs, s_a, s_b, held, last=False):
+def use(pieces, index, start, w_mine, w_theirs, s_a, s_b, held, last=False, carry=()):
     first = held is None
     blocks = len(pieces)
     rows, width = s_a.shape
@@ -91,23 +97,27 @@
     aliases = {}
     if not first:
         n = 1 + len(ins)
-        aliases = {n + 1: 1, n + 2: 2} if last else {n: 0, n + 1: 1, n + 2: 2}
+        aliases = {n + 1: 1} if last else {n: 0, n + 1: 1}
         ins += list(held)
-        specs += [whole(held[0]), pl.BlockSpec(memory_space=pl.ANY), pl.BlockSpec(memory_space=pl.ANY)]
+        specs += [whole(held[0]), pl.BlockSpec(memory_space=pl.ANY)]
+    carries = tuple(c.shape[0] for c in carry)
+    ins += list(carry)
+    specs += [whole(c) for c in carry]
     slot = pl.BlockSpec((blocks, chip, width), lambda i, idx: (start // blocks, 0, 0))
     sums = (rows, width if last else 2 * width)
     outs = [pltpu.HBM(sums, F32) if last else jax.ShapeDtypeStruct(sums, F32)]
-    outs += [pltpu.HBM((total, chip, width), BF)] * 2
+    sent = (sum(carries) + blocks, chip, width)
+    outs += [pltpu.HBM((total, chip, width), BF), jax.ShapeDtypeStruct(sent, BF)]
     extra = []
     if last:
         extra = [jax.ShapeDtypeStruct((rows, width), BF)] * 2 + [jax.ShapeDtypeStruct((2, rows), F32)]
     return pl.pallas_call(
-        functools.partial(use_kernel, blocks, first, last),
+        functools.partial(use_kernel, blocks, first, last, carries),
         grid_spec=pltpu.PrefetchScalarGridSpec(
             num_scalar_prefetch=1,
             grid=(1,),
             in_specs=specs,
-            out_specs=[pl.BlockSpec(sums, lambda i, idx: (0, 0)), slot, slot] + [whole(o) for o in extra],
+            out_specs=[pl.BlockSpec(sums, lambda i, idx: (0, 0)), slot, pl.BlockSpec(sent, lambda i, idx: (0, 0, 0))] + [whole(o) for o in extra],
         ),
         out_shape=outs + extra,
         input_output_aliases=aliases,
@@ -118,9 +128,10 @@
     )(index, *ins)
 
 
-def place_kernel(partner, index, mine, theirs, out):
-    for i, p in enumerate(partner):
-        out[index[i]] = (mine[i].astype(F32) + theirs[p].astype(F32)).astype(BF)
+def place_kernel(partner, index, mine, *refs):
+    theirs, out = refs[:-1], refs[-1]
+    for i, (a, j) in enumerate(partner):
+        out[index[i]] = (mine[i].astype(F32) + theirs[a][j].astype(F32)).astype(BF)
 
 
 def place(index, partner, mine, theirs):
@@ -132,13 +143,13 @@
         grid_spec=pltpu.PrefetchScalarGridSpec(
             num_scalar_prefetch=1,
             grid=(1,),
-            in_specs=[whole(mine), whole(theirs)],
+            in_specs=[whole(mine)] + [whole(t) for t in theirs],
             out_specs=whole(mine),
         ),
         out_shape=jax.ShapeDtypeStruct(mine.shape, BF),
         compiler_params=pltpu.CompilerParams(vmem_limit_bytes=16 * 1024 * 1024),
         cost_estimate=pl.CostEstimate(flops=1000000, bytes_accessed=5000000, transcendentals=0),
-    )(index, mine, theirs)
+    )(index, mine, *theirs)
 
 
 def finish_kernel(index, own, got_a, got_b, gate_ref, up_ref, combine_ref, out_gate, out_up):
@@ -251,7 +262,11 @@
         for step in range(1, half_y):
             order += [step, -step]
         order += [0, half_y]
-        partner = [order.index(-o) if abs(o) < half_y else order.index(o) for o in order]
+        slots = [order.index(-o) if abs(o) < half_y else order.index(o) for o in order]
+        late_slots = [ny - 2, ny - 4, ny - 3, ny - 1]
+        partner = [
+            (half_y - 2, late_slots.index(p)) if p in late_slots else (p // 2, p % 2) for p in slots
+        ]
         spots = [(y + turn * o + 2 * ny - shift_here) % ny for o in order]
         index = jnp.stack(spots + [held_own.astype(jnp.int32), core]).astype(jnp.int32)
         on_a = lambda v: lax.ppermute(v, ("y", "core"), ring_a)
@@ -260,31 +275,33 @@
         block, s_a, s_b = lax.optimization_barrier((block, s_a, s_b))
         a = on_a(block)
         args = (w_down[0].reshape(ny, chip, width), w_moved.reshape(ny, chip, width), s_a, s_b)
-        held = use([block], index, ny - 2, *args, None)
-        block_b, acc = lax.optimization_barrier((block, held[0]))
-        held = (acc, *held[1:])
+        acc, mine, own_part = use([block], index, ny - 2, *args, None)
+        block_b, acc = lax.optimization_barrier((block, acc))
         b = on_b(block_b)
         a_next = on_a(a)
+        swapped = []
         for step in range(1, half_y):
             blocks = [a, b]
             a = a_next
             if step < half_y - 1:
                 b = on_b(b)
-            held = use(blocks, index, 2 * (step - 1), *args, held)
+            acc, mine, theirs = use(blocks, index, 2 * (step - 1), *args, (acc, mine))
             if step < half_y - 1:
-                a, acc = lax.optimization_barrier((a, held[0]))
-                held = (acc, *held[1:])
+                got = lax.ppermute(theirs, "core", swap)
+                a, acc, got = lax.optimization_barrier((a, acc, got))
+                swapped.append(got)
                 a_next = on_a(a)
-        acc, combine_wide = lax.optimization_barrier((held[0], combine_wide))
-        held = (acc, *held[1:])
-        acc, mine, theirs, sum_a, sum_b, mix = use([a], index, ny - 1, *args, held, last=True)
+        acc, combine_wide = lax.optimization_barrier((acc, combine_wide))
+        acc, mine, theirs, sum_a, sum_b, mix = use(
+            [a], index, ny - 1, *args, (acc, mine), last=True, carry=(own_part, theirs)
+        )
 
         got_a = lax.ppermute(sum_a, ("core", "dp"), sums_a)
         got_b = lax.ppermute(sum_b, ("core", "dp"), sums_b)
         members = 2 * ny * 4
         mix = lax.all_to_all(mix.reshape(members, share), ("dp", "y", "xlo", "core"), 0, 0, tiled=True)
         late = lax.ppermute(theirs, "core", swap)
-        grad_weight = place(index, partner, mine, late).reshape(ny * chip, width)
+        grad_weight = place(index, partner, mine, (*swapped, late)).reshape(ny * chip, width)
         grad_gate, grad_upper = finish(index, acc, got_a, got_b, gate_saved[0, 0], up_saved[0, 0], combine_wide)
         mix, grad_gate, grad_upper, grad_weight = lax.optimization_barrier((mix, grad_gate, grad_upper, grad_weight))
         mix = jnp.sum(mix, axis=0)

time: 147 us -> 148 us (level)
  waiting for transfers between devices: 33.2 us -> 30 us
  starting transfers between devices: 80.5 us -> 83.5 us
  local copies, waits for them, and re-layouts: 4.53 us -> 6.08 us
    ppermute x0 -> x2, starting transfers between devices: none -> 9.47 us  [local(): got = lax.ppermute(theirs, 'core', swap)]
    ppermute x4, starting transfers between devices: 16.9 us -> 12.4 us  [local(): on_a = lambda v: lax.ppermute(v, ('y', 'core'), ring_a)]
    ppermute x1, starting transfers between devices: 8.52 us -> 4.08 us  [local(): late = lax.ppermute(theirs, 'core', swap)]
    ppermute x4, waiting for transfers between devices: 7.3 us -> 4 us  [local(): on_a = lambda v: lax.ppermute(v, ('y', 'core'), ring_a)]
    unnamed x13 -> x21, local copies, waits for them, and re-layouts: 2.74 us -> 4.28 us
  transfers between devices with their start and end apart: 17 -> 19, of which waited for: 11 -> 10; matrix products, arithmetic and copies ran while one was open for 3% -> 3% of each run, Pallas kernels for 13% -> 13%
where the time goes in v12:
time: 148 us; the launch traced here: 147 us
  starting transfers between devices  83.5 us (56%)
  waiting for transfers between devices  30 us (20%)
  Pallas kernels  21.6 us (15%)
  local copies, waits for them, and re-layouts  6.08 us (4%)
  other arithmetic  3.38 us (2%)
    pallas_call x5, Pallas kernels, use(): pl.pallas_call(functools.partial(use_kernel, blocks, first, last, carries...  16.1 us
    ppermute x4, starting transfers between devices, local(): on_a = lambda v: lax.ppermute(v, ('y', 'core'), ring_a)  12.4 us
    all_to_all x1, starting transfers between devices, local(): lax.all_to_all(mix.reshape(members, share), ('dp', 'y', 'xlo', 'core'), 0...  10.6 us
    all_to_all x1, starting transfers between devices, local(): lax.all_to_all(outgoing, 'expert', split_axis=0, concat_axis=0, tiled=True)  10.2 us
    ppermute x3, waiting for transfers between devices, local(): on_b = lambda v: lax.ppermute(v, ('y', 'core'), ring_b)  9.79 us
    ppermute x2, starting transfers between devices, local(): got = lax.ppermute(theirs, 'core', swap)  9.47 us
    ppermute x1, starting transfers between devices, local(): lax.ppermute(jnp.concatenate([cotangent[0], ids], axis=1), every, token_m...  8.33 us
    ppermute x3, starting transfers between devices, local(): on_b = lambda v: lax.ppermute(v, ('y', 'core'), ring_b)  7.58 us
  transfers between devices with their start and end apart: 19, of which 10 were waited for; matrix products, arithmetic and copies ran while one was open for 3% of the time, Pallas kernels for 13%

profile of v12, /device:TPU:1, one launch (start us, length us, event | category | flops | bytes accessed | tf_op | source)
XLA Modules:
  0.0 147.0 jit_solution(2763743062796358837)
XLA Ops:
  0.6 1.0 copy.24
  1.6 0.7 convert_bitcast_fusion
  2.3 8.3 %collective-permute-start = (bf16[192,194]{0,1:T(8,128)(2,1)S(1)}, bf16[192,194]{0,1:T(8,128)(2,1)S(1)}, u32[]{:S(2)}, u32[]{:S(2)}) collective-permute-start(bf16[192,194]{0,1:T(8,128)(2,1)S(1)} %pad_maximum_fusion), channel_id=1, source_target_pairs={{0,48},{1,50},{2,52},{3,54},{4,56},{5,58},{6,60},{7,62},{8,0},{9,2... | collective-permute-start | bytes 223496 | tf_op jit(solution)/shard_map/ppermute | solution.py:234
  10.7 4.0 %collective-permute-start.1 = (bf16[192,192]{0,1:T(8,128)(2,1)S(1)}, bf16[192,192]{0,1:T(8,128)(2,1)S(1)}, u32[]{:S(2)}, u32[]{:S(2)}) collective-permute-start(bf16[192,192]{0,1:T(8,128)(2,1)S(1)} %bitcast.57), channel_id=1, source_target_pairs={{0,52},{1,54},{2,48},{3,50},{4,60},{5,62},{6,56},{7,58},{8,4},{9,6... | collective-permute-start | bytes 221192 | tf_op jit(solution)/shard_map/ppermute | solution.py:235
  14.7 1.9 %collective-permute-start.6 = (bf16[3072,256]{1,0:T(8,128)(2,1)}, bf16[3072,256]{1,0:T(8,128)(2,1)S(1)}, u32[]{:S(2)}, u32[]{:S(2)}) collective-permute-start(bf16[3072,256]{1,0:T(8,128)(2,1)} %bitcast.35), channel_id=1, source_target_pairs={{0,2},{2,0},{1,3},{3,1},{4,6},{6,4},{5,7},{7,5},{8,10},{10,8},{9,1... | collective-permute-start | bytes 4718600 | tf_op jit(solution)/shard_map/ppermute | solution.py:250
  16.9 1.6 %collective-permute-done.1 = bf16[192,192]{0,1:T(8,128)(2,1)S(1)} collective-permute-done((bf16[192,192]{0,1:T(8,128)(2,1)S(1)}, bf16[192,192]{0,1:T(8,128)(2,1)S(1)}, u32[]{:S(2)}, u32[]{:S(2)}) %collective-permute-start.1) | collective-permute-done | bytes 73760 | tf_op jit(solution)/shard_map/ppermute | solution.py:235
  18.5 1.2 convolution_convert_fusion
  19.7 10.2 %all-to-all-start = ((bf16[8,96,384]{2,1,0:T(8,128)(2,1)}), bf16[8,96,384]{2,1,0:T(8,128)(2,1)}, u32[]{:S(2)}, u32[]{:S(2)}) async-start(bf16[8,96,384]{2,1,0:T(8,128)(2,1)} %bitcast.55), calls=%async_computation | async-start | bytes 1179648 | tf_op jit(solution)/shard_map/all_to_all | solution.py:241
  30.0 1.3 fusion.5
  31.2 6.0 %collective-permute-start.2 = (bf16[768,256]{1,0:T(8,128)(2,1)S(1)}, bf16[768,256]{1,0:T(8,128)(2,1)S(1)}, u32[]{:S(2)}, u32[]{:S(2)}) collective-permute-start(bf16[768,256]{1,0:T(8,128)(2,1)S(1)} %fusion.5), channel_id=1, source_target_pairs={{0,0},{1,2},{2,1},{3,3},{4,4},{5,6},{6,5},{7,7},{8,8},{9,10},{10,9... | collective-permute-start | bytes 1179656 | tf_op jit(solution)/shard_map/ppermute | solution.py:257
  37.2 1.9 %collective-permute-start.3 = (bf16[768,256]{1,0:T(8,128)(2,1)S(1)}, bf16[768,256]{1,0:T(8,128)(2,1)S(1)}, u32[]{:S(2)}, u32[]{:S(2)}) collective-permute-start(bf16[768,256]{1,0:T(8,128)(2,1)S(1)} %fusion.5), channel_id=1, source_target_pairs={{0,1},{1,3},{2,0},{3,2},{4,5},{5,7},{6,4},{7,6},{8,9},{9,11},{10,8... | collective-permute-start | bytes 1179656 | tf_op jit(solution)/shard_map/ppermute | solution.py:258
  39.2 4.4 %collective-permute-done.2.refs_3_.refs_6_ = bf16[768,256]{1,0:T(8,128)(2,1)S(1)} collective-permute-done((bf16[768,256]{1,0:T(8,128)(2,1)S(1)}, bf16[768,256]{1,0:T(8,128)(2,1)S(1)}, u32[]{:S(2)}, u32[]{:S(2)}) %collective-permute-start.2) | collective-permute-done | bytes 393248 | tf_op jit(solution)/shard_map/ppermute | solution.py:257
  43.6 4.1 %collective-permute-done.3.refs_4_.refs_7_ = bf16[768,256]{1,0:T(8,128)(2,1)S(1)} collective-permute-done((bf16[768,256]{1,0:T(8,128)(2,1)S(1)}, bf16[768,256]{1,0:T(8,128)(2,1)S(1)}, u32[]{:S(2)}, u32[]{:S(2)}) %collective-permute-start.3) | collective-permute-done | bytes 393248 | tf_op jit(solution)/shard_map/ppermute | solution.py:258
  47.7 0.7 copy-done.2
  48.4 1.0 all-to-all-done
  49.4 2.6 %collective-permute-start.4 = (bf16[768,384]{1,0:T(8,128)(2,1)}, bf16[768,384]{1,0:T(8,128)(2,1)}, u32[]{:S(2)}, u32[]{:S(2)}) collective-permute-start(bf16[768,384]{1,0:T(8,128)(2,1)} %bitcast.15.refs_0_), channel_id=1, source_target_pairs={{0,8},{2,58},{8,16},{10,2},{16,24},{18,10},{24,32},{26,18},{32,40}... | collective-permute-start | bytes 1769480 | tf_op jit(solution)/shard_map/ppermute | solution.py:272
  52.2 1.0 copy-done.3
  53.2 3.2 %shard_map.93 = (f32[768,512]{1,0:T(8,128)S(1)}, bf16[8,384,256]{2,1,0:T(8,128)(2,1)}, bf16[1,384,256]{2,1,0:T(8,128)(2,1)S(1)}) custom-call(s32[10]{0:T(128)S(1)} %stack.47.index, bf16[768,384]{1,0:T(8,128)(2,1)} %bitcast.15.refs_0_, bf16[8,384,256]{2,1,0:T(8,128)(2,1)S(1)} %bitcast.36, bf16[8,384,256]{2,1,0:T(8,128)(2,1)S(1)} %bitcast.44, ...), custom_call_target="tpu_custom_call" | custom-call | flops 603979776 | bytes 4000000 | tf_op jit(solution)/shard_map/pallas_call | solution.py:114
  56.4 2.7 %collective-permute-start.7 = (bf16[768,384]{1,0:T(8,128)(2,1)}, bf16[768,384]{1,0:T(8,128)(2,1)S(1)}, u32[]{:S(2)}, u32[]{:S(2)}) collective-permute-start(bf16[768,384]{1,0:T(8,128)(2,1)} %bitcast.15.refs_0_), channel_id=1, source_target_pairs={{0,56},{2,10},{8,0},{10,18},{16,8},{18,26},{24,16},{26,34},{32,24}... | collective-permute-start | bytes 1769480 | tf_op jit(solution)/shard_map/ppermute | solution.py:273
  59.1 1.6 %collective-permute-done.4.refs_0_ = bf16[768,384]{1,0:T(8,128)(2,1)} collective-permute-done((bf16[768,384]{1,0:T(8,128)(2,1)}, bf16[768,384]{1,0:T(8,128)(2,1)}, u32[]{:S(2)}, u32[]{:S(2)}) %collective-permute-start.4) | collective-permute-done | bytes 589856 | tf_op jit(solution)/shard_map/ppermute | solution.py:272
  60.7 4.2 %collective-permute-start.5 = (bf16[768,384]{1,0:T(8,128)(2,1)}, bf16[768,384]{1,0:T(8,128)(2,1)S(1)}, u32[]{:S(2)}, u32[]{:S(2)}) collective-permute-start(bf16[768,384]{1,0:T(8,128)(2,1)} %collective-permute-done.4.refs_0_), channel_id=1, source_target_pairs={{0,8},{2,58},{8,16},{10,2},{16,24},{18,10},{24,32},{26,18},{32,40}... | collective-permute-start | bytes 1769480 | tf_op jit(solution)/shard_map/ppermute | solution.py:272
  64.8 5.2 %collective-permute-done.7.refs_1_ = bf16[768,384]{1,0:T(8,128)(2,1)S(1)} collective-permute-done((bf16[768,384]{1,0:T(8,128)(2,1)}, bf16[768,384]{1,0:T(8,128)(2,1)S(1)}, u32[]{:S(2)}, u32[]{:S(2)}) %collective-permute-start.7) | collective-permute-done | bytes 589856 | tf_op jit(solution)/shard_map/ppermute | solution.py:273
  70.0 1.9 %collective-permute-start.10 = (bf16[768,384]{1,0:T(8,128)(2,1)S(1)}, bf16[768,384]{1,0:T(8,128)(2,1)S(1)}, u32[]{:S(2)}, u32[]{:S(2)}) collective-permute-start(bf16[768,384]{1,0:T(8,128)(2,1)S(1)} %collective-permute-done.7.refs_1_), channel_id=1, source_target_pairs={{0,56},{2,10},{8,0},{10,18},{16,8},{18,26},{24,16},{26,34},{32,24}... | collective-permute-start | bytes 1769480 | tf_op jit(solution)/shard_map/ppermute | solution.py:273
  72.0 4.0 %shard_map.94 = (f32[768,512]{1,0:T(8,128)S(1)}, bf16[8,384,256]{2,1,0:T(8,128)(2,1)}, bf16[2,384,256]{2,1,0:T(8,128)(2,1)S(1)}) custom-call(s32[10]{0:T(128)S(1)} %stack.47.index, bf16[768,384]{1,0:T(8,128)(2,1)} %collective-permute-done.4.refs_0_, ...), custom_call_target="tpu_custom_call", output_to_operand_aliasing={{0}: (9, {}), {1}: (10, {})} | custom-call | flops 1207959552 | bytes 8000000 | tf_op jit(solution)/shard_map/pallas_call | solution.py:114
  76.0 7.2 %collective-permute-start.8 = (bf16[2,384,256]{2,1,0:T(8,128)(2,1)S(1)}, bf16[2,384,256]{2,1,0:T(8,128)(2,1)S(1)}, u32[]{:S(2)}, u32[]{:S(2)}) collective-permute-start(bf16[2,384,256]{2,1,0:T(8,128)(2,1)S(1)} %get-tuple-element.52), channel_id=1, source_target_pairs={{0,2},{2,0},{1,3},{3,1},{4,6},{6,4},{5,7},{7,5},{8,10},{10,8},{9,1... | collective-permute-start | bytes 1179656 | tf_op jit(solution)/shard_map/ppermute | solution.py:290
  83.2 1.3 collective-permute-done.8.refs_0_
  84.5 0.8 copy-done.4
  85.3 1.9 %collective-permute-start.9 = (bf16[768,384]{1,0:T(8,128)(2,1)S(1)}, bf16[768,384]{1,0:T(8,128)(2,1)S(1)}, u32[]{:S(2)}, u32[]{:S(2)}) collective-permute-start(bf16[768,384]{1,0:T(8,128)(2,1)S(1)} %collective-permute-done.5.refs_0_), channel_id=1, source_target_pairs={{0,8},{2,58},{8,16},{10,2},{16,24},{18,10},{24,32},{26,18},{32,40}... | collective-permute-start | bytes 1769480 | tf_op jit(solution)/shard_map/ppermute | solution.py:272
  87.2 3.0 %shard_map.95 = (f32[768,512]{1,0:T(8,128)S(1)}, bf16[8,384,256]{2,1,0:T(8,128)(2,1)}, bf16[2,384,256]{2,1,0:T(8,128)(2,1)S(1)}) custom-call(s32[10]{0:T(128)S(1)} %stack.47.index, bf16[768,384]{1,0:T(8,128)(2,1)S(1)} %collective-permute-done.5.refs_0_, ...), custom_call_target="tpu_custom_call", output_to_operand_aliasing={{0}: (9, {}), {1}: (10, {})} | custom-call | flops 1207959552 | bytes 8000000 | tf_op jit(solution)/shard_map/pallas_call | solution.py:114
  90.2 2.3 %collective-permute-start.11 = (bf16[2,384,256]{2,1,0:T(8,128)(2,1)S(1)}, bf16[2,384,256]{2,1,0:T(8,128)(2,1)S(1)}, u32[]{:S(2)}, u32[]{:S(2)}) collective-permute-start(bf16[2,384,256]{2,1,0:T(8,128)(2,1)S(1)} %get-tuple-element.57), channel_id=1, source_target_pairs={{0,2},{2,0},{1,3},{3,1},{4,6},{6,4},{5,7},{7,5},{8,10},{10,8},{9,1... | collective-permute-start | bytes 1179656 | tf_op jit(solution)/shard_map/ppermute | solution.py:290
  92.5 3.0 %collective-permute-start.13 = (bf16[768,384]{1,0:T(8,128)(2,1)S(1)}, bf16[768,384]{1,0:T(8,128)(2,1)S(1)}, u32[]{:S(2)}, u32[]{:S(2)}) collective-permute-start(bf16[768,384]{1,0:T(8,128)(2,1)S(1)} %collective-permute-done.10.refs_1_), channel_id=1, source_target_pairs={{0,56},{2,10},{8,0},{10,18},{16,8},{18,26},{24,16},{26,34},{32,24}... | collective-permute-start | bytes 1769480 | tf_op jit(solution)/shard_map/ppermute | solution.py:273
  95.5 0.7 copy-done.6
  96.3 3.8 %collective-permute-start.12 = (bf16[768,384]{1,0:T(8,128)(2,1)S(1)}, bf16[768,384]{1,0:T(8,128)(2,1)S(1)}, u32[]{:S(2)}, u32[]{:S(2)}) collective-permute-start(bf16[768,384]{1,0:T(8,128)(2,1)S(1)} %collective-permute-done.9.refs_0_), channel_id=1, source_target_pairs={{0,8},{2,58},{8,16},{10,2},{16,24},{18,10},{24,32},{26,18},{32,40}... | collective-permute-start | bytes 1769480 | tf_op jit(solution)/shard_map/ppermute | solution.py:272
  100.0 4.6 %collective-permute-done.13.refs_1_ = bf16[768,384]{1,0:T(8,128)(2,1)S(1)} collective-permute-done((bf16[768,384]{1,0:T(8,128)(2,1)S(1)}, bf16[768,384]{1,0:T(8,128)(2,1)S(1)}, u32[]{:S(2)}, u32[]{:S(2)}) %collective-permute-start.13) | collective-permute-done | bytes 589856 | tf_op jit(solution)/shard_map/ppermute | solution.py:273
  104.6 3.0 %shard_map.96 = (f32[768,512]{1,0:T(8,128)S(1)}, bf16[8,384,256]{2,1,0:T(8,128)(2,1)}, bf16[2,384,256]{2,1,0:T(8,128)(2,1)S(1)}) custom-call(s32[10]{0:T(128)S(1)} %stack.47.index, bf16[768,384]{1,0:T(8,128)(2,1)S(1)} %collective-permute-done.9.refs_0_, ...), custom_call_target="tpu_custom_call", output_to_operand_aliasing={{0}: (9, {}), {1}: (10, {})} | custom-call | flops 1207959552 | bytes 8000000 | tf_op jit(solution)/shard_map/pallas_call | solution.py:114
  107.6 0.9 broadcast_in_dim.10.combine_ref
  108.5 2.4 %collective-permute-done.12.refs_0_ = bf16[768,384]{1,0:T(8,128)(2,1)S(1)} collective-permute-done((bf16[768,384]{1,0:T(8,128)(2,1)S(1)}, bf16[768,384]{1,0:T(8,128)(2,1)S(1)}, u32[]{:S(2)}, u32[]{:S(2)}) %collective-permute-start.12) | collective-permute-done | bytes 589856 | tf_op jit(solution)/shard_map/ppermute | solution.py:272
  111.0 3.0 %shard_map.97 = (f32[768,256]{1,0:T(8,128)}, bf16[8,384,256]{2,1,0:T(8,128)(2,1)}, bf16[4,384,256]{2,1,0:T(8,128)(2,1)}, bf16[768,256]{1,0:T(8,128)(2,1)}, bf16[...) custom-call(s32[10]{0:T(128)S(1)} %stack.47.index, ...), custom_call_target="tpu_custom_call", output_to_operand_aliasing={{1}: (7, {})} | custom-call | flops 603979776 | bytes 4000000 | tf_op jit(solution)/shard_map/pallas_call | solution.py:114
  113.9 4.1 %collective-permute-start.16 = (bf16[4,384,256]{2,1,0:T(8,128)(2,1)}, bf16[4,384,256]{2,1,0:T(8,128)(2,1)S(1)}, u32[]{:S(2)}, u32[]{:S(2)}) collective-permute-start(bf16[4,384,256]{2,1,0:T(8,128)(2,1)} %get-tuple-element.76), channel_id=1, source_target_pairs={{0,2},{2,0},{1,3},{3,1},{4,6},{6,4},{5,7},{7,5},{8,10},{10,8},{9,1... | collective-permute-start | bytes 2359304 | tf_op jit(solution)/shard_map/ppermute | solution.py:303
  118.0 4.3 %collective-permute-start.14 = (bf16[768,256]{1,0:T(8,128)(2,1)}, bf16[768,256]{1,0:T(8,128)(2,1)S(1)}, u32[]{:S(2)}, u32[]{:S(2)}) collective-permute-start(bf16[768,256]{1,0:T(8,128)(2,1)} %get-tuple-element.68), channel_id=1, source_target_pairs={{2,3},{1,0},{0,2},{3,1},{6,7},{5,4},{4,6},{7,5},{10,11},{9,8},{8,1... | collective-permute-start | bytes 1179656 | tf_op jit(solution)/shard_map/ppermute | solution.py:299
  122.3 2.7 %collective-permute-start.15 = (bf16[768,256]{1,0:T(8,128)(2,1)}, bf16[768,256]{1,0:T(8,128)(2,1)}, u32[]{:S(2)}, u32[]{:S(2)}) collective-permute-start(bf16[768,256]{1,0:T(8,128)(2,1)} %get-tuple-element.69), channel_id=1, source_target_pairs={{2,1},{1,2},{6,5},{5,6},{10,9},{9,10},{14,13},{13,14},{18,17},{17,... | collective-permute-start | bytes 1179656 | tf_op jit(solution)/shard_map/ppermute | solution.py:300
  125.0 0.7 all_to_all.12
  125.7 10.6 %all-to-all-start.1 = ((f32[64,1,24]{2,1,0:T(1,128)}), f32[64,1,24]{2,1,0:T(1,128)}, u32[]{:S(2)}, u32[]{:S(2)}) async-start(f32[64,1,24]{2,1,0:T(1,128)} %bitcast.58), calls=%async_computation.1 | async-start | bytes 65536 | tf_op jit(solution)/shard_map/all_to_all | solution.py:302
  136.3 3.4 %shard_map.98 = (bf16[768,256]{1,0:T(8,128)(2,1)}, bf16[768,256]{1,0:T(8,128)(2,1)}) custom-call(s32[10]{0:T(128)S(1)} %stack.47.index, f32[768,256]{1,0:T(8,128)} %get-tuple-element.67.own, bf16[768,256]{1,0:T(8,128)(2,1)S(1)} %collective-permute-done.14.got_a, bf16[768,256]{1,0:T(8,128)(2,1)} %collective-permute-done.15.got_b, bf16[768,256]{1,0:T(8,128)(2,1)} %bitcast.54, ...), custom_call_target="tpu_custom_call" | custom-call | flops 3000000 | bytes 3500000 | tf_op jit(solution)/shard_map/pallas_call | solution.py:173
  139.8 2.0 %shard_map.99 = bf16[8,384,256]{2,1,0:T(8,128)(2,1)} custom-call(s32[10]{0:T(128)S(1)} %stack.47.index, bf16[8,384,256]{2,1,0:T(8,128)(2,1)S(1)} %copy-done.1, bf16[2,384,256]{2,1,0:T(8,128)(2,1)S(1)} %copy-done.5, bf16[2,384,256]{2,1,0:T(8,128)(2,1)S(1)} %copy-done.7, bf16[4,384,256]{2,1,0:T(8,128)(2,1)S(1)} %collective-permute-done.16.refs_2_), custom_call_target="tpu_custom_call" | custom-call | flops 1000000 | bytes 5000000 | tf_op jit(solution)/shard_map/pallas_call | solution.py:141
  141.8 3.9 %all-to-all-done.1 = f32[64,1,24]{2,1,0:T(1,128)} async-done(((f32[64,1,24]{2,1,0:T(1,128)}), f32[64,1,24]{2,1,0:T(1,128)}, u32[]{:S(2)}, u32[]{:S(2)}) %all-to-all-start.1) | async-done | bytes 6176 | tf_op jit(solution)/shard_map/all_to_all | solution.py:302
  145.7 0.8 reduce_sum.29
  146.4 0.5 divide_bitcast_fusion
  (36 shorter events, 0.5 us)
Async XLA Ops:
  2.3 27.5 %copy-start.9 = (f32[1,1,768]{2,1,0:T(1,128)S(1)}, f32[1,1,768]{2,1,0:T(1,128)}, u32[]{:S(2)}) copy-start(f32[1,1,768]{2,1,0:T(1,128)} %param.8) | copy-start | bytes 9220
  2.3 27.6 %copy-start.8 = (bf16[1,1,768,256]{3,2,1,0:T(8,128)(2,1)S(1)}, bf16[1,1,768,256]{3,2,1,0:T(8,128)(2,1)}, u32[]{:S(2)}) copy-start(bf16[1,1,768,256]{3,2,1,0:T(8,128)(2,1)} %param.10) | copy-start | bytes 1179652
  2.3 14.3 %collective-permute-start = (bf16[192,194]{0,1:T(8,128)(2,1)S(1)}, bf16[192,194]{0,1:T(8,128)(2,1)S(1)}, u32[]{:S(2)}, u32[]{:S(2)}) collective-permute-start(bf16[192,194]{0,1:T(8,128)(2,1)S(1)} %pad_maximum_fusion), channel_id=1, source_target_pairs={{0,48},{1,50},{2,52},{3,54},{4,56},{5,58},{6,60},{7,62},{8,0},{9,2... | collective-permute-start | bytes 223496 | tf_op jit(solution)/shard_map/ppermute | solution.py:234
  10.7 7.8 %collective-permute-start.1 = (bf16[192,192]{0,1:T(8,128)(2,1)S(1)}, bf16[192,192]{0,1:T(8,128)(2,1)S(1)}, u32[]{:S(2)}, u32[]{:S(2)}) collective-permute-start(bf16[192,192]{0,1:T(8,128)(2,1)S(1)} %bitcast.57), channel_id=1, source_target_pairs={{0,52},{1,54},{2,48},{3,50},{4,60},{5,62},{6,56},{7,58},{8,4},{9,6... | collective-permute-start | bytes 221192 | tf_op jit(solution)/shard_map/ppermute | solution.py:235
  14.7 37.5 %collective-permute-start.6 = (bf16[3072,256]{1,0:T(8,128)(2,1)}, bf16[3072,256]{1,0:T(8,128)(2,1)S(1)}, u32[]{:S(2)}, u32[]{:S(2)}) collective-permute-start(bf16[3072,256]{1,0:T(8,128)(2,1)} %bitcast.35), channel_id=1, source_target_pairs={{0,2},{2,0},{1,3},{3,1},{4,6},{6,4},{5,7},{7,5},{8,10},{10,8},{9,1... | collective-permute-start | bytes 4718600 | tf_op jit(solution)/shard_map/ppermute | solution.py:250
  19.7 32.5 %copy-start = (bf16[1,3072,256]{2,1,0:T(8,128)(2,1)S(1)}, bf16[1,3072,256]{2,1,0:T(8,128)(2,1)}, u32[]{:S(2)}) copy-start(bf16[1,3072,256]{2,1,0:T(8,128)(2,1)} %param.11) | copy-start | bytes 4718596
  19.7 29.7 %all-to-all-start = ((bf16[8,96,384]{2,1,0:T(8,128)(2,1)}), bf16[8,96,384]{2,1,0:T(8,128)(2,1)}, u32[]{:S(2)}, u32[]{:S(2)}) async-start(bf16[8,96,384]{2,1,0:T(8,128)(2,1)} %bitcast.55), calls=%async_computation | async-start | bytes 1179648 | tf_op jit(solution)/shard_map/all_to_all | solution.py:241
  31.2 12.3 %collective-permute-start.2 = (bf16[768,256]{1,0:T(8,128)(2,1)S(1)}, bf16[768,256]{1,0:T(8,128)(2,1)S(1)}, u32[]{:S(2)}, u32[]{:S(2)}) collective-permute-start(bf16[768,256]{1,0:T(8,128)(2,1)S(1)} %fusion.5), channel_id=1, source_target_pairs={{0,0},{1,2},{2,1},{3,3},{4,4},{5,6},{6,5},{7,7},{8,8},{9,10},{10,9... | collective-permute-start | bytes 1179656 | tf_op jit(solution)/shard_map/ppermute | solution.py:257
  37.2 10.4 %collective-permute-start.3 = (bf16[768,256]{1,0:T(8,128)(2,1)S(1)}, bf16[768,256]{1,0:T(8,128)(2,1)S(1)}, u32[]{:S(2)}, u32[]{:S(2)}) collective-permute-start(bf16[768,256]{1,0:T(8,128)(2,1)S(1)} %fusion.5), channel_id=1, source_target_pairs={{0,1},{1,3},{2,0},{3,2},{4,5},{5,7},{6,4},{7,6},{8,9},{9,11},{10,8... | collective-permute-start | bytes 1179656 | tf_op jit(solution)/shard_map/ppermute | solution.py:258
  47.7 0.7 copy-start.2
  49.4 11.2 %collective-permute-start.4 = (bf16[768,384]{1,0:T(8,128)(2,1)}, bf16[768,384]{1,0:T(8,128)(2,1)}, u32[]{:S(2)}, u32[]{:S(2)}) collective-permute-start(bf16[768,384]{1,0:T(8,128)(2,1)} %bitcast.15.refs_0_), channel_id=1, source_target_pairs={{0,8},{2,58},{8,16},{10,2},{16,24},{18,10},{24,32},{26,18},{32,40}... | collective-permute-start | bytes 1769480 | tf_op jit(solution)/shard_map/ppermute | solution.py:272
  52.2 1.0 copy-start.3
  56.4 13.6 %collective-permute-start.7 = (bf16[768,384]{1,0:T(8,128)(2,1)}, bf16[768,384]{1,0:T(8,128)(2,1)S(1)}, u32[]{:S(2)}, u32[]{:S(2)}) collective-permute-start(bf16[768,384]{1,0:T(8,128)(2,1)} %bitcast.15.refs_0_), channel_id=1, source_target_pairs={{0,56},{2,10},{8,0},{10,18},{16,8},{18,26},{24,16},{26,34},{32,24}... | collective-permute-start | bytes 1769480 | tf_op jit(solution)/shard_map/ppermute | solution.py:273
  60.7 22.5 %collective-permute-start.5 = (bf16[768,384]{1,0:T(8,128)(2,1)}, bf16[768,384]{1,0:T(8,128)(2,1)S(1)}, u32[]{:S(2)}, u32[]{:S(2)}) collective-permute-start(bf16[768,384]{1,0:T(8,128)(2,1)} %collective-permute-done.4.refs_0_), channel_id=1, source_target_pairs={{0,8},{2,58},{8,16},{10,2},{16,24},{18,10},{24,32},{26,18},{32,40}... | collective-permute-start | bytes 1769480 | tf_op jit(solution)/shard_map/ppermute | solution.py:272
  70.0 17.2 %collective-permute-start.10 = (bf16[768,384]{1,0:T(8,128)(2,1)S(1)}, bf16[768,384]{1,0:T(8,128)(2,1)S(1)}, u32[]{:S(2)}, u32[]{:S(2)}) collective-permute-start(bf16[768,384]{1,0:T(8,128)(2,1)S(1)} %collective-permute-done.7.refs_1_), channel_id=1, source_target_pairs={{0,56},{2,10},{8,0},{10,18},{16,8},{18,26},{24,16},{26,34},{32,24}... | collective-permute-start | bytes 1769480 | tf_op jit(solution)/shard_map/ppermute | solution.py:273
  76.0 8.5 %collective-permute-start.8 = (bf16[2,384,256]{2,1,0:T(8,128)(2,1)S(1)}, bf16[2,384,256]{2,1,0:T(8,128)(2,1)S(1)}, u32[]{:S(2)}, u32[]{:S(2)}) collective-permute-start(bf16[2,384,256]{2,1,0:T(8,128)(2,1)S(1)} %get-tuple-element.52), channel_id=1, source_target_pairs={{0,2},{2,0},{1,3},{3,1},{4,6},{6,4},{5,7},{7,5},{8,10},{10,8},{9,1... | collective-permute-start | bytes 1179656 | tf_op jit(solution)/shard_map/ppermute | solution.py:290
  84.5 0.8 copy-start.4
  85.3 11.0 %collective-permute-start.9 = (bf16[768,384]{1,0:T(8,128)(2,1)S(1)}, bf16[768,384]{1,0:T(8,128)(2,1)S(1)}, u32[]{:S(2)}, u32[]{:S(2)}) collective-permute-start(bf16[768,384]{1,0:T(8,128)(2,1)S(1)} %collective-permute-done.5.refs_0_), channel_id=1, source_target_pairs={{0,8},{2,58},{8,16},{10,2},{16,24},{18,10},{24,32},{26,18},{32,40}... | collective-permute-start | bytes 1769480 | tf_op jit(solution)/shard_map/ppermute | solution.py:272
  90.2 5.3 %collective-permute-start.11 = (bf16[2,384,256]{2,1,0:T(8,128)(2,1)S(1)}, bf16[2,384,256]{2,1,0:T(8,128)(2,1)S(1)}, u32[]{:S(2)}, u32[]{:S(2)}) collective-permute-start(bf16[2,384,256]{2,1,0:T(8,128)(2,1)S(1)} %get-tuple-element.57), channel_id=1, source_target_pairs={{0,2},{2,0},{1,3},{3,1},{4,6},{6,4},{5,7},{7,5},{8,10},{10,8},{9,1... | collective-permute-start | bytes 1179656 | tf_op jit(solution)/shard_map/ppermute | solution.py:290
  92.5 12.1 %collective-permute-start.13 = (bf16[768,384]{1,0:T(8,128)(2,1)S(1)}, bf16[768,384]{1,0:T(8,128)(2,1)S(1)}, u32[]{:S(2)}, u32[]{:S(2)}) collective-permute-start(bf16[768,384]{1,0:T(8,128)(2,1)S(1)} %collective-permute-done.10.refs_1_), channel_id=1, source_target_pairs={{0,56},{2,10},{8,0},{10,18},{16,8},{18,26},{24,16},{26,34},{32,24}... | collective-permute-start | bytes 1769480 | tf_op jit(solution)/shard_map/ppermute | solution.py:273
  95.5 0.7 copy-start.6
  96.3 14.7 %collective-permute-start.12 = (bf16[768,384]{1,0:T(8,128)(2,1)S(1)}, bf16[768,384]{1,0:T(8,128)(2,1)S(1)}, u32[]{:S(2)}, u32[]{:S(2)}) collective-permute-start(bf16[768,384]{1,0:T(8,128)(2,1)S(1)} %collective-permute-done.9.refs_0_), channel_id=1, source_target_pairs={{0,8},{2,58},{8,16},{10,2},{16,24},{18,10},{24,32},{26,18},{32,40}... | collective-permute-start | bytes 1769480 | tf_op jit(solution)/shard_map/ppermute | solution.py:272
  113.9 25.8 %copy-start.1 = (bf16[8,384,256]{2,1,0:T(8,128)(2,1)S(1)}, bf16[8,384,256]{2,1,0:T(8,128)(2,1)}, u32[]{:S(2)}) copy-start(bf16[8,384,256]{2,1,0:T(8,128)(2,1)} %get-tuple-element.73.mine) | copy-start | bytes 4718596
  113.9 25.8 %copy-start.5 = (bf16[2,384,256]{2,1,0:T(8,128)(2,1)S(1)}, bf16[2,384,256]{2,1,0:T(8,128)(2,1)}, u32[]{:S(2)}) copy-start(bf16[2,384,256]{2,1,0:T(8,128)(2,1)} %copy-done.4) | copy-start | bytes 1179652
  113.9 25.8 %copy-start.7 = (bf16[2,384,256]{2,1,0:T(8,128)(2,1)S(1)}, bf16[2,384,256]{2,1,0:T(8,128)(2,1)}, u32[]{:S(2)}) copy-start(bf16[2,384,256]{2,1,0:T(8,128)(2,1)} %copy-done.6) | copy-start | bytes 1179652
  113.9 25.8 %collective-permute-start.16 = (bf16[4,384,256]{2,1,0:T(8,128)(2,1)}, bf16[4,384,256]{2,1,0:T(8,128)(2,1)S(1)}, u32[]{:S(2)}, u32[]{:S(2)}) collective-permute-start(bf16[4,384,256]{2,1,0:T(8,128)(2,1)} %get-tuple-element.76), channel_id=1, source_target_pairs={{0,2},{2,0},{1,3},{3,1},{4,6},{6,4},{5,7},{7,5},{8,10},{10,8},{9,1... | collective-permute-start | bytes 2359304 | tf_op jit(solution)/shard_map/ppermute | solution.py:303
  118.0 18.3 %collective-permute-start.14 = (bf16[768,256]{1,0:T(8,128)(2,1)}, bf16[768,256]{1,0:T(8,128)(2,1)S(1)}, u32[]{:S(2)}, u32[]{:S(2)}) collective-permute-start(bf16[768,256]{1,0:T(8,128)(2,1)} %get-tuple-element.68), channel_id=1, source_target_pairs={{2,3},{1,0},{0,2},{3,1},{6,7},{5,4},{4,6},{7,5},{10,11},{9,8},{8,1... | collective-permute-start | bytes 1179656 | tf_op jit(solution)/shard_map/ppermute | solution.py:299
  122.3 14.0 %collective-permute-start.15 = (bf16[768,256]{1,0:T(8,128)(2,1)}, bf16[768,256]{1,0:T(8,128)(2,1)}, u32[]{:S(2)}, u32[]{:S(2)}) collective-permute-start(bf16[768,256]{1,0:T(8,128)(2,1)} %get-tuple-element.69), channel_id=1, source_target_pairs={{2,1},{1,2},{6,5},{5,6},{10,9},{9,10},{14,13},{13,14},{18,17},{17,... | collective-permute-start | bytes 1179656 | tf_op jit(solution)/shard_map/ppermute | solution.py:300
  125.7 20.0 %all-to-all-start.1 = ((f32[64,1,24]{2,1,0:T(1,128)}), f32[64,1,24]{2,1,0:T(1,128)}, u32[]{:S(2)}, u32[]{:S(2)}) async-start(f32[64,1,24]{2,1,0:T(1,128)} %bitcast.58), calls=%async_computation.1 | async-start | bytes 65536 | tf_op jit(solution)/shard_map/all_to_all | solution.py:302

commit v13 on v12

--- a/solution.py
+++ b/solution.py
@@ -288,10 +288,10 @@
             acc, mine, theirs = use(blocks, index, 2 * (step - 1), *args, (acc, mine))
             if step < half_y - 1:
                 got = lax.ppermute(theirs, "core", swap)
-                a, acc, got = lax.optimization_barrier((a, acc, got))
+                a, acc, *swapped = lax.optimization_barrier((a, acc, *swapped))
                 swapped.append(got)
                 a_next = on_a(a)
-        acc, combine_wide = lax.optimization_barrier((acc, combine_wide))
+        acc, combine_wide, *swapped = lax.optimization_barrier((acc, combine_wide, *swapped))
         acc, mine, theirs, sum_a, sum_b, mix = use(
             [a], index, ny - 1, *args, (acc, mine), last=True, carry=(own_part, theirs)
         )

time: 148 us -> 147 us (level)
  starting transfers between devices: 83.5 us -> 90.6 us
  waiting for transfers between devices: 30 us -> 23.8 us
  local copies, waits for them, and re-layouts: 6.08 us -> 4.56 us
    ppermute x3, waiting for transfers between devices: 9.79 us -> 5.21 us  [local(): on_b = lambda v: lax.ppermute(v, ('y', 'core'), ring_b)]
    ppermute x4, starting transfers between devices: 12.4 us -> 16.5 us  [local(): on_a = lambda v: lax.ppermute(v, ('y', 'core'), ring_a)]
    ppermute x1, starting transfers between devices: 4.29 us -> 7.51 us  [local(): got_a = lax.ppermute(sum_a, ('core', 'dp'), sums_a)]
    unnamed x21, local copies, waits for them, and re-layouts: 4.28 us -> 2.76 us
  transfers between devices with their start and end apart: 19 -> 19, of which waited for: 10 -> 8; matrix products, arithmetic and copies ran while one was open for 3% -> 3% of each run, Pallas kernels for 13% -> 13%
where the time goes in v13:
time: 147 us; the launch traced here: 146 us
  starting transfers between devices  90.6 us (62%)
  waiting for transfers between devices  23.8 us (16%)
  Pallas kernels  21.6 us (15%)
  local copies, waits for them, and re-layouts  4.56 us (3%)
  other arithmetic  3.38 us (2%)
    ppermute x4, starting transfers between devices, local(): on_a = lambda v: lax.ppermute(v, ('y', 'core'), ring_a)  16.5 us
    pallas_call x5, Pallas kernels, use(): pl.pallas_call(functools.partial(use_kernel, blocks, first, last, carries...  16.1 us
    all_to_all x1, starting transfers between devices, local(): lax.all_to_all(mix.reshape(members, share), ('dp', 'y', 'xlo', 'core'), 0...  10.7 us
    all_to_all x1, starting transfers between devices, local(): lax.all_to_all(outgoing, 'expert', split_axis=0, concat_axis=0, tiled=True)  10.2 us
    ppermute x2, starting transfers between devices, local(): got = lax.ppermute(theirs, 'core', swap)  9.09 us
    ppermute x1, starting transfers between devices, local(): lax.ppermute(jnp.concatenate([cotangent[0], ids], axis=1), every, token_m...  8.33 us
    ppermute x1, starting transfers between devices, local(): got_a = lax.ppermute(sum_a, ('core', 'dp'), sums_a)  7.51 us
    ppermute x3, starting transfers between devices, local(): on_b = lambda v: lax.ppermute(v, ('y', 'core'), ring_b)  7.43 us
  transfers between devices with their start and end apart: 19, of which 8 were waited for; matrix products, arithmetic and copies ran while one was open for 3% of the time, Pallas kernels for 13%

profile of v13, /device:TPU:1, one launch (start us, length us, event | category | flops | bytes accessed | tf_op | source)
XLA Modules:
  0.0 146.4 jit_solution(17877565033043790076)
XLA Ops:
  0.6 1.0 copy.24
  1.6 0.7 convert_bitcast_fusion
  2.3 8.3 %collective-permute-start = (bf16[192,194]{0,1:T(8,128)(2,1)S(1)}, bf16[192,194]{0,1:T(8,128)(2,1)S(1)}, u32[]{:S(2)}, u32[]{:S(2)}) collective-permute-start(bf16[192,194]{0,1:T(8,128)(2,1)S(1)} %pad_maximum_fusion), channel_id=1, source_target_pairs={{0,48},{1,50},{2,52},{3,54},{4,56},{5,58},{6,60},{7,62},{8,0},{9,2... | collective-permute-start | bytes 223496 | tf_op jit(solution)/shard_map/ppermute | solution.py:234
  10.7 4.0 %collective-permute-start.1 = (bf16[192,192]{0,1:T(8,128)(2,1)S(1)}, bf16[192,192]{0,1:T(8,128)(2,1)S(1)}, u32[]{:S(2)}, u32[]{:S(2)}) collective-permute-start(bf16[192,192]{0,1:T(8,128)(2,1)S(1)} %bitcast.57), channel_id=1, source_target_pairs={{0,52},{1,54},{2,48},{3,50},{4,60},{5,62},{6,56},{7,58},{8,4},{9,6... | collective-permute-start | bytes 221192 | tf_op jit(solution)/shard_map/ppermute | solution.py:235
  14.7 1.9 %collective-permute-start.6 = (bf16[3072,256]{1,0:T(8,128)(2,1)}, bf16[3072,256]{1,0:T(8,128)(2,1)S(1)}, u32[]{:S(2)}, u32[]{:S(2)}) collective-permute-start(bf16[3072,256]{1,0:T(8,128)(2,1)} %bitcast.35), channel_id=1, source_target_pairs={{0,2},{2,0},{1,3},{3,1},{4,6},{6,4},{5,7},{7,5},{8,10},{10,8},{9,1... | collective-permute-start | bytes 4718600 | tf_op jit(solution)/shard_map/ppermute | solution.py:250
  16.7 0.1 fusion.13
  16.9 1.6 %collective-permute-done.1 = bf16[192,192]{0,1:T(8,128)(2,1)S(1)} collective-permute-done((bf16[192,192]{0,1:T(8,128)(2,1)S(1)}, bf16[192,192]{0,1:T(8,128)(2,1)S(1)}, u32[]{:S(2)}, u32[]{:S(2)}) %collective-permute-start.1) | collective-permute-done | bytes 73760 | tf_op jit(solution)/shard_map/ppermute | solution.py:235
  18.5 1.2 convolution_convert_fusion
  19.7 10.2 %all-to-all-start = ((bf16[8,96,384]{2,1,0:T(8,128)(2,1)}), bf16[8,96,384]{2,1,0:T(8,128)(2,1)}, u32[]{:S(2)}, u32[]{:S(2)}) async-start(bf16[8,96,384]{2,1,0:T(8,128)(2,1)} %bitcast.55), calls=%async_computation | async-start | bytes 1179648 | tf_op jit(solution)/shard_map/all_to_all | solution.py:241
  29.9 0.1 dynamic-slice_bitcast_fusion
  30.0 1.3 fusion.5
  31.2 6.0 %collective-permute-start.2 = (bf16[768,256]{1,0:T(8,128)(2,1)S(1)}, bf16[768,256]{1,0:T(8,128)(2,1)S(1)}, u32[]{:S(2)}, u32[]{:S(2)}) collective-permute-start(bf16[768,256]{1,0:T(8,128)(2,1)S(1)} %fusion.5), channel_id=1, source_target_pairs={{0,0},{1,2},{2,1},{3,3},{4,4},{5,6},{6,5},{7,7},{8,8},{9,10},{10,9... | collective-permute-start | bytes 1179656 | tf_op jit(solution)/shard_map/ppermute | solution.py:257
  37.2 1.9 %collective-permute-start.3 = (bf16[768,256]{1,0:T(8,128)(2,1)S(1)}, bf16[768,256]{1,0:T(8,128)(2,1)S(1)}, u32[]{:S(2)}, u32[]{:S(2)}) collective-permute-start(bf16[768,256]{1,0:T(8,128)(2,1)S(1)} %fusion.5), channel_id=1, source_target_pairs={{0,1},{1,3},{2,0},{3,2},{4,5},{5,7},{6,4},{7,6},{8,9},{9,11},{10,8... | collective-permute-start | bytes 1179656 | tf_op jit(solution)/shard_map/ppermute | solution.py:258
  39.2 4.4 %collective-permute-done.2.refs_3_.refs_6_ = bf16[768,256]{1,0:T(8,128)(2,1)S(1)} collective-permute-done((bf16[768,256]{1,0:T(8,128)(2,1)S(1)}, bf16[768,256]{1,0:T(8,128)(2,1)S(1)}, u32[]{:S(2)}, u32[]{:S(2)}) %collective-permute-start.2) | collective-permute-done | bytes 393248 | tf_op jit(solution)/shard_map/ppermute | solution.py:257
  43.6 4.1 %collective-permute-done.3.refs_4_.refs_7_ = bf16[768,256]{1,0:T(8,128)(2,1)S(1)} collective-permute-done((bf16[768,256]{1,0:T(8,128)(2,1)S(1)}, bf16[768,256]{1,0:T(8,128)(2,1)S(1)}, u32[]{:S(2)}, u32[]{:S(2)}) %collective-permute-start.3) | collective-permute-done | bytes 393248 | tf_op jit(solution)/shard_map/ppermute | solution.py:258
  47.7 0.7 copy-done.2
  48.4 1.0 all-to-all-done
  49.4 2.6 %collective-permute-start.4 = (bf16[768,384]{1,0:T(8,128)(2,1)}, bf16[768,384]{1,0:T(8,128)(2,1)}, u32[]{:S(2)}, u32[]{:S(2)}) collective-permute-start(bf16[768,384]{1,0:T(8,128)(2,1)} %bitcast.15.refs_0_), channel_id=1, source_target_pairs={{0,8},{2,58},{8,16},{10,2},{16,24},{18,10},{24,32},{26,18},{32,40}... | collective-permute-start | bytes 1769480 | tf_op jit(solution)/shard_map/ppermute | solution.py:272
  52.1 0.1 stack.47.index
  52.2 0.0 copy-start.3
  52.2 1.0 copy-done.3
  53.2 3.2 %shard_map.93 = (f32[768,512]{1,0:T(8,128)S(1)}, bf16[8,384,256]{2,1,0:T(8,128)(2,1)}, bf16[1,384,256]{2,1,0:T(8,128)(2,1)S(1)}) custom-call(s32[10]{0:T(128)S(1)} %stack.47.index, bf16[768,384]{1,0:T(8,128)(2,1)} %bitcast.15.refs_0_, bf16[8,384,256]{2,1,0:T(8,128)(2,1)S(1)} %bitcast.36, bf16[8,384,256]{2,1,0:T(8,128)(2,1)S(1)} %bitcast.44, ...), custom_call_target="tpu_custom_call" | custom-call | flops 603979776 | bytes 4000000 | tf_op jit(solution)/shard_map/pallas_call | solution.py:114
  56.4 2.7 %collective-permute-start.7 = (bf16[768,384]{1,0:T(8,128)(2,1)}, bf16[768,384]{1,0:T(8,128)(2,1)S(1)}, u32[]{:S(2)}, u32[]{:S(2)}) collective-permute-start(bf16[768,384]{1,0:T(8,128)(2,1)} %bitcast.15.refs_0_), channel_id=1, source_target_pairs={{0,56},{2,10},{8,0},{10,18},{16,8},{18,26},{24,16},{26,34},{32,24}... | collective-permute-start | bytes 1769480 | tf_op jit(solution)/shard_map/ppermute | solution.py:273
  59.1 1.6 %collective-permute-done.4.refs_0_ = bf16[768,384]{1,0:T(8,128)(2,1)} collective-permute-done((bf16[768,384]{1,0:T(8,128)(2,1)}, bf16[768,384]{1,0:T(8,128)(2,1)}, u32[]{:S(2)}, u32[]{:S(2)}) %collective-permute-start.4) | collective-permute-done | bytes 589856 | tf_op jit(solution)/shard_map/ppermute | solution.py:272
  60.7 4.2 %collective-permute-start.5 = (bf16[768,384]{1,0:T(8,128)(2,1)}, bf16[768,384]{1,0:T(8,128)(2,1)S(1)}, u32[]{:S(2)}, u32[]{:S(2)}) collective-permute-start(bf16[768,384]{1,0:T(8,128)(2,1)} %collective-permute-done.4.refs_0_), channel_id=1, source_target_pairs={{0,8},{2,58},{8,16},{10,2},{16,24},{18,10},{24,32},{26,18},{32,40}... | collective-permute-start | bytes 1769480 | tf_op jit(solution)/shard_map/ppermute | solution.py:272
  64.8 5.2 %collective-permute-done.7.refs_1_ = bf16[768,384]{1,0:T(8,128)(2,1)S(1)} collective-permute-done((bf16[768,384]{1,0:T(8,128)(2,1)}, bf16[768,384]{1,0:T(8,128)(2,1)S(1)}, u32[]{:S(2)}, u32[]{:S(2)}) %collective-permute-start.7) | collective-permute-done | bytes 589856 | tf_op jit(solution)/shard_map/ppermute | solution.py:273
  70.0 1.9 %collective-permute-start.9 = (bf16[768,384]{1,0:T(8,128)(2,1)S(1)}, bf16[768,384]{1,0:T(8,128)(2,1)S(1)}, u32[]{:S(2)}, u32[]{:S(2)}) collective-permute-start(bf16[768,384]{1,0:T(8,128)(2,1)S(1)} %collective-permute-done.7.refs_1_), channel_id=1, source_target_pairs={{0,56},{2,10},{8,0},{10,18},{16,8},{18,26},{24,16},{26,34},{32,24}... | collective-permute-start | bytes 1769480 | tf_op jit(solution)/shard_map/ppermute | solution.py:273
  72.0 4.0 %shard_map.94 = (f32[768,512]{1,0:T(8,128)S(1)}, bf16[8,384,256]{2,1,0:T(8,128)(2,1)}, bf16[2,384,256]{2,1,0:T(8,128)(2,1)S(1)}) custom-call(s32[10]{0:T(128)S(1)} %stack.47.index, bf16[768,384]{1,0:T(8,128)(2,1)} %collective-permute-done.4.refs_0_, ...), custom_call_target="tpu_custom_call", output_to_operand_aliasing={{0}: (9, {}), {1}: (10, {})} | custom-call | flops 1207959552 | bytes 8000000 | tf_op jit(solution)/shard_map/pallas_call | solution.py:114
  76.0 5.1 %collective-permute-start.8 = (bf16[768,384]{1,0:T(8,128)(2,1)S(1)}, bf16[768,384]{1,0:T(8,128)(2,1)S(1)}, u32[]{:S(2)}, u32[]{:S(2)}) collective-permute-start(bf16[768,384]{1,0:T(8,128)(2,1)S(1)} %collective-permute-done.5.refs_0_), channel_id=1, source_target_pairs={{0,8},{2,58},{8,16},{10,2},{16,24},{18,10},{24,32},{26,18},{32,40}... | collective-permute-start | bytes 1769480 | tf_op jit(solution)/shard_map/ppermute | solution.py:272
  81.1 4.0 %collective-permute-start.10 = (bf16[2,384,256]{2,1,0:T(8,128)(2,1)S(1)}, bf16[2,384,256]{2,1,0:T(8,128)(2,1)S(1)}, u32[]{:S(2)}, u32[]{:S(2)}) collective-permute-start(bf16[2,384,256]{2,1,0:T(8,128)(2,1)S(1)} %get-tuple-element.57), channel_id=1, source_target_pairs={{0,2},{2,0},{1,3},{3,1},{4,6},{6,4},{5,7},{7,5},{8,10},{10,8},{9,1... | collective-permute-start | bytes 1179656 | tf_op jit(solution)/shard_map/ppermute | solution.py:290
  85.1 2.9 %collective-permute-start.12 = (bf16[768,384]{1,0:T(8,128)(2,1)S(1)}, bf16[768,384]{1,0:T(8,128)(2,1)S(1)}, u32[]{:S(2)}, u32[]{:S(2)}) collective-permute-start(bf16[768,384]{1,0:T(8,128)(2,1)S(1)} %collective-permute-done.9.refs_1_), channel_id=1, source_target_pairs={{0,56},{2,10},{8,0},{10,18},{16,8},{18,26},{24,16},{26,34},{32,24}... | collective-permute-start | bytes 1769480 | tf_op jit(solution)/shard_map/ppermute | solution.py:273
  88.0 3.0 %shard_map.95 = (f32[768,512]{1,0:T(8,128)S(1)}, bf16[8,384,256]{2,1,0:T(8,128)(2,1)}, bf16[2,384,256]{2,1,0:T(8,128)(2,1)S(1)}) custom-call(s32[10]{0:T(128)S(1)} %stack.47.index, bf16[768,384]{1,0:T(8,128)(2,1)S(1)} %collective-permute-done.5.refs_0_, ...), custom_call_target="tpu_custom_call", output_to_operand_aliasing={{0}: (9, {}), {1}: (10, {})} | custom-call | flops 1207959552 | bytes 8000000 | tf_op jit(solution)/shard_map/pallas_call | solution.py:114
  91.0 4.6 %collective-permute-start.11 = (bf16[768,384]{1,0:T(8,128)(2,1)S(1)}, bf16[768,384]{1,0:T(8,128)(2,1)S(1)}, u32[]{:S(2)}, u32[]{:S(2)}) collective-permute-start(bf16[768,384]{1,0:T(8,128)(2,1)S(1)} %collective-permute-done.8.refs_0_), channel_id=1, source_target_pairs={{0,8},{2,58},{8,16},{10,2},{16,24},{18,10},{24,32},{26,18},{32,40}... | collective-permute-start | bytes 1769480 | tf_op jit(solution)/shard_map/ppermute | solution.py:272
  95.6 5.1 %collective-permute-start.13 = (bf16[2,384,256]{2,1,0:T(8,128)(2,1)S(1)}, bf16[2,384,256]{2,1,0:T(8,128)(2,1)S(1)}, u32[]{:S(2)}, u32[]{:S(2)}) collective-permute-start(bf16[2,384,256]{2,1,0:T(8,128)(2,1)S(1)} %get-tuple-element.63), channel_id=1, source_target_pairs={{0,2},{2,0},{1,3},{3,1},{4,6},{6,4},{5,7},{7,5},{8,10},{10,8},{9,1... | collective-permute-start | bytes 1179656 | tf_op jit(solution)/shard_map/ppermute | solution.py:290
  100.7 3.0 %shard_map.96 = (f32[768,512]{1,0:T(8,128)S(1)}, bf16[8,384,256]{2,1,0:T(8,128)(2,1)}, bf16[2,384,256]{2,1,0:T(8,128)(2,1)S(1)}) custom-call(s32[10]{0:T(128)S(1)} %stack.47.index, bf16[768,384]{1,0:T(8,128)(2,1)S(1)} %collective-permute-done.8.refs_0_, ...), custom_call_target="tpu_custom_call", output_to_operand_aliasing={{0}: (9, {}), {1}: (10, {})} | custom-call | flops 1207959552 | bytes 8000000 | tf_op jit(solution)/shard_map/pallas_call | solution.py:114
  103.7 0.9 broadcast_in_dim.10.combine_ref
  104.6 2.1 %collective-permute-done.11.refs_0_ = bf16[768,384]{1,0:T(8,128)(2,1)S(1)} collective-permute-done((bf16[768,384]{1,0:T(8,128)(2,1)S(1)}, bf16[768,384]{1,0:T(8,128)(2,1)S(1)}, u32[]{:S(2)}, u32[]{:S(2)}) %collective-permute-start.11) | collective-permute-done | bytes 589856 | tf_op jit(solution)/shard_map/ppermute | solution.py:272
  106.7 3.0 %shard_map.97 = (f32[768,256]{1,0:T(8,128)}, bf16[8,384,256]{2,1,0:T(8,128)(2,1)}, bf16[4,384,256]{2,1,0:T(8,128)(2,1)}, bf16[768,256]{1,0:T(8,128)(2,1)}, bf16[...) custom-call(s32[10]{0:T(128)S(1)} %stack.47.index, ...), custom_call_target="tpu_custom_call", output_to_operand_aliasing={{1}: (7, {})} | custom-call | flops 603979776 | bytes 4000000 | tf_op jit(solution)/shard_map/pallas_call | solution.py:114
  109.7 5.1 %collective-permute-start.16 = (bf16[4,384,256]{2,1,0:T(8,128)(2,1)}, bf16[4,384,256]{2,1,0:T(8,128)(2,1)S(1)}, u32[]{:S(2)}, u32[]{:S(2)}) collective-permute-start(bf16[4,384,256]{2,1,0:T(8,128)(2,1)} %get-tuple-element.78), channel_id=1, source_target_pairs={{0,2},{2,0},{1,3},{3,1},{4,6},{6,4},{5,7},{7,5},{8,10},{10,8},{9,1... | collective-permute-start | bytes 2359304 | tf_op jit(solution)/shard_map/ppermute | solution.py:303
  114.9 7.5 %collective-permute-start.14 = (bf16[768,256]{1,0:T(8,128)(2,1)}, bf16[768,256]{1,0:T(8,128)(2,1)S(1)}, u32[]{:S(2)}, u32[]{:S(2)}) collective-permute-start(bf16[768,256]{1,0:T(8,128)(2,1)} %get-tuple-element.70), channel_id=1, source_target_pairs={{2,3},{1,0},{0,2},{3,1},{6,7},{5,4},{4,6},{7,5},{10,11},{9,8},{8,1... | collective-permute-start | bytes 1179656 | tf_op jit(solution)/shard_map/ppermute | solution.py:299
  122.4 1.9 %collective-permute-start.15 = (bf16[768,256]{1,0:T(8,128)(2,1)}, bf16[768,256]{1,0:T(8,128)(2,1)}, u32[]{:S(2)}, u32[]{:S(2)}) collective-permute-start(bf16[768,256]{1,0:T(8,128)(2,1)} %get-tuple-element.71), channel_id=1, source_target_pairs={{2,1},{1,2},{6,5},{5,6},{10,9},{9,10},{14,13},{13,14},{18,17},{17,... | collective-permute-start | bytes 1179656 | tf_op jit(solution)/shard_map/ppermute | solution.py:300
  124.3 0.7 all_to_all.12
  125.0 10.7 %all-to-all-start.1 = ((f32[64,1,24]{2,1,0:T(1,128)}), f32[64,1,24]{2,1,0:T(1,128)}, u32[]{:S(2)}, u32[]{:S(2)}) async-start(f32[64,1,24]{2,1,0:T(1,128)} %bitcast.58), calls=%async_computation.1 | async-start | bytes 65536 | tf_op jit(solution)/shard_map/all_to_all | solution.py:302
  135.7 3.4 %shard_map.98 = (bf16[768,256]{1,0:T(8,128)(2,1)}, bf16[768,256]{1,0:T(8,128)(2,1)}) custom-call(s32[10]{0:T(128)S(1)} %stack.47.index, f32[768,256]{1,0:T(8,128)} %get-tuple-element.69.own, bf16[768,256]{1,0:T(8,128)(2,1)S(1)} %collective-permute-done.14.got_a, bf16[768,256]{1,0:T(8,128)(2,1)} %collective-permute-done.15.got_b, bf16[768,256]{1,0:T(8,128)(2,1)} %bitcast.54, ...), custom_call_target="tpu_custom_call" | custom-call | flops 3000000 | bytes 3500000 | tf_op jit(solution)/shard_map/pallas_call | solution.py:173
  139.2 2.0 %shard_map.99 = bf16[8,384,256]{2,1,0:T(8,128)(2,1)} custom-call(s32[10]{0:T(128)S(1)} %stack.47.index, bf16[8,384,256]{2,1,0:T(8,128)(2,1)S(1)} %copy-done.1, bf16[2,384,256]{2,1,0:T(8,128)(2,1)S(1)} %copy-done.5, bf16[2,384,256]{2,1,0:T(8,128)(2,1)S(1)} %copy-done.7, bf16[4,384,256]{2,1,0:T(8,128)(2,1)S(1)} %collective-permute-done.16.refs_2_), custom_call_target="tpu_custom_call" | custom-call | flops 1000000 | bytes 5000000 | tf_op jit(solution)/shard_map/pallas_call | solution.py:141
  141.2 3.9 %all-to-all-done.1 = f32[64,1,24]{2,1,0:T(1,128)} async-done(((f32[64,1,24]{2,1,0:T(1,128)}), f32[64,1,24]{2,1,0:T(1,128)}, u32[]{:S(2)}, u32[]{:S(2)}) %all-to-all-start.1) | async-done | bytes 6176 | tf_op jit(solution)/shard_map/all_to_all | solution.py:302
  145.1 0.8 reduce_sum.29
  145.8 0.5 divide_bitcast_fusion
  (36 shorter events, 0.2 us)
Async XLA Ops:
  2.3 27.5 %copy-start.9 = (f32[1,1,768]{2,1,0:T(1,128)S(1)}, f32[1,1,768]{2,1,0:T(1,128)}, u32[]{:S(2)}) copy-start(f32[1,1,768]{2,1,0:T(1,128)} %param.8) | copy-start | bytes 9220
  2.3 27.6 %copy-start.8 = (bf16[1,1,768,256]{3,2,1,0:T(8,128)(2,1)S(1)}, bf16[1,1,768,256]{3,2,1,0:T(8,128)(2,1)}, u32[]{:S(2)}) copy-start(bf16[1,1,768,256]{3,2,1,0:T(8,128)(2,1)} %param.10) | copy-start | bytes 1179652
  2.3 14.3 %collective-permute-start = (bf16[192,194]{0,1:T(8,128)(2,1)S(1)}, bf16[192,194]{0,1:T(8,128)(2,1)S(1)}, u32[]{:S(2)}, u32[]{:S(2)}) collective-permute-start(bf16[192,194]{0,1:T(8,128)(2,1)S(1)} %pad_maximum_fusion), channel_id=1, source_target_pairs={{0,48},{1,50},{2,52},{3,54},{4,56},{5,58},{6,60},{7,62},{8,0},{9,2... | collective-permute-start | bytes 223496 | tf_op jit(solution)/shard_map/ppermute | solution.py:234
  10.7 7.8 %collective-permute-start.1 = (bf16[192,192]{0,1:T(8,128)(2,1)S(1)}, bf16[192,192]{0,1:T(8,128)(2,1)S(1)}, u32[]{:S(2)}, u32[]{:S(2)}) collective-permute-start(bf16[192,192]{0,1:T(8,128)(2,1)S(1)} %bitcast.57), channel_id=1, source_target_pairs={{0,52},{1,54},{2,48},{3,50},{4,60},{5,62},{6,56},{7,58},{8,4},{9,6... | collective-permute-start | bytes 221192 | tf_op jit(solution)/shard_map/ppermute | solution.py:235
  14.7 37.5 %collective-permute-start.6 = (bf16[3072,256]{1,0:T(8,128)(2,1)}, bf16[3072,256]{1,0:T(8,128)(2,1)S(1)}, u32[]{:S(2)}, u32[]{:S(2)}) collective-permute-start(bf16[3072,256]{1,0:T(8,128)(2,1)} %bitcast.35), channel_id=1, source_target_pairs={{0,2},{2,0},{1,3},{3,1},{4,6},{6,4},{5,7},{7,5},{8,10},{10,8},{9,1... | collective-permute-start | bytes 4718600 | tf_op jit(solution)/shard_map/ppermute | solution.py:250
  19.7 32.5 %copy-start = (bf16[1,3072,256]{2,1,0:T(8,128)(2,1)S(1)}, bf16[1,3072,256]{2,1,0:T(8,128)(2,1)}, u32[]{:S(2)}) copy-start(bf16[1,3072,256]{2,1,0:T(8,128)(2,1)} %param.11) | copy-start | bytes 4718596
  19.7 29.7 %all-to-all-start = ((bf16[8,96,384]{2,1,0:T(8,128)(2,1)}), bf16[8,96,384]{2,1,0:T(8,128)(2,1)}, u32[]{:S(2)}, u32[]{:S(2)}) async-start(bf16[8,96,384]{2,1,0:T(8,128)(2,1)} %bitcast.55), calls=%async_computation | async-start | bytes 1179648 | tf_op jit(solution)/shard_map/all_to_all | solution.py:241
  31.2 12.3 %collective-permute-start.2 = (bf16[768,256]{1,0:T(8,128)(2,1)S(1)}, bf16[768,256]{1,0:T(8,128)(2,1)S(1)}, u32[]{:S(2)}, u32[]{:S(2)}) collective-permute-start(bf16[768,256]{1,0:T(8,128)(2,1)S(1)} %fusion.5), channel_id=1, source_target_pairs={{0,0},{1,2},{2,1},{3,3},{4,4},{5,6},{6,5},{7,7},{8,8},{9,10},{10,9... | collective-permute-start | bytes 1179656 | tf_op jit(solution)/shard_map/ppermute | solution.py:257
  37.2 10.4 %collective-permute-start.3 = (bf16[768,256]{1,0:T(8,128)(2,1)S(1)}, bf16[768,256]{1,0:T(8,128)(2,1)S(1)}, u32[]{:S(2)}, u32[]{:S(2)}) collective-permute-start(bf16[768,256]{1,0:T(8,128)(2,1)S(1)} %fusion.5), channel_id=1, source_target_pairs={{0,1},{1,3},{2,0},{3,2},{4,5},{5,7},{6,4},{7,6},{8,9},{9,11},{10,8... | collective-permute-start | bytes 1179656 | tf_op jit(solution)/shard_map/ppermute | solution.py:258
  47.7 0.7 copy-start.2
  49.4 11.2 %collective-permute-start.4 = (bf16[768,384]{1,0:T(8,128)(2,1)}, bf16[768,384]{1,0:T(8,128)(2,1)}, u32[]{:S(2)}, u32[]{:S(2)}) collective-permute-start(bf16[768,384]{1,0:T(8,128)(2,1)} %bitcast.15.refs_0_), channel_id=1, source_target_pairs={{0,8},{2,58},{8,16},{10,2},{16,24},{18,10},{24,32},{26,18},{32,40}... | collective-permute-start | bytes 1769480 | tf_op jit(solution)/shard_map/ppermute | solution.py:272
  52.2 1.0 copy-start.3
  56.4 13.6 %collective-permute-start.7 = (bf16[768,384]{1,0:T(8,128)(2,1)}, bf16[768,384]{1,0:T(8,128)(2,1)S(1)}, u32[]{:S(2)}, u32[]{:S(2)}) collective-permute-start(bf16[768,384]{1,0:T(8,128)(2,1)} %bitcast.15.refs_0_), channel_id=1, source_target_pairs={{0,56},{2,10},{8,0},{10,18},{16,8},{18,26},{24,16},{26,34},{32,24}... | collective-permute-start | bytes 1769480 | tf_op jit(solution)/shard_map/ppermute | solution.py:273
  60.7 15.3 %collective-permute-start.5 = (bf16[768,384]{1,0:T(8,128)(2,1)}, bf16[768,384]{1,0:T(8,128)(2,1)S(1)}, u32[]{:S(2)}, u32[]{:S(2)}) collective-permute-start(bf16[768,384]{1,0:T(8,128)(2,1)} %collective-permute-done.4.refs_0_), channel_id=1, source_target_pairs={{0,8},{2,58},{8,16},{10,2},{16,24},{18,10},{24,32},{26,18},{32,40}... | collective-permute-start | bytes 1769480 | tf_op jit(solution)/shard_map/ppermute | solution.py:272
  70.0 15.1 %collective-permute-start.9 = (bf16[768,384]{1,0:T(8,128)(2,1)S(1)}, bf16[768,384]{1,0:T(8,128)(2,1)S(1)}, u32[]{:S(2)}, u32[]{:S(2)}) collective-permute-start(bf16[768,384]{1,0:T(8,128)(2,1)S(1)} %collective-permute-done.7.refs_1_), channel_id=1, source_target_pairs={{0,56},{2,10},{8,0},{10,18},{16,8},{18,26},{24,16},{26,34},{32,24}... | collective-permute-start | bytes 1769480 | tf_op jit(solution)/shard_map/ppermute | solution.py:273
  76.0 15.0 %collective-permute-start.8 = (bf16[768,384]{1,0:T(8,128)(2,1)S(1)}, bf16[768,384]{1,0:T(8,128)(2,1)S(1)}, u32[]{:S(2)}, u32[]{:S(2)}) collective-permute-start(bf16[768,384]{1,0:T(8,128)(2,1)S(1)} %collective-permute-done.5.refs_0_), channel_id=1, source_target_pairs={{0,8},{2,58},{8,16},{10,2},{16,24},{18,10},{24,32},{26,18},{32,40}... | collective-permute-start | bytes 1769480 | tf_op jit(solution)/shard_map/ppermute | solution.py:272
  81.1 9.9 %collective-permute-start.10 = (bf16[2,384,256]{2,1,0:T(8,128)(2,1)S(1)}, bf16[2,384,256]{2,1,0:T(8,128)(2,1)S(1)}, u32[]{:S(2)}, u32[]{:S(2)}) collective-permute-start(bf16[2,384,256]{2,1,0:T(8,128)(2,1)S(1)} %get-tuple-element.57), channel_id=1, source_target_pairs={{0,2},{2,0},{1,3},{3,1},{4,6},{6,4},{5,7},{7,5},{8,10},{10,8},{9,1... | collective-permute-start | bytes 1179656 | tf_op jit(solution)/shard_map/ppermute | solution.py:290
  85.1 15.5 %collective-permute-start.12 = (bf16[768,384]{1,0:T(8,128)(2,1)S(1)}, bf16[768,384]{1,0:T(8,128)(2,1)S(1)}, u32[]{:S(2)}, u32[]{:S(2)}) collective-permute-start(bf16[768,384]{1,0:T(8,128)(2,1)S(1)} %collective-permute-done.9.refs_1_), channel_id=1, source_target_pairs={{0,56},{2,10},{8,0},{10,18},{16,8},{18,26},{24,16},{26,34},{32,24}... | collective-permute-start | bytes 1769480 | tf_op jit(solution)/shard_map/ppermute | solution.py:273
  91.0 12.7 %copy-start.4 = (bf16[2,384,256]{2,1,0:T(8,128)(2,1)}, bf16[2,384,256]{2,1,0:T(8,128)(2,1)S(1)}, u32[]{:S(2)}) copy-start(bf16[2,384,256]{2,1,0:T(8,128)(2,1)S(1)} %collective-permute-done.10.refs_0_) | copy-start | bytes 1179652
  91.0 15.7 %collective-permute-start.11 = (bf16[768,384]{1,0:T(8,128)(2,1)S(1)}, bf16[768,384]{1,0:T(8,128)(2,1)S(1)}, u32[]{:S(2)}, u32[]{:S(2)}) collective-permute-start(bf16[768,384]{1,0:T(8,128)(2,1)S(1)} %collective-permute-done.8.refs_0_), channel_id=1, source_target_pairs={{0,8},{2,58},{8,16},{10,2},{16,24},{18,10},{24,32},{26,18},{32,40}... | collective-permute-start | bytes 1769480 | tf_op jit(solution)/shard_map/ppermute | solution.py:272
  95.6 8.1 %collective-permute-start.13 = (bf16[2,384,256]{2,1,0:T(8,128)(2,1)S(1)}, bf16[2,384,256]{2,1,0:T(8,128)(2,1)S(1)}, u32[]{:S(2)}, u32[]{:S(2)}) collective-permute-start(bf16[2,384,256]{2,1,0:T(8,128)(2,1)S(1)} %get-tuple-element.63), channel_id=1, source_target_pairs={{0,2},{2,0},{1,3},{3,1},{4,6},{6,4},{5,7},{7,5},{8,10},{10,8},{9,1... | collective-permute-start | bytes 1179656 | tf_op jit(solution)/shard_map/ppermute | solution.py:290
  103.7 6.0 %copy-start.6 = (bf16[2,384,256]{2,1,0:T(8,128)(2,1)}, bf16[2,384,256]{2,1,0:T(8,128)(2,1)S(1)}, u32[]{:S(2)}) copy-start(bf16[2,384,256]{2,1,0:T(8,128)(2,1)S(1)} %collective-permute-done.13.refs_1_) | copy-start | bytes 1179652
  109.7 29.5 %copy-start.1 = (bf16[8,384,256]{2,1,0:T(8,128)(2,1)S(1)}, bf16[8,384,256]{2,1,0:T(8,128)(2,1)}, u32[]{:S(2)}) copy-start(bf16[8,384,256]{2,1,0:T(8,128)(2,1)} %get-tuple-element.75.mine) | copy-start | bytes 4718596
  109.7 29.5 %copy-start.5 = (bf16[2,384,256]{2,1,0:T(8,128)(2,1)S(1)}, bf16[2,384,256]{2,1,0:T(8,128)(2,1)}, u32[]{:S(2)}) copy-start(bf16[2,384,256]{2,1,0:T(8,128)(2,1)} %copy-done.4) | copy-start | bytes 1179652
  109.7 29.5 %copy-start.7 = (bf16[2,384,256]{2,1,0:T(8,128)(2,1)S(1)}, bf16[2,384,256]{2,1,0:T(8,128)(2,1)}, u32[]{:S(2)}) copy-start(bf16[2,384,256]{2,1,0:T(8,128)(2,1)} %copy-done.6) | copy-start | bytes 1179652
  109.7 29.4 %collective-permute-start.16 = (bf16[4,384,256]{2,1,0:T(8,128)(2,1)}, bf16[4,384,256]{2,1,0:T(8,128)(2,1)S(1)}, u32[]{:S(2)}, u32[]{:S(2)}) collective-permute-start(bf16[4,384,256]{2,1,0:T(8,128)(2,1)} %get-tuple-element.78), channel_id=1, source_target_pairs={{0,2},{2,0},{1,3},{3,1},{4,6},{6,4},{5,7},{7,5},{8,10},{10,8},{9,1... | collective-permute-start | bytes 2359304 | tf_op jit(solution)/shard_map/ppermute | solution.py:303
  114.9 20.9 %collective-permute-start.14 = (bf16[768,256]{1,0:T(8,128)(2,1)}, bf16[768,256]{1,0:T(8,128)(2,1)S(1)}, u32[]{:S(2)}, u32[]{:S(2)}) collective-permute-start(bf16[768,256]{1,0:T(8,128)(2,1)} %get-tuple-element.70), channel_id=1, source_target_pairs={{2,3},{1,0},{0,2},{3,1},{6,7},{5,4},{4,6},{7,5},{10,11},{9,8},{8,1... | collective-permute-start | bytes 1179656 | tf_op jit(solution)/shard_map/ppermute | solution.py:299
  122.4 13.3 %collective-permute-start.15 = (bf16[768,256]{1,0:T(8,128)(2,1)}, bf16[768,256]{1,0:T(8,128)(2,1)}, u32[]{:S(2)}, u32[]{:S(2)}) collective-permute-start(bf16[768,256]{1,0:T(8,128)(2,1)} %get-tuple-element.71), channel_id=1, source_target_pairs={{2,1},{1,2},{6,5},{5,6},{10,9},{9,10},{14,13},{13,14},{18,17},{17,... | collective-permute-start | bytes 1179656 | tf_op jit(solution)/shard_map/ppermute | solution.py:300
  125.0 20.1 %all-to-all-start.1 = ((f32[64,1,24]{2,1,0:T(1,128)}), f32[64,1,24]{2,1,0:T(1,128)}, u32[]{:S(2)}, u32[]{:S(2)}) async-start(f32[64,1,24]{2,1,0:T(1,128)} %bitcast.58), calls=%async_computation.1 | async-start | bytes 65536 | tf_op jit(solution)/shard_map/all_to_all | solution.py:302

commit v14 on v11

--- a/solution.py
+++ b/solution.py
@@ -127,6 +127,7 @@
     def whole(a):
         return pl.BlockSpec(a.shape, lambda i, idx: (0, 0, 0))
 
+    mine = pltpu.with_memory_space_constraint(mine, pltpu.HBM)
     return pl.pallas_call(
         functools.partial(place_kernel, tuple(partner)),
         grid_spec=pltpu.PrefetchScalarGridSpec(

time: 147 us -> 146 us (level)
  transfers between devices with their start and end apart: 17 -> 17, of which waited for: 11 -> 11; matrix products, arithmetic and copies ran while one was open for 3% -> 3% of each run, Pallas kernels for 13% -> 14%
where the time goes in v14:
time: 146 us; the launch traced here: 145 us
  starting transfers between devices  80.2 us (55%)
  waiting for transfers between devices  32.1 us (22%)
  Pallas kernels  22.9 us (16%)
  local copies, waits for them, and re-layouts  4.54 us (3%)
  other arithmetic  2.62 us (2%)
    ppermute x4, starting transfers between devices, local(): on_a = lambda v: lax.ppermute(v, ('y', 'core'), ring_a)  16.9 us
    pallas_call x5, Pallas kernels, use(): pl.pallas_call(functools.partial(use_kernel, blocks, first, last), grid_s...  16.2 us
    ppermute x3, waiting for transfers between devices, local(): on_b = lambda v: lax.ppermute(v, ('y', 'core'), ring_b)  10.9 us
    all_to_all x1, starting transfers between devices, local(): lax.all_to_all(outgoing, 'expert', split_axis=0, concat_axis=0, tiled=True)  10.2 us
    all_to_all x1, starting transfers between devices, local(): lax.all_to_all(mix.reshape(members, share), ('dp', 'y', 'xlo', 'core'), 0...  9.17 us
    ppermute x1, starting transfers between devices, local(): late = lax.ppermute(theirs, 'core', swap)  8.35 us
    ppermute x1, starting transfers between devices, local(): lax.ppermute(jnp.concatenate([cotangent[0], ids], axis=1), every, token_m...  8.33 us
    ppermute x4, waiting for transfers between devices, local(): on_a = lambda v: lax.ppermute(v, ('y', 'core'), ring_a)  7.32 us
  transfers between devices with their start and end apart: 17, of which 11 were waited for; matrix products, arithmetic and copies ran while one was open for 3% of the time, Pallas kernels for 14%

profile of v14, /device:TPU:1, one launch (start us, length us, event | category | flops | bytes accessed | tf_op | source)
XLA Modules:
  0.0 144.7 jit_solution(9783016939948677078)
XLA Ops:
  0.6 1.0 copy.28
  1.6 0.7 convert_bitcast_fusion
  2.3 8.3 %collective-permute-start = (bf16[192,194]{0,1:T(8,128)(2,1)S(1)}, bf16[192,194]{0,1:T(8,128)(2,1)S(1)}, u32[]{:S(2)}, u32[]{:S(2)}) collective-permute-start(bf16[192,194]{0,1:T(8,128)(2,1)S(1)} %pad_maximum_fusion), channel_id=1, source_target_pairs={{0,48},{1,50},{2,52},{3,54},{4,56},{5,58},{6,60},{7,62},{8,0},{9,2... | collective-permute-start | bytes 223496 | tf_op jit(solution)/shard_map/ppermute | solution.py:224
  10.7 4.0 %collective-permute-start.1 = (bf16[192,192]{0,1:T(8,128)(2,1)S(1)}, bf16[192,192]{0,1:T(8,128)(2,1)S(1)}, u32[]{:S(2)}, u32[]{:S(2)}) collective-permute-start(bf16[192,192]{0,1:T(8,128)(2,1)S(1)} %bitcast.57), channel_id=1, source_target_pairs={{0,52},{1,54},{2,48},{3,50},{4,60},{5,62},{6,56},{7,58},{8,4},{9,6... | collective-permute-start | bytes 221192 | tf_op jit(solution)/shard_map/ppermute | solution.py:225
  14.7 1.9 %collective-permute-start.6 = (bf16[3072,256]{1,0:T(8,128)(2,1)}, bf16[3072,256]{1,0:T(8,128)(2,1)S(1)}, u32[]{:S(2)}, u32[]{:S(2)}) collective-permute-start(bf16[3072,256]{1,0:T(8,128)(2,1)} %bitcast.35), channel_id=1, source_target_pairs={{0,2},{2,0},{1,3},{3,1},{4,6},{6,4},{5,7},{7,5},{8,10},{10,8},{9,1... | collective-permute-start | bytes 4718600 | tf_op jit(solution)/shard_map/ppermute | solution.py:240
  16.7 0.1 fusion.13
  16.9 1.6 %collective-permute-done.1 = bf16[192,192]{0,1:T(8,128)(2,1)S(1)} collective-permute-done((bf16[192,192]{0,1:T(8,128)(2,1)S(1)}, bf16[192,192]{0,1:T(8,128)(2,1)S(1)}, u32[]{:S(2)}, u32[]{:S(2)}) %collective-permute-start.1) | collective-permute-done | bytes 73760 | tf_op jit(solution)/shard_map/ppermute | solution.py:225
  18.5 1.2 convolution_convert_fusion
  19.7 10.2 %all-to-all-start = ((bf16[8,96,384]{2,1,0:T(8,128)(2,1)}), bf16[8,96,384]{2,1,0:T(8,128)(2,1)}, u32[]{:S(2)}, u32[]{:S(2)}) async-start(bf16[8,96,384]{2,1,0:T(8,128)(2,1)} %bitcast.55), calls=%async_computation | async-start | bytes 1179648 | tf_op jit(solution)/shard_map/all_to_all | solution.py:231
  29.9 0.1 dynamic-slice_bitcast_fusion
  30.0 1.3 fusion.5
  31.2 6.0 %collective-permute-start.2 = (bf16[768,256]{1,0:T(8,128)(2,1)S(1)}, bf16[768,256]{1,0:T(8,128)(2,1)S(1)}, u32[]{:S(2)}, u32[]{:S(2)}) collective-permute-start(bf16[768,256]{1,0:T(8,128)(2,1)S(1)} %fusion.5), channel_id=1, source_target_pairs={{0,0},{1,2},{2,1},{3,3},{4,4},{5,6},{6,5},{7,7},{8,8},{9,10},{10,9... | collective-permute-start | bytes 1179656 | tf_op jit(solution)/shard_map/ppermute | solution.py:247
  37.2 1.9 %collective-permute-start.3 = (bf16[768,256]{1,0:T(8,128)(2,1)S(1)}, bf16[768,256]{1,0:T(8,128)(2,1)S(1)}, u32[]{:S(2)}, u32[]{:S(2)}) collective-permute-start(bf16[768,256]{1,0:T(8,128)(2,1)S(1)} %fusion.5), channel_id=1, source_target_pairs={{0,1},{1,3},{2,0},{3,2},{4,5},{5,7},{6,4},{7,6},{8,9},{9,11},{10,8... | collective-permute-start | bytes 1179656 | tf_op jit(solution)/shard_map/ppermute | solution.py:248
  39.2 4.4 %collective-permute-done.2.refs_3_.refs_6_ = bf16[768,256]{1,0:T(8,128)(2,1)S(1)} collective-permute-done((bf16[768,256]{1,0:T(8,128)(2,1)S(1)}, bf16[768,256]{1,0:T(8,128)(2,1)S(1)}, u32[]{:S(2)}, u32[]{:S(2)}) %collective-permute-start.2) | collective-permute-done | bytes 393248 | tf_op jit(solution)/shard_map/ppermute | solution.py:247
  43.6 4.1 %collective-permute-done.3.refs_4_.refs_7_ = bf16[768,256]{1,0:T(8,128)(2,1)S(1)} collective-permute-done((bf16[768,256]{1,0:T(8,128)(2,1)S(1)}, bf16[768,256]{1,0:T(8,128)(2,1)S(1)}, u32[]{:S(2)}, u32[]{:S(2)}) %collective-permute-start.3) | collective-permute-done | bytes 393248 | tf_op jit(solution)/shard_map/ppermute | solution.py:248
  47.7 0.7 copy-done.1
  48.4 1.0 all-to-all-done
  49.4 2.6 %collective-permute-start.4 = (bf16[768,384]{1,0:T(8,128)(2,1)}, bf16[768,384]{1,0:T(8,128)(2,1)}, u32[]{:S(2)}, u32[]{:S(2)}) collective-permute-start(bf16[768,384]{1,0:T(8,128)(2,1)} %bitcast.15.refs_0_), channel_id=1, source_target_pairs={{0,8},{2,58},{8,16},{10,2},{16,24},{18,10},{24,32},{26,18},{32,40}... | collective-permute-start | bytes 1769480 | tf_op jit(solution)/shard_map/ppermute | solution.py:258
  52.1 0.1 stack.47.index
  52.2 0.0 copy-start.2
  52.2 1.0 copy-done.2
  53.2 3.2 %shard_map.93 = (f32[768,512]{1,0:T(8,128)S(1)}, bf16[8,384,256]{2,1,0:T(8,128)(2,1)}, bf16[8,384,256]{2,1,0:T(8,128)(2,1)}) custom-call(s32[10]{0:T(128)S(1)} %stack.47.index, bf16[768,384]{1,0:T(8,128)(2,1)} %bitcast.15.refs_0_, bf16[8,384,256]{2,1,0:T(8,128)(2,1)S(1)} %bitcast.36, bf16[8,384,256]{2,1,0:T(8,128)(2,1)S(1)} %bitcast.44, ...), custom_call_target="tpu_custom_call" | custom-call | flops 603979776 | bytes 4000000 | tf_op jit(solution)/shard_map/pallas_call | solution.py:104
  56.5 2.7 %collective-permute-start.7 = (bf16[768,384]{1,0:T(8,128)(2,1)}, bf16[768,384]{1,0:T(8,128)(2,1)S(1)}, u32[]{:S(2)}, u32[]{:S(2)}) collective-permute-start(bf16[768,384]{1,0:T(8,128)(2,1)} %bitcast.15.refs_0_), channel_id=1, source_target_pairs={{0,56},{2,10},{8,0},{10,18},{16,8},{18,26},{24,16},{26,34},{32,24}... | collective-permute-start | bytes 1769480 | tf_op jit(solution)/shard_map/ppermute | solution.py:259
  59.1 1.5 %collective-permute-done.4.refs_0_ = bf16[768,384]{1,0:T(8,128)(2,1)} collective-permute-done((bf16[768,384]{1,0:T(8,128)(2,1)}, bf16[768,384]{1,0:T(8,128)(2,1)}, u32[]{:S(2)}, u32[]{:S(2)}) %collective-permute-start.4) | collective-permute-done | bytes 589856 | tf_op jit(solution)/shard_map/ppermute | solution.py:258
  60.7 4.2 %collective-permute-start.5 = (bf16[768,384]{1,0:T(8,128)(2,1)}, bf16[768,384]{1,0:T(8,128)(2,1)S(1)}, u32[]{:S(2)}, u32[]{:S(2)}) collective-permute-start(bf16[768,384]{1,0:T(8,128)(2,1)} %collective-permute-done.4.refs_0_), channel_id=1, source_target_pairs={{0,8},{2,58},{8,16},{10,2},{16,24},{18,10},{24,32},{26,18},{32,40}... | collective-permute-start | bytes 1769480 | tf_op jit(solution)/shard_map/ppermute | solution.py:258
  64.8 5.3 %collective-permute-done.7.refs_1_ = bf16[768,384]{1,0:T(8,128)(2,1)S(1)} collective-permute-done((bf16[768,384]{1,0:T(8,128)(2,1)}, bf16[768,384]{1,0:T(8,128)(2,1)S(1)}, u32[]{:S(2)}, u32[]{:S(2)}) %collective-permute-start.7) | collective-permute-done | bytes 589856 | tf_op jit(solution)/shard_map/ppermute | solution.py:259
  70.2 1.9 %collective-permute-start.9 = (bf16[768,384]{1,0:T(8,128)(2,1)S(1)}, bf16[768,384]{1,0:T(8,128)(2,1)S(1)}, u32[]{:S(2)}, u32[]{:S(2)}) collective-permute-start(bf16[768,384]{1,0:T(8,128)(2,1)S(1)} %collective-permute-done.7.refs_1_), channel_id=1, source_target_pairs={{0,56},{2,10},{8,0},{10,18},{16,8},{18,26},{24,16},{26,34},{32,24}... | collective-permute-start | bytes 1769480 | tf_op jit(solution)/shard_map/ppermute | solution.py:259
  72.1 4.2 %shard_map.94 = (f32[768,512]{1,0:T(8,128)S(1)}, bf16[8,384,256]{2,1,0:T(8,128)(2,1)}, bf16[8,384,256]{2,1,0:T(8,128)(2,1)}) custom-call(s32[10]{0:T(128)S(1)} %stack.47.index, bf16[768,384]{1,0:T(8,128)(2,1)} %collective-permute-done.4.refs_0_, ...), custom_call_target="tpu_custom_call", output_to_operand_aliasing={{0}: (9, {}), {1}: (10, {}), {2}: (11, {})} | custom-call | flops 1207959552 | bytes 8000000 | tf_op jit(solution)/shard_map/pallas_call | solution.py:104
  76.2 5.1 %collective-permute-start.8 = (bf16[768,384]{1,0:T(8,128)(2,1)S(1)}, bf16[768,384]{1,0:T(8,128)(2,1)S(1)}, u32[]{:S(2)}, u32[]{:S(2)}) collective-permute-start(bf16[768,384]{1,0:T(8,128)(2,1)S(1)} %collective-permute-done.5.refs_0_), channel_id=1, source_target_pairs={{0,8},{2,58},{8,16},{10,2},{16,24},{18,10},{24,32},{26,18},{32,40}... | collective-permute-start | bytes 1769480 | tf_op jit(solution)/shard_map/ppermute | solution.py:258
  81.4 1.2 collective-permute-done.9.refs_1_
  82.6 1.9 %collective-permute-start.11 = (bf16[768,384]{1,0:T(8,128)(2,1)S(1)}, bf16[768,384]{1,0:T(8,128)(2,1)S(1)}, u32[]{:S(2)}, u32[]{:S(2)}) collective-permute-start(bf16[768,384]{1,0:T(8,128)(2,1)S(1)} %collective-permute-done.9.refs_1_), channel_id=1, source_target_pairs={{0,56},{2,10},{8,0},{10,18},{16,8},{18,26},{24,16},{26,34},{32,24}... | collective-permute-start | bytes 1769480 | tf_op jit(solution)/shard_map/ppermute | solution.py:259
  84.5 3.1 %shard_map.95 = (f32[768,512]{1,0:T(8,128)S(1)}, bf16[8,384,256]{2,1,0:T(8,128)(2,1)}, bf16[8,384,256]{2,1,0:T(8,128)(2,1)}) custom-call(s32[10]{0:T(128)S(1)} %stack.47.index, bf16[768,384]{1,0:T(8,128)(2,1)S(1)} %collective-permute-done.5.refs_0_, ...), custom_call_target="tpu_custom_call", output_to_operand_aliasing={{0}: (9, {}), {1}: (10, {}), {2}: (11, {})} | custom-call | flops 1207959552 | bytes 8000000 | tf_op jit(solution)/shard_map/pallas_call | solution.py:104
  87.6 3.1 %collective-permute-done.8.refs_0_ = bf16[768,384]{1,0:T(8,128)(2,1)S(1)} collective-permute-done((bf16[768,384]{1,0:T(8,128)(2,1)S(1)}, bf16[768,384]{1,0:T(8,128)(2,1)S(1)}, u32[]{:S(2)}, u32[]{:S(2)}) %collective-permute-start.8) | collective-permute-done | bytes 589856 | tf_op jit(solution)/shard_map/ppermute | solution.py:258
  90.7 5.0 %collective-permute-start.10 = (bf16[768,384]{1,0:T(8,128)(2,1)S(1)}, bf16[768,384]{1,0:T(8,128)(2,1)S(1)}, u32[]{:S(2)}, u32[]{:S(2)}) collective-permute-start(bf16[768,384]{1,0:T(8,128)(2,1)S(1)} %collective-permute-done.8.refs_0_), channel_id=1, source_target_pairs={{0,8},{2,58},{8,16},{10,2},{16,24},{18,10},{24,32},{26,18},{32,40}... | collective-permute-start | bytes 1769480 | tf_op jit(solution)/shard_map/ppermute | solution.py:258
  95.7 4.4 %collective-permute-done.11.refs_1_ = bf16[768,384]{1,0:T(8,128)(2,1)S(1)} collective-permute-done((bf16[768,384]{1,0:T(8,128)(2,1)S(1)}, bf16[768,384]{1,0:T(8,128)(2,1)S(1)}, u32[]{:S(2)}, u32[]{:S(2)}) %collective-permute-start.11) | collective-permute-done | bytes 589856 | tf_op jit(solution)/shard_map/ppermute | solution.py:259
  100.2 3.1 %shard_map.96 = (f32[768,512]{1,0:T(8,128)S(1)}, bf16[8,384,256]{2,1,0:T(8,128)(2,1)}, bf16[8,384,256]{2,1,0:T(8,128)(2,1)}) custom-call(s32[10]{0:T(128)S(1)} %stack.47.index, bf16[768,384]{1,0:T(8,128)(2,1)S(1)} %collective-permute-done.8.refs_0_, ...), custom_call_target="tpu_custom_call", output_to_operand_aliasing={{0}: (9, {}), {1}: (10, {}), {2}: (11, {})} | custom-call | flops 1207959552 | bytes 8000000 | tf_op jit(solution)/shard_map/pallas_call | solution.py:104
  103.3 0.9 broadcast_in_dim.10.combine_ref
  104.2 2.7 %collective-permute-done.10.refs_0_ = bf16[768,384]{1,0:T(8,128)(2,1)S(1)} collective-permute-done((bf16[768,384]{1,0:T(8,128)(2,1)S(1)}, bf16[768,384]{1,0:T(8,128)(2,1)S(1)}, u32[]{:S(2)}, u32[]{:S(2)}) %collective-permute-start.10) | collective-permute-done | bytes 589856 | tf_op jit(solution)/shard_map/ppermute | solution.py:258
  106.9 2.5 %shard_map.97 = (f32[768,256]{1,0:T(8,128)}, bf16[8,384,256]{2,1,0:T(8,128)(2,1)}, bf16[8,384,256]{2,1,0:T(8,128)(2,1)}, bf16[768,256]{1,0:T(8,128)(2,1)}, bf16[...) custom-call(s32[10]{0:T(128)S(1)} %stack.47.index, ...), custom_call_target="tpu_custom_call", output_to_operand_aliasing={{1}: (7, {}), {2}: (8, {})} | custom-call | flops 603979776 | bytes 4000000 | tf_op jit(solution)/shard_map/pallas_call | solution.py:104
  109.4 8.3 %collective-permute-start.14 = (bf16[8,384,256]{2,1,0:T(8,128)(2,1)}, bf16[8,384,256]{2,1,0:T(8,128)(2,1)S(1)}, u32[]{:S(2)}, u32[]{:S(2)}) collective-permute-start(bf16[8,384,256]{2,1,0:T(8,128)(2,1)} %get-tuple-element.72), channel_id=1, source_target_pairs={{0,2},{2,0},{1,3},{3,1},{4,6},{6,4},{5,7},{7,5},{8,10},{10,8},{9,1... | collective-permute-start | bytes 4718600 | tf_op jit(solution)/shard_map/ppermute | solution.py:287
  117.8 4.2 %collective-permute-start.12 = (bf16[768,256]{1,0:T(8,128)(2,1)}, bf16[768,256]{1,0:T(8,128)(2,1)S(1)}, u32[]{:S(2)}, u32[]{:S(2)}) collective-permute-start(bf16[768,256]{1,0:T(8,128)(2,1)} %get-tuple-element.66), channel_id=1, source_target_pairs={{2,3},{1,0},{0,2},{3,1},{6,7},{5,4},{4,6},{7,5},{10,11},{9,8},{8,1... | collective-permute-start | bytes 1179656 | tf_op jit(solution)/shard_map/ppermute | solution.py:283
  122.0 2.7 %collective-permute-start.13 = (bf16[768,256]{1,0:T(8,128)(2,1)}, bf16[768,256]{1,0:T(8,128)(2,1)S(1)}, u32[]{:S(2)}, u32[]{:S(2)}) collective-permute-start(bf16[768,256]{1,0:T(8,128)(2,1)} %get-tuple-element.67), channel_id=1, source_target_pairs={{2,1},{1,2},{6,5},{5,6},{10,9},{9,10},{14,13},{13,14},{18,17},{17,... | collective-permute-start | bytes 1179656 | tf_op jit(solution)/shard_map/ppermute | solution.py:284
  124.8 0.7 all_to_all.12
  125.5 9.2 %all-to-all-start.1 = ((f32[64,1,24]{2,1,0:T(1,128)}), f32[64,1,24]{2,1,0:T(1,128)S(1)}, u32[]{:S(2)}, u32[]{:S(2)}) async-start(f32[64,1,24]{2,1,0:T(1,128)} %bitcast.22), calls=%async_computation.1 | async-start | bytes 65536 | tf_op jit(solution)/shard_map/all_to_all | solution.py:286
  134.7 3.3 %shard_map.98 = (bf16[768,256]{1,0:T(8,128)(2,1)}, bf16[768,256]{1,0:T(8,128)(2,1)}) custom-call(s32[10]{0:T(128)S(1)} %stack.47.index, f32[768,256]{1,0:T(8,128)} %get-tuple-element.65.own, bf16[768,256]{1,0:T(8,128)(2,1)S(1)} %collective-permute-done.12.got_a, bf16[768,256]{1,0:T(8,128)(2,1)S(1)} %collective-permute-done.13.got_b, ...), custom_call_target="tpu_custom_call" | custom-call | flops 3000000 | bytes 3500000 | tf_op jit(solution)/shard_map/pallas_call | solution.py:163
  138.0 3.4 %shard_map.99 = bf16[8,384,256]{2,1,0:T(8,128)(2,1)} custom-call(s32[10]{0:T(128)S(1)} %stack.47.index, bf16[8,384,256]{2,1,0:T(8,128)(2,1)} %get-tuple-element.71.mine, bf16[8,384,256]{2,1,0:T(8,128)(2,1)S(1)} %collective-permute-done.14.theirs), custom_call_target="tpu_custom_call" | custom-call | flops 1000000 | bytes 5000000 | tf_op jit(solution)/shard_map/pallas_call | solution.py:131
  141.4 2.7 %all-to-all-done.1 = f32[64,1,24]{2,1,0:T(1,128)S(1)} async-done(((f32[64,1,24]{2,1,0:T(1,128)}), f32[64,1,24]{2,1,0:T(1,128)S(1)}, u32[]{:S(2)}, u32[]{:S(2)}) %all-to-all-start.1) | async-done | bytes 6176 | tf_op jit(solution)/shard_map/all_to_all | solution.py:286
  144.2 0.5 divide_bitcast_fusion
  (22 shorter events, 0.2 us)
Async XLA Ops:
  2.3 27.5 %copy-start.4 = (f32[1,1,768]{2,1,0:T(1,128)S(1)}, f32[1,1,768]{2,1,0:T(1,128)}, u32[]{:S(2)}) copy-start(f32[1,1,768]{2,1,0:T(1,128)} %param.8) | copy-start | bytes 9220
  2.3 27.6 %copy-start.3 = (bf16[1,1,768,256]{3,2,1,0:T(8,128)(2,1)S(1)}, bf16[1,1,768,256]{3,2,1,0:T(8,128)(2,1)}, u32[]{:S(2)}) copy-start(bf16[1,1,768,256]{3,2,1,0:T(8,128)(2,1)} %param.10) | copy-start | bytes 1179652
  2.3 14.3 %collective-permute-start = (bf16[192,194]{0,1:T(8,128)(2,1)S(1)}, bf16[192,194]{0,1:T(8,128)(2,1)S(1)}, u32[]{:S(2)}, u32[]{:S(2)}) collective-permute-start(bf16[192,194]{0,1:T(8,128)(2,1)S(1)} %pad_maximum_fusion), channel_id=1, source_target_pairs={{0,48},{1,50},{2,52},{3,54},{4,56},{5,58},{6,60},{7,62},{8,0},{9,2... | collective-permute-start | bytes 223496 | tf_op jit(solution)/shard_map/ppermute | solution.py:224
  10.7 7.8 %collective-permute-start.1 = (bf16[192,192]{0,1:T(8,128)(2,1)S(1)}, bf16[192,192]{0,1:T(8,128)(2,1)S(1)}, u32[]{:S(2)}, u32[]{:S(2)}) collective-permute-start(bf16[192,192]{0,1:T(8,128)(2,1)S(1)} %bitcast.57), channel_id=1, source_target_pairs={{0,52},{1,54},{2,48},{3,50},{4,60},{5,62},{6,56},{7,58},{8,4},{9,6... | collective-permute-start | bytes 221192 | tf_op jit(solution)/shard_map/ppermute | solution.py:225
  14.7 37.5 %collective-permute-start.6 = (bf16[3072,256]{1,0:T(8,128)(2,1)}, bf16[3072,256]{1,0:T(8,128)(2,1)S(1)}, u32[]{:S(2)}, u32[]{:S(2)}) collective-permute-start(bf16[3072,256]{1,0:T(8,128)(2,1)} %bitcast.35), channel_id=1, source_target_pairs={{0,2},{2,0},{1,3},{3,1},{4,6},{6,4},{5,7},{7,5},{8,10},{10,8},{9,1... | collective-permute-start | bytes 4718600 | tf_op jit(solution)/shard_map/ppermute | solution.py:240
  19.7 32.5 %copy-start = (bf16[1,3072,256]{2,1,0:T(8,128)(2,1)S(1)}, bf16[1,3072,256]{2,1,0:T(8,128)(2,1)}, u32[]{:S(2)}) copy-start(bf16[1,3072,256]{2,1,0:T(8,128)(2,1)} %param.11) | copy-start | bytes 4718596
  19.7 29.7 %all-to-all-start = ((bf16[8,96,384]{2,1,0:T(8,128)(2,1)}), bf16[8,96,384]{2,1,0:T(8,128)(2,1)}, u32[]{:S(2)}, u32[]{:S(2)}) async-start(bf16[8,96,384]{2,1,0:T(8,128)(2,1)} %bitcast.55), calls=%async_computation | async-start | bytes 1179648 | tf_op jit(solution)/shard_map/all_to_all | solution.py:231
  31.2 12.3 %collective-permute-start.2 = (bf16[768,256]{1,0:T(8,128)(2,1)S(1)}, bf16[768,256]{1,0:T(8,128)(2,1)S(1)}, u32[]{:S(2)}, u32[]{:S(2)}) collective-permute-start(bf16[768,256]{1,0:T(8,128)(2,1)S(1)} %fusion.5), channel_id=1, source_target_pairs={{0,0},{1,2},{2,1},{3,3},{4,4},{5,6},{6,5},{7,7},{8,8},{9,10},{10,9... | collective-permute-start | bytes 1179656 | tf_op jit(solution)/shard_map/ppermute | solution.py:247
  37.2 10.4 %collective-permute-start.3 = (bf16[768,256]{1,0:T(8,128)(2,1)S(1)}, bf16[768,256]{1,0:T(8,128)(2,1)S(1)}, u32[]{:S(2)}, u32[]{:S(2)}) collective-permute-start(bf16[768,256]{1,0:T(8,128)(2,1)S(1)} %fusion.5), channel_id=1, source_target_pairs={{0,1},{1,3},{2,0},{3,2},{4,5},{5,7},{6,4},{7,6},{8,9},{9,11},{10,8... | collective-permute-start | bytes 1179656 | tf_op jit(solution)/shard_map/ppermute | solution.py:248
  47.7 0.7 copy-start.1
  49.4 11.2 %collective-permute-start.4 = (bf16[768,384]{1,0:T(8,128)(2,1)}, bf16[768,384]{1,0:T(8,128)(2,1)}, u32[]{:S(2)}, u32[]{:S(2)}) collective-permute-start(bf16[768,384]{1,0:T(8,128)(2,1)} %bitcast.15.refs_0_), channel_id=1, source_target_pairs={{0,8},{2,58},{8,16},{10,2},{16,24},{18,10},{24,32},{26,18},{32,40}... | collective-permute-start | bytes 1769480 | tf_op jit(solution)/shard_map/ppermute | solution.py:258
  52.2 1.0 copy-start.2
  56.5 13.7 %collective-permute-start.7 = (bf16[768,384]{1,0:T(8,128)(2,1)}, bf16[768,384]{1,0:T(8,128)(2,1)S(1)}, u32[]{:S(2)}, u32[]{:S(2)}) collective-permute-start(bf16[768,384]{1,0:T(8,128)(2,1)} %bitcast.15.refs_0_), channel_id=1, source_target_pairs={{0,56},{2,10},{8,0},{10,18},{16,8},{18,26},{24,16},{26,34},{32,24}... | collective-permute-start | bytes 1769480 | tf_op jit(solution)/shard_map/ppermute | solution.py:259
  60.7 15.6 %collective-permute-start.5 = (bf16[768,384]{1,0:T(8,128)(2,1)}, bf16[768,384]{1,0:T(8,128)(2,1)S(1)}, u32[]{:S(2)}, u32[]{:S(2)}) collective-permute-start(bf16[768,384]{1,0:T(8,128)(2,1)} %collective-permute-done.4.refs_0_), channel_id=1, source_target_pairs={{0,8},{2,58},{8,16},{10,2},{16,24},{18,10},{24,32},{26,18},{32,40}... | collective-permute-start | bytes 1769480 | tf_op jit(solution)/shard_map/ppermute | solution.py:258
  70.2 12.4 %collective-permute-start.9 = (bf16[768,384]{1,0:T(8,128)(2,1)S(1)}, bf16[768,384]{1,0:T(8,128)(2,1)S(1)}, u32[]{:S(2)}, u32[]{:S(2)}) collective-permute-start(bf16[768,384]{1,0:T(8,128)(2,1)S(1)} %collective-permute-done.7.refs_1_), channel_id=1, source_target_pairs={{0,56},{2,10},{8,0},{10,18},{16,8},{18,26},{24,16},{26,34},{32,24}... | collective-permute-start | bytes 1769480 | tf_op jit(solution)/shard_map/ppermute | solution.py:259
  76.2 14.5 %collective-permute-start.8 = (bf16[768,384]{1,0:T(8,128)(2,1)S(1)}, bf16[768,384]{1,0:T(8,128)(2,1)S(1)}, u32[]{:S(2)}, u32[]{:S(2)}) collective-permute-start(bf16[768,384]{1,0:T(8,128)(2,1)S(1)} %collective-permute-done.5.refs_0_), channel_id=1, source_target_pairs={{0,8},{2,58},{8,16},{10,2},{16,24},{18,10},{24,32},{26,18},{32,40}... | collective-permute-start | bytes 1769480 | tf_op jit(solution)/shard_map/ppermute | solution.py:258
  82.6 17.6 %collective-permute-start.11 = (bf16[768,384]{1,0:T(8,128)(2,1)S(1)}, bf16[768,384]{1,0:T(8,128)(2,1)S(1)}, u32[]{:S(2)}, u32[]{:S(2)}) collective-permute-start(bf16[768,384]{1,0:T(8,128)(2,1)S(1)} %collective-permute-done.9.refs_1_), channel_id=1, source_target_pairs={{0,56},{2,10},{8,0},{10,18},{16,8},{18,26},{24,16},{26,34},{32,24}... | collective-permute-start | bytes 1769480 | tf_op jit(solution)/shard_map/ppermute | solution.py:259
  90.7 16.2 %collective-permute-start.10 = (bf16[768,384]{1,0:T(8,128)(2,1)S(1)}, bf16[768,384]{1,0:T(8,128)(2,1)S(1)}, u32[]{:S(2)}, u32[]{:S(2)}) collective-permute-start(bf16[768,384]{1,0:T(8,128)(2,1)S(1)} %collective-permute-done.8.refs_0_), channel_id=1, source_target_pairs={{0,8},{2,58},{8,16},{10,2},{16,24},{18,10},{24,32},{26,18},{32,40}... | collective-permute-start | bytes 1769480 | tf_op jit(solution)/shard_map/ppermute | solution.py:258
  109.4 28.5 %collective-permute-start.14 = (bf16[8,384,256]{2,1,0:T(8,128)(2,1)}, bf16[8,384,256]{2,1,0:T(8,128)(2,1)S(1)}, u32[]{:S(2)}, u32[]{:S(2)}) collective-permute-start(bf16[8,384,256]{2,1,0:T(8,128)(2,1)} %get-tuple-element.72), channel_id=1, source_target_pairs={{0,2},{2,0},{1,3},{3,1},{4,6},{6,4},{5,7},{7,5},{8,10},{10,8},{9,1... | collective-permute-start | bytes 4718600 | tf_op jit(solution)/shard_map/ppermute | solution.py:287
  117.8 16.9 %collective-permute-start.12 = (bf16[768,256]{1,0:T(8,128)(2,1)}, bf16[768,256]{1,0:T(8,128)(2,1)S(1)}, u32[]{:S(2)}, u32[]{:S(2)}) collective-permute-start(bf16[768,256]{1,0:T(8,128)(2,1)} %get-tuple-element.66), channel_id=1, source_target_pairs={{2,3},{1,0},{0,2},{3,1},{6,7},{5,4},{4,6},{7,5},{10,11},{9,8},{8,1... | collective-permute-start | bytes 1179656 | tf_op jit(solution)/shard_map/ppermute | solution.py:283
  122.0 12.6 %collective-permute-start.13 = (bf16[768,256]{1,0:T(8,128)(2,1)}, bf16[768,256]{1,0:T(8,128)(2,1)S(1)}, u32[]{:S(2)}, u32[]{:S(2)}) collective-permute-start(bf16[768,256]{1,0:T(8,128)(2,1)} %get-tuple-element.67), channel_id=1, source_target_pairs={{2,1},{1,2},{6,5},{5,6},{10,9},{9,10},{14,13},{13,14},{18,17},{17,... | collective-permute-start | bytes 1179656 | tf_op jit(solution)/shard_map/ppermute | solution.py:284
  125.5 18.7 %all-to-all-start.1 = ((f32[64,1,24]{2,1,0:T(1,128)}), f32[64,1,24]{2,1,0:T(1,128)S(1)}, u32[]{:S(2)}, u32[]{:S(2)}) async-start(f32[64,1,24]{2,1,0:T(1,128)} %bitcast.22), calls=%async_computation.1 | async-start | bytes 65536 | tf_op jit(solution)/shard_map/all_to_all | solution.py:286
